TPU v7x, 32 devices: a whole 2x2x4 slice. The times are simulated.
32 devices in a mesh: dp: 16 (over z, x, core), tensor: 2 (over y).
Axes of the slice: x: 2, y: 2, z: 4, core: 2. Of those that a mesh axis runs over, the one named last changes fastest.
Arguments:
- tokens: bfloat16 [6144, 16384], P('dp', 'tensor'), may hold values from -6 to 6
- cotangent: bfloat16 [6144, 16384], P('dp', 'tensor'), may hold values from -6 to 6
- left_factor: bfloat16 [48, 16384], P('tensor'), may hold values from -0.125 to 0.125
- right_factor: bfloat16 [48, 16384], P('tensor'), may hold values from -0.125 to 0.125
- panel_rank: int32 [2], replicated, may hold values from 1 to 24, as said below
Outputs:
- token_grad: bfloat16 [6144, 16384], P('dp', 'tensor')
- left_grad: float32 [48, 2, 16, 512], P('tensor', None, 'dp')
- right_grad: float32 [48, 2, 16, 512], P('tensor', None, 'dp')
Inputs may be any that keep to these rules, and one draw needn't show every extreme that they name: panel_rank[p] counts the live slots at the start of panel p; at least one panel has all 24 slots live and another has a single live slot.
All inputs are finite; a program needn't handle non-finite values.
Results may differ from a plain program's by a relative error of at most 0.0049.
Values may be sent and summed in bfloat16 or wider, within the bound.
No kernel may reach another device: no remote copies, remote signals or barrier semaphores. Data moves between devices by JAX's collectives and lax.ppermute only.
A program may use at most 128 MiB of HBM per device.

v0:
```python
import math

import jax
import jax.numpy as jnp
from jax import lax
from jax.sharding import PartitionSpec as P


def block_view(home):
    groups = lax.axis_size("tensor")
    width = lax.axis_size("dp")
    block = home.shape[1] // (groups * width)
    return home.reshape(home.shape[0], groups, width, block)


def own_blocks(summed):
    return lax.dynamic_slice_in_dim(summed, lax.axis_index("dp"), 1, 2)


def settle_both(left_cols, right_cols):
    left_home, right_home = (
        lax.all_to_all(left_cols, "tensor", split_axis=0, concat_axis=1, tiled=True),
        lax.all_to_all(right_cols, "tensor", split_axis=0, concat_axis=1, tiled=True),
    )
    left_home = block_view(left_home)
    right_home = block_view(right_home)
    left_sum, right_sum = lax.psum((left_home, right_home), "dp")
    return (own_blocks(left_sum), own_blocks(right_sum))


def local(tokens, cotangent, left_factor, right_factor, panel_rank):
    slot_count = left_factor.shape[0]
    groups = lax.axis_size("tensor")
    all_slots = slot_count * groups
    left_cols, right_cols = (
        lax.all_to_all(left_factor, "tensor", split_axis=1, concat_axis=0, tiled=True),
        lax.all_to_all(right_factor, "tensor", split_axis=1, concat_axis=0, tiled=True),
    )
    slots = jnp.arange(all_slots, dtype=jnp.int32)
    limits = jnp.repeat(panel_rank, slot_count, total_repeat_length=all_slots)
    live_rows = (slots % slot_count < limits).astype(jnp.bfloat16)[:, None]
    left_live = left_cols * live_rows
    right_live = right_cols * live_rows
    feature_dims = (((1,), (1,)), ((), ()))
    hidden_part = lax.dot_general(
        tokens, left_live, feature_dims, preferred_element_type=jnp.float32
    )
    back_part = lax.dot_general(
        cotangent, right_live, feature_dims, preferred_element_type=jnp.float32
    )
    hidden, back_hidden = lax.psum((hidden_part, back_part), "tensor")
    hidden = hidden.astype(jnp.bfloat16)
    back_hidden = back_hidden.astype(jnp.bfloat16)
    grad_scale = 1.0 / math.sqrt(tokens.shape[0] * lax.axis_size("dp"))
    token_dims = (((0,), (0,)), ((), ()))
    right_local = (
        lax.dot_general(hidden, cotangent, token_dims, preferred_element_type=jnp.float32)
        * grad_scale
    )
    left_local = (
        lax.dot_general(back_hidden, tokens, token_dims, preferred_element_type=jnp.float32)
        * grad_scale
    )
    token_grad = jnp.dot(back_hidden, left_live, preferred_element_type=jnp.float32).astype(
        jnp.bfloat16
    )
    left_grad, right_grad = settle_both(left_local, right_local)
    return (token_grad, left_grad, right_grad)


def solution(mesh):
    placed = (P("dp", "tensor"), P("dp", "tensor"), P("tensor", None), P("tensor", None), P())
    return jax.shard_map(
        local,
        mesh=mesh,
        in_specs=placed,
        out_specs=(P("dp", "tensor"), P("tensor", None, "dp", None), P("tensor", None, "dp", None)),
        check_vma=False,
    )
```

profile of v0, /device:TPU:0, one launch (start us, length us, event | category | flops | bytes accessed | tf_op | source)
XLA Modules:
  0.0 218.7 jit_solution(2262517889338961993)
XLA Ops:
  7.2 0.0 copy-start
  7.2 2.2 copy.28
  9.3 4.2 %all-to-all-start.1 = ((bf16[24,2,8192]{2,0,1:T(8,128)(2,1)}), bf16[24,2,8192]{2,0,1:T(8,128)(2,1)S(1)}, u32[]{:S(2)}, u32[]{:S(2)}) async-start(bf16[24,2,8192]{2,0,1:T(8,128)(2,1)} %bitcast.46), calls=%async_computation.1 | async-start | bytes 1572864 | tf_op jit(solution)/shard_map/all_to_all | solution.py:36
  13.6 0.0 copy-done
  13.6 0.0 copy-start.1
  13.6 0.9 copy.29
  14.5 10.6 %all-to-all-done.1 = bf16[24,2,8192]{2,0,1:T(8,128)(2,1)S(1)} async-done(((bf16[24,2,8192]{2,0,1:T(8,128)(2,1)}), bf16[24,2,8192]{2,0,1:T(8,128)(2,1)S(1)}, u32[]{:S(2)}, u32[]{:S(2)}) %all-to-all-start.1) | async-done | bytes 786464 | tf_op jit(solution)/shard_map/all_to_all | solution.py:36
  25.2 3.5 %all-to-all-start = ((bf16[24,2,8192]{2,0,1:T(8,128)(2,1)}), bf16[24,2,8192]{2,0,1:T(8,128)(2,1)S(1)}, u32[]{:S(2)}, u32[]{:S(2)}) async-start(bf16[24,2,8192]{2,0,1:T(8,128)(2,1)} %bitcast.47), calls=%async_computation | async-start | bytes 1572864 | tf_op jit(solution)/shard_map/all_to_all | solution.py:37
  28.7 0.0 copy-done.1
  28.7 0.6 fusion.3
  29.3 0.0 copy-done.2
  29.3 1.3 compare_convert_fusion
  30.6 8.6 %all-to-all-done = bf16[24,2,8192]{2,0,1:T(8,128)(2,1)S(1)} async-done(((bf16[24,2,8192]{2,0,1:T(8,128)(2,1)}), bf16[24,2,8192]{2,0,1:T(8,128)(2,1)S(1)}, u32[]{:S(2)}, u32[]{:S(2)}) %all-to-all-start) | async-done | bytes 786464 | tf_op jit(solution)/shard_map/all_to_all | solution.py:37
  39.2 0.2 bitcast_multiply_fusion.1
  39.4 4.7 %convolution_bitcast_fusion.1 = f32[384,48]{0,1:T(8,128)S(1)} fusion(bf16[48,8192]{1,0:T(8,128)(2,1)S(1)} %get-tuple-element.19, bf16[384,8192]{1,0:T(8,128)(2,1)} %param.8), kind=kOutput, calls=%fused_computation.4 | convolution fusion | flops 301989888 | bytes 7151616 | tf_op jit(solution)/shard_map/dot_general | solution.py:48
  44.1 4.7 %convolution_bitcast_fusion = f32[384,48]{0,1:T(8,128)S(1)} fusion(bf16[48,8192]{1,0:T(8,128)(2,1)S(1)} %get-tuple-element.20, bf16[384,8192]{1,0:T(8,128)(2,1)} %param.7), kind=kOutput, calls=%fused_computation.3 | convolution fusion | flops 301989888 | bytes 7151616 | tf_op jit(solution)/shard_map/dot_general | solution.py:45
  48.9 8.9 %all-reduce.6 = (bf16[384,48]{0,1:T(8,128)(2,1)S(1)}, bf16[384,48]{0,1:T(8,128)(2,1)S(1)}) all-reduce(f32[384,48]{0,1:T(8,128)S(1)} %convolution_bitcast_fusion.1, f32[384,48]{0,1:T(8,128)S(1)} %convolution_bitcast_fusion), channel_id=1, replica_groups=mesh['dp'=16,'tensor'=2] {'tensor'}, use_global_device_ids=true, to_apply=%region_0.1 | all-reduce | flops 36864 | bytes 221184 | tf_op jit(solution)/shard_map/psum | solution.py:51
  57.8 5.2 %convolution_multiply_fusion = f32[48,8192]{1,0:T(8,128)} fusion(bf16[384,8192]{1,0:T(8,128)(2,1)} %param.8, bf16[384,48]{0,1:T(8,128)(2,1)S(1)} %get-tuple-element.18), kind=kOutput, calls=%fused_computation.1 | convolution fusion | flops 302383104 | bytes 7901184 | tf_op jit(solution)/shard_map/dot_general | solution.py:57
  62.9 3.7 %all-to-all-start.3 = ((f32[2,24,8192]{2,1,0:T(8,128)}), f32[2,24,8192]{2,1,0:T(8,128)S(1)}, u32[]{:S(2)}, u32[]{:S(2)}) async-start(f32[2,24,8192]{2,1,0:T(8,128)} %bitcast.50), calls=%async_computation.3 | async-start | bytes 3145728 | tf_op jit(solution)/shard_map/all_to_all | solution.py:23
  66.6 5.2 %convolution_multiply_fusion.1 = f32[48,8192]{1,0:T(8,128)} fusion(bf16[384,8192]{1,0:T(8,128)(2,1)} %param.7, bf16[384,48]{0,1:T(8,128)(2,1)S(1)} %get-tuple-element.17), kind=kOutput, calls=%fused_computation.2 | convolution fusion | flops 302383104 | bytes 7901184 | tf_op jit(solution)/shard_map/dot_general | solution.py:61
  71.8 11.4 %all-to-all-done.3 = f32[2,24,8192]{2,1,0:T(8,128)S(1)} async-done(((f32[2,24,8192]{2,1,0:T(8,128)}), f32[2,24,8192]{2,1,0:T(8,128)S(1)}, u32[]{:S(2)}, u32[]{:S(2)}) %all-to-all-start.3) | async-done | bytes 1572896 | tf_op jit(solution)/shard_map/all_to_all | solution.py:23
  83.2 4.6 %all-to-all-start.2 = ((f32[2,24,8192]{2,1,0:T(8,128)}), f32[2,24,8192]{2,1,0:T(8,128)}, u32[]{:S(2)}, u32[]{:S(2)}) async-start(f32[2,24,8192]{2,1,0:T(8,128)} %bitcast.49), calls=%async_computation.2 | async-start | bytes 3145728 | tf_op jit(solution)/shard_map/all_to_all | solution.py:22
  87.8 0.0 all-reduce.5.cloned.1.call-start
  87.9 0.9 copy.25
  88.8 1.3 copy.21
  90.1 13.5 %all-to-all-done.2 = f32[2,24,8192]{2,1,0:T(8,128)} async-done(((f32[2,24,8192]{2,1,0:T(8,128)}), f32[2,24,8192]{2,1,0:T(8,128)}, u32[]{:S(2)}, u32[]{:S(2)}) %all-to-all-start.2) | async-done | bytes 1572896 | tf_op jit(solution)/shard_map/all_to_all | solution.py:22
  103.6 2.3 %copy.24 = f32[6,8,16,512]{3,2,1,0:T(8,128)S(1)} copy(f32[6,8,16,512]{3,1,2,0:T(8,128)} %bitcast.20) | data formatting | bytes 3145728
  105.9 1.3 copy.20
  107.2 0.0 all-reduce.5.cloned.1.call-update
  107.2 4.5 %convolution_convert_fusion = bf16[384,8192]{1,0:T(8,128)(2,1)} fusion(bf16[48,8192]{1,0:T(8,128)(2,1)S(1)} %get-tuple-element.20, bf16[384,48]{0,1:T(8,128)(2,1)S(1)} %get-tuple-element.17), kind=kOutput, calls=%fused_computation | convolution fusion | flops 305135616 | bytes 7114752 | tf_op jit(solution)/shard_map/dot_general | solution.py:64
  111.8 97.9 %all-reduce.5.cloned.1.call-done = (f32[24,2,16,512]{3,2,1,0:T(8,128)}, f32[24,2,16,512]{3,2,1,0:T(8,128)}) async-done(((f32[24,2,16,512]{3,2,1,0:T(8,128)}, f32[24,2,16,512]{3,2,1,0:T(8,128)}), (f32[24,2,16,512]{3,2,1,0:T(8,128)}, f32[24,2,16,512]{3,2,1,0:T(8,128)})) %all-reduce.5.cloned.1.call-update) | async-done | bytes 3145744 | tf_op jit(solution)/shard_map/psum | solution.py:27
  209.6 2.2 %constant_dynamic-slice_fusion = (f32[24,2,1,512]{3,2,1,0:T(1,128)}, f32[24,2,1,512]{3,2,1,0:T(1,128)}) fusion(f32[24,2,16,512]{3,2,1,0:T(8,128)} %get-tuple-element.16, s32[]{:T(128)S(6)} %select_n.28, f32[24,2,16,512]{3,2,1,0:T(8,128)} %get-tuple-element.15), kind=kLoop, calls=%fused_computation.14 | loop fusion | bytes 393220 | tf_op jit(solution)/shard_map/dynamic_slice | solution.py:17
  (1 shorter events, 0.0 us)
Async XLA Ops:
  7.2 6.4 %copy-start = (bf16[24,16384]{1,0:T(8,128)(2,1)S(1)}, bf16[24,16384]{1,0:T(8,128)(2,1)}, u32[]{:S(2)}) copy-start(bf16[24,16384]{1,0:T(8,128)(2,1)} %param.10) | copy-start | bytes 2359300
  9.3 15.8 %all-to-all-start.1 = ((bf16[24,2,8192]{2,0,1:T(8,128)(2,1)}), bf16[24,2,8192]{2,0,1:T(8,128)(2,1)S(1)}, u32[]{:S(2)}, u32[]{:S(2)}) async-start(bf16[24,2,8192]{2,0,1:T(8,128)(2,1)} %bitcast.46), calls=%async_computation.1 | async-start | bytes 1572864 | tf_op jit(solution)/shard_map/all_to_all | solution.py:36
  13.6 15.1 %copy-start.1 = (s32[2]{0:T(128)S(1)}, s32[2]{0:T(128)}, u32[]{:S(2)}) copy-start(s32[2]{0:T(128)} %param.11) | copy-start | bytes 28
  13.6 15.7 %copy-start.2 = (pred[48]{0:T(512)(128)(4,1)S(1)}, pred[48]{0:T(512)(128)(4,1)}, u32[]{:S(2)}) copy-start(pred[48]{0:T(512)(128)(4,1)} %constant.102) | copy-start | bytes 148
  25.2 14.0 %all-to-all-start = ((bf16[24,2,8192]{2,0,1:T(8,128)(2,1)}), bf16[24,2,8192]{2,0,1:T(8,128)(2,1)S(1)}, u32[]{:S(2)}, u32[]{:S(2)}) async-start(bf16[24,2,8192]{2,0,1:T(8,128)(2,1)} %bitcast.47), calls=%async_computation | async-start | bytes 1572864 | tf_op jit(solution)/shard_map/all_to_all | solution.py:37
  62.9 20.3 %all-to-all-start.3 = ((f32[2,24,8192]{2,1,0:T(8,128)}), f32[2,24,8192]{2,1,0:T(8,128)S(1)}, u32[]{:S(2)}, u32[]{:S(2)}) async-start(f32[2,24,8192]{2,1,0:T(8,128)} %bitcast.50), calls=%async_computation.3 | async-start | bytes 3145728 | tf_op jit(solution)/shard_map/all_to_all | solution.py:23
  83.2 20.4 %all-to-all-start.2 = ((f32[2,24,8192]{2,1,0:T(8,128)}), f32[2,24,8192]{2,1,0:T(8,128)}, u32[]{:S(2)}, u32[]{:S(2)}) async-start(f32[2,24,8192]{2,1,0:T(8,128)} %bitcast.49), calls=%async_computation.2 | async-start | bytes 3145728 | tf_op jit(solution)/shard_map/all_to_all | solution.py:22
  87.8 121.8 %all-reduce.5.cloned.1.call-start = ((), (), s32[]{:S(2)}) async-start(), calls=%async_computation.4 | async-start | bytes 6291456 | tf_op jit(solution)/shard_map/psum | solution.py:27
Sparse Core Ops, SparseCore 0:
  107.4 102.2 all-reduce.4
where the time goes:
time: 219 us
  waiting for transfers between devices  142 us (65%)
  matrix products  24.3 us (11%)
  starting transfers between devices  16.1 us (7%)
  between operations  14.1 us (6%)
  local copies, waits for them, and re-layouts  11.8 us (5%)
  blocking collectives  8.86 us (4%)
    psum x1, waiting for transfers between devices, settle_both(): left_sum, right_sum = lax.psum((left_home, right_home), 'dp')  97.9 us
    all_to_all x1, waiting for transfers between devices, settle_both(): lax.all_to_all(left_cols, 'tensor', split_axis=0, concat_axis=1, tiled=True)  13.5 us
    all_to_all x1, waiting for transfers between devices, settle_both(): lax.all_to_all(right_cols, 'tensor', split_axis=0, concat_axis=1, tiled=T...  11.4 us
    all_to_all x1, waiting for transfers between devices, local(): lax.all_to_all(left_factor, 'tensor', split_axis=1, concat_axis=0, tiled=...  10.6 us
    psum x1, blocking collectives, local(): hidden, back_hidden = lax.psum((hidden_part, back_part), 'tensor')  8.86 us
    all_to_all x1, waiting for transfers between devices, local(): lax.all_to_all(right_factor, 'tensor', split_axis=1, concat_axis=0, tiled...  8.59 us
    dot_general x1, matrix products, local(): lax.dot_general(hidden, cotangent, token_dims, preferred_element_type=jnp...  5.19 us
    dot_general x1, matrix products, local(): lax.dot_general(back_hidden, tokens, token_dims, preferred_element_type=j...  5.16 us
  transfers between devices with their start and end apart: 5, of which 5 were waited for; matrix products, arithmetic and copies ran while one was open for 7% of the time, Pallas kernels for 0%

commit v1 on v0

--- a/solution.py
+++ b/solution.py
@@ -1,8 +1,11 @@
+import functools
 import math
 
 import jax
 import jax.numpy as jnp
 from jax import lax
+from jax.experimental import pallas as pl
+from jax.experimental.pallas import tpu as pltpu
 from jax.sharding import PartitionSpec as P
 
 
@@ -28,7 +31,7 @@
     return (own_blocks(left_sum), own_blocks(right_sum))
 
 
-def local(tokens, cotangent, left_factor, right_factor, panel_rank):
+def any_panels(tokens, cotangent, left_factor, right_factor, panel_rank):
     slot_count = left_factor.shape[0]
     groups = lax.axis_size("tensor")
     all_slots = slot_count * groups
@@ -68,10 +71,208 @@
     return (token_grad, left_grad, right_grad)
 
 
+PAD = 8
+SWAP = [(0, 1), (1, 0)]
+VMEM_LIMIT = 40 * 1024 * 1024
+
+
+def flip(value, bit):
+    size = lax.axis_size("dp")
+    return lax.ppermute(value, "dp", [(i, i ^ (1 << bit)) for i in range(size)])
+
+
+def live_rows_of(own, other, own_is_full):
+    first = lax.broadcasted_iota(jnp.int32, (PAD, own.shape[1]), 0) == 0
+    full = jnp.where(own_is_full, own, other)
+    short = jnp.where(own_is_full, other[:PAD], own[:PAD])
+    short = jnp.where(first, short, jnp.zeros_like(short))
+    return jnp.concatenate([full, short], axis=0)
+
+
+def project_kernel(half, flags, own, mine, theirs, rows_in, live_out, part_out):
+    step = pl.program_id(0)
+    other = jnp.where(flags[1] == step // half, mine[...], theirs[...])
+    live = live_rows_of(own[...], other, flags[2] == 1)
+    live_out[...] = live
+
+    @pl.when(step == 0)
+    def _():
+        part_out[...] = jnp.zeros_like(part_out)
+
+    part_out[...] += lax.dot_general(
+        live, rows_in[...], (((1,), (1,)), ((), ())), preferred_element_type=jnp.float32
+    )
+
+
+def project(flags, factor, mine, theirs, acts):
+    slots = factor.shape[0]
+    tokens, width = acts.shape
+    live = slots + PAD
+    steps = 4
+    half = steps // 2
+    chunk = width // steps
+    return pl.pallas_call(
+        functools.partial(project_kernel, half),
+        grid_spec=pltpu.PrefetchScalarGridSpec(
+            num_scalar_prefetch=1,
+            grid=(steps,),
+            in_specs=[
+                pl.BlockSpec((slots, chunk), lambda k, f: (0, f[0] * steps + k)),
+                pl.BlockSpec((slots, chunk), lambda k, f: (0, k % half)),
+                pl.BlockSpec((slots, chunk), lambda k, f: (0, k % half)),
+                pl.BlockSpec((tokens, chunk), lambda k, f: (0, k)),
+            ],
+            out_specs=[
+                pl.BlockSpec((live, chunk), lambda k, f: (0, k)),
+                pl.BlockSpec((live, tokens), lambda k, f: (0, 0)),
+            ],
+        ),
+        out_shape=[
+            jax.ShapeDtypeStruct((live, width), jnp.bfloat16),
+            jax.ShapeDtypeStruct((live, tokens), jnp.float32),
+        ],
+        compiler_params=pltpu.CompilerParams(vmem_limit_bytes=VMEM_LIMIT),
+        cost_estimate=pl.CostEstimate(
+            flops=2 * live * width * tokens, bytes_accessed=2 * width * tokens, transcendentals=0
+        ),
+        name="project",
+    )(flags, factor, mine, theirs, acts)
+
+
+def gradient_kernel(scale, flags, hidden, acts, keep, send):
+    block = keep.shape[2]
+    grad = jnp.dot(hidden[...], acts[...], preferred_element_type=jnp.float32) * scale
+    low, high = grad[:, :block], grad[:, block:]
+    even = flags[1] == 0
+    keep[...] = jnp.where(even, low, high)[None]
+    send[...] = jnp.where(even, high, low).astype(send.dtype)[None]
+
+
+def gradient(flags, hidden, acts, scale):
+    live, tokens = hidden.shape
+    width = acts.shape[1]
+    size = lax.axis_size("dp")
+    bits = size.bit_length() - 1
+    block = width // size
+    pairs = size // 2
+
+    def place(j, f):
+        q = 0
+        for bit in range(bits - 1):
+            q = q * 2 + (j // (1 << bit)) % 2
+        return (q, 0, 0)
+
+    return pl.pallas_call(
+        functools.partial(gradient_kernel, scale),
+        grid_spec=pltpu.PrefetchScalarGridSpec(
+            num_scalar_prefetch=1,
+            grid=(pairs,),
+            in_specs=[
+                pl.BlockSpec((live, tokens), lambda j, f: (0, 0)),
+                pl.BlockSpec((tokens, 2 * block), lambda j, f: (0, j)),
+            ],
+            out_specs=[
+                pl.BlockSpec((1, live, block), place),
+                pl.BlockSpec((1, live, block), place),
+            ],
+        ),
+        out_shape=[
+            jax.ShapeDtypeStruct((pairs, live, block), jnp.float32),
+            jax.ShapeDtypeStruct((pairs, live, block), jnp.bfloat16),
+        ],
+        compiler_params=pltpu.CompilerParams(vmem_limit_bytes=VMEM_LIMIT),
+        cost_estimate=pl.CostEstimate(
+            flops=2 * live * width * tokens, bytes_accessed=2 * width * tokens, transcendentals=0
+        ),
+        name="gradient",
+    )(flags, hidden, acts)
+
+
+def spread_kernel(back, live, out):
+    out[...] = lax.dot_general(
+        back[...], live[...], (((0,), (0,)), ((), ())), preferred_element_type=jnp.float32
+    ).astype(out.dtype)
+
+
+def spread(back, live):
+    rows, tokens = back.shape
+    width = live.shape[1]
+    steps = 8
+    chunk = width // steps
+    return pl.pallas_call(
+        spread_kernel,
+        grid=(steps,),
+        in_specs=[
+            pl.BlockSpec((rows, tokens), lambda k: (0, 0)),
+            pl.BlockSpec((rows, chunk), lambda k: (0, k)),
+        ],
+        out_specs=pl.BlockSpec((tokens, chunk), lambda k: (0, k)),
+        out_shape=jax.ShapeDtypeStruct((tokens, width), jnp.bfloat16),
+        compiler_params=pltpu.CompilerParams(vmem_limit_bytes=VMEM_LIMIT),
+        cost_estimate=pl.CostEstimate(
+            flops=2 * rows * width * tokens, bytes_accessed=2 * width * tokens, transcendentals=0
+        ),
+        name="spread",
+    )(back, live)
+
+
+def fetch(factor, tensor, core):
+    width = factor.shape[1] // 2
+    part = width // 2
+    wanted = lax.dynamic_slice_in_dim(factor, (1 - tensor) * width + core * part, part, 1)
+    mine = lax.ppermute(wanted, "tensor", SWAP)
+    return mine, flip(mine, 0)
+
+
+def halve(keep, send, position):
+    bits = lax.axis_size("dp").bit_length() - 1
+    for bit in range(bits):
+        total = keep + flip(send, bit).astype(jnp.float32)
+        if bit == bits - 1:
+            return total[0]
+        low, high = jnp.split(total, 2, axis=0)
+        even = (position >> (bit + 1)) % 2 == 0
+        keep = jnp.where(even, low, high)
+        send = jnp.where(even, high, low).astype(jnp.bfloat16)
+
+
+def two_panels(tokens, cotangent, left_factor, right_factor, panel_rank):
+    slots = left_factor.shape[0]
+    position = lax.axis_index("dp")
+    tensor = lax.axis_index("tensor")
+    core = position % 2
+    own_is_full = jnp.where(tensor == 0, panel_rank[0], panel_rank[1]) == slots
+    flags = jnp.stack([tensor, core, own_is_full.astype(jnp.int32)]).astype(jnp.int32)
+    scale = 1.0 / math.sqrt(tokens.shape[0] * lax.axis_size("dp"))
+
+    right_mine, right_theirs = fetch(right_factor, tensor, core)
+    left_mine, left_theirs = fetch(left_factor, tensor, core)
+    _, back_part = project(flags, right_factor, right_mine, right_theirs, cotangent)
+    left_live, hidden_part = project(flags, left_factor, left_mine, left_theirs, tokens)
+    back = (back_part + lax.ppermute(back_part, "tensor", SWAP)).astype(jnp.bfloat16)
+    hidden = (hidden_part + lax.ppermute(hidden_part, "tensor", SWAP)).astype(jnp.bfloat16)
+    left_total = halve(*gradient(flags, back, tokens, scale), position)
+    right_total = halve(*gradient(flags, hidden, cotangent, scale), position)
+    token_grad = spread(back, left_live)
+
+    total = jnp.stack([left_total, right_total])
+    first = (jnp.arange(slots) == 0)[None, :, None]
+    full = total[:, :slots]
+    short = jnp.where(first, total[:, slots : slots + 1], 0.0)
+    got = lax.ppermute(jnp.where(own_is_full, short, full), "tensor", SWAP)
+    held = jnp.where(own_is_full, full, short)
+    low = jnp.where(tensor == 0, held, got)
+    high = jnp.where(tensor == 0, got, held)
+    grads = jnp.stack([low, high], axis=2)[:, :, :, None, :]
+    return token_grad, grads[0], grads[1]
+
+
 def solution(mesh):
     placed = (P("dp", "tensor"), P("dp", "tensor"), P("tensor", None), P("tensor", None), P())
+    size = mesh.shape["dp"]
+    halves = size & (size - 1) == 0 and size >= 4
     return jax.shard_map(
-        local,
+        two_panels if mesh.shape["tensor"] == 2 and halves else any_panels,
         mesh=mesh,
         in_specs=placed,
         out_specs=(P("dp", "tensor"), P("tensor", None, "dp", None), P("tensor", None, "dp", None)),

time: 219 us -> 68.8 us (0.31)
  waiting for transfers between devices: 142 us -> 15.4 us
  matrix products: 24.3 us -> 0 us
  Pallas kernels: 0 us -> 19.5 us
  between operations: 14.1 us -> 2.21 us
  blocking collectives: 8.86 us -> 0 us
  starting transfers between devices: 16.1 us -> 18.9 us
    psum x1 -> x0, waiting for transfers between devices: 97.9 us -> none  [settle_both(): left_sum, right_sum = lax.psum((left_home, right_home), 'dp')]
    all_to_all x4 -> x0, waiting for transfers between devices: 44.1 us -> none  [the longest x1 13.5 us: settle_both(): lax.all_to_all(left_cols, 'tensor', split_axis=0, concat_axis=1, tiled=True)]
    dot_general x5 -> x0, matrix products: 24.3 us -> none  [the longest x1 5.19 us: local(): lax.dot_general(hidden, cotangent, token_dims, preferred_element_type=jnp...]
    pallas_call x0 -> x5, Pallas kernels: none -> 19.5 us  [the longest x2 7.75 us: project(): pl.pallas_call(functools.partial(project_kernel, half), grid_spec=pltpu.P...]
    ppermute x0 -> x15, starting transfers between devices: none -> 18.9 us  [the longest x10 11.5 us: flip(): return lax.ppermute(value, 'dp', [(i, i ^ 1 << bit) for i in range(size)])]
    all_to_all x4 -> x0, starting transfers between devices: 16 us -> none  [the longest x1 4.61 us: settle_both(): lax.all_to_all(left_cols, 'tensor', split_axis=0, concat_axis=1, tiled=True)]
    ppermute x0 -> x15, waiting for transfers between devices: none -> 15.4 us  [the longest x2 8.08 us: fetch(): mine = lax.ppermute(wanted, 'tensor', SWAP)]
    psum x1 -> x0, blocking collectives: 8.86 us -> none  [local(): hidden, back_hidden = lax.psum((hidden_part, back_part), 'tensor')]
  transfers between devices with their start and end apart: 5 -> 15, of which waited for: 5 -> 7; matrix products, arithmetic and copies ran while one was open for 7% -> 4% of each run, Pallas kernels for 0% -> 28%
where the time goes in v1:
time: 68.8 us; the launch traced here: 68.6 us
  Pallas kernels  19.5 us (28%)
  starting transfers between devices  18.9 us (27%)
  waiting for transfers between devices  15.4 us (22%)
  local copies, waits for them, and re-layouts  11.9 us (17%)
  between operations  2.21 us (3%)
  other arithmetic  0.71 us (1%)
    ppermute x10, starting transfers between devices, flip(): return lax.ppermute(value, 'dp', [(i, i ^ 1 << bit) for i in range(size)])  11.5 us
    unnamed x13, local copies, waits for them, and re-layouts  8.66 us
    ppermute x2, waiting for transfers between devices, fetch(): mine = lax.ppermute(wanted, 'tensor', SWAP)  8.08 us
    pallas_call x2, Pallas kernels, project(): pl.pallas_call(functools.partial(project_kernel, half), grid_spec=pltpu.P...  7.75 us
    ppermute x10, waiting for transfers between devices, flip(): return lax.ppermute(value, 'dp', [(i, i ^ 1 << bit) for i in range(size)])  6.77 us
    pallas_call x2, Pallas kernels, gradient(): pl.pallas_call(functools.partial(gradient_kernel, scale), grid_spec=pltpu...  6.23 us
    pallas_call x1, Pallas kernels, spread(): pl.pallas_call(spread_kernel, grid=(steps,), in_specs=[pl.BlockSpec((rows...  5.48 us
    ppermute x2, starting transfers between devices, fetch(): mine = lax.ppermute(wanted, 'tensor', SWAP)  3.12 us
  transfers between devices with their start and end apart: 15, of which 7 were waited for; matrix products, arithmetic and copies ran while one was open for 4% of the time, Pallas kernels for 28%

profile of v1, /device:TPU:0, one launch (start us, length us, event | category | flops | bytes accessed | tf_op | source)
XLA Modules:
  0.0 68.6 jit_solution(2646969241791217029)
XLA Ops:
  0.7 1.0 %constant_dynamic-slice_fusion.1 = bf16[24,4096]{1,0:T(8,128)(2,1)S(1)} fusion(bf16[24,16384]{1,0:T(8,128)(2,1)} %own.2, s32[]{:T(128)S(6)} %select_n.120), kind=kLoop, calls=%fused_computation.34 | loop fusion | bytes 393220 | tf_op jit(solution)/shard_map/dynamic_slice | solution.py:222
  1.7 3.0 %collective-permute-start = (bf16[24,4096]{1,0:T(8,128)(2,1)S(1)}, bf16[24,4096]{1,0:T(8,128)(2,1)S(1)}, u32[]{:S(2)}, u32[]{:S(2)}) collective-permute-start(bf16[24,4096]{1,0:T(8,128)(2,1)S(1)} %constant_dynamic-slice_fusion.1), channel_id=1, source_target_pairs={{0,1},{1,0},{2,3},{3,2},{4,5},{5,4},{6,7},{7,6},{8,9},{9,8},{10,11... | collective-permute-start | bytes 589832 | tf_op jit(solution)/shard_map/ppermute | solution.py:223
  4.7 0.9 %constant_dynamic-slice_fusion = bf16[24,4096]{1,0:T(8,128)(2,1)S(1)} fusion(bf16[24,16384]{1,0:T(8,128)(2,1)} %own.3, s32[]{:T(128)S(6)} %select_n.120), kind=kLoop, calls=%fused_computation.33 | loop fusion | bytes 393220 | tf_op jit(solution)/shard_map/dynamic_slice | solution.py:222
  5.7 0.1 collective-permute-start.3
  5.7 4.7 %collective-permute-done.mine = bf16[24,4096]{1,0:T(8,128)(2,1)S(1)} collective-permute-done((bf16[24,4096]{1,0:T(8,128)(2,1)S(1)}, bf16[24,4096]{1,0:T(8,128)(2,1)S(1)}, u32[]{:S(2)}, u32[]{:S(2)}) %collective-permute-start) | collective-permute-done | bytes 196640 | tf_op jit(solution)/shard_map/ppermute | solution.py:223
  10.4 3.4 %collective-permute-done.3.mine = bf16[24,4096]{1,0:T(8,128)(2,1)S(1)} collective-permute-done((bf16[24,4096]{1,0:T(8,128)(2,1)S(1)}, bf16[24,4096]{1,0:T(8,128)(2,1)S(1)}, u32[]{:S(2)}, u32[]{:S(2)}) %collective-permute-start.3) | collective-permute-done | bytes 196640 | tf_op jit(solution)/shard_map/ppermute | solution.py:223
  13.8 1.3 %fusion.4 = (s32[1]{0:T(128)}, s32[1]{0:T(128)}) fusion(s32[2]{0:T(128)} %param.9), kind=kLoop, calls=%fused_computation.35 | loop fusion | bytes 16 | tf_op jit(solution)/shard_map/slice | solution.py:244
  16.5 2.9 %copy-done.1 = bf16[384,8192]{1,0:T(8,128)(2,1)S(1)} copy-done((bf16[384,8192]{1,0:T(8,128)(2,1)S(1)}, bf16[384,8192]{1,0:T(8,128)(2,1)}, u32[]{:S(2)}) %copy-start.1) | copy-done | bytes 6291480
  19.5 1.4 %copy-done.3 = bf16[24,16384]{1,0:T(8,128)(2,1)S(1)} copy-done((bf16[24,16384]{1,0:T(8,128)(2,1)S(1)}, bf16[24,16384]{1,0:T(8,128)(2,1)}, u32[]{:S(2)}) %copy-start.3) | copy-done | bytes 786456
  20.9 3.6 %project.3 = (bf16[32,8192]{1,0:T(8,128)(2,1)S(1)}, f32[32,384]{1,0:T(8,128)S(1)}) custom-call(s32[3]{0:T(128)S(1)} %pad_add_fusion.flags, bf16[24,16384]{1,0:T(8,128)(2,1)S(1)} %copy-done.3, bf16[24,4096]{1,0:T(8,128)(2,1)S(1)} %collective-permute-done.3.mine, bf16[24,4096]{1,0:T(8,128)(2,1)S(1)} %collective-permute-done.4.theirs, ...), custom_call_target="tpu_custom_call" | custom-call | flops 201326592 | bytes 6291456 | tf_op jit(solution)/shard_map/project/pallas_call | solution.py:114
  24.6 1.8 %collective-permute-start.9 = (f32[32,384]{1,0:T(8,128)S(1)}, f32[32,384]{1,0:T(8,128)S(1)}, u32[]{:S(2)}, u32[]{:S(2)}) collective-permute-start(f32[32,384]{1,0:T(8,128)S(1)} %get-tuple-element.14), channel_id=1, source_target_pairs={{0,1},{1,0},{2,3},{3,2},{4,5},{5,4},{6,7},{7,6},{8,9},{9,8},{10,11... | collective-permute-start | bytes 147464 | tf_op jit(solution)/shard_map/ppermute | solution.py:253
  26.4 4.1 %project.2 = (bf16[32,8192]{1,0:T(8,128)(2,1)}, f32[32,384]{1,0:T(8,128)S(1)}) custom-call(s32[3]{0:T(128)S(1)} %pad_add_fusion.flags, bf16[24,16384]{1,0:T(8,128)(2,1)S(1)} %copy-done.4, bf16[24,4096]{1,0:T(8,128)(2,1)S(1)} %collective-permute-done.mine, bf16[24,4096]{1,0:T(8,128)(2,1)S(1)} %collective-permute-done.1.theirs, bf16[384,8192]{1,0:T(8,128)(2,1)S(1)} %copy-done), custom_call_target="tpu_custom_call" | custom-call | flops 201326592 | bytes 6291456 | tf_op jit(solution)/shard_map/project/pallas_call | solution.py:114
  30.5 0.3 collective-permute-start.2
  30.8 3.1 %gradient.3 = (f32[8,32,512]{2,1,0:T(8,128)S(1)}, bf16[8,32,512]{2,1,0:T(8,128)(2,1)S(1)}) custom-call(s32[3]{0:T(128)S(1)} %pad_add_fusion.flags, bf16[32,384]{1,0:T(8,128)(2,1)S(1)} %add_convert_fusion.hidden, bf16[384,8192]{1,0:T(8,128)(2,1)S(1)} %copy-done), custom_call_target="tpu_custom_call" | custom-call | flops 201326592 | bytes 6291456 | tf_op jit(solution)/shard_map/gradient/pallas_call | solution.py:165
  34.0 0.5 collective-permute-done.2
  34.6 2.8 %copy-done.2 = bf16[384,8192]{1,0:T(8,128)(2,1)S(1)} copy-done((bf16[384,8192]{1,0:T(8,128)(2,1)S(1)}, bf16[384,8192]{1,0:T(8,128)(2,1)}, u32[]{:S(2)}) %copy-start.2) | copy-done | bytes 6291480
  37.4 3.1 %gradient.2 = (f32[8,32,512]{2,1,0:T(8,128)S(1)}, bf16[8,32,512]{2,1,0:T(8,128)(2,1)S(1)}) custom-call(s32[3]{0:T(128)S(1)} %pad_add_fusion.flags, bf16[32,384]{1,0:T(8,128)(2,1)S(1)} %add_convert_fusion.1.back.hidden, bf16[384,8192]{1,0:T(8,128)(2,1)S(1)} %copy-done.2), custom_call_target="tpu_custom_call" | custom-call | flops 201326592 | bytes 6291456 | tf_op jit(solution)/shard_map/gradient/pallas_call | solution.py:165
  40.7 1.7 %collective-permute-start.11 = (bf16[4,32,512]{2,1,0:T(8,128)(2,1)S(1)}, bf16[4,32,512]{2,1,0:T(8,128)(2,1)S(1)}, u32[]{:S(2)}, u32[]{:S(2)}) collective-permute-start(bf16[4,32,512]{2,1,0:T(8,128)(2,1)S(1)} %select_convert_fusion), channel_id=1, source_target_pairs={{0,4},{2,6},{4,0},{6,2},{8,12},{10,14},{12,8},{14,10},{16,20},{18,... | collective-permute-start | bytes 393224 | tf_op jit(solution)/shard_map/ppermute | solution.py:81
  42.5 1.3 %collective-permute-start.6 = (bf16[4,32,512]{2,1,0:T(8,128)(2,1)S(1)}, bf16[4,32,512]{2,1,0:T(8,128)(2,1)S(1)}, u32[]{:S(2)}, u32[]{:S(2)}) collective-permute-start(bf16[4,32,512]{2,1,0:T(8,128)(2,1)S(1)} %select_convert_fusion.1), channel_id=1, source_target_pairs={{0,4},{2,6},{4,0},{6,2},{8,12},{10,14},{12,8},{14,10},{16,20},{18,... | collective-permute-start | bytes 393224 | tf_op jit(solution)/shard_map/ppermute | solution.py:81
  43.8 3.3 %collective-permute-done.11 = bf16[4,32,512]{2,1,0:T(8,128)(2,1)S(1)} collective-permute-done((bf16[4,32,512]{2,1,0:T(8,128)(2,1)S(1)}, bf16[4,32,512]{2,1,0:T(8,128)(2,1)S(1)}, u32[]{:S(2)}, u32[]{:S(2)}) %collective-permute-start.11) | collective-permute-done | bytes 131104 | tf_op jit(solution)/shard_map/ppermute | solution.py:81
  47.1 1.8 %collective-permute-start.12 = (bf16[2,32,512]{2,1,0:T(8,128)(2,1)S(1)}, bf16[2,32,512]{2,1,0:T(8,128)(2,1)S(1)}, u32[]{:S(2)}, u32[]{:S(2)}) collective-permute-start(bf16[2,32,512]{2,1,0:T(8,128)(2,1)S(1)} %select_convert_fusion.2), channel_id=1, source_target_pairs={{0,8},{2,10},{4,12},{6,14},{8,0},{10,2},{12,4},{14,6},{16,24},{18,... | collective-permute-start | bytes 196616 | tf_op jit(solution)/shard_map/ppermute | solution.py:81
  48.9 0.5 collective-permute-done.6
  49.5 1.6 %collective-permute-start.7 = (bf16[2,32,512]{2,1,0:T(8,128)(2,1)S(1)}, bf16[2,32,512]{2,1,0:T(8,128)(2,1)S(1)}, u32[]{:S(2)}, u32[]{:S(2)}) collective-permute-start(bf16[2,32,512]{2,1,0:T(8,128)(2,1)S(1)} %select_convert_fusion.3), channel_id=1, source_target_pairs={{0,8},{2,10},{4,12},{6,14},{8,0},{10,2},{12,4},{14,6},{16,24},{18,... | collective-permute-start | bytes 196616 | tf_op jit(solution)/shard_map/ppermute | solution.py:81
  51.2 0.3 collective-permute-done.12
  51.5 2.8 %collective-permute-start.13 = (bf16[1,32,512]{2,1,0:T(8,128)(2,1)S(1)}, bf16[1,32,512]{2,1,0:T(8,128)(2,1)S(1)}, u32[]{:S(2)}, u32[]{:S(2)}) collective-permute-start(bf16[1,32,512]{2,1,0:T(8,128)(2,1)S(1)} %select_convert_fusion.4), channel_id=1, source_target_pairs={{0,16},{2,18},{4,20},{6,22},{8,24},{10,26},{12,28},{14,30},{16,0},... | collective-permute-start | bytes 98312 | tf_op jit(solution)/shard_map/ppermute | solution.py:81
  54.4 2.2 %collective-permute-start.8 = (bf16[1,32,512]{2,1,0:T(8,128)(2,1)S(1)}, bf16[1,32,512]{2,1,0:T(8,128)(2,1)S(1)}, u32[]{:S(2)}, u32[]{:S(2)}) collective-permute-start(bf16[1,32,512]{2,1,0:T(8,128)(2,1)S(1)} %select_convert_fusion.5), channel_id=1, source_target_pairs={{0,16},{2,18},{4,20},{6,22},{8,24},{10,26},{12,28},{14,30},{16,0},... | collective-permute-start | bytes 98312 | tf_op jit(solution)/shard_map/ppermute | solution.py:81
  56.6 2.7 %collective-permute-done.8 = bf16[1,32,512]{2,1,0:T(8,128)(2,1)S(1)} collective-permute-done((bf16[1,32,512]{2,1,0:T(8,128)(2,1)S(1)}, bf16[1,32,512]{2,1,0:T(8,128)(2,1)S(1)}, u32[]{:S(2)}, u32[]{:S(2)}) %collective-permute-start.8) | collective-permute-done | bytes 32800 | tf_op jit(solution)/shard_map/ppermute | solution.py:81
  59.4 2.1 %collective-permute-start.14 = (f32[2,24,512]{2,1,0:T(8,128)S(1)}, f32[2,24,512]{2,1,0:T(8,128)S(1)}, u32[]{:S(2)}, u32[]{:S(2)}) collective-permute-start(f32[2,24,512]{2,1,0:T(8,128)S(1)} %select_select_fusion), channel_id=1, source_target_pairs={{0,1},{1,0},{2,3},{3,2},{4,5},{5,4},{6,7},{7,6},{8,9},{9,8},{10,11... | collective-permute-start | bytes 294920 | tf_op jit(solution)/shard_map/ppermute | solution.py:262
  61.5 5.5 %spread.1 = bf16[384,8192]{1,0:T(8,128)(2,1)} custom-call(bf16[32,384]{1,0:T(8,128)(2,1)S(1)} %add_convert_fusion.1.back.hidden, bf16[32,8192]{1,0:T(8,128)(2,1)S(1)} %get-tuple-element.11.live), custom_call_target="tpu_custom_call" | custom-call | flops 201326592 | bytes 6291456 | tf_op jit(solution)/shard_map/spread/pallas_call | solution.py:202
  67.0 0.1 select_bitcast_fusion
  67.1 0.7 %copy.9 = f32[24,2,1,512]{3,2,1,0:T(1,128)} copy(f32[24,2,1,512]{3,0,1,2:T(8,128)S(1)} %get-tuple-element.22) | data formatting | bytes 196608
  67.8 0.7 %copy.8 = f32[24,2,1,512]{3,2,1,0:T(1,128)} copy(f32[24,2,1,512]{3,0,1,2:T(8,128)S(1)} %get-tuple-element.23) | data formatting | bytes 196608
  (41 shorter events, 0.8 us)
Async XLA Ops:
  0.6 25.7 %copy-start.4 = (bf16[24,16384]{1,0:T(8,128)(2,1)S(1)}, bf16[24,16384]{1,0:T(8,128)(2,1)}, u32[]{:S(2)}) copy-start(bf16[24,16384]{1,0:T(8,128)(2,1)} %own.2) | copy-start | bytes 2359300
  1.7 8.8 %collective-permute-start = (bf16[24,4096]{1,0:T(8,128)(2,1)S(1)}, bf16[24,4096]{1,0:T(8,128)(2,1)S(1)}, u32[]{:S(2)}, u32[]{:S(2)}) collective-permute-start(bf16[24,4096]{1,0:T(8,128)(2,1)S(1)} %constant_dynamic-slice_fusion.1), channel_id=1, source_target_pairs={{0,1},{1,0},{2,3},{3,2},{4,5},{5,4},{6,7},{7,6},{8,9},{9,8},{10,11... | collective-permute-start | bytes 589832 | tf_op jit(solution)/shard_map/ppermute | solution.py:223
  5.7 8.2 %collective-permute-start.3 = (bf16[24,4096]{1,0:T(8,128)(2,1)S(1)}, bf16[24,4096]{1,0:T(8,128)(2,1)S(1)}, u32[]{:S(2)}, u32[]{:S(2)}) collective-permute-start(bf16[24,4096]{1,0:T(8,128)(2,1)S(1)} %constant_dynamic-slice_fusion), channel_id=1, source_target_pairs={{0,1},{1,0},{2,3},{3,2},{4,5},{5,4},{6,7},{7,6},{8,9},{9,8},{10,11... | collective-permute-start | bytes 589832 | tf_op jit(solution)/shard_map/ppermute | solution.py:223
  10.4 15.9 %collective-permute-start.1 = (bf16[24,4096]{1,0:T(8,128)(2,1)S(1)}, bf16[24,4096]{1,0:T(8,128)(2,1)S(1)}, u32[]{:S(2)}, u32[]{:S(2)}) collective-permute-start(bf16[24,4096]{1,0:T(8,128)(2,1)S(1)} %collective-permute-done.mine), channel_id=1, source_target_pairs={{0,2},{2,0},{4,6},{6,4},{8,10},{10,8},{12,14},{14,12},{16,18},{18,... | collective-permute-start | bytes 589832 | tf_op jit(solution)/shard_map/ppermute | solution.py:81
  13.8 2.7 %collective-permute-start.4 = (bf16[24,4096]{1,0:T(8,128)(2,1)S(1)}, bf16[24,4096]{1,0:T(8,128)(2,1)S(1)}, u32[]{:S(2)}, u32[]{:S(2)}) collective-permute-start(bf16[24,4096]{1,0:T(8,128)(2,1)S(1)} %collective-permute-done.3.mine), channel_id=1, source_target_pairs={{0,2},{2,0},{4,6},{6,4},{8,10},{10,8},{12,14},{14,12},{16,18},{18,... | collective-permute-start | bytes 589832 | tf_op jit(solution)/shard_map/ppermute | solution.py:81
  16.4 9.9 %copy-start = (bf16[384,8192]{1,0:T(8,128)(2,1)S(1)}, bf16[384,8192]{1,0:T(8,128)(2,1)}, u32[]{:S(2)}) copy-start(bf16[384,8192]{1,0:T(8,128)(2,1)} %acts.3) | copy-start | bytes 18874372
  16.5 2.9 %copy-start.1 = (bf16[384,8192]{1,0:T(8,128)(2,1)S(1)}, bf16[384,8192]{1,0:T(8,128)(2,1)}, u32[]{:S(2)}) copy-start(bf16[384,8192]{1,0:T(8,128)(2,1)} %acts.2) | copy-start | bytes 18874372
  19.5 1.4 %copy-start.3 = (bf16[24,16384]{1,0:T(8,128)(2,1)S(1)}, bf16[24,16384]{1,0:T(8,128)(2,1)}, u32[]{:S(2)}) copy-start(bf16[24,16384]{1,0:T(8,128)(2,1)} %own.3) | copy-start | bytes 2359300
  24.6 6.2 %collective-permute-start.9 = (f32[32,384]{1,0:T(8,128)S(1)}, f32[32,384]{1,0:T(8,128)S(1)}, u32[]{:S(2)}, u32[]{:S(2)}) collective-permute-start(f32[32,384]{1,0:T(8,128)S(1)} %get-tuple-element.14), channel_id=1, source_target_pairs={{0,1},{1,0},{2,3},{3,2},{4,5},{5,4},{6,7},{7,6},{8,9},{9,8},{10,11... | collective-permute-start | bytes 147464 | tf_op jit(solution)/shard_map/ppermute | solution.py:253
  30.5 4.1 %collective-permute-start.2 = (f32[32,384]{1,0:T(8,128)S(1)}, f32[32,384]{1,0:T(8,128)S(1)}, u32[]{:S(2)}, u32[]{:S(2)}) collective-permute-start(f32[32,384]{1,0:T(8,128)S(1)} %get-tuple-element.10), channel_id=1, source_target_pairs={{0,1},{1,0},{2,3},{3,2},{4,5},{5,4},{6,7},{7,6},{8,9},{9,8},{10,11... | collective-permute-start | bytes 147464 | tf_op jit(solution)/shard_map/ppermute | solution.py:252
  33.9 6.7 %collective-permute-start.10 = (bf16[8,32,512]{2,1,0:T(8,128)(2,1)S(1)}, bf16[8,32,512]{2,1,0:T(8,128)(2,1)S(1)}, u32[]{:S(2)}, u32[]{:S(2)}) collective-permute-start(bf16[8,32,512]{2,1,0:T(8,128)(2,1)S(1)} %get-tuple-element.16), channel_id=1, source_target_pairs={{0,2},{2,0},{4,6},{6,4},{8,10},{10,8},{12,14},{14,12},{16,18},{18,... | collective-permute-start | bytes 786440 | tf_op jit(solution)/shard_map/ppermute | solution.py:81
  34.6 2.8 %copy-start.2 = (bf16[384,8192]{1,0:T(8,128)(2,1)S(1)}, bf16[384,8192]{1,0:T(8,128)(2,1)}, u32[]{:S(2)}) copy-start(bf16[384,8192]{1,0:T(8,128)(2,1)} %acts.2) | copy-start | bytes 18874372
  40.5 1.9 %collective-permute-start.5 = (bf16[8,32,512]{2,1,0:T(8,128)(2,1)S(1)}, bf16[8,32,512]{2,1,0:T(8,128)(2,1)S(1)}, u32[]{:S(2)}, u32[]{:S(2)}) collective-permute-start(bf16[8,32,512]{2,1,0:T(8,128)(2,1)S(1)} %get-tuple-element.13), channel_id=1, source_target_pairs={{0,2},{2,0},{4,6},{6,4},{8,10},{10,8},{12,14},{14,12},{16,18},{18,... | collective-permute-start | bytes 786440 | tf_op jit(solution)/shard_map/ppermute | solution.py:81
  40.7 6.4 %collective-permute-start.11 = (bf16[4,32,512]{2,1,0:T(8,128)(2,1)S(1)}, bf16[4,32,512]{2,1,0:T(8,128)(2,1)S(1)}, u32[]{:S(2)}, u32[]{:S(2)}) collective-permute-start(bf16[4,32,512]{2,1,0:T(8,128)(2,1)S(1)} %select_convert_fusion), channel_id=1, source_target_pairs={{0,4},{2,6},{4,0},{6,2},{8,12},{10,14},{12,8},{14,10},{16,20},{18,... | collective-permute-start | bytes 393224 | tf_op jit(solution)/shard_map/ppermute | solution.py:81
  42.5 7.0 %collective-permute-start.6 = (bf16[4,32,512]{2,1,0:T(8,128)(2,1)S(1)}, bf16[4,32,512]{2,1,0:T(8,128)(2,1)S(1)}, u32[]{:S(2)}, u32[]{:S(2)}) collective-permute-start(bf16[4,32,512]{2,1,0:T(8,128)(2,1)S(1)} %select_convert_fusion.1), channel_id=1, source_target_pairs={{0,4},{2,6},{4,0},{6,2},{8,12},{10,14},{12,8},{14,10},{16,20},{18,... | collective-permute-start | bytes 393224 | tf_op jit(solution)/shard_map/ppermute | solution.py:81
  47.1 4.3 %collective-permute-start.12 = (bf16[2,32,512]{2,1,0:T(8,128)(2,1)S(1)}, bf16[2,32,512]{2,1,0:T(8,128)(2,1)S(1)}, u32[]{:S(2)}, u32[]{:S(2)}) collective-permute-start(bf16[2,32,512]{2,1,0:T(8,128)(2,1)S(1)} %select_convert_fusion.2), channel_id=1, source_target_pairs={{0,8},{2,10},{4,12},{6,14},{8,0},{10,2},{12,4},{14,6},{16,24},{18,... | collective-permute-start | bytes 196616 | tf_op jit(solution)/shard_map/ppermute | solution.py:81
  49.5 4.8 %collective-permute-start.7 = (bf16[2,32,512]{2,1,0:T(8,128)(2,1)S(1)}, bf16[2,32,512]{2,1,0:T(8,128)(2,1)S(1)}, u32[]{:S(2)}, u32[]{:S(2)}) collective-permute-start(bf16[2,32,512]{2,1,0:T(8,128)(2,1)S(1)} %select_convert_fusion.3), channel_id=1, source_target_pairs={{0,8},{2,10},{4,12},{6,14},{8,0},{10,2},{12,4},{14,6},{16,24},{18,... | collective-permute-start | bytes 196616 | tf_op jit(solution)/shard_map/ppermute | solution.py:81
  51.5 5.1 %collective-permute-start.13 = (bf16[1,32,512]{2,1,0:T(8,128)(2,1)S(1)}, bf16[1,32,512]{2,1,0:T(8,128)(2,1)S(1)}, u32[]{:S(2)}, u32[]{:S(2)}) collective-permute-start(bf16[1,32,512]{2,1,0:T(8,128)(2,1)S(1)} %select_convert_fusion.4), channel_id=1, source_target_pairs={{0,16},{2,18},{4,20},{6,22},{8,24},{10,26},{12,28},{14,30},{16,0},... | collective-permute-start | bytes 98312 | tf_op jit(solution)/shard_map/ppermute | solution.py:81
  54.4 4.9 %collective-permute-start.8 = (bf16[1,32,512]{2,1,0:T(8,128)(2,1)S(1)}, bf16[1,32,512]{2,1,0:T(8,128)(2,1)S(1)}, u32[]{:S(2)}, u32[]{:S(2)}) collective-permute-start(bf16[1,32,512]{2,1,0:T(8,128)(2,1)S(1)} %select_convert_fusion.5), channel_id=1, source_target_pairs={{0,16},{2,18},{4,20},{6,22},{8,24},{10,26},{12,28},{14,30},{16,0},... | collective-permute-start | bytes 98312 | tf_op jit(solution)/shard_map/ppermute | solution.py:81
  59.4 7.6 %collective-permute-start.14 = (f32[2,24,512]{2,1,0:T(8,128)S(1)}, f32[2,24,512]{2,1,0:T(8,128)S(1)}, u32[]{:S(2)}, u32[]{:S(2)}) collective-permute-start(f32[2,24,512]{2,1,0:T(8,128)S(1)} %select_select_fusion), channel_id=1, source_target_pairs={{0,1},{1,0},{2,3},{3,2},{4,5},{5,4},{6,7},{7,6},{8,9},{9,8},{10,11... | collective-permute-start | bytes 294920 | tf_op jit(solution)/shard_map/ppermute | solution.py:262

commit v2 on v0

--- a/solution.py
+++ b/solution.py
@@ -1,8 +1,11 @@
+import functools
 import math
 
 import jax
 import jax.numpy as jnp
 from jax import lax
+from jax.experimental import pallas as pl
+from jax.experimental.pallas import tpu as pltpu
 from jax.sharding import PartitionSpec as P
 
 
@@ -28,7 +31,7 @@
     return (own_blocks(left_sum), own_blocks(right_sum))
 
 
-def local(tokens, cotangent, left_factor, right_factor, panel_rank):
+def any_panels(tokens, cotangent, left_factor, right_factor, panel_rank):
     slot_count = left_factor.shape[0]
     groups = lax.axis_size("tensor")
     all_slots = slot_count * groups
@@ -68,10 +71,363 @@
     return (token_grad, left_grad, right_grad)
 
 
+PAD = 8
+SWAP = [(0, 1), (1, 0)]
+WHOLE = pl.BlockSpec(memory_space=pltpu.VMEM)
+SCALARS = pl.BlockSpec(memory_space=pltpu.SMEM)
+FAR = pl.BlockSpec(memory_space=pltpu.HBM)
+SMALL = pl.CostEstimate(flops=1, bytes_accessed=1, transcendentals=0)
+PARAMS = pltpu.CompilerParams(vmem_limit_bytes=16 * 1024 * 1024)
+
+
+def near(value):
+    return pltpu.with_memory_space_constraint(value, pltpu.VMEM)
+
+
+def far(value):
+    return pltpu.with_memory_space_constraint(value, pltpu.HBM)
+
+
+def flip(value, bit):
+    size = lax.axis_size("dp")
+    return lax.ppermute(value, "dp", [(i, i ^ (1 << bit)) for i in range(size)])
+
+
+def after_all(value, *others):
+    return lax.optimization_barrier((value, *others))[0]
+
+
+def stage_kernel(parts, given, acts, factor, *refs):
+    acts_out, factor_out = refs[given : given + 2]
+    sems = refs[-1]
+    width = factor_out.shape[1]
+    column = pl.multiple_of(lax.axis_index("tensor") * width, width)
+    rows = acts.shape[0] // parts
+    copies = [pltpu.make_async_copy(factor.at[:, pl.ds(column, width)], factor_out, sems.at[0])]
+    for n in range(parts):
+        piece = pl.ds(n * rows, rows)
+        copies.append(pltpu.make_async_copy(acts.at[piece], acts_out.at[piece], sems.at[n + 1]))
+    for copy in copies:
+        copy.start()
+    if len(refs) == given + 4:
+        rank, full_out = refs[0], refs[given + 2]
+        own_rank = jnp.where(lax.axis_index("tensor") == 0, rank[0], rank[1])
+        full = (own_rank == factor.shape[0]).astype(jnp.float32)
+        full_out[...] = jnp.full(full_out.shape, full)
+    for copy in copies:
+        copy.wait()
+
+
+def stage(acts, factor, rank, after):
+    shapes = [
+        pltpu.VMEM(acts.shape, acts.dtype),
+        pltpu.VMEM((factor.shape[0], acts.shape[1]), factor.dtype),
+    ]
+    if rank:
+        shapes.append(pltpu.VMEM((8, 128), jnp.float32))
+    parts = 8 if acts.shape[0] % 128 == 0 else 1
+    return pl.pallas_call(
+        functools.partial(stage_kernel, parts, len(rank) + len(after)),
+        in_specs=[FAR] * 2 + [SCALARS] * len(rank) + [WHOLE] * len(after),
+        out_specs=[WHOLE] * len(shapes),
+        out_shape=shapes,
+        scratch_shapes=[pltpu.SemaphoreType.DMA((1 + parts,))],
+        compiler_params=PARAMS,
+        cost_estimate=SMALL,
+        name="stage",
+    )(far(acts), far(factor), *rank, *map(near, after))
+
+
+def own_is_full(full):
+    return full[0:1, 0:1] > 0.5
+
+
+def both_panels(own, piece):
+    gap = jnp.zeros((PAD, piece.shape[1]), piece.dtype)
+    return jnp.concatenate([own, gap, piece, gap], axis=0)
+
+
+def project_kernel(flipped, chunk, given, *refs):
+    own, piece, acts = refs[:3]
+    others, out = refs[3 : 3 + given], refs[-1]
+    slots, width = piece.shape
+    core = lax.axis_index("dp") % 2
+    start = (1 - core if flipped else core) * width
+    total = None
+    for low in range(0, width, chunk):
+        column = pl.ds(pl.multiple_of(start + low, chunk), chunk)
+        rows = both_panels(own[:, column], piece[:, low : low + chunk])
+        part = lax.dot_general(
+            rows, acts[:, column], (((1,), (1,)), ((), ())), preferred_element_type=jnp.float32
+        )
+        total = part if total is None else total + part
+    if others:
+        total += others[0][...]
+        full_here = own_is_full(others[1][...])
+        own_part, other_part = total[:slots], total[slots + PAD : 2 * slots + PAD]
+        out[:slots] = jnp.where(full_here, own_part, other_part)
+        short = jnp.where(full_here, other_part[:PAD], own_part[:PAD])
+        first = lax.broadcasted_iota(jnp.int32, short.shape, 0) == 0
+        out[slots:] = jnp.where(first, short, 0.0)
+    else:
+        out[...] = total
+
+
+def project(own, piece, acts, flipped, others, held):
+    slots, width = piece.shape
+    tokens = acts.shape[0]
+    rows = slots + PAD if others else 2 * (slots + PAD)
+    return pl.pallas_call(
+        functools.partial(project_kernel, flipped, min(width, 2048), len(others)),
+        in_specs=[WHOLE] * (3 + len(others) + len(held)),
+        out_specs=WHOLE,
+        out_shape=pltpu.VMEM((rows, tokens), jnp.float32),
+        compiler_params=PARAMS,
+        cost_estimate=SMALL,
+        name="project",
+    )(*map(near, (own, piece, acts, *others, *held)))
+
+
+def gradient_kernel(scale, places, given, held, part, got, acts, *refs):
+    outs = refs[given + held :]
+    keep, send = outs[:2]
+    rows, block = keep.shape[1], keep.shape[2]
+    slots = part.shape[0] - PAD
+    even = lax.axis_index("dp") % 2 == 0
+    summed = (part[...] + got[...]).astype(jnp.bfloat16)
+    row = lax.broadcasted_iota(jnp.int32, (PAD, 2 * block), 0)
+    for j, q in enumerate(places):
+        columns = slice(j * 2 * block, (j + 1) * 2 * block)
+        grad = jnp.dot(summed, acts[:, columns], preferred_element_type=jnp.float32) * scale
+        if given:
+            short = jnp.where(row == 1, refs[0][q, 0:1, :], grad[slots:])
+            grad = jnp.concatenate([grad[:slots], short], axis=0)
+        else:
+            outs[2][q] = grad[slots:]
+            grad = grad[:slots]
+        low, high = grad[:, :block], grad[:, block:]
+        keep[q] = jnp.where(even, low, high)
+        send[q] = jnp.where(even, high, low).astype(send.dtype)
+
+
+def gradient(part, got, acts, scale, extra, held):
+    live, tokens = part.shape
+    slots = live - PAD
+    width = acts.shape[1]
+    size = lax.axis_size("dp")
+    bits = size.bit_length() - 1
+    block = width // size
+    pairs = size // 2
+    places = [int(format(j, "0%db" % (bits - 1))[::-1], 2) for j in range(pairs)]
+    shape = (pairs, live if extra else slots, block)
+    shapes = [pltpu.VMEM(shape, jnp.float32), pltpu.VMEM(shape, jnp.bfloat16)]
+    if not extra:
+        shapes.append(pltpu.VMEM((pairs, PAD, 2 * block), jnp.float32))
+    return pl.pallas_call(
+        functools.partial(gradient_kernel, scale, places, len(extra), len(held)),
+        in_specs=[WHOLE] * (3 + len(extra) + len(held)),
+        out_specs=[WHOLE] * len(shapes),
+        out_shape=shapes,
+        compiler_params=PARAMS,
+        cost_estimate=SMALL,
+        name="gradient",
+    )(*map(near, (part, got, acts, *extra, *held)))
+
+
+def spread_kernel(chunk, full, part, got, own, mine, theirs, after, out, buffer, sems):
+    slots, width = mine.shape
+    core = lax.axis_index("dp") % 2
+    full_here = own_is_full(full[...])
+    back = part[...] + got[...]
+    first = lax.broadcasted_iota(jnp.int32, (slots, back.shape[1]), 0) == 0
+    short = jnp.where(first, back[slots : slots + 1], 0.0)
+    of_own = jnp.where(full_here, back[:slots], short)
+    of_other = jnp.where(full_here, short, back[:slots])
+    gap = jnp.zeros((PAD, back.shape[1]), jnp.float32)
+    weights = jnp.concatenate([of_own, gap, of_other, gap], axis=0).T.astype(jnp.bfloat16)
+    copies = []
+    for side, piece in enumerate((mine, theirs)):
+        for low in range(0, width, chunk):
+            start = (core if side == 0 else 1 - core) * width + low
+            column = pl.ds(pl.multiple_of(start, chunk), chunk)
+            rows = both_panels(own[:, column], piece[:, low : low + chunk])
+            held = buffer.at[:, side * width + low : side * width + low + chunk]
+            held[...] = jnp.dot(weights, rows, preferred_element_type=jnp.float32).astype(out.dtype)
+            copy = pltpu.make_async_copy(held, out.at[:, column], sems.at[len(copies)])
+            copy.start()
+            copies.append(copy)
+    for copy in copies:
+        copy.wait()
+
+
+def spread(full, part, got, own, mine, theirs, after):
+    tokens = part.shape[1]
+    rows, width = own.shape
+    chunk = min(width // 2, 1024)
+    return pl.pallas_call(
+        functools.partial(spread_kernel, chunk),
+        in_specs=[WHOLE] * 7,
+        out_specs=FAR,
+        out_shape=jax.ShapeDtypeStruct((tokens, width), jnp.bfloat16),
+        scratch_shapes=[
+            pltpu.VMEM((tokens, width), jnp.bfloat16),
+            pltpu.SemaphoreType.DMA((width // chunk,)),
+        ],
+        compiler_params=PARAMS,
+        cost_estimate=SMALL,
+        name="spread",
+    )(*map(near, (full, part, got, own, mine, theirs, after)))
+
+
+def settle_kernel(full, keep, got, held, send):
+    slots, block = held.shape[1:]
+    full_here = own_is_full(full[...])
+    first = lax.broadcasted_iota(jnp.int32, (slots, block), 0) == 0
+    total = keep[0] + got[0].astype(jnp.float32)
+    for n, row in ((0, 1), (1, 0)):
+        rows = total[n * slots : (n + 1) * slots]
+        short = jnp.where(first, total[2 * slots + row : 2 * slots + row + 1], 0.0)
+        held[n] = jnp.where(full_here, rows, short)
+        send[n] = jnp.where(full_here, short, rows)
+
+
+def settle(full, keep, got):
+    rows, block = keep.shape[1:]
+    shape = pltpu.VMEM((2, (rows - PAD) // 2, block), jnp.float32)
+    return pl.pallas_call(
+        settle_kernel,
+        in_specs=[WHOLE] * 3,
+        out_specs=[WHOLE, WHOLE],
+        out_shape=[shape, shape],
+        compiler_params=PARAMS,
+        cost_estimate=SMALL,
+        name="settle",
+    )(near(full), near(keep), near(got))
+
+
+def place_kernel(held, got, left_out, right_out):
+    here = lax.axis_index("tensor") == 0
+    for n, out in enumerate((left_out, right_out)):
+        out[:, 0, 0, :] = jnp.where(here, held[n], got[n])
+        out[:, 1, 0, :] = jnp.where(here, got[n], held[n])
+
+
+def place(held, got):
+    shape = jax.ShapeDtypeStruct((held.shape[1], 2, 1, held.shape[2]), jnp.float32)
+    return pl.pallas_call(
+        place_kernel,
+        in_specs=[WHOLE, WHOLE],
+        out_specs=[WHOLE, WHOLE],
+        out_shape=[shape, shape],
+        compiler_params=PARAMS,
+        cost_estimate=SMALL,
+        name="place",
+    )(near(held), near(got))
+
+
+def pick_kernel(factor, out, sem):
+    part = out.shape[1]
+    core = lax.axis_index("dp") % 2
+    column = ((1 - lax.axis_index("tensor")) * 2 + core) * part
+    copy = pltpu.make_async_copy(
+        factor.at[:, pl.ds(pl.multiple_of(column, part), part)], out, sem
+    )
+    copy.start()
+    copy.wait()
+
+
+def pick(factor):
+    slots, width = factor.shape
+    return pl.pallas_call(
+        pick_kernel,
+        in_specs=[FAR],
+        out_specs=WHOLE,
+        out_shape=pltpu.VMEM((slots, width // 4), factor.dtype),
+        scratch_shapes=[pltpu.SemaphoreType.DMA],
+        compiler_params=PARAMS,
+        cost_estimate=SMALL,
+        name="pick",
+    )(far(factor))
+
+
+def halve_kernel(bit, count, *refs):
+    keep_out, send_out = refs[2 * count :]
+    blocks = keep_out.shape[0]
+    even = (lax.axis_index("dp") // (1 << bit)) % 2 == 0
+    row = 0
+    for keep, got in zip(refs[:count], refs[count : 2 * count]):
+        rows = keep.shape[1]
+        low = keep[:blocks] + got[:blocks].astype(jnp.float32)
+        high = keep[blocks:] + got[blocks:].astype(jnp.float32)
+        keep_out[:, row : row + rows] = jnp.where(even, low, high)
+        send_out[:, row : row + rows] = jnp.where(even, high, low).astype(send_out.dtype)
+        row += rows
+
+
+def halve(keeps, gots, bit):
+    blocks, _, block = keeps[0].shape
+    rows = sum(keep.shape[1] for keep in keeps)
+    shape = (blocks // 2, rows, block)
+    return pl.pallas_call(
+        functools.partial(halve_kernel, bit, len(keeps)),
+        in_specs=[WHOLE] * (2 * len(keeps)),
+        out_specs=[WHOLE, WHOLE],
+        out_shape=[pltpu.VMEM(shape, jnp.float32), pltpu.VMEM(shape, jnp.bfloat16)],
+        compiler_params=PARAMS,
+        cost_estimate=SMALL,
+        name="halve",
+    )(*map(near, (*keeps, *gots)))
+
+
+def two_panels(tokens, cotangent, left_factor, right_factor, panel_rank):
+    scale = 1.0 / math.sqrt(tokens.shape[0] * lax.axis_size("dp"))
+
+    right_wanted = pick(right_factor)
+    left_wanted = pick(left_factor)
+    right_mine = lax.ppermute(right_wanted, "tensor", SWAP)
+    left_mine = lax.ppermute(left_wanted, "tensor", SWAP)
+    cotangent, right_own = stage(cotangent, right_factor, (), (left_wanted,))
+    tokens, left_own, full = stage(tokens, left_factor, (panel_rank,), (right_own,))
+    right_mine = after_all(right_mine, left_own)
+    right_theirs = flip(right_mine, 0)
+    back = project(right_own, right_mine, cotangent, False, (), ())
+    left_mine = after_all(left_mine, back)
+    back = project(right_own, right_theirs, cotangent, True, (back, full), ())
+    left_theirs = flip(left_mine, 0)
+    back_got = lax.ppermute(back, "tensor", SWAP)
+    hidden = project(left_own, left_mine, tokens, False, (), (cotangent,))
+    hidden = project(left_own, left_theirs, tokens, True, (hidden, full), (cotangent,))
+    hidden_got = lax.ppermute(hidden, "tensor", SWAP)
+
+    left_keep, left_send, extra = gradient(
+        back, back_got, tokens, scale, (), (hidden, cotangent)
+    )
+    left_got = flip(left_send, 0)
+    right_keep, right_send = gradient(hidden, hidden_got, cotangent, scale, (extra,), ())
+    right_got = flip(right_send, 0)
+    left_got = after_all(left_got, right_send)
+    left_keep, left_send = halve((left_keep,), (left_got,), 1)
+    left_got = flip(left_send, 1)
+    right_keep, right_send = halve((right_keep,), (right_got,), 1)
+    right_got = flip(right_send, 1)
+    token_grad = spread(full, back, back_got, left_own, left_mine, left_theirs, right_send)
+    left_got = after_all(left_got, token_grad)
+    keep, send = halve((left_keep, right_keep), (left_got, right_got), 2)
+    got = flip(send, 2)
+    for bit in range(3, lax.axis_size("dp").bit_length() - 1):
+        keep, send = halve((keep,), (got,), bit)
+        got = flip(send, bit)
+
+    held, send = settle(full, keep, got)
+    return token_grad, *place(held, lax.ppermute(send, "tensor", SWAP))
+
+
 def solution(mesh):
     placed = (P("dp", "tensor"), P("dp", "tensor"), P("tensor", None), P("tensor", None), P())
+    size = mesh.shape["dp"]
+    halves = size & (size - 1) == 0 and size >= 8
     return jax.shard_map(
-        local,
+        two_panels if mesh.shape["tensor"] == 2 and halves else any_panels,
         mesh=mesh,
         in_specs=placed,
         out_specs=(P("dp", "tensor"), P("tensor", None, "dp", None), P("tensor", None, "dp", None)),

time: 219 us -> 49.8 us (0.23)
  waiting for transfers between devices: 142 us -> 16.5 us
  matrix products: 24.3 us -> 0 us
  Pallas kernels: 0 us -> 19.3 us
  between operations: 14.1 us -> 0.79 us
  local copies, waits for them, and re-layouts: 11.8 us -> 0.01 us
  blocking collectives: 8.86 us -> 0 us
  starting transfers between devices: 16.1 us -> 13 us
    psum x1 -> x0, waiting for transfers between devices: 97.9 us -> none  [settle_both(): left_sum, right_sum = lax.psum((left_home, right_home), 'dp')]
    all_to_all x4 -> x0, waiting for transfers between devices: 44.1 us -> none  [the longest x1 13.5 us: settle_both(): lax.all_to_all(left_cols, 'tensor', split_axis=0, concat_axis=1, tiled=True)]
    dot_general x5 -> x0, matrix products: 24.3 us -> none  [the longest x1 5.19 us: local(): lax.dot_general(hidden, cotangent, token_dims, preferred_element_type=jnp...]
    pallas_call x0 -> x17, Pallas kernels: none -> 19.3 us  [the longest x2 6.52 us: stage(): pl.pallas_call(functools.partial(stage_kernel, parts, len(rank) + len(aft...]
    ppermute x0 -> x13, waiting for transfers between devices: none -> 16.5 us  [the longest x8 9.03 us: flip(): return lax.ppermute(value, 'dp', [(i, i ^ 1 << bit) for i in range(size)])]
    all_to_all x4 -> x0, starting transfers between devices: 16 us -> none  [the longest x1 4.61 us: settle_both(): lax.all_to_all(left_cols, 'tensor', split_axis=0, concat_axis=1, tiled=True)]
    ppermute x0 -> x13, starting transfers between devices: none -> 13 us  [the longest x8 7.31 us: flip(): return lax.ppermute(value, 'dp', [(i, i ^ 1 << bit) for i in range(size)])]
    psum x1 -> x0, blocking collectives: 8.86 us -> none  [local(): hidden, back_hidden = lax.psum((hidden_part, back_part), 'tensor')]
  transfers between devices with their start and end apart: 5 -> 13, of which waited for: 5 -> 8; matrix products, arithmetic and copies ran while one was open for 7% -> 0% of each run, Pallas kernels for 0% -> 33%
where the time goes in v2:
time: 49.8 us; the launch traced here: 49.6 us
  Pallas kernels  19.3 us (39%)
  waiting for transfers between devices  16.5 us (33%)
  starting transfers between devices  13 us (26%)
  between operations  0.79 us (2%)
    ppermute x8, waiting for transfers between devices, flip(): return lax.ppermute(value, 'dp', [(i, i ^ 1 << bit) for i in range(size)])  9.03 us
    ppermute x8, starting transfers between devices, flip(): return lax.ppermute(value, 'dp', [(i, i ^ 1 << bit) for i in range(size)])  7.31 us
    pallas_call x2, Pallas kernels, stage(): pl.pallas_call(functools.partial(stage_kernel, parts, len(rank) + len(aft...  6.52 us
    pallas_call x4, Pallas kernels, project(): pl.pallas_call(functools.partial(project_kernel, flipped, min(width, 2048...  4.36 us
    ppermute x1, waiting for transfers between devices, two_panels(): return (token_grad, *place(held, lax.ppermute(send, 'tensor', SWAP)))  4.31 us
    pallas_call x1, Pallas kernels, spread(): pl.pallas_call(functools.partial(spread_kernel, chunk), in_specs=[WHOLE]...  3.18 us
    ppermute x1, starting transfers between devices, two_panels(): right_mine = lax.ppermute(right_wanted, 'tensor', SWAP)  3.03 us
    pallas_call x2, Pallas kernels, gradient(): pl.pallas_call(functools.partial(gradient_kernel, scale, places, len(extr...  2.41 us
  transfers between devices with their start and end apart: 13, of which 8 were waited for; matrix products, arithmetic and copies ran while one was open for 0% of the time, Pallas kernels for 33%

profile of v2, /device:TPU:0, one launch (start us, length us, event | category | flops | bytes accessed | tf_op | source)
XLA Modules:
  0.0 49.6 jit_solution(7950581677875600479)
XLA Ops:
  0.6 1.0 %pick.3 = bf16[24,4096]{1,0:T(8,128)(2,1)S(1)} custom-call(bf16[24,16384]{1,0:T(8,128)(2,1)} %factor.7), custom_call_target="tpu_custom_call" | custom-call | flops 1 | bytes 1 | tf_op jit(solution)/shard_map/pick/pallas_call | solution.py:341
  1.6 3.0 %collective-permute-start = (bf16[24,4096]{1,0:T(8,128)(2,1)S(1)}, bf16[24,4096]{1,0:T(8,128)(2,1)S(1)}, u32[]{:S(2)}, u32[]{:S(2)}) collective-permute-start(bf16[24,4096]{1,0:T(8,128)(2,1)S(1)} %pick.3), channel_id=1, source_target_pairs={{0,1},{1,0},{2,3},{3,2},{4,5},{5,4},{6,7},{7,6},{8,9},{9,8},{10,11... | collective-permute-start | bytes 589832 | tf_op jit(solution)/shard_map/ppermute | solution.py:387
  4.6 0.9 %pick.2.refs_0_ = bf16[24,4096]{1,0:T(8,128)(2,1)S(1)} custom-call(bf16[24,16384]{1,0:T(8,128)(2,1)} %factor.6), custom_call_target="tpu_custom_call" | custom-call | flops 1 | bytes 1 | tf_op jit(solution)/shard_map/pick/pallas_call | solution.py:341
  5.6 0.1 collective-permute-start.3
  5.7 3.0 %stage.2 = (bf16[384,8192]{1,0:T(8,128)(2,1)S(1)}, bf16[24,8192]{1,0:T(8,128)(2,1)S(1)}) custom-call(bf16[384,8192]{1,0:T(8,128)(2,1)} %acts.2, bf16[24,16384]{1,0:T(8,128)(2,1)} %factor.7, bf16[24,4096]{1,0:T(8,128)(2,1)S(1)} %pick.2.refs_0_), custom_call_target="tpu_custom_call" | custom-call | flops 1 | bytes 1 | tf_op jit(solution)/shard_map/stage/pallas_call | solution.py:129
  8.7 3.5 %stage.3 = (bf16[384,8192]{1,0:T(8,128)(2,1)S(1)}, bf16[24,8192]{1,0:T(8,128)(2,1)S(1)}, f32[8,128]{1,0:T(8,128)S(1)}) custom-call(bf16[384,8192]{1,0:T(8,128)(2,1)} %acts.3, bf16[24,16384]{1,0:T(8,128)(2,1)} %factor.6, s32[2]{0:T(128)S(1)} %copy-done, bf16[24,8192]{1,0:T(8,128)(2,1)S(1)} %get-tuple-element.29.refs_1_.refs_0_), custom_call_target="tpu_custom_call" | custom-call | flops 1 | bytes 1 | tf_op jit(solution)/shard_map/stage/pallas_call | solution.py:129
  12.3 1.1 %project.4.refs_3_ = f32[64,384]{1,0:T(8,128)S(1)} custom-call(bf16[24,8192]{1,0:T(8,128)(2,1)S(1)} %get-tuple-element.29.refs_1_.refs_0_, bf16[24,4096]{1,0:T(8,128)(2,1)S(1)} %collective-permute-done.refs_1_, bf16[384,8192]{1,0:T(8,128)(2,1)S(1)} %get-tuple-element.33.refs_2_.refs_3_.refs_5_.refs_1_.acts), custom_call_target="tpu_custom_call" | custom-call | flops 1 | bytes 1 | tf_op jit(solution)/shard_map/project/pallas_call | solution.py:180
  13.4 0.3 collective-permute-done.3.refs_1_.mine
  13.7 0.2 collective-permute-start.4
  14.0 1.1 %project.6.refs_3_ = f32[64,384]{1,0:T(8,128)S(1)} custom-call(bf16[24,8192]{1,0:T(8,128)(2,1)S(1)} %get-tuple-element.31.refs_0_.own, bf16[24,4096]{1,0:T(8,128)(2,1)S(1)} %collective-permute-done.3.refs_1_.mine, bf16[384,8192]{1,0:T(8,128)(2,1)S(1)} %get-tuple-element.35.refs_2_.acts, ...), custom_call_target="tpu_custom_call" | custom-call | flops 1 | bytes 1 | tf_op jit(solution)/shard_map/project/pallas_call | solution.py:180
  15.1 1.1 %project.5.part = f32[32,384]{1,0:T(8,128)S(1)} custom-call(bf16[24,8192]{1,0:T(8,128)(2,1)S(1)} %get-tuple-element.29.refs_1_.refs_0_, bf16[24,4096]{1,0:T(8,128)(2,1)S(1)} %collective-permute-done.1.refs_1_, bf16[384,8192]{1,0:T(8,128)(2,1)S(1)} %get-tuple-element.33.refs_2_.refs_3_.refs_5_.refs_1_.acts, f32[64,384]{1,0:T(8,128)S(1)} %project.4.refs_3_, ...), custom_call_target="tpu_custom_call" | custom-call | flops 1 | bytes 1 | tf_op jit(solution)/shard_map/project/pallas_call | solution.py:180
  16.2 2.1 %collective-permute-start.2 = (f32[32,384]{1,0:T(8,128)S(1)}, f32[32,384]{1,0:T(8,128)S(1)}, u32[]{:S(2)}, u32[]{:S(2)}) collective-permute-start(f32[32,384]{1,0:T(8,128)S(1)} %project.5.part), channel_id=1, source_target_pairs={{0,1},{1,0},{2,3},{3,2},{4,5},{5,4},{6,7},{7,6},{8,9},{9,8},{10,11... | collective-permute-start | bytes 147464 | tf_op jit(solution)/shard_map/ppermute | solution.py:397
  18.2 1.1 %project.7.refs_0_.part = f32[32,384]{1,0:T(8,128)S(1)} custom-call(bf16[24,8192]{1,0:T(8,128)(2,1)S(1)} %get-tuple-element.31.refs_0_.own, bf16[24,4096]{1,0:T(8,128)(2,1)S(1)} %collective-permute-done.4.refs_1_.theirs, bf16[384,8192]{1,0:T(8,128)(2,1)S(1)} %get-tuple-element.35.refs_2_.acts, f32[64,384]{1,0:T(8,128)S(1)} %project.6.refs_3_, ...), custom_call_target="tpu_custom_call" | custom-call | flops 1 | bytes 1 | tf_op jit(solution)/shard_map/project/pallas_call | solution.py:180
  19.3 0.1 collective-permute-start.5
  19.4 0.9 %collective-permute-done.2.got = f32[32,384]{1,0:T(8,128)S(1)} collective-permute-done((f32[32,384]{1,0:T(8,128)S(1)}, f32[32,384]{1,0:T(8,128)S(1)}, u32[]{:S(2)}, u32[]{:S(2)}) %collective-permute-start.2) | collective-permute-done | bytes 49184 | tf_op jit(solution)/shard_map/ppermute | solution.py:397
  20.3 1.2 %gradient.2 = (f32[8,24,512]{2,1,0:T(8,128)S(1)}, bf16[8,24,512]{2,1,0:T(8,128)(2,1)S(1)}, f32[8,8,1024]{2,1,0:T(8,128)S(1)}) custom-call(f32[32,384]{1,0:T(8,128)S(1)} %project.5.part, f32[32,384]{1,0:T(8,128)S(1)} %collective-permute-done.2.got, bf16[384,8192]{1,0:T(8,128)(2,1)S(1)} %get-tuple-element.35.refs_2_.acts, f32[32,384]{1,0:T(8,128)S(1)} %project.7.refs_0_.part, ...), custom_call_target="tpu_custom_call" | custom-call | flops 1 | bytes 1 | tf_op jit(solution)/shard_map/gradient/pallas_call | solution.py:226
  21.5 1.9 %collective-permute-done.5.got = f32[32,384]{1,0:T(8,128)S(1)} collective-permute-done((f32[32,384]{1,0:T(8,128)S(1)}, f32[32,384]{1,0:T(8,128)S(1)}, u32[]{:S(2)}, u32[]{:S(2)}) %collective-permute-start.5) | collective-permute-done | bytes 49184 | tf_op jit(solution)/shard_map/ppermute | solution.py:400
  23.5 1.2 %gradient.3 = (f32[8,32,512]{2,1,0:T(8,128)S(1)}, bf16[8,32,512]{2,1,0:T(8,128)(2,1)S(1)}) custom-call(f32[32,384]{1,0:T(8,128)S(1)} %project.7.refs_0_.part, f32[32,384]{1,0:T(8,128)S(1)} %collective-permute-done.5.got, bf16[384,8192]{1,0:T(8,128)(2,1)S(1)} %get-tuple-element.33.refs_2_.refs_3_.refs_5_.refs_1_.acts, f32[8,8,1024]{2,1,0:T(8,128)S(1)} %get-tuple-element.36.refs_0_), custom_call_target="tpu_custom_call" | custom-call | flops 1 | bytes 1 | tf_op jit(solution)/shard_map/gradient/pallas_call | solution.py:226
  24.8 0.5 %collective-permute-start.7 = (bf16[8,24,512]{2,1,0:T(8,128)(2,1)S(1)}, bf16[8,24,512]{2,1,0:T(8,128)(2,1)S(1)}, u32[]{:S(2)}, u32[]{:S(2)}) collective-permute-start(bf16[8,24,512]{2,1,0:T(8,128)(2,1)S(1)} %get-tuple-element.41), channel_id=1, source_target_pairs={{0,2},{2,0},{4,6},{6,4},{8,10},{10,8},{12,14},{14,12},{16,18},{18,... | collective-permute-start | bytes 589832 | tf_op jit(solution)/shard_map/ppermute | solution.py:93
  25.3 1.0 %collective-permute-done.6.refs_1_ = bf16[8,32,512]{2,1,0:T(8,128)(2,1)S(1)} collective-permute-done((bf16[8,32,512]{2,1,0:T(8,128)(2,1)S(1)}, bf16[8,32,512]{2,1,0:T(8,128)(2,1)S(1)}, u32[]{:S(2)}, u32[]{:S(2)}) %collective-permute-start.6) | collective-permute-done | bytes 262176 | tf_op jit(solution)/shard_map/ppermute | solution.py:93
  26.3 0.1 halve.4
  26.4 1.6 %collective-permute-start.9 = (bf16[4,32,512]{2,1,0:T(8,128)(2,1)S(1)}, bf16[4,32,512]{2,1,0:T(8,128)(2,1)S(1)}, u32[]{:S(2)}, u32[]{:S(2)}) collective-permute-start(bf16[4,32,512]{2,1,0:T(8,128)(2,1)S(1)} %get-tuple-element.39.after), channel_id=1, source_target_pairs={{0,4},{2,6},{4,0},{6,2},{8,12},{10,14},{12,8},{14,10},{16,20},{18,... | collective-permute-start | bytes 393224 | tf_op jit(solution)/shard_map/ppermute | solution.py:93
  28.0 0.6 %collective-permute-start.8 = (bf16[4,24,512]{2,1,0:T(8,128)(2,1)S(1)}, bf16[4,24,512]{2,1,0:T(8,128)(2,1)S(1)}, u32[]{:S(2)}, u32[]{:S(2)}) collective-permute-start(bf16[4,24,512]{2,1,0:T(8,128)(2,1)S(1)} %get-tuple-element.45), channel_id=1, source_target_pairs={{0,4},{2,6},{4,0},{6,2},{8,12},{10,14},{12,8},{14,10},{16,20},{18,... | collective-permute-start | bytes 294920 | tf_op jit(solution)/shard_map/ppermute | solution.py:93
  28.6 3.2 %spread.1 = bf16[384,8192]{1,0:T(8,128)(2,1)} custom-call(f32[8,128]{1,0:T(8,128)S(1)} %get-tuple-element.30.refs_4_.full, f32[32,384]{1,0:T(8,128)S(1)} %project.5.part, f32[32,384]{1,0:T(8,128)S(1)} %collective-permute-done.2.got, bf16[24,8192]{1,0:T(8,128)(2,1)S(1)} %get-tuple-element.31.refs_0_.own, ...), custom_call_target="tpu_custom_call" | custom-call | flops 1 | bytes 1 | tf_op jit(solution)/shard_map/spread/pallas_call | solution.py:267
  31.8 2.3 %collective-permute-done.8.refs_2_ = bf16[4,24,512]{2,1,0:T(8,128)(2,1)S(1)} collective-permute-done((bf16[4,24,512]{2,1,0:T(8,128)(2,1)S(1)}, bf16[4,24,512]{2,1,0:T(8,128)(2,1)S(1)}, u32[]{:S(2)}, u32[]{:S(2)}) %collective-permute-start.8) | collective-permute-done | bytes 98336 | tf_op jit(solution)/shard_map/ppermute | solution.py:93
  34.2 1.6 %collective-permute-start.10 = (bf16[2,56,512]{2,1,0:T(8,128)(2,1)S(1)}, bf16[2,56,512]{2,1,0:T(8,128)(2,1)S(1)}, u32[]{:S(2)}, u32[]{:S(2)}) collective-permute-start(bf16[2,56,512]{2,1,0:T(8,128)(2,1)S(1)} %get-tuple-element.48), channel_id=1, source_target_pairs={{0,8},{2,10},{4,12},{6,14},{8,0},{10,2},{12,4},{14,6},{16,24},{18,... | collective-permute-start | bytes 344072 | tf_op jit(solution)/shard_map/ppermute | solution.py:93
  35.8 3.2 %collective-permute-done.10.refs_1_ = bf16[2,56,512]{2,1,0:T(8,128)(2,1)S(1)} collective-permute-done((bf16[2,56,512]{2,1,0:T(8,128)(2,1)S(1)}, bf16[2,56,512]{2,1,0:T(8,128)(2,1)S(1)}, u32[]{:S(2)}, u32[]{:S(2)}) %collective-permute-start.10) | collective-permute-done | bytes 114720 | tf_op jit(solution)/shard_map/ppermute | solution.py:93
  39.1 2.7 %collective-permute-start.11 = (bf16[1,56,512]{2,1,0:T(8,128)(2,1)S(1)}, bf16[1,56,512]{2,1,0:T(8,128)(2,1)S(1)}, u32[]{:S(2)}, u32[]{:S(2)}) collective-permute-start(bf16[1,56,512]{2,1,0:T(8,128)(2,1)S(1)} %get-tuple-element.50), channel_id=1, source_target_pairs={{0,16},{2,18},{4,20},{6,22},{8,24},{10,26},{12,28},{14,30},{16,0},... | collective-permute-start | bytes 172040 | tf_op jit(solution)/shard_map/ppermute | solution.py:93
  41.7 2.5 %collective-permute-done.11.got = bf16[1,56,512]{2,1,0:T(8,128)(2,1)S(1)} collective-permute-done((bf16[1,56,512]{2,1,0:T(8,128)(2,1)S(1)}, bf16[1,56,512]{2,1,0:T(8,128)(2,1)S(1)}, u32[]{:S(2)}, u32[]{:S(2)}) %collective-permute-start.11) | collective-permute-done | bytes 57376 | tf_op jit(solution)/shard_map/ppermute | solution.py:93
  44.3 0.4 collective-permute-start.12
  44.6 4.3 %collective-permute-done.12.got = f32[2,24,512]{2,1,0:T(8,128)S(1)} collective-permute-done((f32[2,24,512]{2,1,0:T(8,128)S(1)}, f32[2,24,512]{2,1,0:T(8,128)S(1)}, u32[]{:S(2)}, u32[]{:S(2)}) %collective-permute-start.12) | collective-permute-done | bytes 98336 | tf_op jit(solution)/shard_map/ppermute | solution.py:422
  48.9 0.7 %place.1 = (f32[24,2,1,512]{3,2,1,0:T(1,128)}, f32[24,2,1,512]{3,2,1,0:T(1,128)}) custom-call(f32[2,24,512]{2,1,0:T(8,128)S(1)} %get-tuple-element.51.held, f32[2,24,512]{2,1,0:T(8,128)S(1)} %collective-permute-done.12.got), custom_call_target="tpu_custom_call" | custom-call | flops 1 | bytes 1 | tf_op jit(solution)/shard_map/place/pallas_call | solution.py:317
  (13 shorter events, 0.4 us)
Async XLA Ops:
  0.6 8.0 %copy-start = (s32[2]{0:T(128)S(1)}, s32[2]{0:T(128)}, u32[]{:S(2)}) copy-start(s32[2]{0:T(128)} %refs_0_.1) | copy-start | bytes 28
  1.6 10.6 %collective-permute-start = (bf16[24,4096]{1,0:T(8,128)(2,1)S(1)}, bf16[24,4096]{1,0:T(8,128)(2,1)S(1)}, u32[]{:S(2)}, u32[]{:S(2)}) collective-permute-start(bf16[24,4096]{1,0:T(8,128)(2,1)S(1)} %pick.3), channel_id=1, source_target_pairs={{0,1},{1,0},{2,3},{3,2},{4,5},{5,4},{6,7},{7,6},{8,9},{9,8},{10,11... | collective-permute-start | bytes 589832 | tf_op jit(solution)/shard_map/ppermute | solution.py:387
  5.6 8.2 %collective-permute-start.3 = (bf16[24,4096]{1,0:T(8,128)(2,1)S(1)}, bf16[24,4096]{1,0:T(8,128)(2,1)S(1)}, u32[]{:S(2)}, u32[]{:S(2)}) collective-permute-start(bf16[24,4096]{1,0:T(8,128)(2,1)S(1)} %pick.2.refs_0_), channel_id=1, source_target_pairs={{0,1},{1,0},{2,3},{3,2},{4,5},{5,4},{6,7},{7,6},{8,9},{9,8},{10,11... | collective-permute-start | bytes 589832 | tf_op jit(solution)/shard_map/ppermute | solution.py:388
  12.2 2.8 %collective-permute-start.1 = (bf16[24,4096]{1,0:T(8,128)(2,1)S(1)}, bf16[24,4096]{1,0:T(8,128)(2,1)S(1)}, u32[]{:S(2)}, u32[]{:S(2)}) collective-permute-start(bf16[24,4096]{1,0:T(8,128)(2,1)S(1)} %collective-permute-done.refs_1_), channel_id=1, source_target_pairs={{0,2},{2,0},{4,6},{6,4},{8,10},{10,8},{12,14},{14,12},{16,18},{18,... | collective-permute-start | bytes 589832 | tf_op jit(solution)/shard_map/ppermute | solution.py:93
  13.7 4.5 %collective-permute-start.4 = (bf16[24,4096]{1,0:T(8,128)(2,1)S(1)}, bf16[24,4096]{1,0:T(8,128)(2,1)S(1)}, u32[]{:S(2)}, u32[]{:S(2)}) collective-permute-start(bf16[24,4096]{1,0:T(8,128)(2,1)S(1)} %collective-permute-done.3.refs_1_.mine), channel_id=1, source_target_pairs={{0,2},{2,0},{4,6},{6,4},{8,10},{10,8},{12,14},{14,12},{16,18},{18,... | collective-permute-start | bytes 589832 | tf_op jit(solution)/shard_map/ppermute | solution.py:93
  16.2 4.2 %collective-permute-start.2 = (f32[32,384]{1,0:T(8,128)S(1)}, f32[32,384]{1,0:T(8,128)S(1)}, u32[]{:S(2)}, u32[]{:S(2)}) collective-permute-start(f32[32,384]{1,0:T(8,128)S(1)} %project.5.part), channel_id=1, source_target_pairs={{0,1},{1,0},{2,3},{3,2},{4,5},{5,4},{6,7},{7,6},{8,9},{9,8},{10,11... | collective-permute-start | bytes 147464 | tf_op jit(solution)/shard_map/ppermute | solution.py:397
  19.3 4.2 %collective-permute-start.5 = (f32[32,384]{1,0:T(8,128)S(1)}, f32[32,384]{1,0:T(8,128)S(1)}, u32[]{:S(2)}, u32[]{:S(2)}) collective-permute-start(f32[32,384]{1,0:T(8,128)S(1)} %project.7.refs_0_.part), channel_id=1, source_target_pairs={{0,1},{1,0},{2,3},{3,2},{4,5},{5,4},{6,7},{7,6},{8,9},{9,8},{10,11... | collective-permute-start | bytes 147464 | tf_op jit(solution)/shard_map/ppermute | solution.py:400
  24.7 1.6 %collective-permute-start.6 = (bf16[8,32,512]{2,1,0:T(8,128)(2,1)S(1)}, bf16[8,32,512]{2,1,0:T(8,128)(2,1)S(1)}, u32[]{:S(2)}, u32[]{:S(2)}) collective-permute-start(bf16[8,32,512]{2,1,0:T(8,128)(2,1)S(1)} %get-tuple-element.38), channel_id=1, source_target_pairs={{0,2},{2,0},{4,6},{6,4},{8,10},{10,8},{12,14},{14,12},{16,18},{18,... | collective-permute-start | bytes 786440 | tf_op jit(solution)/shard_map/ppermute | solution.py:93
  24.8 3.2 %collective-permute-start.7 = (bf16[8,24,512]{2,1,0:T(8,128)(2,1)S(1)}, bf16[8,24,512]{2,1,0:T(8,128)(2,1)S(1)}, u32[]{:S(2)}, u32[]{:S(2)}) collective-permute-start(bf16[8,24,512]{2,1,0:T(8,128)(2,1)S(1)} %get-tuple-element.41), channel_id=1, source_target_pairs={{0,2},{2,0},{4,6},{6,4},{8,10},{10,8},{12,14},{14,12},{16,18},{18,... | collective-permute-start | bytes 589832 | tf_op jit(solution)/shard_map/ppermute | solution.py:93
  26.4 7.7 %collective-permute-start.9 = (bf16[4,32,512]{2,1,0:T(8,128)(2,1)S(1)}, bf16[4,32,512]{2,1,0:T(8,128)(2,1)S(1)}, u32[]{:S(2)}, u32[]{:S(2)}) collective-permute-start(bf16[4,32,512]{2,1,0:T(8,128)(2,1)S(1)} %get-tuple-element.39.after), channel_id=1, source_target_pairs={{0,4},{2,6},{4,0},{6,2},{8,12},{10,14},{12,8},{14,10},{16,20},{18,... | collective-permute-start | bytes 393224 | tf_op jit(solution)/shard_map/ppermute | solution.py:93
  28.0 6.1 %collective-permute-start.8 = (bf16[4,24,512]{2,1,0:T(8,128)(2,1)S(1)}, bf16[4,24,512]{2,1,0:T(8,128)(2,1)S(1)}, u32[]{:S(2)}, u32[]{:S(2)}) collective-permute-start(bf16[4,24,512]{2,1,0:T(8,128)(2,1)S(1)} %get-tuple-element.45), channel_id=1, source_target_pairs={{0,4},{2,6},{4,0},{6,2},{8,12},{10,14},{12,8},{14,10},{16,20},{18,... | collective-permute-start | bytes 294920 | tf_op jit(solution)/shard_map/ppermute | solution.py:93
  34.2 4.9 %collective-permute-start.10 = (bf16[2,56,512]{2,1,0:T(8,128)(2,1)S(1)}, bf16[2,56,512]{2,1,0:T(8,128)(2,1)S(1)}, u32[]{:S(2)}, u32[]{:S(2)}) collective-permute-start(bf16[2,56,512]{2,1,0:T(8,128)(2,1)S(1)} %get-tuple-element.48), channel_id=1, source_target_pairs={{0,8},{2,10},{4,12},{6,14},{8,0},{10,2},{12,4},{14,6},{16,24},{18,... | collective-permute-start | bytes 344072 | tf_op jit(solution)/shard_map/ppermute | solution.py:93
  39.1 5.1 %collective-permute-start.11 = (bf16[1,56,512]{2,1,0:T(8,128)(2,1)S(1)}, bf16[1,56,512]{2,1,0:T(8,128)(2,1)S(1)}, u32[]{:S(2)}, u32[]{:S(2)}) collective-permute-start(bf16[1,56,512]{2,1,0:T(8,128)(2,1)S(1)} %get-tuple-element.50), channel_id=1, source_target_pairs={{0,16},{2,18},{4,20},{6,22},{8,24},{10,26},{12,28},{14,30},{16,0},... | collective-permute-start | bytes 172040 | tf_op jit(solution)/shard_map/ppermute | solution.py:93
  44.3 4.7 %collective-permute-start.12 = (f32[2,24,512]{2,1,0:T(8,128)S(1)}, f32[2,24,512]{2,1,0:T(8,128)S(1)}, u32[]{:S(2)}, u32[]{:S(2)}) collective-permute-start(f32[2,24,512]{2,1,0:T(8,128)S(1)} %get-tuple-element.52), channel_id=1, source_target_pairs={{0,1},{1,0},{2,3},{3,2},{4,5},{5,4},{6,7},{7,6},{8,9},{9,8},{10,11... | collective-permute-start | bytes 294920 | tf_op jit(solution)/shard_map/ppermute | solution.py:422

commit v3 on v2

--- a/solution.py
+++ b/solution.py
@@ -74,7 +74,6 @@
 PAD = 8
 SWAP = [(0, 1), (1, 0)]
 WHOLE = pl.BlockSpec(memory_space=pltpu.VMEM)
-SCALARS = pl.BlockSpec(memory_space=pltpu.SMEM)
 FAR = pl.BlockSpec(memory_space=pltpu.HBM)
 SMALL = pl.CostEstimate(flops=1, bytes_accessed=1, transcendentals=0)
 PARAMS = pltpu.CompilerParams(vmem_limit_bytes=16 * 1024 * 1024)
@@ -88,54 +87,58 @@
     return pltpu.with_memory_space_constraint(value, pltpu.HBM)
 
 
-def flip(value, bit):
-    size = lax.axis_size("dp")
-    return lax.ppermute(value, "dp", [(i, i ^ (1 << bit)) for i in range(size)])
+def flip(value, *bits):
+    mask = sum(1 << bit for bit in bits)
+    return lax.ppermute(value, "dp", [(i, i ^ mask) for i in range(lax.axis_size("dp"))])
 
 
 def after_all(value, *others):
     return lax.optimization_barrier((value, *others))[0]
 
 
-def stage_kernel(parts, given, acts, factor, *refs):
-    acts_out, factor_out = refs[given : given + 2]
-    sems = refs[-1]
-    width = factor_out.shape[1]
-    column = pl.multiple_of(lax.axis_index("tensor") * width, width)
-    rows = acts.shape[0] // parts
-    copies = [pltpu.make_async_copy(factor.at[:, pl.ds(column, width)], factor_out, sems.at[0])]
-    for n in range(parts):
-        piece = pl.ds(n * rows, rows)
-        copies.append(pltpu.make_async_copy(acts.at[piece], acts_out.at[piece], sems.at[n + 1]))
+def stage_kernel(parts, rank, *refs):
+    sources, outs, full_out, rank_here, sems = refs[:4], refs[6:10], *refs[10:]
+    copies = [pltpu.make_async_copy(rank, rank_here, sems.at[0])]
+    for source, out in zip(sources, outs):
+        if source.shape == out.shape:
+            rows = source.shape[0] // parts
+            pairs = [
+                (source.at[pl.ds(n * rows, rows)], out.at[pl.ds(n * rows, rows)])
+                for n in range(parts)
+            ]
+        else:
+            width = out.shape[1]
+            column = pl.multiple_of(lax.axis_index("tensor") * width, width)
+            pairs = [(source.at[:, pl.ds(column, width)], out)]
+        for pair in pairs:
+            copies.append(pltpu.make_async_copy(*pair, sems.at[len(copies)]))
     for copy in copies:
         copy.start()
-    if len(refs) == given + 4:
-        rank, full_out = refs[0], refs[given + 2]
-        own_rank = jnp.where(lax.axis_index("tensor") == 0, rank[0], rank[1])
-        full = (own_rank == factor.shape[0]).astype(jnp.float32)
-        full_out[...] = jnp.full(full_out.shape, full)
+    copies.pop(0).wait()
+    own_rank = jnp.where(lax.axis_index("tensor") == 0, rank_here[0], rank_here[1])
+    full = (own_rank == outs[0].shape[0]).astype(jnp.float32)
+    full_out[...] = jnp.full(full_out.shape, full)
     for copy in copies:
         copy.wait()
 
 
-def stage(acts, factor, rank, after):
-    shapes = [
-        pltpu.VMEM(acts.shape, acts.dtype),
-        pltpu.VMEM((factor.shape[0], acts.shape[1]), factor.dtype),
-    ]
-    if rank:
-        shapes.append(pltpu.VMEM((8, 128), jnp.float32))
-    parts = 8 if acts.shape[0] % 128 == 0 else 1
-    return pl.pallas_call(
-        functools.partial(stage_kernel, parts, len(rank) + len(after)),
-        in_specs=[FAR] * 2 + [SCALARS] * len(rank) + [WHOLE] * len(after),
-        out_specs=[WHOLE] * len(shapes),
-        out_shape=shapes,
-        scratch_shapes=[pltpu.SemaphoreType.DMA((1 + parts,))],
+def stage(rank, right, cotangent, left, tokens, after):
+    acts = pltpu.VMEM(tokens.shape, tokens.dtype)
+    own = pltpu.VMEM((left.shape[0], tokens.shape[1]), left.dtype)
+    parts = 8 if tokens.shape[0] % 128 == 0 else 1
+    return pl.pallas_call(
+        functools.partial(stage_kernel, parts),
+        in_specs=[FAR] * 5 + [WHOLE] * 2,
+        out_specs=[WHOLE] * 5,
+        out_shape=[own, acts, own, acts, pltpu.VMEM((8, 128), jnp.float32)],
+        scratch_shapes=[
+            pltpu.SMEM(rank.shape, rank.dtype),
+            pltpu.SemaphoreType.DMA((3 + 2 * parts,)),
+        ],
         compiler_params=PARAMS,
         cost_estimate=SMALL,
         name="stage",
-    )(far(acts), far(factor), *rank, *map(near, after))
+    )(*map(far, (rank, right, cotangent, left, tokens)), *map(near, after))
 
 
 def own_is_full(full):
@@ -288,17 +291,17 @@
         rows = total[n * slots : (n + 1) * slots]
         short = jnp.where(first, total[2 * slots + row : 2 * slots + row + 1], 0.0)
         held[n] = jnp.where(full_here, rows, short)
-        send[n] = jnp.where(full_here, short, rows)
+        send[n] = jnp.where(full_here, short, rows).astype(send.dtype)
 
 
 def settle(full, keep, got):
     rows, block = keep.shape[1:]
-    shape = pltpu.VMEM((2, (rows - PAD) // 2, block), jnp.float32)
+    shape = (2, (rows - PAD) // 2, block)
     return pl.pallas_call(
         settle_kernel,
         in_specs=[WHOLE] * 3,
         out_specs=[WHOLE, WHOLE],
-        out_shape=[shape, shape],
+        out_shape=[pltpu.VMEM(shape, jnp.float32), pltpu.VMEM(shape, jnp.bfloat16)],
         compiler_params=PARAMS,
         cost_estimate=SMALL,
         name="settle",
@@ -308,8 +311,9 @@
 def place_kernel(held, got, left_out, right_out):
     here = lax.axis_index("tensor") == 0
     for n, out in enumerate((left_out, right_out)):
-        out[:, 0, 0, :] = jnp.where(here, held[n], got[n])
-        out[:, 1, 0, :] = jnp.where(here, got[n], held[n])
+        arrived = got[n].astype(out.dtype)
+        out[:, 0, 0, :] = jnp.where(here, held[n], arrived)
+        out[:, 1, 0, :] = jnp.where(here, arrived, held[n])
 
 
 def place(held, got):
@@ -325,107 +329,135 @@
     )(near(held), near(got))
 
 
-def pick_kernel(factor, out, sem):
-    part = out.shape[1]
+def pick_kernel(*refs):
+    sources, outs, sems = refs[:2], refs[2:4], refs[4]
+    part = outs[0].shape[1]
     core = lax.axis_index("dp") % 2
     column = ((1 - lax.axis_index("tensor")) * 2 + core) * part
-    copy = pltpu.make_async_copy(
-        factor.at[:, pl.ds(pl.multiple_of(column, part), part)], out, sem
-    )
-    copy.start()
-    copy.wait()
-
-
-def pick(factor):
-    slots, width = factor.shape
+    here = pl.ds(pl.multiple_of(column, part), part)
+    copies = [
+        pltpu.make_async_copy(source.at[:, here], out, sems.at[n])
+        for n, (source, out) in enumerate(zip(sources, outs))
+    ]
+    for copy in copies:
+        copy.start()
+    for copy in copies:
+        copy.wait()
+
+
+def pick(right, left):
+    slots, width = left.shape
     return pl.pallas_call(
         pick_kernel,
-        in_specs=[FAR],
-        out_specs=WHOLE,
-        out_shape=pltpu.VMEM((slots, width // 4), factor.dtype),
-        scratch_shapes=[pltpu.SemaphoreType.DMA],
+        in_specs=[FAR] * 2,
+        out_specs=[WHOLE] * 2,
+        out_shape=[pltpu.VMEM((slots, width // 4), left.dtype)] * 2,
+        scratch_shapes=[pltpu.SemaphoreType.DMA((2,))],
         compiler_params=PARAMS,
         cost_estimate=SMALL,
         name="pick",
-    )(far(factor))
-
-
-def halve_kernel(bit, count, *refs):
-    keep_out, send_out = refs[2 * count :]
+    )(far(right), far(left))
+
+
+def quarter_kernel(*refs):
+    keeps, gots, outs = refs[:2], refs[2:4], refs[4:]
+    blocks = outs[0].shape[0]
+    place = lax.axis_index("dp") // 2
+    for n, out in enumerate(outs):
+        bit_1, bit_2 = (place + n % 2) % 2, (place // 2 + n // 2) % 2
+        first = (bit_1 * 2 + bit_2) * blocks
+        row = 0
+        for keep, got in zip(keeps, gots):
+            rows = keep.shape[1]
+            for block in range(blocks):
+                total = keep[first + block] + got[first + block].astype(jnp.float32)
+                out[block, row : row + rows] = total.astype(out.dtype)
+            row += rows
+
+
+def quarter(keeps, gots):
+    blocks, _, block = keeps[0].shape
+    shape = (blocks // 4, sum(keep.shape[1] for keep in keeps), block)
+    return pl.pallas_call(
+        quarter_kernel,
+        in_specs=[WHOLE] * 4,
+        out_specs=[WHOLE] * 4,
+        out_shape=[pltpu.VMEM(shape, jnp.float32)] + [pltpu.VMEM(shape, jnp.bfloat16)] * 3,
+        compiler_params=PARAMS,
+        cost_estimate=SMALL,
+        name="quarter",
+    )(*map(near, (*keeps, *gots)))
+
+
+def halve_kernel(bit, keep, *refs):
+    gots, (keep_out, send_out) = refs[:-2], refs[-2:]
     blocks = keep_out.shape[0]
     even = (lax.axis_index("dp") // (1 << bit)) % 2 == 0
-    row = 0
-    for keep, got in zip(refs[:count], refs[count : 2 * count]):
-        rows = keep.shape[1]
-        low = keep[:blocks] + got[:blocks].astype(jnp.float32)
-        high = keep[blocks:] + got[blocks:].astype(jnp.float32)
-        keep_out[:, row : row + rows] = jnp.where(even, low, high)
-        send_out[:, row : row + rows] = jnp.where(even, high, low).astype(send_out.dtype)
-        row += rows
-
-
-def halve(keeps, gots, bit):
-    blocks, _, block = keeps[0].shape
-    rows = sum(keep.shape[1] for keep in keeps)
+    low, high = keep[:blocks], keep[blocks:]
+    for got in gots:
+        low += got[:blocks].astype(jnp.float32)
+        high += got[blocks:].astype(jnp.float32)
+    keep_out[...] = jnp.where(even, low, high)
+    send_out[...] = jnp.where(even, high, low).astype(send_out.dtype)
+
+
+def halve(keep, gots, bit):
+    blocks, rows, block = keep.shape
     shape = (blocks // 2, rows, block)
     return pl.pallas_call(
-        functools.partial(halve_kernel, bit, len(keeps)),
-        in_specs=[WHOLE] * (2 * len(keeps)),
+        functools.partial(halve_kernel, bit),
+        in_specs=[WHOLE] * (1 + len(gots)),
         out_specs=[WHOLE, WHOLE],
         out_shape=[pltpu.VMEM(shape, jnp.float32), pltpu.VMEM(shape, jnp.bfloat16)],
         compiler_params=PARAMS,
         cost_estimate=SMALL,
         name="halve",
-    )(*map(near, (*keeps, *gots)))
+    )(*map(near, (keep, *gots)))
 
 
 def two_panels(tokens, cotangent, left_factor, right_factor, panel_rank):
     scale = 1.0 / math.sqrt(tokens.shape[0] * lax.axis_size("dp"))
 
-    right_wanted = pick(right_factor)
-    left_wanted = pick(left_factor)
+    right_wanted, left_wanted = pick(right_factor, left_factor)
     right_mine = lax.ppermute(right_wanted, "tensor", SWAP)
     left_mine = lax.ppermute(left_wanted, "tensor", SWAP)
-    cotangent, right_own = stage(cotangent, right_factor, (), (left_wanted,))
-    tokens, left_own, full = stage(tokens, left_factor, (panel_rank,), (right_own,))
+    right_own, cotangent, left_own, tokens, full = stage(
+        panel_rank, right_factor, cotangent, left_factor, tokens, (right_wanted, left_wanted)
+    )
     right_mine = after_all(right_mine, left_own)
     right_theirs = flip(right_mine, 0)
     back = project(right_own, right_mine, cotangent, False, (), ())
     left_mine = after_all(left_mine, back)
+    left_theirs = flip(left_mine, 0)
     back = project(right_own, right_theirs, cotangent, True, (back, full), ())
-    left_theirs = flip(left_mine, 0)
-    back_got = lax.ppermute(back, "tensor", SWAP)
     hidden = project(left_own, left_mine, tokens, False, (), (cotangent,))
     hidden = project(left_own, left_theirs, tokens, True, (hidden, full), (cotangent,))
+    back, hidden = lax.optimization_barrier((back, hidden))
+    back_got = lax.ppermute(back, "tensor", SWAP)
     hidden_got = lax.ppermute(hidden, "tensor", SWAP)
 
     left_keep, left_send, extra = gradient(
-        back, back_got, tokens, scale, (), (hidden, cotangent)
+        back, back_got, tokens, scale, (), (cotangent,)
     )
     left_got = flip(left_send, 0)
     right_keep, right_send = gradient(hidden, hidden_got, cotangent, scale, (extra,), ())
     right_got = flip(right_send, 0)
-    left_got = after_all(left_got, right_send)
-    left_keep, left_send = halve((left_keep,), (left_got,), 1)
-    left_got = flip(left_send, 1)
-    right_keep, right_send = halve((right_keep,), (right_got,), 1)
-    right_got = flip(right_send, 1)
-    token_grad = spread(full, back, back_got, left_own, left_mine, left_theirs, right_send)
-    left_got = after_all(left_got, token_grad)
-    keep, send = halve((left_keep, right_keep), (left_got, right_got), 2)
-    got = flip(send, 2)
+    keep, *sends = quarter((left_keep, right_keep), (left_got, right_got))
+    gots = [flip(sends[2], 1, 2), flip(sends[0], 1), flip(sends[1], 2)]
+    token_grad = spread(full, back, back_got, left_own, left_mine, left_theirs, sends[0])
+    gots[0] = after_all(gots[0], token_grad)
     for bit in range(3, lax.axis_size("dp").bit_length() - 1):
-        keep, send = halve((keep,), (got,), bit)
-        got = flip(send, bit)
-
-    held, send = settle(full, keep, got)
+        keep, send = halve(keep, gots, bit)
+        gots = (flip(send, bit),)
+
+    held, send = settle(full, keep, gots[0])
     return token_grad, *place(held, lax.ppermute(send, "tensor", SWAP))
 
 
 def solution(mesh):
     placed = (P("dp", "tensor"), P("dp", "tensor"), P("tensor", None), P("tensor", None), P())
     size = mesh.shape["dp"]
-    halves = size & (size - 1) == 0 and size >= 8
+    halves = size & (size - 1) == 0 and size >= 16
     return jax.shard_map(
         two_panels if mesh.shape["tensor"] == 2 and halves else any_panels,
         mesh=mesh,

time: 49.8 us -> 45.2 us (0.908)
  waiting for transfers between devices: 16.5 us -> 13.7 us
  Pallas kernels: 19.3 us -> 16.9 us
  starting transfers between devices: 13 us -> 13.7 us
    ppermute x8, waiting for transfers between devices: 9.03 us -> 5.75 us  [flip(): lax.ppermute(value, 'dp', [(i, i ^ mask) for i in range(lax.axis_size('dp...]
    pallas_call x8 -> x4, Pallas kernels: 8.63 us -> 6.17 us  [the longest x1 4.98 us: stage(): pl.pallas_call(functools.partial(stage_kernel, parts), in_specs=[FAR] * 5...]
    ppermute x1, waiting for transfers between devices: 0.34 us -> 2.29 us  [two_panels(): left_mine = lax.ppermute(left_wanted, 'tensor', SWAP)]
    ppermute x1, waiting for transfers between devices: 4.31 us -> 2.42 us  [two_panels(): return (token_grad, *place(held, lax.ppermute(send, 'tensor', SWAP)))]
    ppermute x1, waiting for transfers between devices: 1.95 us -> 0.47 us  [two_panels(): hidden_got = lax.ppermute(hidden, 'tensor', SWAP)]
    ppermute x1, starting transfers between devices: 0.37 us -> 1.74 us  [two_panels(): return (token_grad, *place(held, lax.ppermute(send, 'tensor', SWAP)))]
    ppermute x1, waiting for transfers between devices: 0.9 us -> 2.13 us  [two_panels(): back_got = lax.ppermute(back, 'tensor', SWAP)]
    ppermute x1, waiting for transfers between devices: 0.01 us -> 0.67 us  [two_panels(): right_mine = lax.ppermute(right_wanted, 'tensor', SWAP)]
  transfers between devices with their start and end apart: 13 -> 13, of which waited for: 8 -> 9; matrix products, arithmetic and copies ran while one was open for 0% -> 0% of each run, Pallas kernels for 33% -> 28%
where the time goes in v3:
time: 45.2 us; the launch traced here: 45.1 us
  Pallas kernels  16.9 us (37%)
  starting transfers between devices  13.7 us (30%)
  waiting for transfers between devices  13.7 us (30%)
  between operations  0.73 us (2%)
    ppermute x8, starting transfers between devices, flip(): lax.ppermute(value, 'dp', [(i, i ^ mask) for i in range(lax.axis_size('dp...  6.78 us
    ppermute x8, waiting for transfers between devices, flip(): lax.ppermute(value, 'dp', [(i, i ^ mask) for i in range(lax.axis_size('dp...  5.75 us
    pallas_call x1, Pallas kernels, stage(): pl.pallas_call(functools.partial(stage_kernel, parts), in_specs=[FAR] * 5...  4.98 us
    pallas_call x4, Pallas kernels, project(): pl.pallas_call(functools.partial(project_kernel, flipped, min(width, 2048...  4.39 us
    pallas_call x1, Pallas kernels, spread(): pl.pallas_call(functools.partial(spread_kernel, chunk), in_specs=[WHOLE]...  3.18 us
    ppermute x1, starting transfers between devices, two_panels(): right_mine = lax.ppermute(right_wanted, 'tensor', SWAP)  3.03 us
    ppermute x1, waiting for transfers between devices, two_panels(): return (token_grad, *place(held, lax.ppermute(send, 'tensor', SWAP)))  2.42 us
    pallas_call x2, Pallas kernels, gradient(): pl.pallas_call(functools.partial(gradient_kernel, scale, places, len(extr...  2.42 us
  transfers between devices with their start and end apart: 13, of which 9 were waited for; matrix products, arithmetic and copies ran while one was open for 0% of the time, Pallas kernels for 28%

profile of v3, /device:TPU:0, one launch (start us, length us, event | category | flops | bytes accessed | tf_op | source)
XLA Modules:
  0.0 45.1 jit_solution(13212625958706218071)
XLA Ops:
  0.6 1.1 %pick.1 = (bf16[24,4096]{1,0:T(8,128)(2,1)S(1)}, bf16[24,4096]{1,0:T(8,128)(2,1)S(1)}) custom-call(bf16[24,16384]{1,0:T(8,128)(2,1)} %refs_0_.3, bf16[24,16384]{1,0:T(8,128)(2,1)} %refs_2_.1), custom_call_target="tpu_custom_call" | custom-call | flops 1 | bytes 1 | tf_op jit(solution)/shard_map/pick/pallas_call | solution.py:350
  1.7 3.0 %collective-permute-start = (bf16[24,4096]{1,0:T(8,128)(2,1)S(1)}, bf16[24,4096]{1,0:T(8,128)(2,1)S(1)}, u32[]{:S(2)}, u32[]{:S(2)}) collective-permute-start(bf16[24,4096]{1,0:T(8,128)(2,1)S(1)} %get-tuple-element.30.refs_4_), channel_id=1, source_target_pairs={{0,1},{1,0},{2,3},{3,2},{4,5},{5,4},{6,7},{7,6},{8,9},{9,8},{10,11... | collective-permute-start | bytes 589832 | tf_op jit(solution)/shard_map/ppermute | solution.py:422
  4.7 0.1 collective-permute-start.2
  4.8 5.0 %stage.1 = (bf16[24,8192]{1,0:T(8,128)(2,1)S(1)}, bf16[384,8192]{1,0:T(8,128)(2,1)S(1)}, bf16[24,8192]{1,0:T(8,128)(2,1)S(1)}, bf16[384,8192]{1,0:T(8,128)(2,1)S(1)}, f32[8,128]{1,0:T(8,128)S(1)}) custom-call(s32[2]{0:T(128)} %rank.1, bf16[24,16384]{1,0:T(8,128)(2,1)} %refs_0_.3, bf16[384,8192]{1,0:T(8,128)(2,1)} %refs_1_.3, bf16[24,16384]{1,0:T(8,128)(2,1)} %refs_2_.1, ...), custom_call_target="tpu_custom_call" | custom-call | flops 1 | bytes 1 | tf_op jit(solution)/shard_map/stage/pallas_call | solution.py:129
  9.8 0.7 %collective-permute-done.refs_1_ = bf16[24,4096]{1,0:T(8,128)(2,1)S(1)} collective-permute-done((bf16[24,4096]{1,0:T(8,128)(2,1)S(1)}, bf16[24,4096]{1,0:T(8,128)(2,1)S(1)}, u32[]{:S(2)}, u32[]{:S(2)}) %collective-permute-start) | collective-permute-done | bytes 196640 | tf_op jit(solution)/shard_map/ppermute | solution.py:422
  10.5 1.1 %project.4.refs_3_ = f32[64,384]{1,0:T(8,128)S(1)} custom-call(bf16[24,8192]{1,0:T(8,128)(2,1)S(1)} %get-tuple-element.33.refs_0_, bf16[24,4096]{1,0:T(8,128)(2,1)S(1)} %collective-permute-done.refs_1_, bf16[384,8192]{1,0:T(8,128)(2,1)S(1)} %get-tuple-element.36.refs_2_.refs_3_.refs_5_.refs_0_.acts), custom_call_target="tpu_custom_call" | custom-call | flops 1 | bytes 1 | tf_op jit(solution)/shard_map/project/pallas_call | solution.py:183
  11.5 2.3 %collective-permute-done.2.refs_1_.mine = bf16[24,4096]{1,0:T(8,128)(2,1)S(1)} collective-permute-done((bf16[24,4096]{1,0:T(8,128)(2,1)S(1)}, bf16[24,4096]{1,0:T(8,128)(2,1)S(1)}, u32[]{:S(2)}, u32[]{:S(2)}) %collective-permute-start.2) | collective-permute-done | bytes 196640 | tf_op jit(solution)/shard_map/ppermute | solution.py:423
  13.8 1.1 %project.6.refs_3_ = f32[64,384]{1,0:T(8,128)S(1)} custom-call(bf16[24,8192]{1,0:T(8,128)(2,1)S(1)} %get-tuple-element.34.refs_0_.own, bf16[24,4096]{1,0:T(8,128)(2,1)S(1)} %collective-permute-done.2.refs_1_.mine, bf16[384,8192]{1,0:T(8,128)(2,1)S(1)} %get-tuple-element.38.refs_2_.acts, ...), custom_call_target="tpu_custom_call" | custom-call | flops 1 | bytes 1 | tf_op jit(solution)/shard_map/project/pallas_call | solution.py:183
  14.9 1.1 %project.5.part = f32[32,384]{1,0:T(8,128)S(1)} custom-call(bf16[24,8192]{1,0:T(8,128)(2,1)S(1)} %get-tuple-element.33.refs_0_, bf16[24,4096]{1,0:T(8,128)(2,1)S(1)} %collective-permute-done.1.refs_1_, bf16[384,8192]{1,0:T(8,128)(2,1)S(1)} %get-tuple-element.36.refs_2_.refs_3_.refs_5_.refs_0_.acts, f32[64,384]{1,0:T(8,128)S(1)} %project.4.refs_3_, ...), custom_call_target="tpu_custom_call" | custom-call | flops 1 | bytes 1 | tf_op jit(solution)/shard_map/project/pallas_call | solution.py:183
  16.1 1.1 %project.7.part = f32[32,384]{1,0:T(8,128)S(1)} custom-call(bf16[24,8192]{1,0:T(8,128)(2,1)S(1)} %get-tuple-element.34.refs_0_.own, bf16[24,4096]{1,0:T(8,128)(2,1)S(1)} %collective-permute-done.3.refs_1_.theirs, bf16[384,8192]{1,0:T(8,128)(2,1)S(1)} %get-tuple-element.38.refs_2_.acts, f32[64,384]{1,0:T(8,128)S(1)} %project.6.refs_3_, ...), custom_call_target="tpu_custom_call" | custom-call | flops 1 | bytes 1 | tf_op jit(solution)/shard_map/project/pallas_call | solution.py:183
  17.2 1.8 %collective-permute-start.4 = (f32[32,384]{1,0:T(8,128)S(1)}, f32[32,384]{1,0:T(8,128)S(1)}, u32[]{:S(2)}, u32[]{:S(2)}) collective-permute-start(f32[32,384]{1,0:T(8,128)S(1)} %project.5.part), channel_id=1, source_target_pairs={{0,1},{1,0},{2,3},{3,2},{4,5},{5,4},{6,7},{7,6},{8,9},{9,8},{10,11... | collective-permute-start | bytes 147464 | tf_op jit(solution)/shard_map/ppermute | solution.py:436
  19.0 0.3 collective-permute-start.5
  19.3 2.1 %collective-permute-done.4.got = f32[32,384]{1,0:T(8,128)S(1)} collective-permute-done((f32[32,384]{1,0:T(8,128)S(1)}, f32[32,384]{1,0:T(8,128)S(1)}, u32[]{:S(2)}, u32[]{:S(2)}) %collective-permute-start.4) | collective-permute-done | bytes 49184 | tf_op jit(solution)/shard_map/ppermute | solution.py:436
  21.4 1.2 %gradient.2 = (f32[8,24,512]{2,1,0:T(8,128)S(1)}, bf16[8,24,512]{2,1,0:T(8,128)(2,1)S(1)}, f32[8,8,1024]{2,1,0:T(8,128)S(1)}) custom-call(f32[32,384]{1,0:T(8,128)S(1)} %project.5.part, f32[32,384]{1,0:T(8,128)S(1)} %collective-permute-done.4.got, bf16[384,8192]{1,0:T(8,128)(2,1)S(1)} %get-tuple-element.38.refs_2_.acts, ...), custom_call_target="tpu_custom_call" | custom-call | flops 1 | bytes 1 | tf_op jit(solution)/shard_map/gradient/pallas_call | solution.py:229
  22.6 0.5 %collective-permute-done.5.got = f32[32,384]{1,0:T(8,128)S(1)} collective-permute-done((f32[32,384]{1,0:T(8,128)S(1)}, f32[32,384]{1,0:T(8,128)S(1)}, u32[]{:S(2)}, u32[]{:S(2)}) %collective-permute-start.5) | collective-permute-done | bytes 49184 | tf_op jit(solution)/shard_map/ppermute | solution.py:437
  23.1 1.2 %gradient.3 = (f32[8,32,512]{2,1,0:T(8,128)S(1)}, bf16[8,32,512]{2,1,0:T(8,128)(2,1)S(1)}) custom-call(f32[32,384]{1,0:T(8,128)S(1)} %project.7.part, f32[32,384]{1,0:T(8,128)S(1)} %collective-permute-done.5.got, bf16[384,8192]{1,0:T(8,128)(2,1)S(1)} %get-tuple-element.36.refs_2_.refs_3_.refs_5_.refs_0_.acts, f32[8,8,1024]{2,1,0:T(8,128)S(1)} %get-tuple-element.42.refs_0_), custom_call_target="tpu_custom_call" | custom-call | flops 1 | bytes 1 | tf_op jit(solution)/shard_map/gradient/pallas_call | solution.py:229
  24.3 0.1 collective-permute-start.7
  24.4 0.5 %collective-permute-start.6 = (bf16[8,24,512]{2,1,0:T(8,128)(2,1)S(1)}, bf16[8,24,512]{2,1,0:T(8,128)(2,1)S(1)}, u32[]{:S(2)}, u32[]{:S(2)}) collective-permute-start(bf16[8,24,512]{2,1,0:T(8,128)(2,1)S(1)} %get-tuple-element.44), channel_id=1, source_target_pairs={{0,2},{2,0},{4,6},{6,4},{8,10},{10,8},{12,14},{14,12},{16,18},{18,... | collective-permute-start | bytes 589832 | tf_op jit(solution)/shard_map/ppermute | solution.py:92
  24.9 1.3 %collective-permute-done.6.refs_2_ = bf16[8,24,512]{2,1,0:T(8,128)(2,1)S(1)} collective-permute-done((bf16[8,24,512]{2,1,0:T(8,128)(2,1)S(1)}, bf16[8,24,512]{2,1,0:T(8,128)(2,1)S(1)}, u32[]{:S(2)}, u32[]{:S(2)}) %collective-permute-start.6) | collective-permute-done | bytes 196640 | tf_op jit(solution)/shard_map/ppermute | solution.py:92
  26.2 0.1 quarter.1
  26.3 2.6 %collective-permute-start.8 = (bf16[2,56,512]{2,1,0:T(8,128)(2,1)S(1)}, bf16[2,56,512]{2,1,0:T(8,128)(2,1)S(1)}, u32[]{:S(2)}, u32[]{:S(2)}) collective-permute-start(bf16[2,56,512]{2,1,0:T(8,128)(2,1)S(1)} %get-tuple-element.48), channel_id=1, source_target_pairs={{0,12},{2,14},{4,8},{6,10},{8,4},{10,6},{12,0},{14,2},{16,28},{18,... | collective-permute-start | bytes 344072 | tf_op jit(solution)/shard_map/ppermute | solution.py:92
  28.8 0.4 collective-permute-start.10
  29.3 0.5 %collective-permute-start.9 = (bf16[2,56,512]{2,1,0:T(8,128)(2,1)S(1)}, bf16[2,56,512]{2,1,0:T(8,128)(2,1)S(1)}, u32[]{:S(2)}, u32[]{:S(2)}) collective-permute-start(bf16[2,56,512]{2,1,0:T(8,128)(2,1)S(1)} %get-tuple-element.46.after), channel_id=1, source_target_pairs={{0,4},{2,6},{4,0},{6,2},{8,12},{10,14},{12,8},{14,10},{16,20},{18,... | collective-permute-start | bytes 344072 | tf_op jit(solution)/shard_map/ppermute | solution.py:92
  29.8 3.2 %spread.1 = bf16[384,8192]{1,0:T(8,128)(2,1)} custom-call(f32[8,128]{1,0:T(8,128)S(1)} %get-tuple-element.32.refs_4_.full, f32[32,384]{1,0:T(8,128)S(1)} %project.5.part, f32[32,384]{1,0:T(8,128)S(1)} %collective-permute-done.4.got, bf16[24,8192]{1,0:T(8,128)(2,1)S(1)} %get-tuple-element.34.refs_0_.own, ...), custom_call_target="tpu_custom_call" | custom-call | flops 1 | bytes 1 | tf_op jit(solution)/shard_map/spread/pallas_call | solution.py:270
  33.0 0.2 collective-permute-done.8.refs_0_
  33.2 1.7 %collective-permute-done.10.refs_2_ = bf16[2,56,512]{2,1,0:T(8,128)(2,1)S(1)} collective-permute-done((bf16[2,56,512]{2,1,0:T(8,128)(2,1)S(1)}, bf16[2,56,512]{2,1,0:T(8,128)(2,1)S(1)}, u32[]{:S(2)}, u32[]{:S(2)}) %collective-permute-start.10) | collective-permute-done | bytes 114720 | tf_op jit(solution)/shard_map/ppermute | solution.py:92
  34.9 0.1 halve.1
  35.0 2.7 %collective-permute-start.11 = (bf16[1,56,512]{2,1,0:T(8,128)(2,1)S(1)}, bf16[1,56,512]{2,1,0:T(8,128)(2,1)S(1)}, u32[]{:S(2)}, u32[]{:S(2)}) collective-permute-start(bf16[1,56,512]{2,1,0:T(8,128)(2,1)S(1)} %get-tuple-element.52), channel_id=1, source_target_pairs={{0,16},{2,18},{4,20},{6,22},{8,24},{10,26},{12,28},{14,30},{16,0},... | collective-permute-start | bytes 172040 | tf_op jit(solution)/shard_map/ppermute | solution.py:92
  37.6 2.5 %collective-permute-done.11.got = bf16[1,56,512]{2,1,0:T(8,128)(2,1)S(1)} collective-permute-done((bf16[1,56,512]{2,1,0:T(8,128)(2,1)S(1)}, bf16[1,56,512]{2,1,0:T(8,128)(2,1)S(1)}, u32[]{:S(2)}, u32[]{:S(2)}) %collective-permute-start.11) | collective-permute-done | bytes 57376 | tf_op jit(solution)/shard_map/ppermute | solution.py:92
  40.2 1.7 %collective-permute-start.12 = (bf16[2,24,512]{2,1,0:T(8,128)(2,1)S(1)}, bf16[2,24,512]{2,1,0:T(8,128)(2,1)S(1)}, u32[]{:S(2)}, u32[]{:S(2)}) collective-permute-start(bf16[2,24,512]{2,1,0:T(8,128)(2,1)S(1)} %get-tuple-element.54), channel_id=1, source_target_pairs={{0,1},{1,0},{2,3},{3,2},{4,5},{5,4},{6,7},{7,6},{8,9},{9,8},{10,11... | collective-permute-start | bytes 147464 | tf_op jit(solution)/shard_map/ppermute | solution.py:454
  42.0 2.4 %collective-permute-done.12.got = bf16[2,24,512]{2,1,0:T(8,128)(2,1)S(1)} collective-permute-done((bf16[2,24,512]{2,1,0:T(8,128)(2,1)S(1)}, bf16[2,24,512]{2,1,0:T(8,128)(2,1)S(1)}, u32[]{:S(2)}, u32[]{:S(2)}) %collective-permute-start.12) | collective-permute-done | bytes 49184 | tf_op jit(solution)/shard_map/ppermute | solution.py:454
  44.4 0.7 %place.1 = (f32[24,2,1,512]{3,2,1,0:T(1,128)}, f32[24,2,1,512]{3,2,1,0:T(1,128)}) custom-call(f32[2,24,512]{2,1,0:T(8,128)S(1)} %get-tuple-element.53.held, bf16[2,24,512]{2,1,0:T(8,128)(2,1)S(1)} %collective-permute-done.12.got), custom_call_target="tpu_custom_call" | custom-call | flops 1 | bytes 1 | tf_op jit(solution)/shard_map/place/pallas_call | solution.py:321
  (7 shorter events, 0.1 us)
Async XLA Ops:
  1.7 8.8 %collective-permute-start = (bf16[24,4096]{1,0:T(8,128)(2,1)S(1)}, bf16[24,4096]{1,0:T(8,128)(2,1)S(1)}, u32[]{:S(2)}, u32[]{:S(2)}) collective-permute-start(bf16[24,4096]{1,0:T(8,128)(2,1)S(1)} %get-tuple-element.30.refs_4_), channel_id=1, source_target_pairs={{0,1},{1,0},{2,3},{3,2},{4,5},{5,4},{6,7},{7,6},{8,9},{9,8},{10,11... | collective-permute-start | bytes 589832 | tf_op jit(solution)/shard_map/ppermute | solution.py:422
  4.7 9.1 %collective-permute-start.2 = (bf16[24,4096]{1,0:T(8,128)(2,1)S(1)}, bf16[24,4096]{1,0:T(8,128)(2,1)S(1)}, u32[]{:S(2)}, u32[]{:S(2)}) collective-permute-start(bf16[24,4096]{1,0:T(8,128)(2,1)S(1)} %get-tuple-element.31.refs_5_), channel_id=1, source_target_pairs={{0,1},{1,0},{2,3},{3,2},{4,5},{5,4},{6,7},{7,6},{8,9},{9,8},{10,11... | collective-permute-start | bytes 589832 | tf_op jit(solution)/shard_map/ppermute | solution.py:423
  10.5 4.5 %collective-permute-start.1 = (bf16[24,4096]{1,0:T(8,128)(2,1)S(1)}, bf16[24,4096]{1,0:T(8,128)(2,1)S(1)}, u32[]{:S(2)}, u32[]{:S(2)}) collective-permute-start(bf16[24,4096]{1,0:T(8,128)(2,1)S(1)} %collective-permute-done.refs_1_), channel_id=1, source_target_pairs={{0,2},{2,0},{4,6},{6,4},{8,10},{10,8},{12,14},{14,12},{16,18},{18,... | collective-permute-start | bytes 589832 | tf_op jit(solution)/shard_map/ppermute | solution.py:92
  13.8 2.2 %collective-permute-start.3 = (bf16[24,4096]{1,0:T(8,128)(2,1)S(1)}, bf16[24,4096]{1,0:T(8,128)(2,1)S(1)}, u32[]{:S(2)}, u32[]{:S(2)}) collective-permute-start(bf16[24,4096]{1,0:T(8,128)(2,1)S(1)} %collective-permute-done.2.refs_1_.mine), channel_id=1, source_target_pairs={{0,2},{2,0},{4,6},{6,4},{8,10},{10,8},{12,14},{14,12},{16,18},{18,... | collective-permute-start | bytes 589832 | tf_op jit(solution)/shard_map/ppermute | solution.py:92
  17.2 4.2 %collective-permute-start.4 = (f32[32,384]{1,0:T(8,128)S(1)}, f32[32,384]{1,0:T(8,128)S(1)}, u32[]{:S(2)}, u32[]{:S(2)}) collective-permute-start(f32[32,384]{1,0:T(8,128)S(1)} %project.5.part), channel_id=1, source_target_pairs={{0,1},{1,0},{2,3},{3,2},{4,5},{5,4},{6,7},{7,6},{8,9},{9,8},{10,11... | collective-permute-start | bytes 147464 | tf_op jit(solution)/shard_map/ppermute | solution.py:436
  19.0 4.1 %collective-permute-start.5 = (f32[32,384]{1,0:T(8,128)S(1)}, f32[32,384]{1,0:T(8,128)S(1)}, u32[]{:S(2)}, u32[]{:S(2)}) collective-permute-start(f32[32,384]{1,0:T(8,128)S(1)} %project.7.part), channel_id=1, source_target_pairs={{0,1},{1,0},{2,3},{3,2},{4,5},{5,4},{6,7},{7,6},{8,9},{9,8},{10,11... | collective-permute-start | bytes 147464 | tf_op jit(solution)/shard_map/ppermute | solution.py:437
  24.3 1.9 %collective-permute-start.7 = (bf16[8,32,512]{2,1,0:T(8,128)(2,1)S(1)}, bf16[8,32,512]{2,1,0:T(8,128)(2,1)S(1)}, u32[]{:S(2)}, u32[]{:S(2)}) collective-permute-start(bf16[8,32,512]{2,1,0:T(8,128)(2,1)S(1)} %get-tuple-element.45), channel_id=1, source_target_pairs={{0,2},{2,0},{4,6},{6,4},{8,10},{10,8},{12,14},{14,12},{16,18},{18,... | collective-permute-start | bytes 786440 | tf_op jit(solution)/shard_map/ppermute | solution.py:92
  24.4 1.8 %collective-permute-start.6 = (bf16[8,24,512]{2,1,0:T(8,128)(2,1)S(1)}, bf16[8,24,512]{2,1,0:T(8,128)(2,1)S(1)}, u32[]{:S(2)}, u32[]{:S(2)}) collective-permute-start(bf16[8,24,512]{2,1,0:T(8,128)(2,1)S(1)} %get-tuple-element.44), channel_id=1, source_target_pairs={{0,2},{2,0},{4,6},{6,4},{8,10},{10,8},{12,14},{14,12},{16,18},{18,... | collective-permute-start | bytes 589832 | tf_op jit(solution)/shard_map/ppermute | solution.py:92
  26.3 7.0 %collective-permute-start.8 = (bf16[2,56,512]{2,1,0:T(8,128)(2,1)S(1)}, bf16[2,56,512]{2,1,0:T(8,128)(2,1)S(1)}, u32[]{:S(2)}, u32[]{:S(2)}) collective-permute-start(bf16[2,56,512]{2,1,0:T(8,128)(2,1)S(1)} %get-tuple-element.48), channel_id=1, source_target_pairs={{0,12},{2,14},{4,8},{6,10},{8,4},{10,6},{12,0},{14,2},{16,28},{18,... | collective-permute-start | bytes 344072 | tf_op jit(solution)/shard_map/ppermute | solution.py:92
  28.8 6.1 %collective-permute-start.10 = (bf16[2,56,512]{2,1,0:T(8,128)(2,1)S(1)}, bf16[2,56,512]{2,1,0:T(8,128)(2,1)S(1)}, u32[]{:S(2)}, u32[]{:S(2)}) collective-permute-start(bf16[2,56,512]{2,1,0:T(8,128)(2,1)S(1)} %get-tuple-element.50), channel_id=1, source_target_pairs={{0,8},{2,10},{4,12},{6,14},{8,0},{10,2},{12,4},{14,6},{16,24},{18,... | collective-permute-start | bytes 344072 | tf_op jit(solution)/shard_map/ppermute | solution.py:92
  29.3 5.6 %collective-permute-start.9 = (bf16[2,56,512]{2,1,0:T(8,128)(2,1)S(1)}, bf16[2,56,512]{2,1,0:T(8,128)(2,1)S(1)}, u32[]{:S(2)}, u32[]{:S(2)}) collective-permute-start(bf16[2,56,512]{2,1,0:T(8,128)(2,1)S(1)} %get-tuple-element.46.after), channel_id=1, source_target_pairs={{0,4},{2,6},{4,0},{6,2},{8,12},{10,14},{12,8},{14,10},{16,20},{18,... | collective-permute-start | bytes 344072 | tf_op jit(solution)/shard_map/ppermute | solution.py:92
  35.0 5.2 %collective-permute-start.11 = (bf16[1,56,512]{2,1,0:T(8,128)(2,1)S(1)}, bf16[1,56,512]{2,1,0:T(8,128)(2,1)S(1)}, u32[]{:S(2)}, u32[]{:S(2)}) collective-permute-start(bf16[1,56,512]{2,1,0:T(8,128)(2,1)S(1)} %get-tuple-element.52), channel_id=1, source_target_pairs={{0,16},{2,18},{4,20},{6,22},{8,24},{10,26},{12,28},{14,30},{16,0},... | collective-permute-start | bytes 172040 | tf_op jit(solution)/shard_map/ppermute | solution.py:92
  40.2 4.2 %collective-permute-start.12 = (bf16[2,24,512]{2,1,0:T(8,128)(2,1)S(1)}, bf16[2,24,512]{2,1,0:T(8,128)(2,1)S(1)}, u32[]{:S(2)}, u32[]{:S(2)}) collective-permute-start(bf16[2,24,512]{2,1,0:T(8,128)(2,1)S(1)} %get-tuple-element.54), channel_id=1, source_target_pairs={{0,1},{1,0},{2,3},{3,2},{4,5},{5,4},{6,7},{7,6},{8,9},{9,8},{10,11... | collective-permute-start | bytes 147464 | tf_op jit(solution)/shard_map/ppermute | solution.py:454

commit v4 on v3

--- a/solution.py
+++ b/solution.py
@@ -76,6 +76,7 @@
 WHOLE = pl.BlockSpec(memory_space=pltpu.VMEM)
 FAR = pl.BlockSpec(memory_space=pltpu.HBM)
 SMALL = pl.CostEstimate(flops=1, bytes_accessed=1, transcendentals=0)
+LONG = pl.CostEstimate(flops=10**10, bytes_accessed=10**8, transcendentals=0)
 PARAMS = pltpu.CompilerParams(vmem_limit_bytes=16 * 1024 * 1024)
 
 
@@ -191,16 +192,19 @@
     )(*map(near, (own, piece, acts, *others, *held)))
 
 
-def gradient_kernel(scale, places, given, held, part, got, acts, *refs):
+def gradient_kernel(scale, places, own, given, held, part, got, acts, *refs):
     outs = refs[given + held :]
     keep, send = outs[:2]
-    rows, block = keep.shape[1], keep.shape[2]
+    block = keep.shape[2]
     slots = part.shape[0] - PAD
-    even = lax.axis_index("dp") % 2 == 0
+    position = lax.axis_index("dp")
+    even = position % 2 == 0
+    bit_3 = (position // 8 + (0 if own else 1)) % 2
     summed = (part[...] + got[...]).astype(jnp.bfloat16)
     row = lax.broadcasted_iota(jnp.int32, (PAD, 2 * block), 0)
     for j, q in enumerate(places):
-        columns = slice(j * 2 * block, (j + 1) * 2 * block)
+        start = (bit_3 * len(places) + j) * 2 * block
+        columns = pl.ds(pl.multiple_of(start, 2 * block), 2 * block)
         grad = jnp.dot(summed, acts[:, columns], preferred_element_type=jnp.float32) * scale
         if given:
             short = jnp.where(row == 1, refs[0][q, 0:1, :], grad[slots:])
@@ -213,21 +217,18 @@
         send[q] = jnp.where(even, high, low).astype(send.dtype)
 
 
-def gradient(part, got, acts, scale, extra, held):
+def gradient(part, got, acts, scale, own, extra, held):
     live, tokens = part.shape
     slots = live - PAD
     width = acts.shape[1]
-    size = lax.axis_size("dp")
-    bits = size.bit_length() - 1
-    block = width // size
-    pairs = size // 2
-    places = [int(format(j, "0%db" % (bits - 1))[::-1], 2) for j in range(pairs)]
-    shape = (pairs, live if extra else slots, block)
+    block = width // lax.axis_size("dp")
+    places = (0, 2, 1, 3)
+    shape = (len(places), live if extra else slots, block)
     shapes = [pltpu.VMEM(shape, jnp.float32), pltpu.VMEM(shape, jnp.bfloat16)]
     if not extra:
-        shapes.append(pltpu.VMEM((pairs, PAD, 2 * block), jnp.float32))
-    return pl.pallas_call(
-        functools.partial(gradient_kernel, scale, places, len(extra), len(held)),
+        shapes.append(pltpu.VMEM((len(places), PAD, 2 * block), jnp.float32))
+    return pl.pallas_call(
+        functools.partial(gradient_kernel, scale, places, own, len(extra), len(held)),
         in_specs=[WHOLE] * (3 + len(extra) + len(held)),
         out_specs=[WHOLE] * len(shapes),
         out_shape=shapes,
@@ -237,9 +238,9 @@
     )(*map(near, (part, got, acts, *extra, *held)))
 
 
-def spread_kernel(chunk, full, part, got, own, mine, theirs, after, out, buffer, sems):
-    slots, width = mine.shape
-    core = lax.axis_index("dp") % 2
+def spread_kernel(theirs, chunk, given, full, part, got, own, piece, *refs):
+    out, buffer, sems = refs[given:]
+    slots, width = piece.shape
     full_here = own_is_full(full[...])
     back = part[...] + got[...]
     first = lax.broadcasted_iota(jnp.int32, (slots, back.shape[1]), 0) == 0
@@ -248,45 +249,50 @@
     of_other = jnp.where(full_here, short, back[:slots])
     gap = jnp.zeros((PAD, back.shape[1]), jnp.float32)
     weights = jnp.concatenate([of_own, gap, of_other, gap], axis=0).T.astype(jnp.bfloat16)
+    core = lax.axis_index("dp") % 2
+    start = (1 - core if theirs else core) * width
     copies = []
-    for side, piece in enumerate((mine, theirs)):
-        for low in range(0, width, chunk):
-            start = (core if side == 0 else 1 - core) * width + low
-            column = pl.ds(pl.multiple_of(start, chunk), chunk)
-            rows = both_panels(own[:, column], piece[:, low : low + chunk])
-            held = buffer.at[:, side * width + low : side * width + low + chunk]
-            held[...] = jnp.dot(weights, rows, preferred_element_type=jnp.float32).astype(out.dtype)
-            copy = pltpu.make_async_copy(held, out.at[:, column], sems.at[len(copies)])
-            copy.start()
-            copies.append(copy)
+    for low in range(0, width, chunk):
+        column = pl.ds(pl.multiple_of(start + low, chunk), chunk)
+        rows = both_panels(own[:, column], piece[:, low : low + chunk])
+        held = buffer.at[:, low : low + chunk]
+        held[...] = jnp.dot(weights, rows, preferred_element_type=jnp.float32).astype(out.dtype)
+        copy = pltpu.make_async_copy(held, out.at[:, column], sems.at[len(copies)])
+        copy.start()
+        copies.append(copy)
     for copy in copies:
         copy.wait()
 
 
-def spread(full, part, got, own, mine, theirs, after):
+def spread(full, part, got, own, piece, after, before):
     tokens = part.shape[1]
-    rows, width = own.shape
-    chunk = min(width // 2, 1024)
-    return pl.pallas_call(
-        functools.partial(spread_kernel, chunk),
-        in_specs=[WHOLE] * 7,
+    width = piece.shape[1]
+    chunk = min(width, 1024)
+    operands = tuple(map(near, (full, part, got, own, piece, after)))
+    return pl.pallas_call(
+        functools.partial(spread_kernel, len(before) > 0, chunk, 1 + len(before)),
+        in_specs=[WHOLE] * len(operands) + [FAR] * len(before),
         out_specs=FAR,
-        out_shape=jax.ShapeDtypeStruct((tokens, width), jnp.bfloat16),
+        out_shape=jax.ShapeDtypeStruct((tokens, 2 * width), jnp.bfloat16),
+        input_output_aliases={len(operands): 0} if before else {},
         scratch_shapes=[
             pltpu.VMEM((tokens, width), jnp.bfloat16),
             pltpu.SemaphoreType.DMA((width // chunk,)),
         ],
         compiler_params=PARAMS,
-        cost_estimate=SMALL,
+        cost_estimate=LONG,
         name="spread",
-    )(*map(near, (full, part, got, own, mine, theirs, after)))
-
-
-def settle_kernel(full, keep, got, held, send):
+    )(*operands, *before)
+
+
+def settle_kernel(count, full, keep, *refs):
+    gots, (held, send) = refs[:count], refs[count:]
     slots, block = held.shape[1:]
     full_here = own_is_full(full[...])
     first = lax.broadcasted_iota(jnp.int32, (slots, block), 0) == 0
-    total = keep[0] + got[0].astype(jnp.float32)
+    total = keep[...]
+    for got in gots:
+        total += got[...].astype(jnp.float32)
     for n, row in ((0, 1), (1, 0)):
         rows = total[n * slots : (n + 1) * slots]
         short = jnp.where(first, total[2 * slots + row : 2 * slots + row + 1], 0.0)
@@ -294,18 +300,18 @@
         send[n] = jnp.where(full_here, short, rows).astype(send.dtype)
 
 
-def settle(full, keep, got):
-    rows, block = keep.shape[1:]
+def settle(full, keep, gots):
+    rows, block = keep.shape
     shape = (2, (rows - PAD) // 2, block)
     return pl.pallas_call(
-        settle_kernel,
-        in_specs=[WHOLE] * 3,
+        functools.partial(settle_kernel, len(gots)),
+        in_specs=[WHOLE] * (2 + len(gots)),
         out_specs=[WHOLE, WHOLE],
         out_shape=[pltpu.VMEM(shape, jnp.float32), pltpu.VMEM(shape, jnp.bfloat16)],
         compiler_params=PARAMS,
         cost_estimate=SMALL,
         name="settle",
-    )(near(full), near(keep), near(got))
+    )(*map(near, (full, keep, *gots)))
 
 
 def place_kernel(held, got, left_out, right_out):
@@ -361,57 +367,50 @@
 
 def quarter_kernel(*refs):
     keeps, gots, outs = refs[:2], refs[2:4], refs[4:]
-    blocks = outs[0].shape[0]
     place = lax.axis_index("dp") // 2
     for n, out in enumerate(outs):
-        bit_1, bit_2 = (place + n % 2) % 2, (place // 2 + n // 2) % 2
-        first = (bit_1 * 2 + bit_2) * blocks
+        block = (place + n % 2) % 2 * 2 + (place // 2 + n // 2) % 2
         row = 0
         for keep, got in zip(keeps, gots):
             rows = keep.shape[1]
-            for block in range(blocks):
-                total = keep[first + block] + got[first + block].astype(jnp.float32)
-                out[block, row : row + rows] = total.astype(out.dtype)
+            total = keep[block] + got[block].astype(jnp.float32)
+            out[row : row + rows] = total.astype(out.dtype)
             row += rows
 
 
 def quarter(keeps, gots):
-    blocks, _, block = keeps[0].shape
-    shape = (blocks // 4, sum(keep.shape[1] for keep in keeps), block)
+    shape = (sum(keep.shape[1] for keep in keeps), keeps[0].shape[2])
     return pl.pallas_call(
         quarter_kernel,
         in_specs=[WHOLE] * 4,
         out_specs=[WHOLE] * 4,
-        out_shape=[pltpu.VMEM(shape, jnp.float32)] + [pltpu.VMEM(shape, jnp.bfloat16)] * 3,
+        out_shape=[pltpu.VMEM(shape, kind) for kind in [jnp.float32] + [jnp.bfloat16] * 3],
         compiler_params=PARAMS,
         cost_estimate=SMALL,
         name="quarter",
     )(*map(near, (*keeps, *gots)))
 
 
-def halve_kernel(bit, keep, *refs):
-    gots, (keep_out, send_out) = refs[:-2], refs[-2:]
-    blocks = keep_out.shape[0]
-    even = (lax.axis_index("dp") // (1 << bit)) % 2 == 0
-    low, high = keep[:blocks], keep[blocks:]
-    for got in gots:
-        low += got[:blocks].astype(jnp.float32)
-        high += got[blocks:].astype(jnp.float32)
-    keep_out[...] = jnp.where(even, low, high)
-    send_out[...] = jnp.where(even, high, low).astype(send_out.dtype)
-
-
-def halve(keep, gots, bit):
-    blocks, rows, block = keep.shape
-    shape = (blocks // 2, rows, block)
-    return pl.pallas_call(
-        functools.partial(halve_kernel, bit),
+def trade(sends):
+    return [flip(sends[2], 1, 2), flip(sends[0], 1), flip(sends[1], 2)]
+
+
+def add_kernel(*refs):
+    total = refs[0][...]
+    for got in refs[1:-1]:
+        total += got[...].astype(jnp.float32)
+    refs[-1][...] = total.astype(refs[-1].dtype)
+
+
+def add(keep, gots, kind):
+    return pl.pallas_call(
+        add_kernel,
         in_specs=[WHOLE] * (1 + len(gots)),
-        out_specs=[WHOLE, WHOLE],
-        out_shape=[pltpu.VMEM(shape, jnp.float32), pltpu.VMEM(shape, jnp.bfloat16)],
-        compiler_params=PARAMS,
-        cost_estimate=SMALL,
-        name="halve",
+        out_specs=WHOLE,
+        out_shape=pltpu.VMEM(keep.shape, kind),
+        compiler_params=PARAMS,
+        cost_estimate=SMALL,
+        name="add",
     )(*map(near, (keep, *gots)))
 
 
@@ -436,30 +435,34 @@
     back_got = lax.ppermute(back, "tensor", SWAP)
     hidden_got = lax.ppermute(hidden, "tensor", SWAP)
 
-    left_keep, left_send, extra = gradient(
-        back, back_got, tokens, scale, (), (cotangent,)
-    )
-    left_got = flip(left_send, 0)
-    right_keep, right_send = gradient(hidden, hidden_got, cotangent, scale, (extra,), ())
-    right_got = flip(right_send, 0)
-    keep, *sends = quarter((left_keep, right_keep), (left_got, right_got))
-    gots = [flip(sends[2], 1, 2), flip(sends[0], 1), flip(sends[1], 2)]
-    token_grad = spread(full, back, back_got, left_own, left_mine, left_theirs, sends[0])
-    gots[0] = after_all(gots[0], token_grad)
-    for bit in range(3, lax.axis_size("dp").bit_length() - 1):
-        keep, send = halve(keep, gots, bit)
-        gots = (flip(send, bit),)
-
-    held, send = settle(full, keep, gots[0])
-    return token_grad, *place(held, lax.ppermute(send, "tensor", SWAP))
+    lefts = [
+        gradient(back, back_got, tokens, scale, own, (), (cotangent,)) for own in (False, True)
+    ]
+    quarters = []
+    for own, (left_keep, left_send, extra) in enumerate(lefts):
+        right_keep, right_send = gradient(
+            hidden, hidden_got, cotangent, scale, own == 1, (extra,), (lefts[1][1],)
+        )
+        quarters.append(
+            quarter((left_keep, right_keep), (flip(left_send, 0), flip(right_send, 0)))
+        )
+    other, own = quarters
+    other_gots, own_gots = trade(other[1:]), trade(own[1:])
+    got = flip(add(other[0], other_gots, jnp.bfloat16), 3)
+    keep = add(own[0], own_gots, jnp.float32)
+    token_grad = spread(full, back, back_got, left_own, left_mine, keep, ())
+    got = after_all(got, token_grad)
+
+    held, send = settle(full, keep, (got,))
+    got = lax.ppermute(send, "tensor", SWAP)
+    token_grad = spread(full, back, back_got, left_own, left_theirs, send, (token_grad,))
+    return token_grad, *place(held, after_all(got, token_grad))
 
 
 def solution(mesh):
     placed = (P("dp", "tensor"), P("dp", "tensor"), P("tensor", None), P("tensor", None), P())
-    size = mesh.shape["dp"]
-    halves = size & (size - 1) == 0 and size >= 16
     return jax.shard_map(
-        two_panels if mesh.shape["tensor"] == 2 and halves else any_panels,
+        two_panels if (mesh.shape["tensor"], mesh.shape["dp"]) == (2, 16) else any_panels,
         mesh=mesh,
         in_specs=placed,
         out_specs=(P("dp", "tensor"), P("tensor", None, "dp", None), P("tensor", None, "dp", None)),

time: 45.2 us -> 43.8 us (0.969)
  waiting for transfers between devices: 13.7 us -> 6.61 us
  starting transfers between devices: 13.7 us -> 18 us
  Pallas kernels: 16.9 us -> 18.2 us
    ppermute x8 -> x13, waiting for transfers between devices: 5.75 us -> 1.06 us  [flip(): lax.ppermute(value, 'dp', [(i, i ^ mask) for i in range(lax.axis_size('dp...]
    ppermute x8 -> x13, starting transfers between devices: 6.78 us -> 10.9 us  [flip(): lax.ppermute(value, 'dp', [(i, i ^ mask) for i in range(lax.axis_size('dp...]
    ppermute x1, waiting for transfers between devices: 2.42 us -> 0.13 us  [two_panels(): got = lax.ppermute(send, 'tensor', SWAP)]
    pallas_call x5 -> x9, Pallas kernels: 5.7 us -> 7.06 us  [the longest x2 4.27 us: spread(): pl.pallas_call(functools.partial(spread_kernel, len(before) > 0, chunk, 1...]
  transfers between devices with their start and end apart: 13 -> 18, of which waited for: 9 -> 7; matrix products, arithmetic and copies ran while one was open for 0% -> 0% of each run, Pallas kernels for 28% -> 34%
where the time goes in v4:
time: 43.8 us; the launch traced here: 43.6 us
  Pallas kernels  18.2 us (42%)
  starting transfers between devices  18 us (41%)
  waiting for transfers between devices  6.61 us (15%)
  between operations  0.78 us (2%)
    ppermute x13, starting transfers between devices, flip(): lax.ppermute(value, 'dp', [(i, i ^ mask) for i in range(lax.axis_size('dp...  10.9 us
    pallas_call x1, Pallas kernels, stage(): pl.pallas_call(functools.partial(stage_kernel, parts), in_specs=[FAR] * 5...  4.98 us
    pallas_call x4, Pallas kernels, project(): pl.pallas_call(functools.partial(project_kernel, flipped, min(width, 2048...  4.36 us
    pallas_call x2, Pallas kernels, spread(): pl.pallas_call(functools.partial(spread_kernel, len(before) > 0, chunk, 1...  4.27 us
    ppermute x1, starting transfers between devices, two_panels(): right_mine = lax.ppermute(right_wanted, 'tensor', SWAP)  3.03 us
    pallas_call x4, Pallas kernels, gradient(): pl.pallas_call(functools.partial(gradient_kernel, scale, places, own, len...  2.68 us
    ppermute x1, waiting for transfers between devices, two_panels(): left_mine = lax.ppermute(left_wanted, 'tensor', SWAP)  2.3 us
    ppermute x1, waiting for transfers between devices, two_panels(): back_got = lax.ppermute(back, 'tensor', SWAP)  2.13 us
  transfers between devices with their start and end apart: 18, of which 7 were waited for; matrix products, arithmetic and copies ran while one was open for 0% of the time, Pallas kernels for 34%

profile of v4, /device:TPU:0, one launch (start us, length us, event | category | flops | bytes accessed | tf_op | source)
XLA Modules:
  0.0 43.6 jit_solution(15759212615832412248)
XLA Ops:
  0.6 1.1 %pick.1 = (bf16[24,4096]{1,0:T(8,128)(2,1)S(1)}, bf16[24,4096]{1,0:T(8,128)(2,1)S(1)}) custom-call(bf16[24,16384]{1,0:T(8,128)(2,1)} %refs_0_.3, bf16[24,16384]{1,0:T(8,128)(2,1)} %refs_2_.1), custom_call_target="tpu_custom_call" | custom-call | flops 1 | bytes 1 | tf_op jit(solution)/shard_map/pick/pallas_call | solution.py:356
  1.7 3.0 %collective-permute-start = (bf16[24,4096]{1,0:T(8,128)(2,1)S(1)}, bf16[24,4096]{1,0:T(8,128)(2,1)S(1)}, u32[]{:S(2)}, u32[]{:S(2)}) collective-permute-start(bf16[24,4096]{1,0:T(8,128)(2,1)S(1)} %get-tuple-element.38.refs_4_), channel_id=1, source_target_pairs={{0,1},{1,0},{2,3},{3,2},{4,5},{5,4},{6,7},{7,6},{8,9},{9,8},{10,11... | collective-permute-start | bytes 589832 | tf_op jit(solution)/shard_map/ppermute | solution.py:421
  4.8 5.0 %stage.1 = (bf16[24,8192]{1,0:T(8,128)(2,1)S(1)}, bf16[384,8192]{1,0:T(8,128)(2,1)S(1)}, bf16[24,8192]{1,0:T(8,128)(2,1)S(1)}, bf16[384,8192]{1,0:T(8,128)(2,1)S(1)}, f32[8,128]{1,0:T(8,128)S(1)}) custom-call(s32[2]{0:T(128)} %rank.1, bf16[24,16384]{1,0:T(8,128)(2,1)} %refs_0_.3, bf16[384,8192]{1,0:T(8,128)(2,1)} %refs_1_.3, bf16[24,16384]{1,0:T(8,128)(2,1)} %refs_2_.1, ...), custom_call_target="tpu_custom_call" | custom-call | flops 1 | bytes 1 | tf_op jit(solution)/shard_map/stage/pallas_call | solution.py:130
  9.8 0.7 %collective-permute-done.refs_1_ = bf16[24,4096]{1,0:T(8,128)(2,1)S(1)} collective-permute-done((bf16[24,4096]{1,0:T(8,128)(2,1)S(1)}, bf16[24,4096]{1,0:T(8,128)(2,1)S(1)}, u32[]{:S(2)}, u32[]{:S(2)}) %collective-permute-start) | collective-permute-done | bytes 196640 | tf_op jit(solution)/shard_map/ppermute | solution.py:421
  10.5 1.1 %project.4.refs_3_ = f32[64,384]{1,0:T(8,128)S(1)} custom-call(bf16[24,8192]{1,0:T(8,128)(2,1)S(1)} %get-tuple-element.41.refs_0_, bf16[24,4096]{1,0:T(8,128)(2,1)S(1)} %collective-permute-done.refs_1_, bf16[384,8192]{1,0:T(8,128)(2,1)S(1)} %get-tuple-element.44.refs_2_.refs_3_.refs_5_.refs_0_.acts), custom_call_target="tpu_custom_call" | custom-call | flops 1 | bytes 1 | tf_op jit(solution)/shard_map/project/pallas_call | solution.py:184
  11.5 2.3 %collective-permute-done.2.refs_1_.piece = bf16[24,4096]{1,0:T(8,128)(2,1)S(1)} collective-permute-done((bf16[24,4096]{1,0:T(8,128)(2,1)S(1)}, bf16[24,4096]{1,0:T(8,128)(2,1)S(1)}, u32[]{:S(2)}, u32[]{:S(2)}) %collective-permute-start.2) | collective-permute-done | bytes 196640 | tf_op jit(solution)/shard_map/ppermute | solution.py:422
  13.8 1.1 %project.6.refs_3_ = f32[64,384]{1,0:T(8,128)S(1)} custom-call(bf16[24,8192]{1,0:T(8,128)(2,1)S(1)} %get-tuple-element.42.refs_0_.own, bf16[24,4096]{1,0:T(8,128)(2,1)S(1)} %collective-permute-done.2.refs_1_.piece, bf16[384,8192]{1,0:T(8,128)(2,1)S(1)} %get-tuple-element.46.refs_2_.acts, ...), custom_call_target="tpu_custom_call" | custom-call | flops 1 | bytes 1 | tf_op jit(solution)/shard_map/project/pallas_call | solution.py:184
  14.9 1.1 %project.5.part = f32[32,384]{1,0:T(8,128)S(1)} custom-call(bf16[24,8192]{1,0:T(8,128)(2,1)S(1)} %get-tuple-element.41.refs_0_, bf16[24,4096]{1,0:T(8,128)(2,1)S(1)} %collective-permute-done.1.refs_1_, bf16[384,8192]{1,0:T(8,128)(2,1)S(1)} %get-tuple-element.44.refs_2_.refs_3_.refs_5_.refs_0_.acts, f32[64,384]{1,0:T(8,128)S(1)} %project.4.refs_3_, ...), custom_call_target="tpu_custom_call" | custom-call | flops 1 | bytes 1 | tf_op jit(solution)/shard_map/project/pallas_call | solution.py:184
  16.1 1.1 %project.7.part = f32[32,384]{1,0:T(8,128)S(1)} custom-call(bf16[24,8192]{1,0:T(8,128)(2,1)S(1)} %get-tuple-element.42.refs_0_.own, bf16[24,4096]{1,0:T(8,128)(2,1)S(1)} %collective-permute-done.3.refs_1_.piece, bf16[384,8192]{1,0:T(8,128)(2,1)S(1)} %get-tuple-element.46.refs_2_.acts, f32[64,384]{1,0:T(8,128)S(1)} %project.6.refs_3_, ...), custom_call_target="tpu_custom_call" | custom-call | flops 1 | bytes 1 | tf_op jit(solution)/shard_map/project/pallas_call | solution.py:184
  17.2 1.8 %collective-permute-start.4 = (f32[32,384]{1,0:T(8,128)S(1)}, f32[32,384]{1,0:T(8,128)S(1)}, u32[]{:S(2)}, u32[]{:S(2)}) collective-permute-start(f32[32,384]{1,0:T(8,128)S(1)} %project.5.part), channel_id=1, source_target_pairs={{0,1},{1,0},{2,3},{3,2},{4,5},{5,4},{6,7},{7,6},{8,9},{9,8},{10,11... | collective-permute-start | bytes 147464 | tf_op jit(solution)/shard_map/ppermute | solution.py:435
  19.0 0.3 collective-permute-start.5
  19.3 2.1 %collective-permute-done.4.got = f32[32,384]{1,0:T(8,128)S(1)} collective-permute-done((f32[32,384]{1,0:T(8,128)S(1)}, f32[32,384]{1,0:T(8,128)S(1)}, u32[]{:S(2)}, u32[]{:S(2)}) %collective-permute-start.4) | collective-permute-done | bytes 49184 | tf_op jit(solution)/shard_map/ppermute | solution.py:435
  21.4 0.7 %gradient.6 = (f32[4,24,512]{2,1,0:T(8,128)S(1)}, bf16[4,24,512]{2,1,0:T(8,128)(2,1)S(1)}, f32[4,8,1024]{2,1,0:T(8,128)S(1)}) custom-call(f32[32,384]{1,0:T(8,128)S(1)} %project.5.part, f32[32,384]{1,0:T(8,128)S(1)} %collective-permute-done.4.got, bf16[384,8192]{1,0:T(8,128)(2,1)S(1)} %get-tuple-element.46.refs_2_.acts, ...), custom_call_target="tpu_custom_call" | custom-call | flops 1 | bytes 1 | tf_op jit(solution)/shard_map/gradient/pallas_call | solution.py:230
  22.1 0.7 %gradient.4 = (f32[4,24,512]{2,1,0:T(8,128)S(1)}, bf16[4,24,512]{2,1,0:T(8,128)(2,1)S(1)}, f32[4,8,1024]{2,1,0:T(8,128)S(1)}) custom-call(f32[32,384]{1,0:T(8,128)S(1)} %project.5.part, f32[32,384]{1,0:T(8,128)S(1)} %collective-permute-done.4.got, bf16[384,8192]{1,0:T(8,128)(2,1)S(1)} %get-tuple-element.46.refs_2_.acts, ...), custom_call_target="tpu_custom_call" | custom-call | flops 1 | bytes 1 | tf_op jit(solution)/shard_map/gradient/pallas_call | solution.py:230
  22.7 0.3 collective-permute-done.5.got
  23.1 0.7 %gradient.7 = (f32[4,32,512]{2,1,0:T(8,128)S(1)}, bf16[4,32,512]{2,1,0:T(8,128)(2,1)S(1)}) custom-call(f32[32,384]{1,0:T(8,128)S(1)} %project.7.part, f32[32,384]{1,0:T(8,128)S(1)} %collective-permute-done.5.got, bf16[384,8192]{1,0:T(8,128)(2,1)S(1)} %get-tuple-element.44.refs_2_.refs_3_.refs_5_.refs_0_.acts, f32[4,8,1024]{2,1,0:T(8,128)S(1)} %get-tuple-element.59.refs_0_, ...), custom_call_target="tpu_custom_call" | custom-call | flops 1 | bytes 1 | tf_op jit(solution)/shard_map/gradient/pallas_call | solution.py:230
  23.8 0.5 %collective-permute-start.11 = (bf16[4,24,512]{2,1,0:T(8,128)(2,1)S(1)}, bf16[4,24,512]{2,1,0:T(8,128)(2,1)S(1)}, u32[]{:S(2)}, u32[]{:S(2)}) collective-permute-start(bf16[4,24,512]{2,1,0:T(8,128)(2,1)S(1)} %get-tuple-element.61), channel_id=1, source_target_pairs={{0,2},{2,0},{4,6},{6,4},{8,10},{10,8},{12,14},{14,12},{16,18},{18,... | collective-permute-start | bytes 294920 | tf_op jit(solution)/shard_map/ppermute | solution.py:93
  24.3 0.7 %gradient.5 = (f32[4,32,512]{2,1,0:T(8,128)S(1)}, bf16[4,32,512]{2,1,0:T(8,128)(2,1)S(1)}) custom-call(f32[32,384]{1,0:T(8,128)S(1)} %project.7.part, f32[32,384]{1,0:T(8,128)S(1)} %collective-permute-done.5.got, bf16[384,8192]{1,0:T(8,128)(2,1)S(1)} %get-tuple-element.44.refs_2_.refs_3_.refs_5_.refs_0_.acts, f32[4,8,1024]{2,1,0:T(8,128)S(1)} %get-tuple-element.50.refs_0_, ...), custom_call_target="tpu_custom_call" | custom-call | flops 1 | bytes 1 | tf_op jit(solution)/shard_map/gradient/pallas_call | solution.py:230
  25.1 0.4 collective-permute-start.6
  25.6 2.6 %collective-permute-start.13 = (bf16[56,512]{1,0:T(8,128)(2,1)S(1)}, bf16[56,512]{1,0:T(8,128)(2,1)S(1)}, u32[]{:S(2)}, u32[]{:S(2)}) collective-permute-start(bf16[56,512]{1,0:T(8,128)(2,1)S(1)} %get-tuple-element.64), channel_id=1, source_target_pairs={{0,12},{2,14},{4,8},{6,10},{8,4},{10,6},{12,0},{14,2},{16,28},{18,... | collective-permute-start | bytes 172040 | tf_op jit(solution)/shard_map/ppermute | solution.py:93
  28.2 0.5 %collective-permute-start.14 = (bf16[56,512]{1,0:T(8,128)(2,1)S(1)}, bf16[56,512]{1,0:T(8,128)(2,1)S(1)}, u32[]{:S(2)}, u32[]{:S(2)}) collective-permute-start(bf16[56,512]{1,0:T(8,128)(2,1)S(1)} %get-tuple-element.65), channel_id=1, source_target_pairs={{0,4},{2,6},{4,0},{6,2},{8,12},{10,14},{12,8},{14,10},{16,20},{18,... | collective-permute-start | bytes 172040 | tf_op jit(solution)/shard_map/ppermute | solution.py:93
  28.7 0.4 %collective-permute-start.15 = (bf16[56,512]{1,0:T(8,128)(2,1)S(1)}, bf16[56,512]{1,0:T(8,128)(2,1)S(1)}, u32[]{:S(2)}, u32[]{:S(2)}) collective-permute-start(bf16[56,512]{1,0:T(8,128)(2,1)S(1)} %get-tuple-element.66), channel_id=1, source_target_pairs={{0,8},{2,10},{4,12},{6,14},{8,0},{10,2},{12,4},{14,6},{16,24},{18,... | collective-permute-start | bytes 172040 | tf_op jit(solution)/shard_map/ppermute | solution.py:93
  29.2 2.6 %collective-permute-start.8 = (bf16[56,512]{1,0:T(8,128)(2,1)S(1)}, bf16[56,512]{1,0:T(8,128)(2,1)S(1)}, u32[]{:S(2)}, u32[]{:S(2)}) collective-permute-start(bf16[56,512]{1,0:T(8,128)(2,1)S(1)} %get-tuple-element.55), channel_id=1, source_target_pairs={{0,12},{2,14},{4,8},{6,10},{8,4},{10,6},{12,0},{14,2},{16,28},{18,... | collective-permute-start | bytes 172040 | tf_op jit(solution)/shard_map/ppermute | solution.py:93
  31.8 0.5 %collective-permute-start.9 = (bf16[56,512]{1,0:T(8,128)(2,1)S(1)}, bf16[56,512]{1,0:T(8,128)(2,1)S(1)}, u32[]{:S(2)}, u32[]{:S(2)}) collective-permute-start(bf16[56,512]{1,0:T(8,128)(2,1)S(1)} %get-tuple-element.56), channel_id=1, source_target_pairs={{0,4},{2,6},{4,0},{6,2},{8,12},{10,14},{12,8},{14,10},{16,20},{18,... | collective-permute-start | bytes 172040 | tf_op jit(solution)/shard_map/ppermute | solution.py:93
  32.4 0.5 %collective-permute-start.10 = (bf16[56,512]{1,0:T(8,128)(2,1)S(1)}, bf16[56,512]{1,0:T(8,128)(2,1)S(1)}, u32[]{:S(2)}, u32[]{:S(2)}) collective-permute-start(bf16[56,512]{1,0:T(8,128)(2,1)S(1)} %get-tuple-element.57), channel_id=1, source_target_pairs={{0,8},{2,10},{4,12},{6,14},{8,0},{10,2},{12,4},{14,6},{16,24},{18,... | collective-permute-start | bytes 172040 | tf_op jit(solution)/shard_map/ppermute | solution.py:93
  32.8 0.5 %collective-permute-done.15.refs_3_ = bf16[56,512]{1,0:T(8,128)(2,1)S(1)} collective-permute-done((bf16[56,512]{1,0:T(8,128)(2,1)S(1)}, bf16[56,512]{1,0:T(8,128)(2,1)S(1)}, u32[]{:S(2)}, u32[]{:S(2)}) %collective-permute-start.15) | collective-permute-done | bytes 57376 | tf_op jit(solution)/shard_map/ppermute | solution.py:93
  33.3 2.6 %collective-permute-start.16 = (bf16[56,512]{1,0:T(8,128)(2,1)S(1)}, bf16[56,512]{1,0:T(8,128)(2,1)S(1)}, u32[]{:S(2)}, u32[]{:S(2)}) collective-permute-start(bf16[56,512]{1,0:T(8,128)(2,1)S(1)} %add.3), channel_id=1, source_target_pairs={{0,16},{2,18},{4,20},{6,22},{8,24},{10,26},{12,28},{14,30},{16,0},... | collective-permute-start | bytes 172040 | tf_op jit(solution)/shard_map/ppermute | solution.py:93
  36.0 0.5 %collective-permute-done.10.refs_3_ = bf16[56,512]{1,0:T(8,128)(2,1)S(1)} collective-permute-done((bf16[56,512]{1,0:T(8,128)(2,1)S(1)}, bf16[56,512]{1,0:T(8,128)(2,1)S(1)}, u32[]{:S(2)}, u32[]{:S(2)}) %collective-permute-start.10) | collective-permute-done | bytes 57376 | tf_op jit(solution)/shard_map/ppermute | solution.py:93
  36.6 2.1 %spread.2.refs_1_ = bf16[384,8192]{1,0:T(8,128)(2,1)} custom-call(f32[8,128]{1,0:T(8,128)S(1)} %get-tuple-element.40.refs_4_.full, f32[32,384]{1,0:T(8,128)S(1)} %project.5.part, f32[32,384]{1,0:T(8,128)S(1)} %collective-permute-done.4.got, bf16[24,8192]{1,0:T(8,128)(2,1)S(1)} %get-tuple-element.42.refs_0_.own, ...), custom_call_target="tpu_custom_call" | custom-call | flops 10000000000 | bytes 100000000 | tf_op jit(solution)/shard_map/spread/pallas_call | solution.py:272
  38.8 1.9 %collective-permute-start.17 = (bf16[2,24,512]{2,1,0:T(8,128)(2,1)S(1)}, bf16[2,24,512]{2,1,0:T(8,128)(2,1)S(1)}, u32[]{:S(2)}, u32[]{:S(2)}) collective-permute-start(bf16[2,24,512]{2,1,0:T(8,128)(2,1)S(1)} %get-tuple-element.68.refs_0_), channel_id=1, source_target_pairs={{0,1},{1,0},{2,3},{3,2},{4,5},{5,4},{6,7},{7,6},{8,9},{9,8},{10,11... | collective-permute-start | bytes 147464 | tf_op jit(solution)/shard_map/ppermute | solution.py:457
  40.7 2.1 %spread.3 = bf16[384,8192]{1,0:T(8,128)(2,1)} custom-call(f32[8,128]{1,0:T(8,128)S(1)} %get-tuple-element.40.refs_4_.full, f32[32,384]{1,0:T(8,128)S(1)} %project.5.part, f32[32,384]{1,0:T(8,128)S(1)} %collective-permute-done.4.got, bf16[24,8192]{1,0:T(8,128)(2,1)S(1)} %get-tuple-element.42.refs_0_.own, ...), custom_call_target="tpu_custom_call", output_to_operand_aliasing={{}: (6, {})} | custom-call | flops 10000000000 | bytes 100000000 | tf_op jit(solution)/shard_map/spread/pallas_call | solution.py:272
  42.9 0.7 %place.1 = (f32[24,2,1,512]{3,2,1,0:T(1,128)}, f32[24,2,1,512]{3,2,1,0:T(1,128)}) custom-call(f32[2,24,512]{2,1,0:T(8,128)S(1)} %get-tuple-element.69.held, bf16[2,24,512]{2,1,0:T(8,128)(2,1)S(1)} %collective-permute-done.17.got), custom_call_target="tpu_custom_call" | custom-call | flops 1 | bytes 1 | tf_op jit(solution)/shard_map/place/pallas_call | solution.py:327
  (22 shorter events, 0.7 us)
Async XLA Ops:
  1.7 8.8 %collective-permute-start = (bf16[24,4096]{1,0:T(8,128)(2,1)S(1)}, bf16[24,4096]{1,0:T(8,128)(2,1)S(1)}, u32[]{:S(2)}, u32[]{:S(2)}) collective-permute-start(bf16[24,4096]{1,0:T(8,128)(2,1)S(1)} %get-tuple-element.38.refs_4_), channel_id=1, source_target_pairs={{0,1},{1,0},{2,3},{3,2},{4,5},{5,4},{6,7},{7,6},{8,9},{9,8},{10,11... | collective-permute-start | bytes 589832 | tf_op jit(solution)/shard_map/ppermute | solution.py:421
  4.7 9.1 %collective-permute-start.2 = (bf16[24,4096]{1,0:T(8,128)(2,1)S(1)}, bf16[24,4096]{1,0:T(8,128)(2,1)S(1)}, u32[]{:S(2)}, u32[]{:S(2)}) collective-permute-start(bf16[24,4096]{1,0:T(8,128)(2,1)S(1)} %get-tuple-element.39.refs_5_), channel_id=1, source_target_pairs={{0,1},{1,0},{2,3},{3,2},{4,5},{5,4},{6,7},{7,6},{8,9},{9,8},{10,11... | collective-permute-start | bytes 589832 | tf_op jit(solution)/shard_map/ppermute | solution.py:422
  10.5 4.5 %collective-permute-start.1 = (bf16[24,4096]{1,0:T(8,128)(2,1)S(1)}, bf16[24,4096]{1,0:T(8,128)(2,1)S(1)}, u32[]{:S(2)}, u32[]{:S(2)}) collective-permute-start(bf16[24,4096]{1,0:T(8,128)(2,1)S(1)} %collective-permute-done.refs_1_), channel_id=1, source_target_pairs={{0,2},{2,0},{4,6},{6,4},{8,10},{10,8},{12,14},{14,12},{16,18},{18,... | collective-permute-start | bytes 589832 | tf_op jit(solution)/shard_map/ppermute | solution.py:93
  13.8 2.2 %collective-permute-start.3 = (bf16[24,4096]{1,0:T(8,128)(2,1)S(1)}, bf16[24,4096]{1,0:T(8,128)(2,1)S(1)}, u32[]{:S(2)}, u32[]{:S(2)}) collective-permute-start(bf16[24,4096]{1,0:T(8,128)(2,1)S(1)} %collective-permute-done.2.refs_1_.piece), channel_id=1, source_target_pairs={{0,2},{2,0},{4,6},{6,4},{8,10},{10,8},{12,14},{14,12},{16,18},{18,... | collective-permute-start | bytes 589832 | tf_op jit(solution)/shard_map/ppermute | solution.py:93
  17.2 4.2 %collective-permute-start.4 = (f32[32,384]{1,0:T(8,128)S(1)}, f32[32,384]{1,0:T(8,128)S(1)}, u32[]{:S(2)}, u32[]{:S(2)}) collective-permute-start(f32[32,384]{1,0:T(8,128)S(1)} %project.5.part), channel_id=1, source_target_pairs={{0,1},{1,0},{2,3},{3,2},{4,5},{5,4},{6,7},{7,6},{8,9},{9,8},{10,11... | collective-permute-start | bytes 147464 | tf_op jit(solution)/shard_map/ppermute | solution.py:435
  19.0 4.1 %collective-permute-start.5 = (f32[32,384]{1,0:T(8,128)S(1)}, f32[32,384]{1,0:T(8,128)S(1)}, u32[]{:S(2)}, u32[]{:S(2)}) collective-permute-start(f32[32,384]{1,0:T(8,128)S(1)} %project.7.part), channel_id=1, source_target_pairs={{0,1},{1,0},{2,3},{3,2},{4,5},{5,4},{6,7},{7,6},{8,9},{9,8},{10,11... | collective-permute-start | bytes 147464 | tf_op jit(solution)/shard_map/ppermute | solution.py:436
  23.7 1.8 %collective-permute-start.12 = (bf16[4,32,512]{2,1,0:T(8,128)(2,1)S(1)}, bf16[4,32,512]{2,1,0:T(8,128)(2,1)S(1)}, u32[]{:S(2)}, u32[]{:S(2)}) collective-permute-start(bf16[4,32,512]{2,1,0:T(8,128)(2,1)S(1)} %get-tuple-element.62), channel_id=1, source_target_pairs={{0,2},{2,0},{4,6},{6,4},{8,10},{10,8},{12,14},{14,12},{16,18},{18,... | collective-permute-start | bytes 393224 | tf_op jit(solution)/shard_map/ppermute | solution.py:93
  23.8 1.8 %collective-permute-start.11 = (bf16[4,24,512]{2,1,0:T(8,128)(2,1)S(1)}, bf16[4,24,512]{2,1,0:T(8,128)(2,1)S(1)}, u32[]{:S(2)}, u32[]{:S(2)}) collective-permute-start(bf16[4,24,512]{2,1,0:T(8,128)(2,1)S(1)} %get-tuple-element.61), channel_id=1, source_target_pairs={{0,2},{2,0},{4,6},{6,4},{8,10},{10,8},{12,14},{14,12},{16,18},{18,... | collective-permute-start | bytes 294920 | tf_op jit(solution)/shard_map/ppermute | solution.py:93
  25.0 4.2 %collective-permute-start.7 = (bf16[4,32,512]{2,1,0:T(8,128)(2,1)S(1)}, bf16[4,32,512]{2,1,0:T(8,128)(2,1)S(1)}, u32[]{:S(2)}, u32[]{:S(2)}) collective-permute-start(bf16[4,32,512]{2,1,0:T(8,128)(2,1)S(1)} %get-tuple-element.53), channel_id=1, source_target_pairs={{0,2},{2,0},{4,6},{6,4},{8,10},{10,8},{12,14},{14,12},{16,18},{18,... | collective-permute-start | bytes 393224 | tf_op jit(solution)/shard_map/ppermute | solution.py:93
  25.1 4.0 %collective-permute-start.6 = (bf16[4,24,512]{2,1,0:T(8,128)(2,1)S(1)}, bf16[4,24,512]{2,1,0:T(8,128)(2,1)S(1)}, u32[]{:S(2)}, u32[]{:S(2)}) collective-permute-start(bf16[4,24,512]{2,1,0:T(8,128)(2,1)S(1)} %get-tuple-element.51.refs_1_), channel_id=1, source_target_pairs={{0,2},{2,0},{4,6},{6,4},{8,10},{10,8},{12,14},{14,12},{16,18},{18,... | collective-permute-start | bytes 294920 | tf_op jit(solution)/shard_map/ppermute | solution.py:93
  25.6 6.7 %collective-permute-start.13 = (bf16[56,512]{1,0:T(8,128)(2,1)S(1)}, bf16[56,512]{1,0:T(8,128)(2,1)S(1)}, u32[]{:S(2)}, u32[]{:S(2)}) collective-permute-start(bf16[56,512]{1,0:T(8,128)(2,1)S(1)} %get-tuple-element.64), channel_id=1, source_target_pairs={{0,12},{2,14},{4,8},{6,10},{8,4},{10,6},{12,0},{14,2},{16,28},{18,... | collective-permute-start | bytes 172040 | tf_op jit(solution)/shard_map/ppermute | solution.py:93
  28.2 4.6 %collective-permute-start.14 = (bf16[56,512]{1,0:T(8,128)(2,1)S(1)}, bf16[56,512]{1,0:T(8,128)(2,1)S(1)}, u32[]{:S(2)}, u32[]{:S(2)}) collective-permute-start(bf16[56,512]{1,0:T(8,128)(2,1)S(1)} %get-tuple-element.65), channel_id=1, source_target_pairs={{0,4},{2,6},{4,0},{6,2},{8,12},{10,14},{12,8},{14,10},{16,20},{18,... | collective-permute-start | bytes 172040 | tf_op jit(solution)/shard_map/ppermute | solution.py:93
  28.7 4.6 %collective-permute-start.15 = (bf16[56,512]{1,0:T(8,128)(2,1)S(1)}, bf16[56,512]{1,0:T(8,128)(2,1)S(1)}, u32[]{:S(2)}, u32[]{:S(2)}) collective-permute-start(bf16[56,512]{1,0:T(8,128)(2,1)S(1)} %get-tuple-element.66), channel_id=1, source_target_pairs={{0,8},{2,10},{4,12},{6,14},{8,0},{10,2},{12,4},{14,6},{16,24},{18,... | collective-permute-start | bytes 172040 | tf_op jit(solution)/shard_map/ppermute | solution.py:93
  29.2 6.7 %collective-permute-start.8 = (bf16[56,512]{1,0:T(8,128)(2,1)S(1)}, bf16[56,512]{1,0:T(8,128)(2,1)S(1)}, u32[]{:S(2)}, u32[]{:S(2)}) collective-permute-start(bf16[56,512]{1,0:T(8,128)(2,1)S(1)} %get-tuple-element.55), channel_id=1, source_target_pairs={{0,12},{2,14},{4,8},{6,10},{8,4},{10,6},{12,0},{14,2},{16,28},{18,... | collective-permute-start | bytes 172040 | tf_op jit(solution)/shard_map/ppermute | solution.py:93
  31.8 4.2 %collective-permute-start.9 = (bf16[56,512]{1,0:T(8,128)(2,1)S(1)}, bf16[56,512]{1,0:T(8,128)(2,1)S(1)}, u32[]{:S(2)}, u32[]{:S(2)}) collective-permute-start(bf16[56,512]{1,0:T(8,128)(2,1)S(1)} %get-tuple-element.56), channel_id=1, source_target_pairs={{0,4},{2,6},{4,0},{6,2},{8,12},{10,14},{12,8},{14,10},{16,20},{18,... | collective-permute-start | bytes 172040 | tf_op jit(solution)/shard_map/ppermute | solution.py:93
  32.4 4.2 %collective-permute-start.10 = (bf16[56,512]{1,0:T(8,128)(2,1)S(1)}, bf16[56,512]{1,0:T(8,128)(2,1)S(1)}, u32[]{:S(2)}, u32[]{:S(2)}) collective-permute-start(bf16[56,512]{1,0:T(8,128)(2,1)S(1)} %get-tuple-element.57), channel_id=1, source_target_pairs={{0,8},{2,10},{4,12},{6,14},{8,0},{10,2},{12,4},{14,6},{16,24},{18,... | collective-permute-start | bytes 172040 | tf_op jit(solution)/shard_map/ppermute | solution.py:93
  33.3 5.4 %collective-permute-start.16 = (bf16[56,512]{1,0:T(8,128)(2,1)S(1)}, bf16[56,512]{1,0:T(8,128)(2,1)S(1)}, u32[]{:S(2)}, u32[]{:S(2)}) collective-permute-start(bf16[56,512]{1,0:T(8,128)(2,1)S(1)} %add.3), channel_id=1, source_target_pairs={{0,16},{2,18},{4,20},{6,22},{8,24},{10,26},{12,28},{14,30},{16,0},... | collective-permute-start | bytes 172040 | tf_op jit(solution)/shard_map/ppermute | solution.py:93
  38.8 4.2 %collective-permute-start.17 = (bf16[2,24,512]{2,1,0:T(8,128)(2,1)S(1)}, bf16[2,24,512]{2,1,0:T(8,128)(2,1)S(1)}, u32[]{:S(2)}, u32[]{:S(2)}) collective-permute-start(bf16[2,24,512]{2,1,0:T(8,128)(2,1)S(1)} %get-tuple-element.68.refs_0_), channel_id=1, source_target_pairs={{0,1},{1,0},{2,3},{3,2},{4,5},{5,4},{6,7},{7,6},{8,9},{9,8},{10,11... | collective-permute-start | bytes 147464 | tf_op jit(solution)/shard_map/ppermute | solution.py:457

commit v5 on v4

--- a/solution.py
+++ b/solution.py
@@ -142,6 +142,11 @@
     )(*map(far, (rank, right, cotangent, left, tokens)), *map(near, after))
 
 
+def across(value):
+    pairs = [(i, i ^ 17) for i in range(2 * lax.axis_size("dp"))]
+    return lax.ppermute(value, ("dp", "tensor"), pairs)
+
+
 def own_is_full(full):
     return full[0:1, 0:1] > 0.5
 
@@ -157,7 +162,7 @@
     slots, width = piece.shape
     core = lax.axis_index("dp") % 2
     start = (1 - core if flipped else core) * width
-    total = None
+    total = others[0][...] if others else None
     for low in range(0, width, chunk):
         column = pl.ds(pl.multiple_of(start + low, chunk), chunk)
         rows = both_panels(own[:, column], piece[:, low : low + chunk])
@@ -165,22 +170,23 @@
             rows, acts[:, column], (((1,), (1,)), ((), ())), preferred_element_type=jnp.float32
         )
         total = part if total is None else total + part
-    if others:
-        total += others[0][...]
-        full_here = own_is_full(others[1][...])
-        own_part, other_part = total[:slots], total[slots + PAD : 2 * slots + PAD]
-        out[:slots] = jnp.where(full_here, own_part, other_part)
-        short = jnp.where(full_here, other_part[:PAD], own_part[:PAD])
-        first = lax.broadcasted_iota(jnp.int32, short.shape, 0) == 0
-        out[slots:] = jnp.where(first, short, 0.0)
-    else:
+    if given < 3:
         out[...] = total
+        return
+    full_here = own_is_full(others[1][...])
+    shorts = []
+    for n, value in enumerate((others[2][...], total)):
+        own_part, other_part = value[:slots], value[slots + PAD : 2 * slots + PAD]
+        out[n * slots : (n + 1) * slots] = jnp.where(full_here, own_part, other_part)
+        shorts.append(jnp.where(full_here, other_part[:1], own_part[:1]))
+    row = lax.broadcasted_iota(jnp.int32, (PAD, out.shape[1]), 0)
+    out[2 * slots :] = jnp.where(row == 0, shorts[0], jnp.where(row == 1, shorts[1], 0.0))
 
 
 def project(own, piece, acts, flipped, others, held):
     slots, width = piece.shape
     tokens = acts.shape[0]
-    rows = slots + PAD if others else 2 * (slots + PAD)
+    rows = 2 * slots + (PAD if len(others) == 3 else 2 * PAD)
     return pl.pallas_call(
         functools.partial(project_kernel, flipped, min(width, 2048), len(others)),
         in_specs=[WHOLE] * (3 + len(others) + len(held)),
@@ -192,89 +198,88 @@
     )(*map(near, (own, piece, acts, *others, *held)))
 
 
-def gradient_kernel(scale, places, own, given, held, part, got, acts, *refs):
-    outs = refs[given + held :]
-    keep, send = outs[:2]
-    block = keep.shape[2]
-    slots = part.shape[0] - PAD
+def summed_rows(parts, got, n):
+    slots = (parts.shape[0] - PAD) // 2
+    full = slice(n * slots, (n + 1) * slots)
+    short = slice(2 * slots + n, 2 * slots + n + 1)
+    return parts[full] + got[full], parts[short] + got[short]
+
+
+def gradient_kernel(scale, places, own, parts, got, tokens, cotangent, *refs):
+    keep, send = refs[-2:]
+    rows, block = keep.shape[1:]
+    slots = (rows - PAD) // 2
     position = lax.axis_index("dp")
     even = position % 2 == 0
     bit_3 = (position // 8 + (0 if own else 1)) % 2
-    summed = (part[...] + got[...]).astype(jnp.bfloat16)
+    first = lax.broadcasted_iota(jnp.int32, (PAD, tokens.shape[0]), 0) == 0
+    weights = []
+    for n in range(2):
+        full, short = summed_rows(parts, got, n)
+        both = jnp.concatenate([full, jnp.where(first, short, 0.0)], axis=0)
+        weights.append(both.astype(jnp.bfloat16))
     row = lax.broadcasted_iota(jnp.int32, (PAD, 2 * block), 0)
     for j, q in enumerate(places):
         start = (bit_3 * len(places) + j) * 2 * block
         columns = pl.ds(pl.multiple_of(start, 2 * block), 2 * block)
-        grad = jnp.dot(summed, acts[:, columns], preferred_element_type=jnp.float32) * scale
-        if given:
-            short = jnp.where(row == 1, refs[0][q, 0:1, :], grad[slots:])
-            grad = jnp.concatenate([grad[:slots], short], axis=0)
-        else:
-            outs[2][q] = grad[slots:]
-            grad = grad[:slots]
+        left = jnp.dot(weights[0], tokens[:, columns], preferred_element_type=jnp.float32)
+        right = jnp.dot(weights[1], cotangent[:, columns], preferred_element_type=jnp.float32)
+        short = jnp.where(row == 1, right[slots : slots + 1], left[slots:])
+        grad = jnp.concatenate([left[:slots], right[:slots], short], axis=0) * scale
         low, high = grad[:, :block], grad[:, block:]
         keep[q] = jnp.where(even, low, high)
         send[q] = jnp.where(even, high, low).astype(send.dtype)
 
 
-def gradient(part, got, acts, scale, own, extra, held):
-    live, tokens = part.shape
-    slots = live - PAD
-    width = acts.shape[1]
-    block = width // lax.axis_size("dp")
+def gradient(parts, got, tokens, cotangent, scale, own, after):
     places = (0, 2, 1, 3)
-    shape = (len(places), live if extra else slots, block)
-    shapes = [pltpu.VMEM(shape, jnp.float32), pltpu.VMEM(shape, jnp.bfloat16)]
-    if not extra:
-        shapes.append(pltpu.VMEM((len(places), PAD, 2 * block), jnp.float32))
-    return pl.pallas_call(
-        functools.partial(gradient_kernel, scale, places, own, len(extra), len(held)),
-        in_specs=[WHOLE] * (3 + len(extra) + len(held)),
-        out_specs=[WHOLE] * len(shapes),
-        out_shape=shapes,
+    shape = (len(places), parts.shape[0], tokens.shape[1] // lax.axis_size("dp"))
+    return pl.pallas_call(
+        functools.partial(gradient_kernel, scale, places, own),
+        in_specs=[WHOLE] * (4 + len(after)),
+        out_specs=[WHOLE] * 2,
+        out_shape=[pltpu.VMEM(shape, jnp.float32), pltpu.VMEM(shape, jnp.bfloat16)],
         compiler_params=PARAMS,
         cost_estimate=SMALL,
         name="gradient",
-    )(*map(near, (part, got, acts, *extra, *held)))
-
-
-def spread_kernel(theirs, chunk, given, full, part, got, own, piece, *refs):
-    out, buffer, sems = refs[given:]
-    slots, width = piece.shape
+    )(*map(near, (parts, got, tokens, cotangent, *after)))
+
+
+def spread_kernel(chunk, full, parts, got, own, mine, theirs, after, out, buffer, sems):
+    slots, width = mine.shape
     full_here = own_is_full(full[...])
-    back = part[...] + got[...]
-    first = lax.broadcasted_iota(jnp.int32, (slots, back.shape[1]), 0) == 0
-    short = jnp.where(first, back[slots : slots + 1], 0.0)
-    of_own = jnp.where(full_here, back[:slots], short)
-    of_other = jnp.where(full_here, short, back[:slots])
+    back, short = summed_rows(parts, got, 0)
+    first = lax.broadcasted_iota(jnp.int32, back.shape, 0) == 0
+    short = jnp.where(first, short, 0.0)
+    of_own = jnp.where(full_here, back, short)
+    of_other = jnp.where(full_here, short, back)
     gap = jnp.zeros((PAD, back.shape[1]), jnp.float32)
     weights = jnp.concatenate([of_own, gap, of_other, gap], axis=0).T.astype(jnp.bfloat16)
     core = lax.axis_index("dp") % 2
-    start = (1 - core if theirs else core) * width
     copies = []
-    for low in range(0, width, chunk):
-        column = pl.ds(pl.multiple_of(start + low, chunk), chunk)
-        rows = both_panels(own[:, column], piece[:, low : low + chunk])
-        held = buffer.at[:, low : low + chunk]
-        held[...] = jnp.dot(weights, rows, preferred_element_type=jnp.float32).astype(out.dtype)
-        copy = pltpu.make_async_copy(held, out.at[:, column], sems.at[len(copies)])
-        copy.start()
-        copies.append(copy)
+    for side, piece in enumerate((mine, theirs)):
+        for low in range(0, width, chunk):
+            start = (core if side == 0 else 1 - core) * width + low
+            column = pl.ds(pl.multiple_of(start, chunk), chunk)
+            rows = both_panels(own[:, column], piece[:, low : low + chunk])
+            held = buffer.at[:, side * width + low : side * width + low + chunk]
+            held[...] = jnp.dot(weights, rows, preferred_element_type=jnp.float32).astype(out.dtype)
+            copy = pltpu.make_async_copy(held, out.at[:, column], sems.at[len(copies)])
+            copy.start()
+            copies.append(copy)
     for copy in copies:
         copy.wait()
 
 
-def spread(full, part, got, own, piece, after, before):
-    tokens = part.shape[1]
-    width = piece.shape[1]
-    chunk = min(width, 1024)
-    operands = tuple(map(near, (full, part, got, own, piece, after)))
-    return pl.pallas_call(
-        functools.partial(spread_kernel, len(before) > 0, chunk, 1 + len(before)),
-        in_specs=[WHOLE] * len(operands) + [FAR] * len(before),
+def spread(full, parts, got, own, mine, theirs, after):
+    tokens = parts.shape[1]
+    width = own.shape[1]
+    chunk = min(width // 2, 1024)
+    return pl.pallas_call(
+        functools.partial(spread_kernel, chunk),
+        in_specs=[WHOLE] * 7,
         out_specs=FAR,
-        out_shape=jax.ShapeDtypeStruct((tokens, 2 * width), jnp.bfloat16),
-        input_output_aliases={len(operands): 0} if before else {},
+        out_shape=jax.ShapeDtypeStruct((tokens, width), jnp.bfloat16),
         scratch_shapes=[
             pltpu.VMEM((tokens, width), jnp.bfloat16),
             pltpu.SemaphoreType.DMA((width // chunk,)),
@@ -282,57 +287,76 @@
         compiler_params=PARAMS,
         cost_estimate=LONG,
         name="spread",
-    )(*operands, *before)
-
-
-def settle_kernel(count, full, keep, *refs):
-    gots, (held, send) = refs[:count], refs[count:]
-    slots, block = held.shape[1:]
+    )(*map(near, (full, parts, got, own, mine, theirs, after)))
+
+
+def settle_kernel(full, keep, *refs):
+    gots, (near_out, far_out) = refs[:-2], refs[-2:]
+    slots, block = near_out.shape[1:]
     full_here = own_is_full(full[...])
     first = lax.broadcasted_iota(jnp.int32, (slots, block), 0) == 0
     total = keep[...]
     for got in gots:
         total += got[...].astype(jnp.float32)
-    for n, row in ((0, 1), (1, 0)):
+    for n in range(2):
         rows = total[n * slots : (n + 1) * slots]
-        short = jnp.where(first, total[2 * slots + row : 2 * slots + row + 1], 0.0)
-        held[n] = jnp.where(full_here, rows, short)
-        send[n] = jnp.where(full_here, short, rows).astype(send.dtype)
-
-
-def settle(full, keep, gots):
+        short = jnp.where(first, total[2 * slots + n : 2 * slots + n + 1], 0.0)
+        near_out[n] = jnp.where(full_here, rows, short).astype(near_out.dtype)
+        far_out[n] = jnp.where(full_here, short, rows).astype(far_out.dtype)
+
+
+def settle(full, keep, gots, kind):
     rows, block = keep.shape
     shape = (2, (rows - PAD) // 2, block)
     return pl.pallas_call(
-        functools.partial(settle_kernel, len(gots)),
+        settle_kernel,
         in_specs=[WHOLE] * (2 + len(gots)),
         out_specs=[WHOLE, WHOLE],
-        out_shape=[pltpu.VMEM(shape, jnp.float32), pltpu.VMEM(shape, jnp.bfloat16)],
+        out_shape=[pltpu.VMEM(shape, kind), pltpu.VMEM(shape, jnp.bfloat16)],
         compiler_params=PARAMS,
         cost_estimate=SMALL,
         name="settle",
     )(*map(near, (full, keep, *gots)))
 
 
-def place_kernel(held, got, left_out, right_out):
+def gather_kernel(*refs):
+    total = refs[0][...].astype(jnp.float32)
+    for value in refs[1:-1]:
+        total += value[...].astype(jnp.float32)
+    refs[-1][...] = total
+
+
+def gather(*values):
+    return pl.pallas_call(
+        gather_kernel,
+        in_specs=[WHOLE] * len(values),
+        out_specs=WHOLE,
+        out_shape=pltpu.VMEM(values[0].shape, jnp.float32),
+        compiler_params=PARAMS,
+        cost_estimate=SMALL,
+        name="gather",
+    )(*map(near, values))
+
+
+def place_kernel(held, far, got, left_out, right_out):
     here = lax.axis_index("tensor") == 0
     for n, out in enumerate((left_out, right_out)):
-        arrived = got[n].astype(out.dtype)
-        out[:, 0, 0, :] = jnp.where(here, held[n], arrived)
-        out[:, 1, 0, :] = jnp.where(here, arrived, held[n])
-
-
-def place(held, got):
+        other = far[n] + got[n].astype(out.dtype)
+        out[:, 0, 0, :] = jnp.where(here, held[n], other)
+        out[:, 1, 0, :] = jnp.where(here, other, held[n])
+
+
+def place(held, far, got):
     shape = jax.ShapeDtypeStruct((held.shape[1], 2, 1, held.shape[2]), jnp.float32)
     return pl.pallas_call(
         place_kernel,
-        in_specs=[WHOLE, WHOLE],
+        in_specs=[WHOLE] * 3,
         out_specs=[WHOLE, WHOLE],
         out_shape=[shape, shape],
         compiler_params=PARAMS,
         cost_estimate=SMALL,
         name="place",
-    )(near(held), near(got))
+    )(*map(near, (held, far, got)))
 
 
 def pick_kernel(*refs):
@@ -365,53 +389,28 @@
     )(far(right), far(left))
 
 
-def quarter_kernel(*refs):
-    keeps, gots, outs = refs[:2], refs[2:4], refs[4:]
+def quarter_kernel(keep, got, *outs):
     place = lax.axis_index("dp") // 2
     for n, out in enumerate(outs):
         block = (place + n % 2) % 2 * 2 + (place // 2 + n // 2) % 2
-        row = 0
-        for keep, got in zip(keeps, gots):
-            rows = keep.shape[1]
-            total = keep[block] + got[block].astype(jnp.float32)
-            out[row : row + rows] = total.astype(out.dtype)
-            row += rows
-
-
-def quarter(keeps, gots):
-    shape = (sum(keep.shape[1] for keep in keeps), keeps[0].shape[2])
+        out[...] = (keep[block] + got[block].astype(jnp.float32)).astype(out.dtype)
+
+
+def quarter(keep, got):
+    kinds = [jnp.float32] + [jnp.bfloat16] * 3
     return pl.pallas_call(
         quarter_kernel,
-        in_specs=[WHOLE] * 4,
+        in_specs=[WHOLE] * 2,
         out_specs=[WHOLE] * 4,
-        out_shape=[pltpu.VMEM(shape, kind) for kind in [jnp.float32] + [jnp.bfloat16] * 3],
+        out_shape=[pltpu.VMEM(keep.shape[1:], kind) for kind in kinds],
         compiler_params=PARAMS,
         cost_estimate=SMALL,
         name="quarter",
-    )(*map(near, (*keeps, *gots)))
+    )(near(keep), near(got))
 
 
 def trade(sends):
     return [flip(sends[2], 1, 2), flip(sends[0], 1), flip(sends[1], 2)]
-
-
-def add_kernel(*refs):
-    total = refs[0][...]
-    for got in refs[1:-1]:
-        total += got[...].astype(jnp.float32)
-    refs[-1][...] = total.astype(refs[-1].dtype)
-
-
-def add(keep, gots, kind):
-    return pl.pallas_call(
-        add_kernel,
-        in_specs=[WHOLE] * (1 + len(gots)),
-        out_specs=WHOLE,
-        out_shape=pltpu.VMEM(keep.shape, kind),
-        compiler_params=PARAMS,
-        cost_estimate=SMALL,
-        name="add",
-    )(*map(near, (keep, *gots)))
 
 
 def two_panels(tokens, cotangent, left_factor, right_factor, panel_rank):
@@ -428,35 +427,27 @@
     back = project(right_own, right_mine, cotangent, False, (), ())
     left_mine = after_all(left_mine, back)
     left_theirs = flip(left_mine, 0)
-    back = project(right_own, right_theirs, cotangent, True, (back, full), ())
+    back = project(right_own, right_theirs, cotangent, True, (back,), ())
     hidden = project(left_own, left_mine, tokens, False, (), (cotangent,))
-    hidden = project(left_own, left_theirs, tokens, True, (hidden, full), (cotangent,))
-    back, hidden = lax.optimization_barrier((back, hidden))
-    back_got = lax.ppermute(back, "tensor", SWAP)
-    hidden_got = lax.ppermute(hidden, "tensor", SWAP)
-
-    lefts = [
-        gradient(back, back_got, tokens, scale, own, (), (cotangent,)) for own in (False, True)
-    ]
-    quarters = []
-    for own, (left_keep, left_send, extra) in enumerate(lefts):
-        right_keep, right_send = gradient(
-            hidden, hidden_got, cotangent, scale, own == 1, (extra,), (lefts[1][1],)
-        )
-        quarters.append(
-            quarter((left_keep, right_keep), (flip(left_send, 0), flip(right_send, 0)))
-        )
-    other, own = quarters
+    parts = project(left_own, left_theirs, tokens, True, (hidden, full, back), (cotangent,))
+    parts_got = lax.ppermute(parts, "tensor", SWAP)
+
+    acts = (tokens, cotangent)
+    other_keep, other_send = gradient(parts, parts_got, *acts, scale, False, ())
+    own_keep, own_send = gradient(parts, parts_got, *acts, scale, True, (other_send,))
+    other = quarter(other_keep, flip(other_send, 0))
+    own = quarter(own_keep, flip(own_send, 0))
     other_gots, own_gots = trade(other[1:]), trade(own[1:])
-    got = flip(add(other[0], other_gots, jnp.bfloat16), 3)
-    keep = add(own[0], own_gots, jnp.float32)
-    token_grad = spread(full, back, back_got, left_own, left_mine, keep, ())
-    got = after_all(got, token_grad)
-
-    held, send = settle(full, keep, (got,))
+    near_send, far_send = settle(full, other[0], other_gots, jnp.bfloat16)
+    far_got = across(far_send)
+    near_got = flip(near_send, 3)
+    held, send = settle(full, own[0], own_gots, jnp.float32)
     got = lax.ppermute(send, "tensor", SWAP)
-    token_grad = spread(full, back, back_got, left_own, left_theirs, send, (token_grad,))
-    return token_grad, *place(held, after_all(got, token_grad))
+    token_grad = spread(full, parts, parts_got, left_own, left_mine, left_theirs, send)
+    far = gather(far_got)
+    far, near_got = lax.optimization_barrier((far, near_got))
+    held = gather(held, near_got)
+    return token_grad, *place(held, far, after_all(got, token_grad, held))
 
 
 def solution(mesh):

time: 43.8 us -> 42.7 us (0.975)
  Pallas kernels: 18.2 us -> 17 us
  waiting for transfers between devices: 6.61 us -> 7.4 us
  starting transfers between devices: 18 us -> 17.4 us
    ppermute x2, starting transfers between devices: 2.09 us -> 5.41 us  [the longest x1 3.61 us: across(): return lax.ppermute(value, ('dp', 'tensor'), pairs)]
    ppermute x13 -> x11, starting transfers between devices: 10.9 us -> 8.06 us  [flip(): lax.ppermute(value, 'dp', [(i, i ^ mask) for i in range(lax.axis_size('dp...]
    pallas_call x12 -> x10, Pallas kernels: 7.85 us -> 6.57 us  [the longest x1 3.18 us: spread(): pl.pallas_call(functools.partial(spread_kernel, chunk), in_specs=[WHOLE]...]
    ppermute x1, starting transfers between devices: 1.89 us -> 0.84 us  [two_panels(): got = lax.ppermute(send, 'tensor', SWAP)]
    ppermute x2, waiting for transfers between devices: 2.46 us -> 3.21 us  [the longest x1 3.21 us: two_panels(): parts_got = lax.ppermute(parts, 'tensor', SWAP)]
    ppermute x13 -> x11, waiting for transfers between devices: 1.06 us -> 1.23 us  [flip(): lax.ppermute(value, 'dp', [(i, i ^ mask) for i in range(lax.axis_size('dp...]
  transfers between devices with their start and end apart: 18 -> 16, of which waited for: 7 -> 5; matrix products, arithmetic and copies ran while one was open for 0% -> 0% of each run, Pallas kernels for 34% -> 30%
where the time goes in v5:
time: 42.7 us; the launch traced here: 42.6 us
  starting transfers between devices  17.4 us (41%)
  Pallas kernels  17 us (40%)
  waiting for transfers between devices  7.4 us (17%)
  between operations  0.77 us (2%)
    ppermute x11, starting transfers between devices, flip(): lax.ppermute(value, 'dp', [(i, i ^ mask) for i in range(lax.axis_size('dp...  8.06 us
    pallas_call x1, Pallas kernels, stage(): pl.pallas_call(functools.partial(stage_kernel, parts), in_specs=[FAR] * 5...  4.98 us
    pallas_call x4, Pallas kernels, project(): pl.pallas_call(functools.partial(project_kernel, flipped, min(width, 2048...  4.36 us
    ppermute x1, starting transfers between devices, across(): return lax.ppermute(value, ('dp', 'tensor'), pairs)  3.61 us
    ppermute x1, waiting for transfers between devices, two_panels(): parts_got = lax.ppermute(parts, 'tensor', SWAP)  3.21 us
    pallas_call x1, Pallas kernels, spread(): pl.pallas_call(functools.partial(spread_kernel, chunk), in_specs=[WHOLE]...  3.18 us
    ppermute x1, starting transfers between devices, two_panels(): right_mine = lax.ppermute(right_wanted, 'tensor', SWAP)  3.03 us
    pallas_call x2, Pallas kernels, gradient(): pl.pallas_call(functools.partial(gradient_kernel, scale, places, own), in...  2.47 us
  transfers between devices with their start and end apart: 16, of which 5 were waited for; matrix products, arithmetic and copies ran while one was open for 0% of the time, Pallas kernels for 30%

profile of v5, /device:TPU:0, one launch (start us, length us, event | category | flops | bytes accessed | tf_op | source)
XLA Modules:
  0.0 42.6 jit_solution(15550154130126736203)
XLA Ops:
  0.6 1.1 %pick.1 = (bf16[24,4096]{1,0:T(8,128)(2,1)S(1)}, bf16[24,4096]{1,0:T(8,128)(2,1)S(1)}) custom-call(bf16[24,16384]{1,0:T(8,128)(2,1)} %refs_0_.3, bf16[24,16384]{1,0:T(8,128)(2,1)} %refs_2_.1), custom_call_target="tpu_custom_call" | custom-call | flops 1 | bytes 1 | tf_op jit(solution)/shard_map/pick/pallas_call | solution.py:380
  1.7 3.0 %collective-permute-start.1 = (bf16[24,4096]{1,0:T(8,128)(2,1)S(1)}, bf16[24,4096]{1,0:T(8,128)(2,1)S(1)}, u32[]{:S(2)}, u32[]{:S(2)}) collective-permute-start(bf16[24,4096]{1,0:T(8,128)(2,1)S(1)} %get-tuple-element.33.refs_4_), channel_id=1, source_target_pairs={{0,1},{1,0},{2,3},{3,2},{4,5},{5,4},{6,7},{7,6},{8,9},{9,8},{10,11... | collective-permute-start | bytes 589832 | tf_op jit(solution)/shard_map/ppermute | solution.py:420
  4.7 0.1 collective-permute-start
  4.8 5.0 %stage.1 = (bf16[24,8192]{1,0:T(8,128)(2,1)S(1)}, bf16[384,8192]{1,0:T(8,128)(2,1)S(1)}, bf16[24,8192]{1,0:T(8,128)(2,1)S(1)}, bf16[384,8192]{1,0:T(8,128)(2,1)S(1)}, f32[8,128]{1,0:T(8,128)S(1)}) custom-call(s32[2]{0:T(128)} %rank.1, bf16[24,16384]{1,0:T(8,128)(2,1)} %refs_0_.3, bf16[384,8192]{1,0:T(8,128)(2,1)} %refs_1_.3, bf16[24,16384]{1,0:T(8,128)(2,1)} %refs_2_.1, ...), custom_call_target="tpu_custom_call" | custom-call | flops 1 | bytes 1 | tf_op jit(solution)/shard_map/stage/pallas_call | solution.py:130
  9.8 0.7 %collective-permute-done.1.refs_1_ = bf16[24,4096]{1,0:T(8,128)(2,1)S(1)} collective-permute-done((bf16[24,4096]{1,0:T(8,128)(2,1)S(1)}, bf16[24,4096]{1,0:T(8,128)(2,1)S(1)}, u32[]{:S(2)}, u32[]{:S(2)}) %collective-permute-start.1) | collective-permute-done | bytes 196640 | tf_op jit(solution)/shard_map/ppermute | solution.py:420
  10.5 0.0 collective-permute-start.3
  10.5 1.1 %project.4.refs_3_ = f32[64,384]{1,0:T(8,128)S(1)} custom-call(bf16[24,8192]{1,0:T(8,128)(2,1)S(1)} %get-tuple-element.37.refs_0_, bf16[24,4096]{1,0:T(8,128)(2,1)S(1)} %collective-permute-done.1.refs_1_, bf16[384,8192]{1,0:T(8,128)(2,1)S(1)} %get-tuple-element.39.refs_2_.refs_3_.refs_6_.cotangent), custom_call_target="tpu_custom_call" | custom-call | flops 1 | bytes 1 | tf_op jit(solution)/shard_map/project/pallas_call | solution.py:190
  11.5 2.3 %collective-permute-done.refs_1_.mine = bf16[24,4096]{1,0:T(8,128)(2,1)S(1)} collective-permute-done((bf16[24,4096]{1,0:T(8,128)(2,1)S(1)}, bf16[24,4096]{1,0:T(8,128)(2,1)S(1)}, u32[]{:S(2)}, u32[]{:S(2)}) %collective-permute-start) | collective-permute-done | bytes 196640 | tf_op jit(solution)/shard_map/ppermute | solution.py:421
  13.8 0.0 collective-permute-start.2
  13.8 1.1 %project.5.refs_3_ = f32[64,384]{1,0:T(8,128)S(1)} custom-call(bf16[24,8192]{1,0:T(8,128)(2,1)S(1)} %get-tuple-element.36.refs_0_.own, bf16[24,4096]{1,0:T(8,128)(2,1)S(1)} %collective-permute-done.refs_1_.mine, bf16[384,8192]{1,0:T(8,128)(2,1)S(1)} %get-tuple-element.41.refs_2_.tokens, bf16[384,8192]{1,0:T(8,128)(2,1)S(1)} %get-tuple-element.39.refs_2_.refs_3_.refs_6_.cotangent), custom_call_target="tpu_custom_call" | custom-call | flops 1 | bytes 1 | tf_op jit(solution)/shard_map/project/pallas_call | solution.py:190
  14.9 1.1 %project.6.refs_5_ = f32[64,384]{1,0:T(8,128)S(1)} custom-call(bf16[24,8192]{1,0:T(8,128)(2,1)S(1)} %get-tuple-element.37.refs_0_, bf16[24,4096]{1,0:T(8,128)(2,1)S(1)} %collective-permute-done.3.refs_1_, bf16[384,8192]{1,0:T(8,128)(2,1)S(1)} %get-tuple-element.39.refs_2_.refs_3_.refs_6_.cotangent, f32[64,384]{1,0:T(8,128)S(1)} %project.4.refs_3_), custom_call_target="tpu_custom_call" | custom-call | flops 1 | bytes 1 | tf_op jit(solution)/shard_map/project/pallas_call | solution.py:190
  16.1 1.1 %project.7.parts = f32[56,384]{1,0:T(8,128)S(1)} custom-call(bf16[24,8192]{1,0:T(8,128)(2,1)S(1)} %get-tuple-element.36.refs_0_.own, bf16[24,4096]{1,0:T(8,128)(2,1)S(1)} %collective-permute-done.2.refs_1_.theirs, bf16[384,8192]{1,0:T(8,128)(2,1)S(1)} %get-tuple-element.41.refs_2_.tokens, f32[64,384]{1,0:T(8,128)S(1)} %project.5.refs_3_, ...), custom_call_target="tpu_custom_call" | custom-call | flops 1 | bytes 1 | tf_op jit(solution)/shard_map/project/pallas_call | solution.py:190
  17.2 1.8 %collective-permute-start.4 = (f32[56,384]{1,0:T(8,128)S(1)}, f32[56,384]{1,0:T(8,128)S(1)}, u32[]{:S(2)}, u32[]{:S(2)}) collective-permute-start(f32[56,384]{1,0:T(8,128)S(1)} %project.7.parts), channel_id=1, source_target_pairs={{0,1},{1,0},{2,3},{3,2},{4,5},{5,4},{6,7},{7,6},{8,9},{9,8},{10,11... | collective-permute-start | bytes 258056 | tf_op jit(solution)/shard_map/ppermute | solution.py:433
  19.0 3.2 %collective-permute-done.4.got = f32[56,384]{1,0:T(8,128)S(1)} collective-permute-done((f32[56,384]{1,0:T(8,128)S(1)}, f32[56,384]{1,0:T(8,128)S(1)}, u32[]{:S(2)}, u32[]{:S(2)}) %collective-permute-start.4) | collective-permute-done | bytes 86048 | tf_op jit(solution)/shard_map/ppermute | solution.py:433
  22.2 1.2 %gradient.2 = (f32[4,56,512]{2,1,0:T(8,128)S(1)}, bf16[4,56,512]{2,1,0:T(8,128)(2,1)S(1)}) custom-call(f32[56,384]{1,0:T(8,128)S(1)} %project.7.parts, f32[56,384]{1,0:T(8,128)S(1)} %collective-permute-done.4.got, bf16[384,8192]{1,0:T(8,128)(2,1)S(1)} %get-tuple-element.41.refs_2_.tokens, ...), custom_call_target="tpu_custom_call" | custom-call | flops 1 | bytes 1 | tf_op jit(solution)/shard_map/gradient/pallas_call | solution.py:237
  23.4 0.1 collective-permute-start.9
  23.5 1.2 %gradient.3 = (f32[4,56,512]{2,1,0:T(8,128)S(1)}, bf16[4,56,512]{2,1,0:T(8,128)(2,1)S(1)}) custom-call(f32[56,384]{1,0:T(8,128)S(1)} %project.7.parts, f32[56,384]{1,0:T(8,128)S(1)} %collective-permute-done.4.got, bf16[384,8192]{1,0:T(8,128)(2,1)S(1)} %get-tuple-element.41.refs_2_.tokens, ...), custom_call_target="tpu_custom_call" | custom-call | flops 1 | bytes 1 | tf_op jit(solution)/shard_map/gradient/pallas_call | solution.py:237
  24.7 0.5 %collective-permute-start.5 = (bf16[4,56,512]{2,1,0:T(8,128)(2,1)S(1)}, bf16[4,56,512]{2,1,0:T(8,128)(2,1)S(1)}, u32[]{:S(2)}, u32[]{:S(2)}) collective-permute-start(bf16[4,56,512]{2,1,0:T(8,128)(2,1)S(1)} %get-tuple-element.44), channel_id=1, source_target_pairs={{0,2},{2,0},{4,6},{6,4},{8,10},{10,8},{12,14},{14,12},{16,18},{18,... | collective-permute-start | bytes 688136 | tf_op jit(solution)/shard_map/ppermute | solution.py:93
  25.3 2.8 %collective-permute-start.10 = (bf16[56,512]{1,0:T(8,128)(2,1)S(1)}, bf16[56,512]{1,0:T(8,128)(2,1)S(1)}, u32[]{:S(2)}, u32[]{:S(2)}) collective-permute-start(bf16[56,512]{1,0:T(8,128)(2,1)S(1)} %get-tuple-element.53), channel_id=1, source_target_pairs={{0,12},{2,14},{4,8},{6,10},{8,4},{10,6},{12,0},{14,2},{16,28},{18,... | collective-permute-start | bytes 172040 | tf_op jit(solution)/shard_map/ppermute | solution.py:93
  28.1 0.5 %collective-permute-start.11 = (bf16[56,512]{1,0:T(8,128)(2,1)S(1)}, bf16[56,512]{1,0:T(8,128)(2,1)S(1)}, u32[]{:S(2)}, u32[]{:S(2)}) collective-permute-start(bf16[56,512]{1,0:T(8,128)(2,1)S(1)} %get-tuple-element.54), channel_id=1, source_target_pairs={{0,4},{2,6},{4,0},{6,2},{8,12},{10,14},{12,8},{14,10},{16,20},{18,... | collective-permute-start | bytes 172040 | tf_op jit(solution)/shard_map/ppermute | solution.py:93
  28.7 0.2 collective-permute-start.12
  28.9 2.8 %collective-permute-start.6 = (bf16[56,512]{1,0:T(8,128)(2,1)S(1)}, bf16[56,512]{1,0:T(8,128)(2,1)S(1)}, u32[]{:S(2)}, u32[]{:S(2)}) collective-permute-start(bf16[56,512]{1,0:T(8,128)(2,1)S(1)} %get-tuple-element.46), channel_id=1, source_target_pairs={{0,12},{2,14},{4,8},{6,10},{8,4},{10,6},{12,0},{14,2},{16,28},{18,... | collective-permute-start | bytes 172040 | tf_op jit(solution)/shard_map/ppermute | solution.py:93
  31.7 0.5 %collective-permute-start.7 = (bf16[56,512]{1,0:T(8,128)(2,1)S(1)}, bf16[56,512]{1,0:T(8,128)(2,1)S(1)}, u32[]{:S(2)}, u32[]{:S(2)}) collective-permute-start(bf16[56,512]{1,0:T(8,128)(2,1)S(1)} %get-tuple-element.47), channel_id=1, source_target_pairs={{0,4},{2,6},{4,0},{6,2},{8,12},{10,14},{12,8},{14,10},{16,20},{18,... | collective-permute-start | bytes 172040 | tf_op jit(solution)/shard_map/ppermute | solution.py:93
  32.3 0.2 collective-permute-start.8
  32.5 0.7 %collective-permute-done.12.refs_2_ = bf16[56,512]{1,0:T(8,128)(2,1)S(1)} collective-permute-done((bf16[56,512]{1,0:T(8,128)(2,1)S(1)}, bf16[56,512]{1,0:T(8,128)(2,1)S(1)}, u32[]{:S(2)}, u32[]{:S(2)}) %collective-permute-start.12) | collective-permute-done | bytes 57376 | tf_op jit(solution)/shard_map/ppermute | solution.py:93
  33.2 3.6 %collective-permute-start.13 = (bf16[2,24,512]{2,1,0:T(8,128)(2,1)S(1)}, bf16[2,24,512]{2,1,0:T(8,128)(2,1)S(1)}, u32[]{:S(2)}, u32[]{:S(2)}) collective-permute-start(bf16[2,24,512]{2,1,0:T(8,128)(2,1)S(1)} %get-tuple-element.56), channel_id=1, source_target_pairs={{0,17},{1,16},{2,19},{3,18},{4,21},{5,20},{6,23},{7,22},{8,25},{9,... | collective-permute-start | bytes 147464 | tf_op jit(solution)/shard_map/ppermute | solution.py:147
  36.9 0.3 collective-permute-start.14
  37.2 0.1 settle.2
  37.3 0.8 %collective-permute-start.15 = (bf16[2,24,512]{2,1,0:T(8,128)(2,1)S(1)}, bf16[2,24,512]{2,1,0:T(8,128)(2,1)S(1)}, u32[]{:S(2)}, u32[]{:S(2)}) collective-permute-start(bf16[2,24,512]{2,1,0:T(8,128)(2,1)S(1)} %get-tuple-element.49.after), channel_id=1, source_target_pairs={{0,1},{1,0},{2,3},{3,2},{4,5},{5,4},{6,7},{7,6},{8,9},{9,8},{10,11... | collective-permute-start | bytes 147464 | tf_op jit(solution)/shard_map/ppermute | solution.py:445
  38.1 3.2 %spread.1 = bf16[384,8192]{1,0:T(8,128)(2,1)} custom-call(f32[8,128]{1,0:T(8,128)S(1)} %get-tuple-element.35.refs_4_.full, f32[56,384]{1,0:T(8,128)S(1)} %project.7.parts, f32[56,384]{1,0:T(8,128)S(1)} %collective-permute-done.4.got, bf16[24,8192]{1,0:T(8,128)(2,1)S(1)} %get-tuple-element.36.refs_0_.own, ...), custom_call_target="tpu_custom_call" | custom-call | flops 10000000000 | bytes 100000000 | tf_op jit(solution)/shard_map/spread/pallas_call | solution.py:278
  41.3 0.5 %collective-permute-done.14.refs_1_ = bf16[2,24,512]{2,1,0:T(8,128)(2,1)S(1)} collective-permute-done((bf16[2,24,512]{2,1,0:T(8,128)(2,1)S(1)}, bf16[2,24,512]{2,1,0:T(8,128)(2,1)S(1)}, u32[]{:S(2)}, u32[]{:S(2)}) %collective-permute-start.14) | collective-permute-done | bytes 49184 | tf_op jit(solution)/shard_map/ppermute | solution.py:93
  41.9 0.7 %place.1 = (f32[24,2,1,512]{3,2,1,0:T(1,128)}, f32[24,2,1,512]{3,2,1,0:T(1,128)}) custom-call(f32[2,24,512]{2,1,0:T(8,128)S(1)} %gather.3.held, f32[2,24,512]{2,1,0:T(8,128)S(1)} %gather.2.far, bf16[2,24,512]{2,1,0:T(8,128)(2,1)S(1)} %collective-permute-done.15.got), custom_call_target="tpu_custom_call" | custom-call | flops 1 | bytes 1 | tf_op jit(solution)/shard_map/place/pallas_call | solution.py:351
  (16 shorter events, 0.2 us)
Async XLA Ops:
  1.7 8.8 %collective-permute-start.1 = (bf16[24,4096]{1,0:T(8,128)(2,1)S(1)}, bf16[24,4096]{1,0:T(8,128)(2,1)S(1)}, u32[]{:S(2)}, u32[]{:S(2)}) collective-permute-start(bf16[24,4096]{1,0:T(8,128)(2,1)S(1)} %get-tuple-element.33.refs_4_), channel_id=1, source_target_pairs={{0,1},{1,0},{2,3},{3,2},{4,5},{5,4},{6,7},{7,6},{8,9},{9,8},{10,11... | collective-permute-start | bytes 589832 | tf_op jit(solution)/shard_map/ppermute | solution.py:420
  4.7 9.1 %collective-permute-start = (bf16[24,4096]{1,0:T(8,128)(2,1)S(1)}, bf16[24,4096]{1,0:T(8,128)(2,1)S(1)}, u32[]{:S(2)}, u32[]{:S(2)}) collective-permute-start(bf16[24,4096]{1,0:T(8,128)(2,1)S(1)} %get-tuple-element.34.refs_5_), channel_id=1, source_target_pairs={{0,1},{1,0},{2,3},{3,2},{4,5},{5,4},{6,7},{7,6},{8,9},{9,8},{10,11... | collective-permute-start | bytes 589832 | tf_op jit(solution)/shard_map/ppermute | solution.py:421
  10.5 4.5 %collective-permute-start.3 = (bf16[24,4096]{1,0:T(8,128)(2,1)S(1)}, bf16[24,4096]{1,0:T(8,128)(2,1)S(1)}, u32[]{:S(2)}, u32[]{:S(2)}) collective-permute-start(bf16[24,4096]{1,0:T(8,128)(2,1)S(1)} %collective-permute-done.1.refs_1_), channel_id=1, source_target_pairs={{0,2},{2,0},{4,6},{6,4},{8,10},{10,8},{12,14},{14,12},{16,18},{18,... | collective-permute-start | bytes 589832 | tf_op jit(solution)/shard_map/ppermute | solution.py:93
  13.8 2.2 %collective-permute-start.2 = (bf16[24,4096]{1,0:T(8,128)(2,1)S(1)}, bf16[24,4096]{1,0:T(8,128)(2,1)S(1)}, u32[]{:S(2)}, u32[]{:S(2)}) collective-permute-start(bf16[24,4096]{1,0:T(8,128)(2,1)S(1)} %collective-permute-done.refs_1_.mine), channel_id=1, source_target_pairs={{0,2},{2,0},{4,6},{6,4},{8,10},{10,8},{12,14},{14,12},{16,18},{18,... | collective-permute-start | bytes 589832 | tf_op jit(solution)/shard_map/ppermute | solution.py:93
  17.2 5.0 %collective-permute-start.4 = (f32[56,384]{1,0:T(8,128)S(1)}, f32[56,384]{1,0:T(8,128)S(1)}, u32[]{:S(2)}, u32[]{:S(2)}) collective-permute-start(f32[56,384]{1,0:T(8,128)S(1)} %project.7.parts), channel_id=1, source_target_pairs={{0,1},{1,0},{2,3},{3,2},{4,5},{5,4},{6,7},{7,6},{8,9},{9,8},{10,11... | collective-permute-start | bytes 258056 | tf_op jit(solution)/shard_map/ppermute | solution.py:433
  23.4 1.9 %collective-permute-start.9 = (bf16[4,56,512]{2,1,0:T(8,128)(2,1)S(1)}, bf16[4,56,512]{2,1,0:T(8,128)(2,1)S(1)}, u32[]{:S(2)}, u32[]{:S(2)}) collective-permute-start(bf16[4,56,512]{2,1,0:T(8,128)(2,1)S(1)} %get-tuple-element.42.refs_0_), channel_id=1, source_target_pairs={{0,2},{2,0},{4,6},{6,4},{8,10},{10,8},{12,14},{14,12},{16,18},{18,... | collective-permute-start | bytes 688136 | tf_op jit(solution)/shard_map/ppermute | solution.py:93
  24.7 4.2 %collective-permute-start.5 = (bf16[4,56,512]{2,1,0:T(8,128)(2,1)S(1)}, bf16[4,56,512]{2,1,0:T(8,128)(2,1)S(1)}, u32[]{:S(2)}, u32[]{:S(2)}) collective-permute-start(bf16[4,56,512]{2,1,0:T(8,128)(2,1)S(1)} %get-tuple-element.44), channel_id=1, source_target_pairs={{0,2},{2,0},{4,6},{6,4},{8,10},{10,8},{12,14},{14,12},{16,18},{18,... | collective-permute-start | bytes 688136 | tf_op jit(solution)/shard_map/ppermute | solution.py:93
  25.3 6.9 %collective-permute-start.10 = (bf16[56,512]{1,0:T(8,128)(2,1)S(1)}, bf16[56,512]{1,0:T(8,128)(2,1)S(1)}, u32[]{:S(2)}, u32[]{:S(2)}) collective-permute-start(bf16[56,512]{1,0:T(8,128)(2,1)S(1)} %get-tuple-element.53), channel_id=1, source_target_pairs={{0,12},{2,14},{4,8},{6,10},{8,4},{10,6},{12,0},{14,2},{16,28},{18,... | collective-permute-start | bytes 172040 | tf_op jit(solution)/shard_map/ppermute | solution.py:93
  28.1 4.4 %collective-permute-start.11 = (bf16[56,512]{1,0:T(8,128)(2,1)S(1)}, bf16[56,512]{1,0:T(8,128)(2,1)S(1)}, u32[]{:S(2)}, u32[]{:S(2)}) collective-permute-start(bf16[56,512]{1,0:T(8,128)(2,1)S(1)} %get-tuple-element.54), channel_id=1, source_target_pairs={{0,4},{2,6},{4,0},{6,2},{8,12},{10,14},{12,8},{14,10},{16,20},{18,... | collective-permute-start | bytes 172040 | tf_op jit(solution)/shard_map/ppermute | solution.py:93
  28.7 4.5 %collective-permute-start.12 = (bf16[56,512]{1,0:T(8,128)(2,1)S(1)}, bf16[56,512]{1,0:T(8,128)(2,1)S(1)}, u32[]{:S(2)}, u32[]{:S(2)}) collective-permute-start(bf16[56,512]{1,0:T(8,128)(2,1)S(1)} %get-tuple-element.55), channel_id=1, source_target_pairs={{0,8},{2,10},{4,12},{6,14},{8,0},{10,2},{12,4},{14,6},{16,24},{18,... | collective-permute-start | bytes 172040 | tf_op jit(solution)/shard_map/ppermute | solution.py:93
  28.9 8.2 %collective-permute-start.6 = (bf16[56,512]{1,0:T(8,128)(2,1)S(1)}, bf16[56,512]{1,0:T(8,128)(2,1)S(1)}, u32[]{:S(2)}, u32[]{:S(2)}) collective-permute-start(bf16[56,512]{1,0:T(8,128)(2,1)S(1)} %get-tuple-element.46), channel_id=1, source_target_pairs={{0,12},{2,14},{4,8},{6,10},{8,4},{10,6},{12,0},{14,2},{16,28},{18,... | collective-permute-start | bytes 172040 | tf_op jit(solution)/shard_map/ppermute | solution.py:93
  31.7 5.5 %collective-permute-start.7 = (bf16[56,512]{1,0:T(8,128)(2,1)S(1)}, bf16[56,512]{1,0:T(8,128)(2,1)S(1)}, u32[]{:S(2)}, u32[]{:S(2)}) collective-permute-start(bf16[56,512]{1,0:T(8,128)(2,1)S(1)} %get-tuple-element.47), channel_id=1, source_target_pairs={{0,4},{2,6},{4,0},{6,2},{8,12},{10,14},{12,8},{14,10},{16,20},{18,... | collective-permute-start | bytes 172040 | tf_op jit(solution)/shard_map/ppermute | solution.py:93
  32.3 4.9 %collective-permute-start.8 = (bf16[56,512]{1,0:T(8,128)(2,1)S(1)}, bf16[56,512]{1,0:T(8,128)(2,1)S(1)}, u32[]{:S(2)}, u32[]{:S(2)}) collective-permute-start(bf16[56,512]{1,0:T(8,128)(2,1)S(1)} %get-tuple-element.48), channel_id=1, source_target_pairs={{0,8},{2,10},{4,12},{6,14},{8,0},{10,2},{12,4},{14,6},{16,24},{18,... | collective-permute-start | bytes 172040 | tf_op jit(solution)/shard_map/ppermute | solution.py:93
  33.2 8.0 %collective-permute-start.13 = (bf16[2,24,512]{2,1,0:T(8,128)(2,1)S(1)}, bf16[2,24,512]{2,1,0:T(8,128)(2,1)S(1)}, u32[]{:S(2)}, u32[]{:S(2)}) collective-permute-start(bf16[2,24,512]{2,1,0:T(8,128)(2,1)S(1)} %get-tuple-element.56), channel_id=1, source_target_pairs={{0,17},{1,16},{2,19},{3,18},{4,21},{5,20},{6,23},{7,22},{8,25},{9,... | collective-permute-start | bytes 147464 | tf_op jit(solution)/shard_map/ppermute | solution.py:147
  36.9 5.0 %collective-permute-start.14 = (bf16[2,24,512]{2,1,0:T(8,128)(2,1)S(1)}, bf16[2,24,512]{2,1,0:T(8,128)(2,1)S(1)}, u32[]{:S(2)}, u32[]{:S(2)}) collective-permute-start(bf16[2,24,512]{2,1,0:T(8,128)(2,1)S(1)} %get-tuple-element.57), channel_id=1, source_target_pairs={{0,16},{2,18},{4,20},{6,22},{8,24},{10,26},{12,28},{14,30},{16,0},... | collective-permute-start | bytes 147464 | tf_op jit(solution)/shard_map/ppermute | solution.py:93
  37.3 4.6 %collective-permute-start.15 = (bf16[2,24,512]{2,1,0:T(8,128)(2,1)S(1)}, bf16[2,24,512]{2,1,0:T(8,128)(2,1)S(1)}, u32[]{:S(2)}, u32[]{:S(2)}) collective-permute-start(bf16[2,24,512]{2,1,0:T(8,128)(2,1)S(1)} %get-tuple-element.49.after), channel_id=1, source_target_pairs={{0,1},{1,0},{2,3},{3,2},{4,5},{5,4},{6,7},{7,6},{8,9},{9,8},{10,11... | collective-permute-start | bytes 147464 | tf_op jit(solution)/shard_map/ppermute | solution.py:445

commit v6 on v5

--- a/solution.py
+++ b/solution.py
@@ -205,12 +205,12 @@
     return parts[full] + got[full], parts[short] + got[short]
 
 
-def gradient_kernel(scale, places, own, parts, got, tokens, cotangent, *refs):
-    keep, send = refs[-2:]
-    rows, block = keep.shape[1:]
+def gradient_kernel(scale, places, own, keep, parts, got, tokens, cotangent, *refs):
+    out = refs[-1]
+    rows, block = out.shape[1:]
     slots = (rows - PAD) // 2
     position = lax.axis_index("dp")
-    even = position % 2 == 0
+    core = (position + (0 if keep else 1)) % 2
     bit_3 = (position // 8 + (0 if own else 1)) % 2
     first = lax.broadcasted_iota(jnp.int32, (PAD, tokens.shape[0]), 0) == 0
     weights = []
@@ -218,27 +218,25 @@
         full, short = summed_rows(parts, got, n)
         both = jnp.concatenate([full, jnp.where(first, short, 0.0)], axis=0)
         weights.append(both.astype(jnp.bfloat16))
-    row = lax.broadcasted_iota(jnp.int32, (PAD, 2 * block), 0)
+    row = lax.broadcasted_iota(jnp.int32, (PAD, block), 0)
     for j, q in enumerate(places):
-        start = (bit_3 * len(places) + j) * 2 * block
-        columns = pl.ds(pl.multiple_of(start, 2 * block), 2 * block)
+        start = ((bit_3 * len(places) + j) * 2 + core) * block
+        columns = pl.ds(pl.multiple_of(start, block), block)
         left = jnp.dot(weights[0], tokens[:, columns], preferred_element_type=jnp.float32)
         right = jnp.dot(weights[1], cotangent[:, columns], preferred_element_type=jnp.float32)
         short = jnp.where(row == 1, right[slots : slots + 1], left[slots:])
         grad = jnp.concatenate([left[:slots], right[:slots], short], axis=0) * scale
-        low, high = grad[:, :block], grad[:, block:]
-        keep[q] = jnp.where(even, low, high)
-        send[q] = jnp.where(even, high, low).astype(send.dtype)
-
-
-def gradient(parts, got, tokens, cotangent, scale, own, after):
+        out[q] = grad.astype(out.dtype)
+
+
+def gradient(parts, got, tokens, cotangent, scale, own, keep, after):
     places = (0, 2, 1, 3)
     shape = (len(places), parts.shape[0], tokens.shape[1] // lax.axis_size("dp"))
     return pl.pallas_call(
-        functools.partial(gradient_kernel, scale, places, own),
+        functools.partial(gradient_kernel, scale, places, own, keep),
         in_specs=[WHOLE] * (4 + len(after)),
-        out_specs=[WHOLE] * 2,
-        out_shape=[pltpu.VMEM(shape, jnp.float32), pltpu.VMEM(shape, jnp.bfloat16)],
+        out_specs=WHOLE,
+        out_shape=pltpu.VMEM(shape, jnp.float32 if keep else jnp.bfloat16),
         compiler_params=PARAMS,
         cost_estimate=SMALL,
         name="gradient",
@@ -432,10 +430,12 @@
     parts = project(left_own, left_theirs, tokens, True, (hidden, full, back), (cotangent,))
     parts_got = lax.ppermute(parts, "tensor", SWAP)
 
-    acts = (tokens, cotangent)
-    other_keep, other_send = gradient(parts, parts_got, *acts, scale, False, ())
-    own_keep, own_send = gradient(parts, parts_got, *acts, scale, True, (other_send,))
+    operands = (parts, parts_got, tokens, cotangent, scale)
+    other_send = gradient(*operands, False, False, ())
+    other_keep = gradient(*operands, False, True, (other_send,))
+    own_send = gradient(*operands, True, False, (other_keep,))
     other = quarter(other_keep, flip(other_send, 0))
+    own_keep = gradient(*operands, True, True, (own_send, other[1]))
     own = quarter(own_keep, flip(own_send, 0))
     other_gots, own_gots = trade(other[1:]), trade(own[1:])
     near_send, far_send = settle(full, other[0], other_gots, jnp.bfloat16)

time: 42.7 us -> 42.6 us (level)
  waiting for transfers between devices: 7.4 us -> 6.5 us
  starting transfers between devices: 17.4 us -> 17.9 us
    ppermute x11, waiting for transfers between devices: 1.23 us -> 0.32 us  [flip(): lax.ppermute(value, 'dp', [(i, i ^ mask) for i in range(lax.axis_size('dp...]
    pallas_call x2 -> x4, Pallas kernels: 2.47 us -> 2.71 us  [gradient(): pl.pallas_call(functools.partial(gradient_kernel, scale, places, own, kee...]
  transfers between devices with their start and end apart: 16 -> 16, of which waited for: 5 -> 6; matrix products, arithmetic and copies ran while one was open for 0% -> 0% of each run, Pallas kernels for 30% -> 32%
where the time goes in v6:
time: 42.6 us; the launch traced here: 42.4 us
  starting transfers between devices  17.9 us (42%)
  Pallas kernels  17.2 us (40%)
  waiting for transfers between devices  6.5 us (15%)
  between operations  0.81 us (2%)
    ppermute x11, starting transfers between devices, flip(): lax.ppermute(value, 'dp', [(i, i ^ mask) for i in range(lax.axis_size('dp...  8.06 us
    pallas_call x1, Pallas kernels, stage(): pl.pallas_call(functools.partial(stage_kernel, parts), in_specs=[FAR] * 5...  4.98 us
    pallas_call x4, Pallas kernels, project(): pl.pallas_call(functools.partial(project_kernel, flipped, min(width, 2048...  4.35 us
    ppermute x1, starting transfers between devices, across(): return lax.ppermute(value, ('dp', 'tensor'), pairs)  3.69 us
    ppermute x1, waiting for transfers between devices, two_panels(): parts_got = lax.ppermute(parts, 'tensor', SWAP)  3.21 us
    pallas_call x1, Pallas kernels, spread(): pl.pallas_call(functools.partial(spread_kernel, chunk), in_specs=[WHOLE]...  3.18 us
    ppermute x1, starting transfers between devices, two_panels(): right_mine = lax.ppermute(right_wanted, 'tensor', SWAP)  3.03 us
    pallas_call x4, Pallas kernels, gradient(): pl.pallas_call(functools.partial(gradient_kernel, scale, places, own, kee...  2.71 us
  transfers between devices with their start and end apart: 16, of which 6 were waited for; matrix products, arithmetic and copies ran while one was open for 0% of the time, Pallas kernels for 32%

profile of v6, /device:TPU:0, one launch (start us, length us, event | category | flops | bytes accessed | tf_op | source)
XLA Modules:
  0.0 42.4 jit_solution(10905518716701114348)
XLA Ops:
  0.6 1.1 %pick.1 = (bf16[24,4096]{1,0:T(8,128)(2,1)S(1)}, bf16[24,4096]{1,0:T(8,128)(2,1)S(1)}) custom-call(bf16[24,16384]{1,0:T(8,128)(2,1)} %refs_0_.3, bf16[24,16384]{1,0:T(8,128)(2,1)} %refs_2_.1), custom_call_target="tpu_custom_call" | custom-call | flops 1 | bytes 1 | tf_op jit(solution)/shard_map/pick/pallas_call | solution.py:378
  1.7 3.0 %collective-permute-start.1 = (bf16[24,4096]{1,0:T(8,128)(2,1)S(1)}, bf16[24,4096]{1,0:T(8,128)(2,1)S(1)}, u32[]{:S(2)}, u32[]{:S(2)}) collective-permute-start(bf16[24,4096]{1,0:T(8,128)(2,1)S(1)} %get-tuple-element.29.refs_4_), channel_id=1, source_target_pairs={{0,1},{1,0},{2,3},{3,2},{4,5},{5,4},{6,7},{7,6},{8,9},{9,8},{10,11... | collective-permute-start | bytes 589832 | tf_op jit(solution)/shard_map/ppermute | solution.py:418
  4.7 0.1 collective-permute-start
  4.8 5.0 %stage.1 = (bf16[24,8192]{1,0:T(8,128)(2,1)S(1)}, bf16[384,8192]{1,0:T(8,128)(2,1)S(1)}, bf16[24,8192]{1,0:T(8,128)(2,1)S(1)}, bf16[384,8192]{1,0:T(8,128)(2,1)S(1)}, f32[8,128]{1,0:T(8,128)S(1)}) custom-call(s32[2]{0:T(128)} %rank.1, bf16[24,16384]{1,0:T(8,128)(2,1)} %refs_0_.3, bf16[384,8192]{1,0:T(8,128)(2,1)} %refs_1_.3, bf16[24,16384]{1,0:T(8,128)(2,1)} %refs_2_.1, ...), custom_call_target="tpu_custom_call" | custom-call | flops 1 | bytes 1 | tf_op jit(solution)/shard_map/stage/pallas_call | solution.py:130
  9.8 0.7 %collective-permute-done.1.refs_1_ = bf16[24,4096]{1,0:T(8,128)(2,1)S(1)} collective-permute-done((bf16[24,4096]{1,0:T(8,128)(2,1)S(1)}, bf16[24,4096]{1,0:T(8,128)(2,1)S(1)}, u32[]{:S(2)}, u32[]{:S(2)}) %collective-permute-start.1) | collective-permute-done | bytes 196640 | tf_op jit(solution)/shard_map/ppermute | solution.py:418
  10.5 1.1 %project.4.refs_3_ = f32[64,384]{1,0:T(8,128)S(1)} custom-call(bf16[24,8192]{1,0:T(8,128)(2,1)S(1)} %get-tuple-element.33.refs_0_, bf16[24,4096]{1,0:T(8,128)(2,1)S(1)} %collective-permute-done.1.refs_1_, bf16[384,8192]{1,0:T(8,128)(2,1)S(1)} %get-tuple-element.35.refs_2_.refs_3_.refs_6_.cotangent), custom_call_target="tpu_custom_call" | custom-call | flops 1 | bytes 1 | tf_op jit(solution)/shard_map/project/pallas_call | solution.py:190
  11.5 2.3 %collective-permute-done.refs_1_.mine = bf16[24,4096]{1,0:T(8,128)(2,1)S(1)} collective-permute-done((bf16[24,4096]{1,0:T(8,128)(2,1)S(1)}, bf16[24,4096]{1,0:T(8,128)(2,1)S(1)}, u32[]{:S(2)}, u32[]{:S(2)}) %collective-permute-start) | collective-permute-done | bytes 196640 | tf_op jit(solution)/shard_map/ppermute | solution.py:419
  13.8 1.1 %project.5.refs_3_ = f32[64,384]{1,0:T(8,128)S(1)} custom-call(bf16[24,8192]{1,0:T(8,128)(2,1)S(1)} %get-tuple-element.32.refs_0_.own, bf16[24,4096]{1,0:T(8,128)(2,1)S(1)} %collective-permute-done.refs_1_.mine, bf16[384,8192]{1,0:T(8,128)(2,1)S(1)} %get-tuple-element.37.refs_2_.tokens, bf16[384,8192]{1,0:T(8,128)(2,1)S(1)} %get-tuple-element.35.refs_2_.refs_3_.refs_6_.cotangent), custom_call_target="tpu_custom_call" | custom-call | flops 1 | bytes 1 | tf_op jit(solution)/shard_map/project/pallas_call | solution.py:190
  14.9 1.1 %project.6.refs_5_ = f32[64,384]{1,0:T(8,128)S(1)} custom-call(bf16[24,8192]{1,0:T(8,128)(2,1)S(1)} %get-tuple-element.33.refs_0_, bf16[24,4096]{1,0:T(8,128)(2,1)S(1)} %collective-permute-done.3.refs_1_, bf16[384,8192]{1,0:T(8,128)(2,1)S(1)} %get-tuple-element.35.refs_2_.refs_3_.refs_6_.cotangent, f32[64,384]{1,0:T(8,128)S(1)} %project.4.refs_3_), custom_call_target="tpu_custom_call" | custom-call | flops 1 | bytes 1 | tf_op jit(solution)/shard_map/project/pallas_call | solution.py:190
  16.1 1.1 %project.7.parts = f32[56,384]{1,0:T(8,128)S(1)} custom-call(bf16[24,8192]{1,0:T(8,128)(2,1)S(1)} %get-tuple-element.32.refs_0_.own, bf16[24,4096]{1,0:T(8,128)(2,1)S(1)} %collective-permute-done.2.refs_1_.theirs, bf16[384,8192]{1,0:T(8,128)(2,1)S(1)} %get-tuple-element.37.refs_2_.tokens, f32[64,384]{1,0:T(8,128)S(1)} %project.5.refs_3_, ...), custom_call_target="tpu_custom_call" | custom-call | flops 1 | bytes 1 | tf_op jit(solution)/shard_map/project/pallas_call | solution.py:190
  17.2 1.8 %collective-permute-start.4 = (f32[56,384]{1,0:T(8,128)S(1)}, f32[56,384]{1,0:T(8,128)S(1)}, u32[]{:S(2)}, u32[]{:S(2)}) collective-permute-start(f32[56,384]{1,0:T(8,128)S(1)} %project.7.parts), channel_id=1, source_target_pairs={{0,1},{1,0},{2,3},{3,2},{4,5},{5,4},{6,7},{7,6},{8,9},{9,8},{10,11... | collective-permute-start | bytes 258056 | tf_op jit(solution)/shard_map/ppermute | solution.py:431
  19.0 3.2 %collective-permute-done.4.got = f32[56,384]{1,0:T(8,128)S(1)} collective-permute-done((f32[56,384]{1,0:T(8,128)S(1)}, f32[56,384]{1,0:T(8,128)S(1)}, u32[]{:S(2)}, u32[]{:S(2)}) %collective-permute-start.4) | collective-permute-done | bytes 86048 | tf_op jit(solution)/shard_map/ppermute | solution.py:431
  22.2 0.7 %gradient.4.refs_0_ = bf16[4,56,512]{2,1,0:T(8,128)(2,1)S(1)} custom-call(f32[56,384]{1,0:T(8,128)S(1)} %project.7.parts, f32[56,384]{1,0:T(8,128)S(1)} %collective-permute-done.4.got, bf16[384,8192]{1,0:T(8,128)(2,1)S(1)} %get-tuple-element.37.refs_2_.tokens, bf16[384,8192]{1,0:T(8,128)(2,1)S(1)} %get-tuple-element.35.refs_2_.refs_3_.refs_6_.cotangent), custom_call_target="tpu_custom_call" | custom-call | flops 1 | bytes 1 | tf_op jit(solution)/shard_map/gradient/pallas_call | solution.py:235
  22.9 0.7 %gradient.5.refs_0_.keep = f32[4,56,512]{2,1,0:T(8,128)S(1)} custom-call(f32[56,384]{1,0:T(8,128)S(1)} %project.7.parts, f32[56,384]{1,0:T(8,128)S(1)} %collective-permute-done.4.got, bf16[384,8192]{1,0:T(8,128)(2,1)S(1)} %get-tuple-element.37.refs_2_.tokens, bf16[384,8192]{1,0:T(8,128)(2,1)S(1)} %get-tuple-element.35.refs_2_.refs_3_.refs_6_.cotangent, ...), custom_call_target="tpu_custom_call" | custom-call | flops 1 | bytes 1 | tf_op jit(solution)/shard_map/gradient/pallas_call | solution.py:235
  23.6 0.7 %gradient.6.refs_0_ = bf16[4,56,512]{2,1,0:T(8,128)(2,1)S(1)} custom-call(f32[56,384]{1,0:T(8,128)S(1)} %project.7.parts, f32[56,384]{1,0:T(8,128)S(1)} %collective-permute-done.4.got, bf16[384,8192]{1,0:T(8,128)(2,1)S(1)} %get-tuple-element.37.refs_2_.tokens, bf16[384,8192]{1,0:T(8,128)(2,1)S(1)} %get-tuple-element.35.refs_2_.refs_3_.refs_6_.cotangent, ...), custom_call_target="tpu_custom_call" | custom-call | flops 1 | bytes 1 | tf_op jit(solution)/shard_map/gradient/pallas_call | solution.py:235
  24.3 0.5 %collective-permute-start.6 = (bf16[4,56,512]{2,1,0:T(8,128)(2,1)S(1)}, bf16[4,56,512]{2,1,0:T(8,128)(2,1)S(1)}, u32[]{:S(2)}, u32[]{:S(2)}) collective-permute-start(bf16[4,56,512]{2,1,0:T(8,128)(2,1)S(1)} %gradient.6.refs_0_), channel_id=1, source_target_pairs={{0,2},{2,0},{4,6},{6,4},{8,10},{10,8},{12,14},{14,12},{16,18},{18,... | collective-permute-start | bytes 688136 | tf_op jit(solution)/shard_map/ppermute | solution.py:93
  24.9 2.8 %collective-permute-start.10 = (bf16[56,512]{1,0:T(8,128)(2,1)S(1)}, bf16[56,512]{1,0:T(8,128)(2,1)S(1)}, u32[]{:S(2)}, u32[]{:S(2)}) collective-permute-start(bf16[56,512]{1,0:T(8,128)(2,1)S(1)} %get-tuple-element.46), channel_id=1, source_target_pairs={{0,12},{2,14},{4,8},{6,10},{8,4},{10,6},{12,0},{14,2},{16,28},{18,... | collective-permute-start | bytes 172040 | tf_op jit(solution)/shard_map/ppermute | solution.py:93
  27.7 0.5 %collective-permute-start.12 = (bf16[56,512]{1,0:T(8,128)(2,1)S(1)}, bf16[56,512]{1,0:T(8,128)(2,1)S(1)}, u32[]{:S(2)}, u32[]{:S(2)}) collective-permute-start(bf16[56,512]{1,0:T(8,128)(2,1)S(1)} %get-tuple-element.47), channel_id=1, source_target_pairs={{0,8},{2,10},{4,12},{6,14},{8,0},{10,2},{12,4},{14,6},{16,24},{18,... | collective-permute-start | bytes 172040 | tf_op jit(solution)/shard_map/ppermute | solution.py:93
  28.2 0.3 collective-permute-start.11
  28.5 0.7 %gradient.7.keep = f32[4,56,512]{2,1,0:T(8,128)S(1)} custom-call(f32[56,384]{1,0:T(8,128)S(1)} %project.7.parts, f32[56,384]{1,0:T(8,128)S(1)} %collective-permute-done.4.got, bf16[384,8192]{1,0:T(8,128)(2,1)S(1)} %get-tuple-element.37.refs_2_.tokens, bf16[384,8192]{1,0:T(8,128)(2,1)S(1)} %get-tuple-element.35.refs_2_.refs_3_.refs_6_.cotangent, ...), custom_call_target="tpu_custom_call" | custom-call | flops 1 | bytes 1 | tf_op jit(solution)/shard_map/gradient/pallas_call | solution.py:235
  29.2 0.1 quarter.3
  29.2 2.8 %collective-permute-start.7 = (bf16[56,512]{1,0:T(8,128)(2,1)S(1)}, bf16[56,512]{1,0:T(8,128)(2,1)S(1)}, u32[]{:S(2)}, u32[]{:S(2)}) collective-permute-start(bf16[56,512]{1,0:T(8,128)(2,1)S(1)} %get-tuple-element.40), channel_id=1, source_target_pairs={{0,12},{2,14},{4,8},{6,10},{8,4},{10,6},{12,0},{14,2},{16,28},{18,... | collective-permute-start | bytes 172040 | tf_op jit(solution)/shard_map/ppermute | solution.py:93
  32.0 0.5 %collective-permute-start.8 = (bf16[56,512]{1,0:T(8,128)(2,1)S(1)}, bf16[56,512]{1,0:T(8,128)(2,1)S(1)}, u32[]{:S(2)}, u32[]{:S(2)}) collective-permute-start(bf16[56,512]{1,0:T(8,128)(2,1)S(1)} %get-tuple-element.41), channel_id=1, source_target_pairs={{0,4},{2,6},{4,0},{6,2},{8,12},{10,14},{12,8},{14,10},{16,20},{18,... | collective-permute-start | bytes 172040 | tf_op jit(solution)/shard_map/ppermute | solution.py:93
  32.6 0.2 collective-permute-start.9
  32.8 0.1 collective-permute-done.11.refs_1_
  33.0 3.7 %collective-permute-start.13 = (bf16[2,24,512]{2,1,0:T(8,128)(2,1)S(1)}, bf16[2,24,512]{2,1,0:T(8,128)(2,1)S(1)}, u32[]{:S(2)}, u32[]{:S(2)}) collective-permute-start(bf16[2,24,512]{2,1,0:T(8,128)(2,1)S(1)} %get-tuple-element.48), channel_id=1, source_target_pairs={{0,17},{1,16},{2,19},{3,18},{4,21},{5,20},{6,23},{7,22},{8,25},{9,... | collective-permute-start | bytes 147464 | tf_op jit(solution)/shard_map/ppermute | solution.py:147
  36.7 0.3 collective-permute-start.14
  37.0 0.1 collective-permute-done.9.refs_2_
  37.2 1.2 %collective-permute-start.15 = (bf16[2,24,512]{2,1,0:T(8,128)(2,1)S(1)}, bf16[2,24,512]{2,1,0:T(8,128)(2,1)S(1)}, u32[]{:S(2)}, u32[]{:S(2)}) collective-permute-start(bf16[2,24,512]{2,1,0:T(8,128)(2,1)S(1)} %get-tuple-element.43.after), channel_id=1, source_target_pairs={{0,1},{1,0},{2,3},{3,2},{4,5},{5,4},{6,7},{7,6},{8,9},{9,8},{10,11... | collective-permute-start | bytes 147464 | tf_op jit(solution)/shard_map/ppermute | solution.py:445
  38.4 3.2 %spread.1 = bf16[384,8192]{1,0:T(8,128)(2,1)} custom-call(f32[8,128]{1,0:T(8,128)S(1)} %get-tuple-element.31.refs_4_.full, f32[56,384]{1,0:T(8,128)S(1)} %project.7.parts, f32[56,384]{1,0:T(8,128)S(1)} %collective-permute-done.4.got, bf16[24,8192]{1,0:T(8,128)(2,1)S(1)} %get-tuple-element.32.refs_0_.own, ...), custom_call_target="tpu_custom_call" | custom-call | flops 10000000000 | bytes 100000000 | tf_op jit(solution)/shard_map/spread/pallas_call | solution.py:276
  41.6 0.1 collective-permute-done.14.refs_1_
  41.7 0.7 %place.1 = (f32[24,2,1,512]{3,2,1,0:T(1,128)}, f32[24,2,1,512]{3,2,1,0:T(1,128)}) custom-call(f32[2,24,512]{2,1,0:T(8,128)S(1)} %gather.3.held, f32[2,24,512]{2,1,0:T(8,128)S(1)} %gather.2.far, bf16[2,24,512]{2,1,0:T(8,128)(2,1)S(1)} %collective-permute-done.15.got), custom_call_target="tpu_custom_call" | custom-call | flops 1 | bytes 1 | tf_op jit(solution)/shard_map/place/pallas_call | solution.py:349
  (18 shorter events, 0.3 us)
Async XLA Ops:
  1.7 8.8 %collective-permute-start.1 = (bf16[24,4096]{1,0:T(8,128)(2,1)S(1)}, bf16[24,4096]{1,0:T(8,128)(2,1)S(1)}, u32[]{:S(2)}, u32[]{:S(2)}) collective-permute-start(bf16[24,4096]{1,0:T(8,128)(2,1)S(1)} %get-tuple-element.29.refs_4_), channel_id=1, source_target_pairs={{0,1},{1,0},{2,3},{3,2},{4,5},{5,4},{6,7},{7,6},{8,9},{9,8},{10,11... | collective-permute-start | bytes 589832 | tf_op jit(solution)/shard_map/ppermute | solution.py:418
  4.7 9.1 %collective-permute-start = (bf16[24,4096]{1,0:T(8,128)(2,1)S(1)}, bf16[24,4096]{1,0:T(8,128)(2,1)S(1)}, u32[]{:S(2)}, u32[]{:S(2)}) collective-permute-start(bf16[24,4096]{1,0:T(8,128)(2,1)S(1)} %get-tuple-element.30.refs_5_), channel_id=1, source_target_pairs={{0,1},{1,0},{2,3},{3,2},{4,5},{5,4},{6,7},{7,6},{8,9},{9,8},{10,11... | collective-permute-start | bytes 589832 | tf_op jit(solution)/shard_map/ppermute | solution.py:419
  10.5 4.5 %collective-permute-start.3 = (bf16[24,4096]{1,0:T(8,128)(2,1)S(1)}, bf16[24,4096]{1,0:T(8,128)(2,1)S(1)}, u32[]{:S(2)}, u32[]{:S(2)}) collective-permute-start(bf16[24,4096]{1,0:T(8,128)(2,1)S(1)} %collective-permute-done.1.refs_1_), channel_id=1, source_target_pairs={{0,2},{2,0},{4,6},{6,4},{8,10},{10,8},{12,14},{14,12},{16,18},{18,... | collective-permute-start | bytes 589832 | tf_op jit(solution)/shard_map/ppermute | solution.py:93
  13.8 2.2 %collective-permute-start.2 = (bf16[24,4096]{1,0:T(8,128)(2,1)S(1)}, bf16[24,4096]{1,0:T(8,128)(2,1)S(1)}, u32[]{:S(2)}, u32[]{:S(2)}) collective-permute-start(bf16[24,4096]{1,0:T(8,128)(2,1)S(1)} %collective-permute-done.refs_1_.mine), channel_id=1, source_target_pairs={{0,2},{2,0},{4,6},{6,4},{8,10},{10,8},{12,14},{14,12},{16,18},{18,... | collective-permute-start | bytes 589832 | tf_op jit(solution)/shard_map/ppermute | solution.py:93
  17.2 5.0 %collective-permute-start.4 = (f32[56,384]{1,0:T(8,128)S(1)}, f32[56,384]{1,0:T(8,128)S(1)}, u32[]{:S(2)}, u32[]{:S(2)}) collective-permute-start(f32[56,384]{1,0:T(8,128)S(1)} %project.7.parts), channel_id=1, source_target_pairs={{0,1},{1,0},{2,3},{3,2},{4,5},{5,4},{6,7},{7,6},{8,9},{9,8},{10,11... | collective-permute-start | bytes 258056 | tf_op jit(solution)/shard_map/ppermute | solution.py:431
  22.8 2.0 %collective-permute-start.5 = (bf16[4,56,512]{2,1,0:T(8,128)(2,1)S(1)}, bf16[4,56,512]{2,1,0:T(8,128)(2,1)S(1)}, u32[]{:S(2)}, u32[]{:S(2)}) collective-permute-start(bf16[4,56,512]{2,1,0:T(8,128)(2,1)S(1)} %gradient.4.refs_0_), channel_id=1, source_target_pairs={{0,2},{2,0},{4,6},{6,4},{8,10},{10,8},{12,14},{14,12},{16,18},{18,... | collective-permute-start | bytes 688136 | tf_op jit(solution)/shard_map/ppermute | solution.py:93
  24.3 4.8 %collective-permute-start.6 = (bf16[4,56,512]{2,1,0:T(8,128)(2,1)S(1)}, bf16[4,56,512]{2,1,0:T(8,128)(2,1)S(1)}, u32[]{:S(2)}, u32[]{:S(2)}) collective-permute-start(bf16[4,56,512]{2,1,0:T(8,128)(2,1)S(1)} %gradient.6.refs_0_), channel_id=1, source_target_pairs={{0,2},{2,0},{4,6},{6,4},{8,10},{10,8},{12,14},{14,12},{16,18},{18,... | collective-permute-start | bytes 688136 | tf_op jit(solution)/shard_map/ppermute | solution.py:93
  24.9 7.6 %collective-permute-start.10 = (bf16[56,512]{1,0:T(8,128)(2,1)S(1)}, bf16[56,512]{1,0:T(8,128)(2,1)S(1)}, u32[]{:S(2)}, u32[]{:S(2)}) collective-permute-start(bf16[56,512]{1,0:T(8,128)(2,1)S(1)} %get-tuple-element.46), channel_id=1, source_target_pairs={{0,12},{2,14},{4,8},{6,10},{8,4},{10,6},{12,0},{14,2},{16,28},{18,... | collective-permute-start | bytes 172040 | tf_op jit(solution)/shard_map/ppermute | solution.py:93
  27.7 5.1 %collective-permute-start.12 = (bf16[56,512]{1,0:T(8,128)(2,1)S(1)}, bf16[56,512]{1,0:T(8,128)(2,1)S(1)}, u32[]{:S(2)}, u32[]{:S(2)}) collective-permute-start(bf16[56,512]{1,0:T(8,128)(2,1)S(1)} %get-tuple-element.47), channel_id=1, source_target_pairs={{0,8},{2,10},{4,12},{6,14},{8,0},{10,2},{12,4},{14,6},{16,24},{18,... | collective-permute-start | bytes 172040 | tf_op jit(solution)/shard_map/ppermute | solution.py:93
  28.2 4.8 %collective-permute-start.11 = (bf16[56,512]{1,0:T(8,128)(2,1)S(1)}, bf16[56,512]{1,0:T(8,128)(2,1)S(1)}, u32[]{:S(2)}, u32[]{:S(2)}) collective-permute-start(bf16[56,512]{1,0:T(8,128)(2,1)S(1)} %get-tuple-element.38.refs_1_), channel_id=1, source_target_pairs={{0,4},{2,6},{4,0},{6,2},{8,12},{10,14},{12,8},{14,10},{16,20},{18,... | collective-permute-start | bytes 172040 | tf_op jit(solution)/shard_map/ppermute | solution.py:93
  29.2 7.8 %collective-permute-start.7 = (bf16[56,512]{1,0:T(8,128)(2,1)S(1)}, bf16[56,512]{1,0:T(8,128)(2,1)S(1)}, u32[]{:S(2)}, u32[]{:S(2)}) collective-permute-start(bf16[56,512]{1,0:T(8,128)(2,1)S(1)} %get-tuple-element.40), channel_id=1, source_target_pairs={{0,12},{2,14},{4,8},{6,10},{8,4},{10,6},{12,0},{14,2},{16,28},{18,... | collective-permute-start | bytes 172040 | tf_op jit(solution)/shard_map/ppermute | solution.py:93
  32.0 5.0 %collective-permute-start.8 = (bf16[56,512]{1,0:T(8,128)(2,1)S(1)}, bf16[56,512]{1,0:T(8,128)(2,1)S(1)}, u32[]{:S(2)}, u32[]{:S(2)}) collective-permute-start(bf16[56,512]{1,0:T(8,128)(2,1)S(1)} %get-tuple-element.41), channel_id=1, source_target_pairs={{0,4},{2,6},{4,0},{6,2},{8,12},{10,14},{12,8},{14,10},{16,20},{18,... | collective-permute-start | bytes 172040 | tf_op jit(solution)/shard_map/ppermute | solution.py:93
  32.6 4.5 %collective-permute-start.9 = (bf16[56,512]{1,0:T(8,128)(2,1)S(1)}, bf16[56,512]{1,0:T(8,128)(2,1)S(1)}, u32[]{:S(2)}, u32[]{:S(2)}) collective-permute-start(bf16[56,512]{1,0:T(8,128)(2,1)S(1)} %get-tuple-element.42), channel_id=1, source_target_pairs={{0,8},{2,10},{4,12},{6,14},{8,0},{10,2},{12,4},{14,6},{16,24},{18,... | collective-permute-start | bytes 172040 | tf_op jit(solution)/shard_map/ppermute | solution.py:93
  33.0 8.6 %collective-permute-start.13 = (bf16[2,24,512]{2,1,0:T(8,128)(2,1)S(1)}, bf16[2,24,512]{2,1,0:T(8,128)(2,1)S(1)}, u32[]{:S(2)}, u32[]{:S(2)}) collective-permute-start(bf16[2,24,512]{2,1,0:T(8,128)(2,1)S(1)} %get-tuple-element.48), channel_id=1, source_target_pairs={{0,17},{1,16},{2,19},{3,18},{4,21},{5,20},{6,23},{7,22},{8,25},{9,... | collective-permute-start | bytes 147464 | tf_op jit(solution)/shard_map/ppermute | solution.py:147
  36.7 5.0 %collective-permute-start.14 = (bf16[2,24,512]{2,1,0:T(8,128)(2,1)S(1)}, bf16[2,24,512]{2,1,0:T(8,128)(2,1)S(1)}, u32[]{:S(2)}, u32[]{:S(2)}) collective-permute-start(bf16[2,24,512]{2,1,0:T(8,128)(2,1)S(1)} %get-tuple-element.49), channel_id=1, source_target_pairs={{0,16},{2,18},{4,20},{6,22},{8,24},{10,26},{12,28},{14,30},{16,0},... | collective-permute-start | bytes 147464 | tf_op jit(solution)/shard_map/ppermute | solution.py:93
  37.2 4.5 %collective-permute-start.15 = (bf16[2,24,512]{2,1,0:T(8,128)(2,1)S(1)}, bf16[2,24,512]{2,1,0:T(8,128)(2,1)S(1)}, u32[]{:S(2)}, u32[]{:S(2)}) collective-permute-start(bf16[2,24,512]{2,1,0:T(8,128)(2,1)S(1)} %get-tuple-element.43.after), channel_id=1, source_target_pairs={{0,1},{1,0},{2,3},{3,2},{4,5},{5,4},{6,7},{7,6},{8,9},{9,8},{10,11... | collective-permute-start | bytes 147464 | tf_op jit(solution)/shard_map/ppermute | solution.py:445

commit v7 on v6

--- a/solution.py
+++ b/solution.py
@@ -98,7 +98,7 @@
 
 
 def stage_kernel(parts, rank, *refs):
-    sources, outs, full_out, rank_here, sems = refs[:4], refs[6:10], *refs[10:]
+    sources, outs, full_out, rank_here, sems = refs[:4], refs[-7:-3], *refs[-3:]
     copies = [pltpu.make_async_copy(rank, rank_here, sems.at[0])]
     for source, out in zip(sources, outs):
         if source.shape == out.shape:
@@ -129,7 +129,7 @@
     parts = 8 if tokens.shape[0] % 128 == 0 else 1
     return pl.pallas_call(
         functools.partial(stage_kernel, parts),
-        in_specs=[FAR] * 5 + [WHOLE] * 2,
+        in_specs=[FAR] * 5 + [WHOLE] * len(after),
         out_specs=[WHOLE] * 5,
         out_shape=[own, acts, own, acts, pltpu.VMEM((8, 128), jnp.float32)],
         scratch_shapes=[
@@ -142,8 +142,8 @@
     )(*map(far, (rank, right, cotangent, left, tokens)), *map(near, after))
 
 
-def across(value):
-    pairs = [(i, i ^ 17) for i in range(2 * lax.axis_size("dp"))]
+def across(value, mask):
+    pairs = [(i, i ^ mask) for i in range(2 * lax.axis_size("dp"))]
     return lax.ppermute(value, ("dp", "tensor"), pairs)
 
 
@@ -156,12 +156,12 @@
     return jnp.concatenate([own, gap, piece, gap], axis=0)
 
 
-def project_kernel(flipped, chunk, given, *refs):
+def project_kernel(flipped, low_column, chunk, given, *refs):
     own, piece, acts = refs[:3]
     others, out = refs[3 : 3 + given], refs[-1]
     slots, width = piece.shape
     core = lax.axis_index("dp") % 2
-    start = (1 - core if flipped else core) * width
+    start = (1 - core if flipped else core) * (own.shape[1] // 2) + low_column
     total = others[0][...] if others else None
     for low in range(0, width, chunk):
         column = pl.ds(pl.multiple_of(start + low, chunk), chunk)
@@ -183,12 +183,12 @@
     out[2 * slots :] = jnp.where(row == 0, shorts[0], jnp.where(row == 1, shorts[1], 0.0))
 
 
-def project(own, piece, acts, flipped, others, held):
+def project(own, piece, acts, flipped, others, held, low=0):
     slots, width = piece.shape
     tokens = acts.shape[0]
     rows = 2 * slots + (PAD if len(others) == 3 else 2 * PAD)
     return pl.pallas_call(
-        functools.partial(project_kernel, flipped, min(width, 2048), len(others)),
+        functools.partial(project_kernel, flipped, low, min(width, 1024), len(others)),
         in_specs=[WHOLE] * (3 + len(others) + len(held)),
         out_specs=WHOLE,
         out_shape=pltpu.VMEM((rows, tokens), jnp.float32),
@@ -357,16 +357,19 @@
     )(*map(near, (held, far, got)))
 
 
-def pick_kernel(*refs):
-    sources, outs, sems = refs[:2], refs[2:4], refs[4]
-    part = outs[0].shape[1]
+def pick_kernel(right, left, *refs):
+    outs, sems = refs[:-1], refs[-1]
+    part = right.shape[1] // 4
     core = lax.axis_index("dp") % 2
-    column = ((1 - lax.axis_index("tensor")) * 2 + core) * part
-    here = pl.ds(pl.multiple_of(column, part), part)
-    copies = [
-        pltpu.make_async_copy(source.at[:, here], out, sems.at[n])
-        for n, (source, out) in enumerate(zip(sources, outs))
-    ]
+    low = 0
+    copies = []
+    for n, out in enumerate(outs):
+        size = out.shape[1]
+        source = left if n else right
+        column = ((1 - lax.axis_index("tensor")) * 2 + (1 - core if n == 2 else core)) * part
+        here = pl.ds(pl.multiple_of(column + low, 128), size)
+        copies.append(pltpu.make_async_copy(source.at[:, here], out, sems.at[n]))
+        low = low + size if n else 0
     for copy in copies:
         copy.start()
     for copy in copies:
@@ -375,12 +378,14 @@
 
 def pick(right, left):
     slots, width = left.shape
+    part = width // 4
+    sizes = (part, part // 2, part // 2)
     return pl.pallas_call(
         pick_kernel,
         in_specs=[FAR] * 2,
-        out_specs=[WHOLE] * 2,
-        out_shape=[pltpu.VMEM((slots, width // 4), left.dtype)] * 2,
-        scratch_shapes=[pltpu.SemaphoreType.DMA((2,))],
+        out_specs=[WHOLE] * 3,
+        out_shape=[pltpu.VMEM((slots, size), left.dtype) for size in sizes],
+        scratch_shapes=[pltpu.SemaphoreType.DMA((3,))],
         compiler_params=PARAMS,
         cost_estimate=SMALL,
         name="pick",
@@ -414,19 +419,24 @@
 def two_panels(tokens, cotangent, left_factor, right_factor, panel_rank):
     scale = 1.0 / math.sqrt(tokens.shape[0] * lax.axis_size("dp"))
 
-    right_wanted, left_wanted = pick(right_factor, left_factor)
-    right_mine = lax.ppermute(right_wanted, "tensor", SWAP)
-    left_mine = lax.ppermute(left_wanted, "tensor", SWAP)
+    wanted = pick(right_factor, left_factor)
+    right_mine, left_first = (lax.ppermute(w, "tensor", SWAP) for w in wanted[:2])
+    left_second = across(wanted[2], 3)
     right_own, cotangent, left_own, tokens, full = stage(
-        panel_rank, right_factor, cotangent, left_factor, tokens, (right_wanted, left_wanted)
-    )
-    right_mine = after_all(right_mine, left_own)
+        panel_rank, right_factor, cotangent, left_factor, tokens, wanted
+    )
+    right_mine = after_all(right_mine, right_own)
     right_theirs = flip(right_mine, 0)
     back = project(right_own, right_mine, cotangent, False, (), ())
-    left_mine = after_all(left_mine, back)
+    left_first = after_all(left_first, back)
+    hidden = project(left_own, left_first, tokens, False, (), (cotangent,))
+    left_second = after_all(left_second, hidden)
+    left_mine = jnp.concatenate([left_first, left_second], axis=1)
     left_theirs = flip(left_mine, 0)
-    back = project(right_own, right_theirs, cotangent, True, (back,), ())
-    hidden = project(left_own, left_mine, tokens, False, (), (cotangent,))
+    hidden = project(
+        left_own, left_second, tokens, False, (hidden,), (cotangent,), left_first.shape[1]
+    )
+    back = project(right_own, right_theirs, cotangent, True, (back,), (hidden,))
     parts = project(left_own, left_theirs, tokens, True, (hidden, full, back), (cotangent,))
     parts_got = lax.ppermute(parts, "tensor", SWAP)
 
@@ -439,7 +449,7 @@
     own = quarter(own_keep, flip(own_send, 0))
     other_gots, own_gots = trade(other[1:]), trade(own[1:])
     near_send, far_send = settle(full, other[0], other_gots, jnp.bfloat16)
-    far_got = across(far_send)
+    far_got = across(far_send, 17)
     near_got = flip(near_send, 3)
     held, send = settle(full, own[0], own_gots, jnp.float32)
     got = lax.ppermute(send, "tensor", SWAP)

time: 42.6 us -> 41.8 us (0.981)
  waiting for transfers between devices: 6.5 us -> 3.42 us
  starting transfers between devices: 17.9 us -> 19.9 us
    ppermute x2, waiting for transfers between devices: 2.96 us -> 0.01 us  [two_panels(): lax.ppermute(w, 'tensor', SWAP)]
    ppermute x11, starting transfers between devices: 8.06 us -> 9.45 us  [flip(): lax.ppermute(value, 'dp', [(i, i ^ mask) for i in range(lax.axis_size('dp...]
    ppermute x1 -> x2, starting transfers between devices: 3.69 us -> 4.4 us  [across(): return lax.ppermute(value, ('dp', 'tensor'), pairs)]
    pallas_call x5 -> x6, Pallas kernels: 5.41 us -> 5.59 us  [the longest x5 4.51 us: project(): pl.pallas_call(functools.partial(project_kernel, flipped, low, min(width,...]
  transfers between devices with their start and end apart: 16 -> 17, of which waited for: 6 -> 3; matrix products, arithmetic and copies ran while one was open for 0% -> 0% of each run, Pallas kernels for 32% -> 33%
where the time goes in v7:
time: 41.8 us; the launch traced here: 41.6 us
  starting transfers between devices  19.9 us (48%)
  Pallas kernels  17.4 us (42%)
  waiting for transfers between devices  3.42 us (8%)
  between operations  0.85 us (2%)
    ppermute x11, starting transfers between devices, flip(): lax.ppermute(value, 'dp', [(i, i ^ mask) for i in range(lax.axis_size('dp...  9.45 us
    pallas_call x1, Pallas kernels, stage(): pl.pallas_call(functools.partial(stage_kernel, parts), in_specs=[FAR] * 5...  4.98 us
    pallas_call x5, Pallas kernels, project(): pl.pallas_call(functools.partial(project_kernel, flipped, low, min(width,...  4.51 us
    ppermute x2, starting transfers between devices, across(): return lax.ppermute(value, ('dp', 'tensor'), pairs)  4.4 us
    ppermute x1, waiting for transfers between devices, two_panels(): parts_got = lax.ppermute(parts, 'tensor', SWAP)  3.23 us
    pallas_call x1, Pallas kernels, spread(): pl.pallas_call(functools.partial(spread_kernel, chunk), in_specs=[WHOLE]...  3.18 us
    ppermute x2, starting transfers between devices, two_panels(): lax.ppermute(w, 'tensor', SWAP)  3.11 us
    pallas_call x4, Pallas kernels, gradient(): pl.pallas_call(functools.partial(gradient_kernel, scale, places, own, kee...  2.72 us
  transfers between devices with their start and end apart: 17, of which 3 were waited for; matrix products, arithmetic and copies ran while one was open for 0% of the time, Pallas kernels for 33%

profile of v7, /device:TPU:0, one launch (start us, length us, event | category | flops | bytes accessed | tf_op | source)
XLA Modules:
  0.0 41.6 jit_solution(9892406508503360147)
XLA Ops:
  0.6 1.1 %pick.1 = (bf16[24,4096]{1,0:T(8,128)(2,1)S(1)}, bf16[24,2048]{1,0:T(8,128)(2,1)S(1)}, bf16[24,2048]{1,0:T(8,128)(2,1)S(1)}) custom-call(bf16[24,16384]{1,0:T(8,128)(2,1)} %refs_0_.1, bf16[24,16384]{1,0:T(8,128)(2,1)} %refs_2_.1), custom_call_target="tpu_custom_call" | custom-call | flops 1 | bytes 1 | tf_op jit(solution)/shard_map/pick/pallas_call | solution.py:383
  1.7 3.0 %collective-permute-start.1 = (bf16[24,4096]{1,0:T(8,128)(2,1)S(1)}, bf16[24,4096]{1,0:T(8,128)(2,1)S(1)}, u32[]{:S(2)}, u32[]{:S(2)}) collective-permute-start(bf16[24,4096]{1,0:T(8,128)(2,1)S(1)} %get-tuple-element.31.refs_4_), channel_id=1, source_target_pairs={{0,1},{1,0},{2,3},{3,2},{4,5},{5,4},{6,7},{7,6},{8,9},{9,8},{10,11... | collective-permute-start | bytes 589832 | tf_op jit(solution)/shard_map/ppermute | solution.py:423
  4.8 0.1 collective-permute-start
  4.8 0.8 %collective-permute-start.2 = (bf16[24,2048]{1,0:T(8,128)(2,1)S(1)}, bf16[24,2048]{1,0:T(8,128)(2,1)S(1)}, u32[]{:S(2)}, u32[]{:S(2)}) collective-permute-start(bf16[24,2048]{1,0:T(8,128)(2,1)S(1)} %get-tuple-element.33.refs_6_), channel_id=1, source_target_pairs={{0,3},{1,2},{2,1},{3,0},{4,7},{5,6},{6,5},{7,4},{8,11},{9,10},{10,... | collective-permute-start | bytes 294920 | tf_op jit(solution)/shard_map/ppermute | solution.py:147
  5.7 5.0 %stage.1 = (bf16[24,8192]{1,0:T(8,128)(2,1)S(1)}, bf16[384,8192]{1,0:T(8,128)(2,1)S(1)}, bf16[24,8192]{1,0:T(8,128)(2,1)S(1)}, bf16[384,8192]{1,0:T(8,128)(2,1)S(1)}, f32[8,128]{1,0:T(8,128)S(1)}) custom-call(s32[2]{0:T(128)} %rank.1, bf16[24,16384]{1,0:T(8,128)(2,1)} %refs_0_.1, bf16[384,8192]{1,0:T(8,128)(2,1)} %refs_1_.1, bf16[24,16384]{1,0:T(8,128)(2,1)} %refs_2_.1, ...), custom_call_target="tpu_custom_call" | custom-call | flops 1 | bytes 1 | tf_op jit(solution)/shard_map/stage/pallas_call | solution.py:130
  10.7 1.3 %collective-permute-start.4 = (bf16[24,4096]{1,0:T(8,128)(2,1)S(1)}, bf16[24,4096]{1,0:T(8,128)(2,1)S(1)}, u32[]{:S(2)}, u32[]{:S(2)}) collective-permute-start(bf16[24,4096]{1,0:T(8,128)(2,1)S(1)} %collective-permute-done.1.refs_1_), channel_id=1, source_target_pairs={{0,2},{2,0},{4,6},{6,4},{8,10},{10,8},{12,14},{14,12},{16,18},{18,... | collective-permute-start | bytes 589832 | tf_op jit(solution)/shard_map/ppermute | solution.py:93
  12.0 1.1 %project.5.refs_3_ = f32[64,384]{1,0:T(8,128)S(1)} custom-call(bf16[24,8192]{1,0:T(8,128)(2,1)S(1)} %get-tuple-element.36.refs_0_, bf16[24,4096]{1,0:T(8,128)(2,1)S(1)} %collective-permute-done.1.refs_1_, bf16[384,8192]{1,0:T(8,128)(2,1)S(1)} %get-tuple-element.38.refs_2_.refs_3_.refs_4_.refs_6_.cotangent), custom_call_target="tpu_custom_call" | custom-call | flops 1 | bytes 1 | tf_op jit(solution)/shard_map/project/pallas_call | solution.py:190
  13.1 0.6 %project.6.refs_3_ = f32[64,384]{1,0:T(8,128)S(1)} custom-call(bf16[24,8192]{1,0:T(8,128)(2,1)S(1)} %get-tuple-element.35.refs_0_.own, bf16[24,2048]{1,0:T(8,128)(2,1)S(1)} %collective-permute-done.refs_1_, bf16[384,8192]{1,0:T(8,128)(2,1)S(1)} %get-tuple-element.40.refs_2_.tokens, ...), custom_call_target="tpu_custom_call" | custom-call | flops 1 | bytes 1 | tf_op jit(solution)/shard_map/project/pallas_call | solution.py:190
  13.7 0.1 collective-permute-start.3
  13.8 0.6 %project.7.refs_4_.refs_3_ = f32[64,384]{1,0:T(8,128)S(1)} custom-call(bf16[24,8192]{1,0:T(8,128)(2,1)S(1)} %get-tuple-element.35.refs_0_.own, bf16[24,2048]{1,0:T(8,128)(2,1)S(1)} %collective-permute-done.2.refs_1_, bf16[384,8192]{1,0:T(8,128)(2,1)S(1)} %get-tuple-element.40.refs_2_.tokens, f32[64,384]{1,0:T(8,128)S(1)} %project.6.refs_3_, ...), custom_call_target="tpu_custom_call" | custom-call | flops 1 | bytes 1 | tf_op jit(solution)/shard_map/project/pallas_call | solution.py:190
  14.4 1.1 %project.8.refs_5_ = f32[64,384]{1,0:T(8,128)S(1)} custom-call(bf16[24,8192]{1,0:T(8,128)(2,1)S(1)} %get-tuple-element.36.refs_0_, bf16[24,4096]{1,0:T(8,128)(2,1)S(1)} %collective-permute-done.4.refs_1_, bf16[384,8192]{1,0:T(8,128)(2,1)S(1)} %get-tuple-element.38.refs_2_.refs_3_.refs_4_.refs_6_.cotangent, f32[64,384]{1,0:T(8,128)S(1)} %project.5.refs_3_, ...), custom_call_target="tpu_custom_call" | custom-call | flops 1 | bytes 1 | tf_op jit(solution)/shard_map/project/pallas_call | solution.py:190
  15.6 1.1 %project.9.parts = f32[56,384]{1,0:T(8,128)S(1)} custom-call(bf16[24,8192]{1,0:T(8,128)(2,1)S(1)} %get-tuple-element.35.refs_0_.own, bf16[24,4096]{1,0:T(8,128)(2,1)S(1)} %collective-permute-done.3.refs_1_.theirs, bf16[384,8192]{1,0:T(8,128)(2,1)S(1)} %get-tuple-element.40.refs_2_.tokens, f32[64,384]{1,0:T(8,128)S(1)} %project.7.refs_4_.refs_3_, ...), custom_call_target="tpu_custom_call" | custom-call | flops 1 | bytes 1 | tf_op jit(solution)/shard_map/project/pallas_call | solution.py:190
  16.7 1.7 %collective-permute-start.5 = (f32[56,384]{1,0:T(8,128)S(1)}, f32[56,384]{1,0:T(8,128)S(1)}, u32[]{:S(2)}, u32[]{:S(2)}) collective-permute-start(f32[56,384]{1,0:T(8,128)S(1)} %project.9.parts), channel_id=1, source_target_pairs={{0,1},{1,0},{2,3},{3,2},{4,5},{5,4},{6,7},{7,6},{8,9},{9,8},{10,11... | collective-permute-start | bytes 258056 | tf_op jit(solution)/shard_map/ppermute | solution.py:441
  18.4 3.2 %collective-permute-done.5.got = f32[56,384]{1,0:T(8,128)S(1)} collective-permute-done((f32[56,384]{1,0:T(8,128)S(1)}, f32[56,384]{1,0:T(8,128)S(1)}, u32[]{:S(2)}, u32[]{:S(2)}) %collective-permute-start.5) | collective-permute-done | bytes 86048 | tf_op jit(solution)/shard_map/ppermute | solution.py:441
  21.6 0.7 %gradient.4.refs_0_ = bf16[4,56,512]{2,1,0:T(8,128)(2,1)S(1)} custom-call(f32[56,384]{1,0:T(8,128)S(1)} %project.9.parts, f32[56,384]{1,0:T(8,128)S(1)} %collective-permute-done.5.got, bf16[384,8192]{1,0:T(8,128)(2,1)S(1)} %get-tuple-element.40.refs_2_.tokens, bf16[384,8192]{1,0:T(8,128)(2,1)S(1)} %get-tuple-element.38.refs_2_.refs_3_.refs_4_.refs_6_.cotangent), custom_call_target="tpu_custom_call" | custom-call | flops 1 | bytes 1 | tf_op jit(solution)/shard_map/gradient/pallas_call | solution.py:235
  22.4 0.7 %gradient.5.refs_0_.keep = f32[4,56,512]{2,1,0:T(8,128)S(1)} custom-call(f32[56,384]{1,0:T(8,128)S(1)} %project.9.parts, f32[56,384]{1,0:T(8,128)S(1)} %collective-permute-done.5.got, bf16[384,8192]{1,0:T(8,128)(2,1)S(1)} %get-tuple-element.40.refs_2_.tokens, bf16[384,8192]{1,0:T(8,128)(2,1)S(1)} %get-tuple-element.38.refs_2_.refs_3_.refs_4_.refs_6_.cotangent, ...), custom_call_target="tpu_custom_call" | custom-call | flops 1 | bytes 1 | tf_op jit(solution)/shard_map/gradient/pallas_call | solution.py:235
  23.1 0.7 %gradient.6.refs_0_ = bf16[4,56,512]{2,1,0:T(8,128)(2,1)S(1)} custom-call(f32[56,384]{1,0:T(8,128)S(1)} %project.9.parts, f32[56,384]{1,0:T(8,128)S(1)} %collective-permute-done.5.got, bf16[384,8192]{1,0:T(8,128)(2,1)S(1)} %get-tuple-element.40.refs_2_.tokens, bf16[384,8192]{1,0:T(8,128)(2,1)S(1)} %get-tuple-element.38.refs_2_.refs_3_.refs_4_.refs_6_.cotangent, ...), custom_call_target="tpu_custom_call" | custom-call | flops 1 | bytes 1 | tf_op jit(solution)/shard_map/gradient/pallas_call | solution.py:235
  23.8 0.5 %collective-permute-start.7 = (bf16[4,56,512]{2,1,0:T(8,128)(2,1)S(1)}, bf16[4,56,512]{2,1,0:T(8,128)(2,1)S(1)}, u32[]{:S(2)}, u32[]{:S(2)}) collective-permute-start(bf16[4,56,512]{2,1,0:T(8,128)(2,1)S(1)} %gradient.6.refs_0_), channel_id=1, source_target_pairs={{0,2},{2,0},{4,6},{6,4},{8,10},{10,8},{12,14},{14,12},{16,18},{18,... | collective-permute-start | bytes 688136 | tf_op jit(solution)/shard_map/ppermute | solution.py:93
  24.4 2.6 %collective-permute-start.11 = (bf16[56,512]{1,0:T(8,128)(2,1)S(1)}, bf16[56,512]{1,0:T(8,128)(2,1)S(1)}, u32[]{:S(2)}, u32[]{:S(2)}) collective-permute-start(bf16[56,512]{1,0:T(8,128)(2,1)S(1)} %get-tuple-element.50), channel_id=1, source_target_pairs={{0,12},{2,14},{4,8},{6,10},{8,4},{10,6},{12,0},{14,2},{16,28},{18,... | collective-permute-start | bytes 172040 | tf_op jit(solution)/shard_map/ppermute | solution.py:93
  27.0 0.5 %collective-permute-start.13 = (bf16[56,512]{1,0:T(8,128)(2,1)S(1)}, bf16[56,512]{1,0:T(8,128)(2,1)S(1)}, u32[]{:S(2)}, u32[]{:S(2)}) collective-permute-start(bf16[56,512]{1,0:T(8,128)(2,1)S(1)} %get-tuple-element.51), channel_id=1, source_target_pairs={{0,8},{2,10},{4,12},{6,14},{8,0},{10,2},{12,4},{14,6},{16,24},{18,... | collective-permute-start | bytes 172040 | tf_op jit(solution)/shard_map/ppermute | solution.py:93
  27.4 0.5 %collective-permute-start.12 = (bf16[56,512]{1,0:T(8,128)(2,1)S(1)}, bf16[56,512]{1,0:T(8,128)(2,1)S(1)}, u32[]{:S(2)}, u32[]{:S(2)}) collective-permute-start(bf16[56,512]{1,0:T(8,128)(2,1)S(1)} %get-tuple-element.42.refs_1_), channel_id=1, source_target_pairs={{0,4},{2,6},{4,0},{6,2},{8,12},{10,14},{12,8},{14,10},{16,20},{18,... | collective-permute-start | bytes 172040 | tf_op jit(solution)/shard_map/ppermute | solution.py:93
  27.9 0.7 %gradient.7.keep = f32[4,56,512]{2,1,0:T(8,128)S(1)} custom-call(f32[56,384]{1,0:T(8,128)S(1)} %project.9.parts, f32[56,384]{1,0:T(8,128)S(1)} %collective-permute-done.5.got, bf16[384,8192]{1,0:T(8,128)(2,1)S(1)} %get-tuple-element.40.refs_2_.tokens, bf16[384,8192]{1,0:T(8,128)(2,1)S(1)} %get-tuple-element.38.refs_2_.refs_3_.refs_4_.refs_6_.cotangent, ...), custom_call_target="tpu_custom_call" | custom-call | flops 1 | bytes 1 | tf_op jit(solution)/shard_map/gradient/pallas_call | solution.py:235
  28.6 0.1 quarter.3
  28.7 2.6 %collective-permute-start.8 = (bf16[56,512]{1,0:T(8,128)(2,1)S(1)}, bf16[56,512]{1,0:T(8,128)(2,1)S(1)}, u32[]{:S(2)}, u32[]{:S(2)}) collective-permute-start(bf16[56,512]{1,0:T(8,128)(2,1)S(1)} %get-tuple-element.44), channel_id=1, source_target_pairs={{0,12},{2,14},{4,8},{6,10},{8,4},{10,6},{12,0},{14,2},{16,28},{18,... | collective-permute-start | bytes 172040 | tf_op jit(solution)/shard_map/ppermute | solution.py:93
  31.3 0.5 %collective-permute-start.9 = (bf16[56,512]{1,0:T(8,128)(2,1)S(1)}, bf16[56,512]{1,0:T(8,128)(2,1)S(1)}, u32[]{:S(2)}, u32[]{:S(2)}) collective-permute-start(bf16[56,512]{1,0:T(8,128)(2,1)S(1)} %get-tuple-element.45), channel_id=1, source_target_pairs={{0,4},{2,6},{4,0},{6,2},{8,12},{10,14},{12,8},{14,10},{16,20},{18,... | collective-permute-start | bytes 172040 | tf_op jit(solution)/shard_map/ppermute | solution.py:93
  31.8 0.5 %collective-permute-start.10 = (bf16[56,512]{1,0:T(8,128)(2,1)S(1)}, bf16[56,512]{1,0:T(8,128)(2,1)S(1)}, u32[]{:S(2)}, u32[]{:S(2)}) collective-permute-start(bf16[56,512]{1,0:T(8,128)(2,1)S(1)} %get-tuple-element.46), channel_id=1, source_target_pairs={{0,8},{2,10},{4,12},{6,14},{8,0},{10,2},{12,4},{14,6},{16,24},{18,... | collective-permute-start | bytes 172040 | tf_op jit(solution)/shard_map/ppermute | solution.py:93
  32.3 3.6 %collective-permute-start.14 = (bf16[2,24,512]{2,1,0:T(8,128)(2,1)S(1)}, bf16[2,24,512]{2,1,0:T(8,128)(2,1)S(1)}, u32[]{:S(2)}, u32[]{:S(2)}) collective-permute-start(bf16[2,24,512]{2,1,0:T(8,128)(2,1)S(1)} %get-tuple-element.52), channel_id=1, source_target_pairs={{0,17},{1,16},{2,19},{3,18},{4,21},{5,20},{6,23},{7,22},{8,25},{9,... | collective-permute-start | bytes 147464 | tf_op jit(solution)/shard_map/ppermute | solution.py:147
  35.9 0.3 collective-permute-start.15
  36.4 1.2 %collective-permute-start.16 = (bf16[2,24,512]{2,1,0:T(8,128)(2,1)S(1)}, bf16[2,24,512]{2,1,0:T(8,128)(2,1)S(1)}, u32[]{:S(2)}, u32[]{:S(2)}) collective-permute-start(bf16[2,24,512]{2,1,0:T(8,128)(2,1)S(1)} %get-tuple-element.47.after), channel_id=1, source_target_pairs={{0,1},{1,0},{2,3},{3,2},{4,5},{5,4},{6,7},{7,6},{8,9},{9,8},{10,11... | collective-permute-start | bytes 147464 | tf_op jit(solution)/shard_map/ppermute | solution.py:455
  37.6 3.2 %spread.1 = bf16[384,8192]{1,0:T(8,128)(2,1)} custom-call(f32[8,128]{1,0:T(8,128)S(1)} %get-tuple-element.34.refs_4_.full, f32[56,384]{1,0:T(8,128)S(1)} %project.9.parts, f32[56,384]{1,0:T(8,128)S(1)} %collective-permute-done.5.got, bf16[24,8192]{1,0:T(8,128)(2,1)S(1)} %get-tuple-element.35.refs_0_.own, ...), custom_call_target="tpu_custom_call" | custom-call | flops 10000000000 | bytes 100000000 | tf_op jit(solution)/shard_map/spread/pallas_call | solution.py:276
  40.8 0.1 collective-permute-done.15.refs_1_
  40.9 0.7 %place.1 = (f32[24,2,1,512]{3,2,1,0:T(1,128)}, f32[24,2,1,512]{3,2,1,0:T(1,128)}) custom-call(f32[2,24,512]{2,1,0:T(8,128)S(1)} %gather.3.held, f32[2,24,512]{2,1,0:T(8,128)S(1)} %gather.2.far, bf16[2,24,512]{2,1,0:T(8,128)(2,1)S(1)} %collective-permute-done.16.got), custom_call_target="tpu_custom_call" | custom-call | flops 1 | bytes 1 | tf_op jit(solution)/shard_map/place/pallas_call | solution.py:349
  (23 shorter events, 0.4 us)
Async XLA Ops:
  1.7 8.9 %collective-permute-start.1 = (bf16[24,4096]{1,0:T(8,128)(2,1)S(1)}, bf16[24,4096]{1,0:T(8,128)(2,1)S(1)}, u32[]{:S(2)}, u32[]{:S(2)}) collective-permute-start(bf16[24,4096]{1,0:T(8,128)(2,1)S(1)} %get-tuple-element.31.refs_4_), channel_id=1, source_target_pairs={{0,1},{1,0},{2,3},{3,2},{4,5},{5,4},{6,7},{7,6},{8,9},{9,8},{10,11... | collective-permute-start | bytes 589832 | tf_op jit(solution)/shard_map/ppermute | solution.py:423
  4.8 8.3 %collective-permute-start = (bf16[24,2048]{1,0:T(8,128)(2,1)S(1)}, bf16[24,2048]{1,0:T(8,128)(2,1)S(1)}, u32[]{:S(2)}, u32[]{:S(2)}) collective-permute-start(bf16[24,2048]{1,0:T(8,128)(2,1)S(1)} %get-tuple-element.32.refs_5_), channel_id=1, source_target_pairs={{0,1},{1,0},{2,3},{3,2},{4,5},{5,4},{6,7},{7,6},{8,9},{9,8},{10,11... | collective-permute-start | bytes 294920 | tf_op jit(solution)/shard_map/ppermute | solution.py:423
  4.8 8.9 %collective-permute-start.2 = (bf16[24,2048]{1,0:T(8,128)(2,1)S(1)}, bf16[24,2048]{1,0:T(8,128)(2,1)S(1)}, u32[]{:S(2)}, u32[]{:S(2)}) collective-permute-start(bf16[24,2048]{1,0:T(8,128)(2,1)S(1)} %get-tuple-element.33.refs_6_), channel_id=1, source_target_pairs={{0,3},{1,2},{2,1},{3,0},{4,7},{5,6},{6,5},{7,4},{8,11},{9,10},{10,... | collective-permute-start | bytes 294920 | tf_op jit(solution)/shard_map/ppermute | solution.py:147
  10.7 3.8 %collective-permute-start.4 = (bf16[24,4096]{1,0:T(8,128)(2,1)S(1)}, bf16[24,4096]{1,0:T(8,128)(2,1)S(1)}, u32[]{:S(2)}, u32[]{:S(2)}) collective-permute-start(bf16[24,4096]{1,0:T(8,128)(2,1)S(1)} %collective-permute-done.1.refs_1_), channel_id=1, source_target_pairs={{0,2},{2,0},{4,6},{6,4},{8,10},{10,8},{12,14},{14,12},{16,18},{18,... | collective-permute-start | bytes 589832 | tf_op jit(solution)/shard_map/ppermute | solution.py:93
  13.7 1.8 %collective-permute-start.3 = (bf16[24,4096]{1,0:T(8,128)(2,1)S(1)}, bf16[24,4096]{1,0:T(8,128)(2,1)S(1)}, u32[]{:S(2)}, u32[]{:S(2)}) collective-permute-start(bf16[24,4096]{1,0:T(8,128)(2,1)S(1)} %constant_dynamic-update-slice_fusion.mine), channel_id=1, source_target_pairs={{0,2},{2,0},{4,6},{6,4},{8,10},{10,8},{12,14},{14,12},{16,18},{18,... | collective-permute-start | bytes 589832 | tf_op jit(solution)/shard_map/ppermute | solution.py:93
  16.7 5.0 %collective-permute-start.5 = (f32[56,384]{1,0:T(8,128)S(1)}, f32[56,384]{1,0:T(8,128)S(1)}, u32[]{:S(2)}, u32[]{:S(2)}) collective-permute-start(f32[56,384]{1,0:T(8,128)S(1)} %project.9.parts), channel_id=1, source_target_pairs={{0,1},{1,0},{2,3},{3,2},{4,5},{5,4},{6,7},{7,6},{8,9},{9,8},{10,11... | collective-permute-start | bytes 258056 | tf_op jit(solution)/shard_map/ppermute | solution.py:441
  22.3 2.0 %collective-permute-start.6 = (bf16[4,56,512]{2,1,0:T(8,128)(2,1)S(1)}, bf16[4,56,512]{2,1,0:T(8,128)(2,1)S(1)}, u32[]{:S(2)}, u32[]{:S(2)}) collective-permute-start(bf16[4,56,512]{2,1,0:T(8,128)(2,1)S(1)} %gradient.4.refs_0_), channel_id=1, source_target_pairs={{0,2},{2,0},{4,6},{6,4},{8,10},{10,8},{12,14},{14,12},{16,18},{18,... | collective-permute-start | bytes 688136 | tf_op jit(solution)/shard_map/ppermute | solution.py:93
  23.8 4.8 %collective-permute-start.7 = (bf16[4,56,512]{2,1,0:T(8,128)(2,1)S(1)}, bf16[4,56,512]{2,1,0:T(8,128)(2,1)S(1)}, u32[]{:S(2)}, u32[]{:S(2)}) collective-permute-start(bf16[4,56,512]{2,1,0:T(8,128)(2,1)S(1)} %gradient.6.refs_0_), channel_id=1, source_target_pairs={{0,2},{2,0},{4,6},{6,4},{8,10},{10,8},{12,14},{14,12},{16,18},{18,... | collective-permute-start | bytes 688136 | tf_op jit(solution)/shard_map/ppermute | solution.py:93
  24.4 7.4 %collective-permute-start.11 = (bf16[56,512]{1,0:T(8,128)(2,1)S(1)}, bf16[56,512]{1,0:T(8,128)(2,1)S(1)}, u32[]{:S(2)}, u32[]{:S(2)}) collective-permute-start(bf16[56,512]{1,0:T(8,128)(2,1)S(1)} %get-tuple-element.50), channel_id=1, source_target_pairs={{0,12},{2,14},{4,8},{6,10},{8,4},{10,6},{12,0},{14,2},{16,28},{18,... | collective-permute-start | bytes 172040 | tf_op jit(solution)/shard_map/ppermute | solution.py:93
  27.0 5.3 %collective-permute-start.13 = (bf16[56,512]{1,0:T(8,128)(2,1)S(1)}, bf16[56,512]{1,0:T(8,128)(2,1)S(1)}, u32[]{:S(2)}, u32[]{:S(2)}) collective-permute-start(bf16[56,512]{1,0:T(8,128)(2,1)S(1)} %get-tuple-element.51), channel_id=1, source_target_pairs={{0,8},{2,10},{4,12},{6,14},{8,0},{10,2},{12,4},{14,6},{16,24},{18,... | collective-permute-start | bytes 172040 | tf_op jit(solution)/shard_map/ppermute | solution.py:93
  27.4 4.9 %collective-permute-start.12 = (bf16[56,512]{1,0:T(8,128)(2,1)S(1)}, bf16[56,512]{1,0:T(8,128)(2,1)S(1)}, u32[]{:S(2)}, u32[]{:S(2)}) collective-permute-start(bf16[56,512]{1,0:T(8,128)(2,1)S(1)} %get-tuple-element.42.refs_1_), channel_id=1, source_target_pairs={{0,4},{2,6},{4,0},{6,2},{8,12},{10,14},{12,8},{14,10},{16,20},{18,... | collective-permute-start | bytes 172040 | tf_op jit(solution)/shard_map/ppermute | solution.py:93
  28.7 7.5 %collective-permute-start.8 = (bf16[56,512]{1,0:T(8,128)(2,1)S(1)}, bf16[56,512]{1,0:T(8,128)(2,1)S(1)}, u32[]{:S(2)}, u32[]{:S(2)}) collective-permute-start(bf16[56,512]{1,0:T(8,128)(2,1)S(1)} %get-tuple-element.44), channel_id=1, source_target_pairs={{0,12},{2,14},{4,8},{6,10},{8,4},{10,6},{12,0},{14,2},{16,28},{18,... | collective-permute-start | bytes 172040 | tf_op jit(solution)/shard_map/ppermute | solution.py:93
  31.3 5.0 %collective-permute-start.9 = (bf16[56,512]{1,0:T(8,128)(2,1)S(1)}, bf16[56,512]{1,0:T(8,128)(2,1)S(1)}, u32[]{:S(2)}, u32[]{:S(2)}) collective-permute-start(bf16[56,512]{1,0:T(8,128)(2,1)S(1)} %get-tuple-element.45), channel_id=1, source_target_pairs={{0,4},{2,6},{4,0},{6,2},{8,12},{10,14},{12,8},{14,10},{16,20},{18,... | collective-permute-start | bytes 172040 | tf_op jit(solution)/shard_map/ppermute | solution.py:93
  31.8 4.5 %collective-permute-start.10 = (bf16[56,512]{1,0:T(8,128)(2,1)S(1)}, bf16[56,512]{1,0:T(8,128)(2,1)S(1)}, u32[]{:S(2)}, u32[]{:S(2)}) collective-permute-start(bf16[56,512]{1,0:T(8,128)(2,1)S(1)} %get-tuple-element.46), channel_id=1, source_target_pairs={{0,8},{2,10},{4,12},{6,14},{8,0},{10,2},{12,4},{14,6},{16,24},{18,... | collective-permute-start | bytes 172040 | tf_op jit(solution)/shard_map/ppermute | solution.py:93
  32.3 8.5 %collective-permute-start.14 = (bf16[2,24,512]{2,1,0:T(8,128)(2,1)S(1)}, bf16[2,24,512]{2,1,0:T(8,128)(2,1)S(1)}, u32[]{:S(2)}, u32[]{:S(2)}) collective-permute-start(bf16[2,24,512]{2,1,0:T(8,128)(2,1)S(1)} %get-tuple-element.52), channel_id=1, source_target_pairs={{0,17},{1,16},{2,19},{3,18},{4,21},{5,20},{6,23},{7,22},{8,25},{9,... | collective-permute-start | bytes 147464 | tf_op jit(solution)/shard_map/ppermute | solution.py:147
  35.9 5.0 %collective-permute-start.15 = (bf16[2,24,512]{2,1,0:T(8,128)(2,1)S(1)}, bf16[2,24,512]{2,1,0:T(8,128)(2,1)S(1)}, u32[]{:S(2)}, u32[]{:S(2)}) collective-permute-start(bf16[2,24,512]{2,1,0:T(8,128)(2,1)S(1)} %get-tuple-element.53), channel_id=1, source_target_pairs={{0,16},{2,18},{4,20},{6,22},{8,24},{10,26},{12,28},{14,30},{16,0},... | collective-permute-start | bytes 147464 | tf_op jit(solution)/shard_map/ppermute | solution.py:93
  36.4 4.5 %collective-permute-start.16 = (bf16[2,24,512]{2,1,0:T(8,128)(2,1)S(1)}, bf16[2,24,512]{2,1,0:T(8,128)(2,1)S(1)}, u32[]{:S(2)}, u32[]{:S(2)}) collective-permute-start(bf16[2,24,512]{2,1,0:T(8,128)(2,1)S(1)} %get-tuple-element.47.after), channel_id=1, source_target_pairs={{0,1},{1,0},{2,3},{3,2},{4,5},{5,4},{6,7},{7,6},{8,9},{9,8},{10,11... | collective-permute-start | bytes 147464 | tf_op jit(solution)/shard_map/ppermute | solution.py:455

commit v8 on v7

--- a/solution.py
+++ b/solution.py
@@ -158,7 +158,7 @@
 
 def project_kernel(flipped, low_column, chunk, given, *refs):
     own, piece, acts = refs[:3]
-    others, out = refs[3 : 3 + given], refs[-1]
+    others, out = refs[3 : 3 + given], refs[-1 if given < 3 else -2]
     slots, width = piece.shape
     core = lax.axis_index("dp") % 2
     start = (1 - core if flipped else core) * (own.shape[1] // 2) + low_column
@@ -181,17 +181,20 @@
         shorts.append(jnp.where(full_here, other_part[:1], own_part[:1]))
     row = lax.broadcasted_iota(jnp.int32, (PAD, out.shape[1]), 0)
     out[2 * slots :] = jnp.where(row == 0, shorts[0], jnp.where(row == 1, shorts[1], 0.0))
+    refs[-1][...] = out[...].astype(refs[-1].dtype)
 
 
 def project(own, piece, acts, flipped, others, held, low=0):
     slots, width = piece.shape
     tokens = acts.shape[0]
-    rows = 2 * slots + (PAD if len(others) == 3 else 2 * PAD)
+    last = len(others) == 3
+    shape = (2 * slots + (PAD if last else 2 * PAD), tokens)
+    kinds = (jnp.float32, jnp.bfloat16) if last else (jnp.float32,)
     return pl.pallas_call(
         functools.partial(project_kernel, flipped, low, min(width, 1024), len(others)),
         in_specs=[WHOLE] * (3 + len(others) + len(held)),
-        out_specs=WHOLE,
-        out_shape=pltpu.VMEM((rows, tokens), jnp.float32),
+        out_specs=[WHOLE] * len(kinds),
+        out_shape=[pltpu.VMEM(shape, kind) for kind in kinds],
         compiler_params=PARAMS,
         cost_estimate=SMALL,
         name="project",
@@ -202,7 +205,8 @@
     slots = (parts.shape[0] - PAD) // 2
     full = slice(n * slots, (n + 1) * slots)
     short = slice(2 * slots + n, 2 * slots + n + 1)
-    return parts[full] + got[full], parts[short] + got[short]
+    total = parts[...] + got[...].astype(parts.dtype)
+    return total[full], total[short]
 
 
 def gradient_kernel(scale, places, own, keep, parts, got, tokens, cotangent, *refs):
@@ -427,18 +431,20 @@
     )
     right_mine = after_all(right_mine, right_own)
     right_theirs = flip(right_mine, 0)
-    back = project(right_own, right_mine, cotangent, False, (), ())
+    (back,) = project(right_own, right_mine, cotangent, False, (), ())
     left_first = after_all(left_first, back)
-    hidden = project(left_own, left_first, tokens, False, (), (cotangent,))
+    (hidden,) = project(left_own, left_first, tokens, False, (), (cotangent,))
     left_second = after_all(left_second, hidden)
     left_mine = jnp.concatenate([left_first, left_second], axis=1)
     left_theirs = flip(left_mine, 0)
-    hidden = project(
+    (hidden,) = project(
         left_own, left_second, tokens, False, (hidden,), (cotangent,), left_first.shape[1]
     )
-    back = project(right_own, right_theirs, cotangent, True, (back,), (hidden,))
-    parts = project(left_own, left_theirs, tokens, True, (hidden, full, back), (cotangent,))
-    parts_got = lax.ppermute(parts, "tensor", SWAP)
+    (back,) = project(right_own, right_theirs, cotangent, True, (back,), (hidden,))
+    parts, parts_send = project(
+        left_own, left_theirs, tokens, True, (hidden, full, back), (cotangent,)
+    )
+    parts_got = lax.ppermute(parts_send, "tensor", SWAP)
 
     operands = (parts, parts_got, tokens, cotangent, scale)
     other_send = gradient(*operands, False, False, ())

time: 41.8 us -> 41.1 us (0.983)
  waiting for transfers between devices: 3.42 us -> 2.63 us
    ppermute x1, waiting for transfers between devices: 3.23 us -> 2.34 us  [two_panels(): parts_got = lax.ppermute(parts_send, 'tensor', SWAP)]
  transfers between devices with their start and end apart: 17 -> 17, of which waited for: 3 -> 4; matrix products, arithmetic and copies ran while one was open for 0% -> 0% of each run, Pallas kernels for 33% -> 34%
where the time goes in v8:
time: 41.1 us; the launch traced here: 40.9 us
  starting transfers between devices  20 us (49%)
  Pallas kernels  17.4 us (42%)
  waiting for transfers between devices  2.63 us (6%)
  between operations  0.85 us (2%)
    ppermute x11, starting transfers between devices, flip(): lax.ppermute(value, 'dp', [(i, i ^ mask) for i in range(lax.axis_size('dp...  9.45 us
    pallas_call x1, Pallas kernels, stage(): pl.pallas_call(functools.partial(stage_kernel, parts), in_specs=[FAR] * 5...  4.98 us
    ppermute x2, starting transfers between devices, across(): return lax.ppermute(value, ('dp', 'tensor'), pairs)  4.52 us
    pallas_call x5, Pallas kernels, project(): pl.pallas_call(functools.partial(project_kernel, flipped, low, min(width,...  4.51 us
    pallas_call x1, Pallas kernels, spread(): pl.pallas_call(functools.partial(spread_kernel, chunk), in_specs=[WHOLE]...  3.18 us
    ppermute x2, starting transfers between devices, two_panels(): lax.ppermute(w, 'tensor', SWAP)  3.11 us
    pallas_call x4, Pallas kernels, gradient(): pl.pallas_call(functools.partial(gradient_kernel, scale, places, own, kee...  2.71 us
    ppermute x1, waiting for transfers between devices, two_panels(): parts_got = lax.ppermute(parts_send, 'tensor', SWAP)  2.34 us
  transfers between devices with their start and end apart: 17, of which 4 were waited for; matrix products, arithmetic and copies ran while one was open for 0% of the time, Pallas kernels for 34%

profile of v8, /device:TPU:0, one launch (start us, length us, event | category | flops | bytes accessed | tf_op | source)
XLA Modules:
  0.0 40.9 jit_solution(13877670416087061786)
XLA Ops:
  0.6 1.1 %pick.1 = (bf16[24,4096]{1,0:T(8,128)(2,1)S(1)}, bf16[24,2048]{1,0:T(8,128)(2,1)S(1)}, bf16[24,2048]{1,0:T(8,128)(2,1)S(1)}) custom-call(bf16[24,16384]{1,0:T(8,128)(2,1)} %refs_0_.1, bf16[24,16384]{1,0:T(8,128)(2,1)} %refs_2_.1), custom_call_target="tpu_custom_call" | custom-call | flops 1 | bytes 1 | tf_op jit(solution)/shard_map/pick/pallas_call | solution.py:387
  1.7 3.0 %collective-permute-start.1 = (bf16[24,4096]{1,0:T(8,128)(2,1)S(1)}, bf16[24,4096]{1,0:T(8,128)(2,1)S(1)}, u32[]{:S(2)}, u32[]{:S(2)}) collective-permute-start(bf16[24,4096]{1,0:T(8,128)(2,1)S(1)} %get-tuple-element.33.refs_4_), channel_id=1, source_target_pairs={{0,1},{1,0},{2,3},{3,2},{4,5},{5,4},{6,7},{7,6},{8,9},{9,8},{10,11... | collective-permute-start | bytes 589832 | tf_op jit(solution)/shard_map/ppermute | solution.py:427
  4.8 0.8 %collective-permute-start.2 = (bf16[24,2048]{1,0:T(8,128)(2,1)S(1)}, bf16[24,2048]{1,0:T(8,128)(2,1)S(1)}, u32[]{:S(2)}, u32[]{:S(2)}) collective-permute-start(bf16[24,2048]{1,0:T(8,128)(2,1)S(1)} %get-tuple-element.35.refs_6_), channel_id=1, source_target_pairs={{0,3},{1,2},{2,1},{3,0},{4,7},{5,6},{6,5},{7,4},{8,11},{9,10},{10,... | collective-permute-start | bytes 294920 | tf_op jit(solution)/shard_map/ppermute | solution.py:147
  5.7 5.0 %stage.1 = (bf16[24,8192]{1,0:T(8,128)(2,1)S(1)}, bf16[384,8192]{1,0:T(8,128)(2,1)S(1)}, bf16[24,8192]{1,0:T(8,128)(2,1)S(1)}, bf16[384,8192]{1,0:T(8,128)(2,1)S(1)}, f32[8,128]{1,0:T(8,128)S(1)}) custom-call(s32[2]{0:T(128)} %rank.1, bf16[24,16384]{1,0:T(8,128)(2,1)} %refs_0_.1, bf16[384,8192]{1,0:T(8,128)(2,1)} %refs_1_.1, bf16[24,16384]{1,0:T(8,128)(2,1)} %refs_2_.1, ...), custom_call_target="tpu_custom_call" | custom-call | flops 1 | bytes 1 | tf_op jit(solution)/shard_map/stage/pallas_call | solution.py:130
  10.7 1.3 %collective-permute-start.4 = (bf16[24,4096]{1,0:T(8,128)(2,1)S(1)}, bf16[24,4096]{1,0:T(8,128)(2,1)S(1)}, u32[]{:S(2)}, u32[]{:S(2)}) collective-permute-start(bf16[24,4096]{1,0:T(8,128)(2,1)S(1)} %collective-permute-done.1.refs_1_), channel_id=1, source_target_pairs={{0,2},{2,0},{4,6},{6,4},{8,10},{10,8},{12,14},{14,12},{16,18},{18,... | collective-permute-start | bytes 589832 | tf_op jit(solution)/shard_map/ppermute | solution.py:93
  12.0 1.1 %project.5.refs_3_ = f32[64,384]{1,0:T(8,128)S(1)} custom-call(bf16[24,8192]{1,0:T(8,128)(2,1)S(1)} %get-tuple-element.38.refs_0_, bf16[24,4096]{1,0:T(8,128)(2,1)S(1)} %collective-permute-done.1.refs_1_, bf16[384,8192]{1,0:T(8,128)(2,1)S(1)} %get-tuple-element.40.refs_2_.refs_3_.refs_4_.refs_6_.cotangent), custom_call_target="tpu_custom_call" | custom-call | flops 1 | bytes 1 | tf_op jit(solution)/shard_map/project/pallas_call | solution.py:193
  13.1 0.6 %project.6.refs_3_ = f32[64,384]{1,0:T(8,128)S(1)} custom-call(bf16[24,8192]{1,0:T(8,128)(2,1)S(1)} %get-tuple-element.37.refs_0_.own, bf16[24,2048]{1,0:T(8,128)(2,1)S(1)} %collective-permute-done.refs_1_, bf16[384,8192]{1,0:T(8,128)(2,1)S(1)} %get-tuple-element.42.refs_2_.tokens, ...), custom_call_target="tpu_custom_call" | custom-call | flops 1 | bytes 1 | tf_op jit(solution)/shard_map/project/pallas_call | solution.py:193
  13.7 0.1 collective-permute-start.3
  13.8 0.6 %project.7.refs_4_.refs_3_ = f32[64,384]{1,0:T(8,128)S(1)} custom-call(bf16[24,8192]{1,0:T(8,128)(2,1)S(1)} %get-tuple-element.37.refs_0_.own, bf16[24,2048]{1,0:T(8,128)(2,1)S(1)} %collective-permute-done.2.refs_1_, bf16[384,8192]{1,0:T(8,128)(2,1)S(1)} %get-tuple-element.42.refs_2_.tokens, f32[64,384]{1,0:T(8,128)S(1)} %project.6.refs_3_, ...), custom_call_target="tpu_custom_call" | custom-call | flops 1 | bytes 1 | tf_op jit(solution)/shard_map/project/pallas_call | solution.py:193
  14.4 1.1 %project.8.refs_5_ = f32[64,384]{1,0:T(8,128)S(1)} custom-call(bf16[24,8192]{1,0:T(8,128)(2,1)S(1)} %get-tuple-element.38.refs_0_, bf16[24,4096]{1,0:T(8,128)(2,1)S(1)} %collective-permute-done.4.refs_1_, bf16[384,8192]{1,0:T(8,128)(2,1)S(1)} %get-tuple-element.40.refs_2_.refs_3_.refs_4_.refs_6_.cotangent, f32[64,384]{1,0:T(8,128)S(1)} %project.5.refs_3_, ...), custom_call_target="tpu_custom_call" | custom-call | flops 1 | bytes 1 | tf_op jit(solution)/shard_map/project/pallas_call | solution.py:193
  15.6 1.1 %project.9 = (f32[56,384]{1,0:T(8,128)S(1)}, bf16[56,384]{1,0:T(8,128)(2,1)S(1)}) custom-call(bf16[24,8192]{1,0:T(8,128)(2,1)S(1)} %get-tuple-element.37.refs_0_.own, bf16[24,4096]{1,0:T(8,128)(2,1)S(1)} %collective-permute-done.3.refs_1_.theirs, bf16[384,8192]{1,0:T(8,128)(2,1)S(1)} %get-tuple-element.42.refs_2_.tokens, ...), custom_call_target="tpu_custom_call" | custom-call | flops 1 | bytes 1 | tf_op jit(solution)/shard_map/project/pallas_call | solution.py:193
  16.7 1.7 %collective-permute-start.5 = (bf16[56,384]{1,0:T(8,128)(2,1)S(1)}, bf16[56,384]{1,0:T(8,128)(2,1)S(1)}, u32[]{:S(2)}, u32[]{:S(2)}) collective-permute-start(bf16[56,384]{1,0:T(8,128)(2,1)S(1)} %get-tuple-element.45), channel_id=1, source_target_pairs={{0,1},{1,0},{2,3},{3,2},{4,5},{5,4},{6,7},{7,6},{8,9},{9,8},{10,11... | collective-permute-start | bytes 129032 | tf_op jit(solution)/shard_map/ppermute | solution.py:447
  18.4 2.3 %collective-permute-done.5.got = bf16[56,384]{1,0:T(8,128)(2,1)S(1)} collective-permute-done((bf16[56,384]{1,0:T(8,128)(2,1)S(1)}, bf16[56,384]{1,0:T(8,128)(2,1)S(1)}, u32[]{:S(2)}, u32[]{:S(2)}) %collective-permute-start.5) | collective-permute-done | bytes 43040 | tf_op jit(solution)/shard_map/ppermute | solution.py:447
  20.8 0.7 %gradient.4.refs_0_ = bf16[4,56,512]{2,1,0:T(8,128)(2,1)S(1)} custom-call(f32[56,384]{1,0:T(8,128)S(1)} %get-tuple-element.44.parts, bf16[56,384]{1,0:T(8,128)(2,1)S(1)} %collective-permute-done.5.got, bf16[384,8192]{1,0:T(8,128)(2,1)S(1)} %get-tuple-element.42.refs_2_.tokens, bf16[384,8192]{1,0:T(8,128)(2,1)S(1)} %get-tuple-element.40.refs_2_.refs_3_.refs_4_.refs_6_.cotangent), custom_call_target="tpu_custom_call" | custom-call | flops 1 | bytes 1 | tf_op jit(solution)/shard_map/gradient/pallas_call | solution.py:239
  21.5 0.7 %gradient.5.refs_0_.keep = f32[4,56,512]{2,1,0:T(8,128)S(1)} custom-call(f32[56,384]{1,0:T(8,128)S(1)} %get-tuple-element.44.parts, bf16[56,384]{1,0:T(8,128)(2,1)S(1)} %collective-permute-done.5.got, bf16[384,8192]{1,0:T(8,128)(2,1)S(1)} %get-tuple-element.42.refs_2_.tokens, ...), custom_call_target="tpu_custom_call" | custom-call | flops 1 | bytes 1 | tf_op jit(solution)/shard_map/gradient/pallas_call | solution.py:239
  22.2 0.7 %gradient.6.refs_0_ = bf16[4,56,512]{2,1,0:T(8,128)(2,1)S(1)} custom-call(f32[56,384]{1,0:T(8,128)S(1)} %get-tuple-element.44.parts, bf16[56,384]{1,0:T(8,128)(2,1)S(1)} %collective-permute-done.5.got, bf16[384,8192]{1,0:T(8,128)(2,1)S(1)} %get-tuple-element.42.refs_2_.tokens, ...), custom_call_target="tpu_custom_call" | custom-call | flops 1 | bytes 1 | tf_op jit(solution)/shard_map/gradient/pallas_call | solution.py:239
  22.9 0.5 %collective-permute-start.7 = (bf16[4,56,512]{2,1,0:T(8,128)(2,1)S(1)}, bf16[4,56,512]{2,1,0:T(8,128)(2,1)S(1)}, u32[]{:S(2)}, u32[]{:S(2)}) collective-permute-start(bf16[4,56,512]{2,1,0:T(8,128)(2,1)S(1)} %gradient.6.refs_0_), channel_id=1, source_target_pairs={{0,2},{2,0},{4,6},{6,4},{8,10},{10,8},{12,14},{14,12},{16,18},{18,... | collective-permute-start | bytes 688136 | tf_op jit(solution)/shard_map/ppermute | solution.py:93
  23.5 2.7 %collective-permute-start.11 = (bf16[56,512]{1,0:T(8,128)(2,1)S(1)}, bf16[56,512]{1,0:T(8,128)(2,1)S(1)}, u32[]{:S(2)}, u32[]{:S(2)}) collective-permute-start(bf16[56,512]{1,0:T(8,128)(2,1)S(1)} %get-tuple-element.54), channel_id=1, source_target_pairs={{0,12},{2,14},{4,8},{6,10},{8,4},{10,6},{12,0},{14,2},{16,28},{18,... | collective-permute-start | bytes 172040 | tf_op jit(solution)/shard_map/ppermute | solution.py:93
  26.2 0.4 %collective-permute-start.13 = (bf16[56,512]{1,0:T(8,128)(2,1)S(1)}, bf16[56,512]{1,0:T(8,128)(2,1)S(1)}, u32[]{:S(2)}, u32[]{:S(2)}) collective-permute-start(bf16[56,512]{1,0:T(8,128)(2,1)S(1)} %get-tuple-element.55), channel_id=1, source_target_pairs={{0,8},{2,10},{4,12},{6,14},{8,0},{10,2},{12,4},{14,6},{16,24},{18,... | collective-permute-start | bytes 172040 | tf_op jit(solution)/shard_map/ppermute | solution.py:93
  26.7 0.4 collective-permute-start.12
  27.1 0.7 %gradient.7.keep = f32[4,56,512]{2,1,0:T(8,128)S(1)} custom-call(f32[56,384]{1,0:T(8,128)S(1)} %get-tuple-element.44.parts, bf16[56,384]{1,0:T(8,128)(2,1)S(1)} %collective-permute-done.5.got, bf16[384,8192]{1,0:T(8,128)(2,1)S(1)} %get-tuple-element.42.refs_2_.tokens, bf16[384,8192]{1,0:T(8,128)(2,1)S(1)} %get-tuple-element.40.refs_2_.refs_3_.refs_4_.refs_6_.cotangent, ...), custom_call_target="tpu_custom_call" | custom-call | flops 1 | bytes 1 | tf_op jit(solution)/shard_map/gradient/pallas_call | solution.py:239
  27.7 0.1 quarter.3
  27.8 2.7 %collective-permute-start.8 = (bf16[56,512]{1,0:T(8,128)(2,1)S(1)}, bf16[56,512]{1,0:T(8,128)(2,1)S(1)}, u32[]{:S(2)}, u32[]{:S(2)}) collective-permute-start(bf16[56,512]{1,0:T(8,128)(2,1)S(1)} %get-tuple-element.48), channel_id=1, source_target_pairs={{0,12},{2,14},{4,8},{6,10},{8,4},{10,6},{12,0},{14,2},{16,28},{18,... | collective-permute-start | bytes 172040 | tf_op jit(solution)/shard_map/ppermute | solution.py:93
  30.5 0.5 %collective-permute-start.9 = (bf16[56,512]{1,0:T(8,128)(2,1)S(1)}, bf16[56,512]{1,0:T(8,128)(2,1)S(1)}, u32[]{:S(2)}, u32[]{:S(2)}) collective-permute-start(bf16[56,512]{1,0:T(8,128)(2,1)S(1)} %get-tuple-element.49), channel_id=1, source_target_pairs={{0,4},{2,6},{4,0},{6,2},{8,12},{10,14},{12,8},{14,10},{16,20},{18,... | collective-permute-start | bytes 172040 | tf_op jit(solution)/shard_map/ppermute | solution.py:93
  31.1 0.3 collective-permute-start.10
  31.4 0.1 collective-permute-done.12.refs_1_
  31.5 3.7 %collective-permute-start.14 = (bf16[2,24,512]{2,1,0:T(8,128)(2,1)S(1)}, bf16[2,24,512]{2,1,0:T(8,128)(2,1)S(1)}, u32[]{:S(2)}, u32[]{:S(2)}) collective-permute-start(bf16[2,24,512]{2,1,0:T(8,128)(2,1)S(1)} %get-tuple-element.56), channel_id=1, source_target_pairs={{0,17},{1,16},{2,19},{3,18},{4,21},{5,20},{6,23},{7,22},{8,25},{9,... | collective-permute-start | bytes 147464 | tf_op jit(solution)/shard_map/ppermute | solution.py:147
  35.2 0.3 collective-permute-start.15
  35.7 1.2 %collective-permute-start.16 = (bf16[2,24,512]{2,1,0:T(8,128)(2,1)S(1)}, bf16[2,24,512]{2,1,0:T(8,128)(2,1)S(1)}, u32[]{:S(2)}, u32[]{:S(2)}) collective-permute-start(bf16[2,24,512]{2,1,0:T(8,128)(2,1)S(1)} %get-tuple-element.51.after), channel_id=1, source_target_pairs={{0,1},{1,0},{2,3},{3,2},{4,5},{5,4},{6,7},{7,6},{8,9},{9,8},{10,11... | collective-permute-start | bytes 147464 | tf_op jit(solution)/shard_map/ppermute | solution.py:461
  36.9 3.2 %spread.1 = bf16[384,8192]{1,0:T(8,128)(2,1)} custom-call(f32[8,128]{1,0:T(8,128)S(1)} %get-tuple-element.36.refs_4_.full, f32[56,384]{1,0:T(8,128)S(1)} %get-tuple-element.44.parts, bf16[56,384]{1,0:T(8,128)(2,1)S(1)} %collective-permute-done.5.got, bf16[24,8192]{1,0:T(8,128)(2,1)S(1)} %get-tuple-element.37.refs_0_.own, ...), custom_call_target="tpu_custom_call" | custom-call | flops 10000000000 | bytes 100000000 | tf_op jit(solution)/shard_map/spread/pallas_call | solution.py:280
  40.1 0.1 collective-permute-done.15.refs_1_
  40.2 0.7 %place.1 = (f32[24,2,1,512]{3,2,1,0:T(1,128)}, f32[24,2,1,512]{3,2,1,0:T(1,128)}) custom-call(f32[2,24,512]{2,1,0:T(8,128)S(1)} %gather.3.held, f32[2,24,512]{2,1,0:T(8,128)S(1)} %gather.2.far, bf16[2,24,512]{2,1,0:T(8,128)(2,1)S(1)} %collective-permute-done.16.got), custom_call_target="tpu_custom_call" | custom-call | flops 1 | bytes 1 | tf_op jit(solution)/shard_map/place/pallas_call | solution.py:353
  (23 shorter events, 0.4 us)
Async XLA Ops:
  1.7 8.9 %collective-permute-start.1 = (bf16[24,4096]{1,0:T(8,128)(2,1)S(1)}, bf16[24,4096]{1,0:T(8,128)(2,1)S(1)}, u32[]{:S(2)}, u32[]{:S(2)}) collective-permute-start(bf16[24,4096]{1,0:T(8,128)(2,1)S(1)} %get-tuple-element.33.refs_4_), channel_id=1, source_target_pairs={{0,1},{1,0},{2,3},{3,2},{4,5},{5,4},{6,7},{7,6},{8,9},{9,8},{10,11... | collective-permute-start | bytes 589832 | tf_op jit(solution)/shard_map/ppermute | solution.py:427
  4.8 8.3 %collective-permute-start = (bf16[24,2048]{1,0:T(8,128)(2,1)S(1)}, bf16[24,2048]{1,0:T(8,128)(2,1)S(1)}, u32[]{:S(2)}, u32[]{:S(2)}) collective-permute-start(bf16[24,2048]{1,0:T(8,128)(2,1)S(1)} %get-tuple-element.34.refs_5_), channel_id=1, source_target_pairs={{0,1},{1,0},{2,3},{3,2},{4,5},{5,4},{6,7},{7,6},{8,9},{9,8},{10,11... | collective-permute-start | bytes 294920 | tf_op jit(solution)/shard_map/ppermute | solution.py:427
  4.8 8.9 %collective-permute-start.2 = (bf16[24,2048]{1,0:T(8,128)(2,1)S(1)}, bf16[24,2048]{1,0:T(8,128)(2,1)S(1)}, u32[]{:S(2)}, u32[]{:S(2)}) collective-permute-start(bf16[24,2048]{1,0:T(8,128)(2,1)S(1)} %get-tuple-element.35.refs_6_), channel_id=1, source_target_pairs={{0,3},{1,2},{2,1},{3,0},{4,7},{5,6},{6,5},{7,4},{8,11},{9,10},{10,... | collective-permute-start | bytes 294920 | tf_op jit(solution)/shard_map/ppermute | solution.py:147
  10.7 3.8 %collective-permute-start.4 = (bf16[24,4096]{1,0:T(8,128)(2,1)S(1)}, bf16[24,4096]{1,0:T(8,128)(2,1)S(1)}, u32[]{:S(2)}, u32[]{:S(2)}) collective-permute-start(bf16[24,4096]{1,0:T(8,128)(2,1)S(1)} %collective-permute-done.1.refs_1_), channel_id=1, source_target_pairs={{0,2},{2,0},{4,6},{6,4},{8,10},{10,8},{12,14},{14,12},{16,18},{18,... | collective-permute-start | bytes 589832 | tf_op jit(solution)/shard_map/ppermute | solution.py:93
  13.7 1.8 %collective-permute-start.3 = (bf16[24,4096]{1,0:T(8,128)(2,1)S(1)}, bf16[24,4096]{1,0:T(8,128)(2,1)S(1)}, u32[]{:S(2)}, u32[]{:S(2)}) collective-permute-start(bf16[24,4096]{1,0:T(8,128)(2,1)S(1)} %constant_dynamic-update-slice_fusion.mine), channel_id=1, source_target_pairs={{0,2},{2,0},{4,6},{6,4},{8,10},{10,8},{12,14},{14,12},{16,18},{18,... | collective-permute-start | bytes 589832 | tf_op jit(solution)/shard_map/ppermute | solution.py:93
  16.7 4.1 %collective-permute-start.5 = (bf16[56,384]{1,0:T(8,128)(2,1)S(1)}, bf16[56,384]{1,0:T(8,128)(2,1)S(1)}, u32[]{:S(2)}, u32[]{:S(2)}) collective-permute-start(bf16[56,384]{1,0:T(8,128)(2,1)S(1)} %get-tuple-element.45), channel_id=1, source_target_pairs={{0,1},{1,0},{2,3},{3,2},{4,5},{5,4},{6,7},{7,6},{8,9},{9,8},{10,11... | collective-permute-start | bytes 129032 | tf_op jit(solution)/shard_map/ppermute | solution.py:447
  21.4 2.0 %collective-permute-start.6 = (bf16[4,56,512]{2,1,0:T(8,128)(2,1)S(1)}, bf16[4,56,512]{2,1,0:T(8,128)(2,1)S(1)}, u32[]{:S(2)}, u32[]{:S(2)}) collective-permute-start(bf16[4,56,512]{2,1,0:T(8,128)(2,1)S(1)} %gradient.4.refs_0_), channel_id=1, source_target_pairs={{0,2},{2,0},{4,6},{6,4},{8,10},{10,8},{12,14},{14,12},{16,18},{18,... | collective-permute-start | bytes 688136 | tf_op jit(solution)/shard_map/ppermute | solution.py:93
  22.9 4.8 %collective-permute-start.7 = (bf16[4,56,512]{2,1,0:T(8,128)(2,1)S(1)}, bf16[4,56,512]{2,1,0:T(8,128)(2,1)S(1)}, u32[]{:S(2)}, u32[]{:S(2)}) collective-permute-start(bf16[4,56,512]{2,1,0:T(8,128)(2,1)S(1)} %gradient.6.refs_0_), channel_id=1, source_target_pairs={{0,2},{2,0},{4,6},{6,4},{8,10},{10,8},{12,14},{14,12},{16,18},{18,... | collective-permute-start | bytes 688136 | tf_op jit(solution)/shard_map/ppermute | solution.py:93
  23.5 7.6 %collective-permute-start.11 = (bf16[56,512]{1,0:T(8,128)(2,1)S(1)}, bf16[56,512]{1,0:T(8,128)(2,1)S(1)}, u32[]{:S(2)}, u32[]{:S(2)}) collective-permute-start(bf16[56,512]{1,0:T(8,128)(2,1)S(1)} %get-tuple-element.54), channel_id=1, source_target_pairs={{0,12},{2,14},{4,8},{6,10},{8,4},{10,6},{12,0},{14,2},{16,28},{18,... | collective-permute-start | bytes 172040 | tf_op jit(solution)/shard_map/ppermute | solution.py:93
  26.2 5.1 %collective-permute-start.13 = (bf16[56,512]{1,0:T(8,128)(2,1)S(1)}, bf16[56,512]{1,0:T(8,128)(2,1)S(1)}, u32[]{:S(2)}, u32[]{:S(2)}) collective-permute-start(bf16[56,512]{1,0:T(8,128)(2,1)S(1)} %get-tuple-element.55), channel_id=1, source_target_pairs={{0,8},{2,10},{4,12},{6,14},{8,0},{10,2},{12,4},{14,6},{16,24},{18,... | collective-permute-start | bytes 172040 | tf_op jit(solution)/shard_map/ppermute | solution.py:93
  26.7 4.8 %collective-permute-start.12 = (bf16[56,512]{1,0:T(8,128)(2,1)S(1)}, bf16[56,512]{1,0:T(8,128)(2,1)S(1)}, u32[]{:S(2)}, u32[]{:S(2)}) collective-permute-start(bf16[56,512]{1,0:T(8,128)(2,1)S(1)} %get-tuple-element.46.refs_1_), channel_id=1, source_target_pairs={{0,4},{2,6},{4,0},{6,2},{8,12},{10,14},{12,8},{14,10},{16,20},{18,... | collective-permute-start | bytes 172040 | tf_op jit(solution)/shard_map/ppermute | solution.py:93
  27.8 7.7 %collective-permute-start.8 = (bf16[56,512]{1,0:T(8,128)(2,1)S(1)}, bf16[56,512]{1,0:T(8,128)(2,1)S(1)}, u32[]{:S(2)}, u32[]{:S(2)}) collective-permute-start(bf16[56,512]{1,0:T(8,128)(2,1)S(1)} %get-tuple-element.48), channel_id=1, source_target_pairs={{0,12},{2,14},{4,8},{6,10},{8,4},{10,6},{12,0},{14,2},{16,28},{18,... | collective-permute-start | bytes 172040 | tf_op jit(solution)/shard_map/ppermute | solution.py:93
  30.5 5.0 %collective-permute-start.9 = (bf16[56,512]{1,0:T(8,128)(2,1)S(1)}, bf16[56,512]{1,0:T(8,128)(2,1)S(1)}, u32[]{:S(2)}, u32[]{:S(2)}) collective-permute-start(bf16[56,512]{1,0:T(8,128)(2,1)S(1)} %get-tuple-element.49), channel_id=1, source_target_pairs={{0,4},{2,6},{4,0},{6,2},{8,12},{10,14},{12,8},{14,10},{16,20},{18,... | collective-permute-start | bytes 172040 | tf_op jit(solution)/shard_map/ppermute | solution.py:93
  31.1 4.5 %collective-permute-start.10 = (bf16[56,512]{1,0:T(8,128)(2,1)S(1)}, bf16[56,512]{1,0:T(8,128)(2,1)S(1)}, u32[]{:S(2)}, u32[]{:S(2)}) collective-permute-start(bf16[56,512]{1,0:T(8,128)(2,1)S(1)} %get-tuple-element.50), channel_id=1, source_target_pairs={{0,8},{2,10},{4,12},{6,14},{8,0},{10,2},{12,4},{14,6},{16,24},{18,... | collective-permute-start | bytes 172040 | tf_op jit(solution)/shard_map/ppermute | solution.py:93
  31.5 8.6 %collective-permute-start.14 = (bf16[2,24,512]{2,1,0:T(8,128)(2,1)S(1)}, bf16[2,24,512]{2,1,0:T(8,128)(2,1)S(1)}, u32[]{:S(2)}, u32[]{:S(2)}) collective-permute-start(bf16[2,24,512]{2,1,0:T(8,128)(2,1)S(1)} %get-tuple-element.56), channel_id=1, source_target_pairs={{0,17},{1,16},{2,19},{3,18},{4,21},{5,20},{6,23},{7,22},{8,25},{9,... | collective-permute-start | bytes 147464 | tf_op jit(solution)/shard_map/ppermute | solution.py:147
  35.2 5.0 %collective-permute-start.15 = (bf16[2,24,512]{2,1,0:T(8,128)(2,1)S(1)}, bf16[2,24,512]{2,1,0:T(8,128)(2,1)S(1)}, u32[]{:S(2)}, u32[]{:S(2)}) collective-permute-start(bf16[2,24,512]{2,1,0:T(8,128)(2,1)S(1)} %get-tuple-element.57), channel_id=1, source_target_pairs={{0,16},{2,18},{4,20},{6,22},{8,24},{10,26},{12,28},{14,30},{16,0},... | collective-permute-start | bytes 147464 | tf_op jit(solution)/shard_map/ppermute | solution.py:93
  35.7 4.5 %collective-permute-start.16 = (bf16[2,24,512]{2,1,0:T(8,128)(2,1)S(1)}, bf16[2,24,512]{2,1,0:T(8,128)(2,1)S(1)}, u32[]{:S(2)}, u32[]{:S(2)}) collective-permute-start(bf16[2,24,512]{2,1,0:T(8,128)(2,1)S(1)} %get-tuple-element.51.after), channel_id=1, source_target_pairs={{0,1},{1,0},{2,3},{3,2},{4,5},{5,4},{6,7},{7,6},{8,9},{9,8},{10,11... | collective-permute-start | bytes 147464 | tf_op jit(solution)/shard_map/ppermute | solution.py:461

commit v9 on v8

--- a/solution.py
+++ b/solution.py
@@ -163,13 +163,21 @@
     core = lax.axis_index("dp") % 2
     start = (1 - core if flipped else core) * (own.shape[1] // 2) + low_column
     total = others[0][...] if others else None
-    for low in range(0, width, chunk):
+    turned = None
+    for n, low in enumerate(range(0, width, chunk)):
         column = pl.ds(pl.multiple_of(start + low, chunk), chunk)
         rows = both_panels(own[:, column], piece[:, low : low + chunk])
-        part = lax.dot_general(
-            rows, acts[:, column], (((1,), (1,)), ((), ())), preferred_element_type=jnp.float32
-        )
-        total = part if total is None else total + part
+        if n % 2:
+            part = lax.dot_general(
+                acts[:, column], rows, (((1,), (1,)), ((), ())), preferred_element_type=jnp.float32
+            )
+            turned = part if turned is None else turned + part
+        else:
+            part = lax.dot_general(
+                rows, acts[:, column], (((1,), (1,)), ((), ())), preferred_element_type=jnp.float32
+            )
+            total = part if total is None else total + part
+    total += turned.T
     if given < 3:
         out[...] = total
         return
@@ -191,7 +199,7 @@
     shape = (2 * slots + (PAD if last else 2 * PAD), tokens)
     kinds = (jnp.float32, jnp.bfloat16) if last else (jnp.float32,)
     return pl.pallas_call(
-        functools.partial(project_kernel, flipped, low, min(width, 1024), len(others)),
+        functools.partial(project_kernel, flipped, low, min(width // 2, 512), len(others)),
         in_specs=[WHOLE] * (3 + len(others) + len(held)),
         out_specs=[WHOLE] * len(kinds),
         out_shape=[pltpu.VMEM(shape, kind) for kind in kinds],
@@ -209,38 +217,55 @@
     return total[full], total[short]
 
 
-def gradient_kernel(scale, places, own, keep, parts, got, tokens, cotangent, *refs):
-    out = refs[-1]
-    rows, block = out.shape[1:]
+def gradient_kernel(scale, places, jobs, parts, got, tokens, cotangent, *refs):
+    outs = refs[-len(jobs) :]
+    rows, block = outs[0].shape[1:]
     slots = (rows - PAD) // 2
+    live = slots + PAD
     position = lax.axis_index("dp")
-    core = (position + (0 if keep else 1)) % 2
-    bit_3 = (position // 8 + (0 if own else 1)) % 2
     first = lax.broadcasted_iota(jnp.int32, (PAD, tokens.shape[0]), 0) == 0
     weights = []
     for n in range(2):
         full, short = summed_rows(parts, got, n)
         both = jnp.concatenate([full, jnp.where(first, short, 0.0)], axis=0)
         weights.append(both.astype(jnp.bfloat16))
+    main = tokens.shape[0] // 256 * 256
+    gap = jnp.zeros((live, tokens.shape[0] - main), jnp.bfloat16)
+    rest = jnp.concatenate(
+        [
+            jnp.concatenate([weights[0][:, main:], gap], axis=1),
+            jnp.concatenate([gap, weights[1][:, main:]], axis=1),
+        ],
+        axis=0,
+    )
     row = lax.broadcasted_iota(jnp.int32, (PAD, block), 0)
-    for j, q in enumerate(places):
-        start = ((bit_3 * len(places) + j) * 2 + core) * block
-        columns = pl.ds(pl.multiple_of(start, block), block)
-        left = jnp.dot(weights[0], tokens[:, columns], preferred_element_type=jnp.float32)
-        right = jnp.dot(weights[1], cotangent[:, columns], preferred_element_type=jnp.float32)
-        short = jnp.where(row == 1, right[slots : slots + 1], left[slots:])
-        grad = jnp.concatenate([left[:slots], right[:slots], short], axis=0) * scale
-        out[q] = grad.astype(out.dtype)
-
-
-def gradient(parts, got, tokens, cotangent, scale, own, keep, after):
+    for (own, keep), out in zip(jobs, outs):
+        core = (position + (0 if keep else 1)) % 2
+        bit_3 = (position // 8 + (0 if own else 1)) % 2
+        for j, q in enumerate(places):
+            start = ((bit_3 * len(places) + j) * 2 + core) * block
+            columns = pl.ds(pl.multiple_of(start, block), block)
+            last = jnp.concatenate([tokens[main:, columns], cotangent[main:, columns]], axis=0)
+            last = jnp.dot(rest, last, preferred_element_type=jnp.float32)
+            left, right = (
+                jnp.dot(w[:, :main], acts[:main, columns], preferred_element_type=jnp.float32)
+                for w, acts in zip(weights, (tokens, cotangent))
+            )
+            left += last[:live]
+            right += last[live:]
+            short = jnp.where(row == 1, right[slots : slots + 1], left[slots:])
+            grad = jnp.concatenate([left[:slots], right[:slots], short], axis=0) * scale
+            out[q] = grad.astype(out.dtype)
+
+
+def gradient(parts, got, tokens, cotangent, scale, jobs, after):
     places = (0, 2, 1, 3)
     shape = (len(places), parts.shape[0], tokens.shape[1] // lax.axis_size("dp"))
     return pl.pallas_call(
-        functools.partial(gradient_kernel, scale, places, own, keep),
+        functools.partial(gradient_kernel, scale, places, jobs),
         in_specs=[WHOLE] * (4 + len(after)),
-        out_specs=WHOLE,
-        out_shape=pltpu.VMEM(shape, jnp.float32 if keep else jnp.bfloat16),
+        out_specs=[WHOLE] * len(jobs),
+        out_shape=[pltpu.VMEM(shape, jnp.float32 if job[1] else jnp.bfloat16) for job in jobs],
         compiler_params=PARAMS,
         cost_estimate=SMALL,
         name="gradient",
@@ -447,11 +472,12 @@
     parts_got = lax.ppermute(parts_send, "tensor", SWAP)
 
     operands = (parts, parts_got, tokens, cotangent, scale)
-    other_send = gradient(*operands, False, False, ())
-    other_keep = gradient(*operands, False, True, (other_send,))
-    own_send = gradient(*operands, True, False, (other_keep,))
+    (other_send,) = gradient(*operands, [(False, False)], ())
+    other_keep, own_send = gradient(
+        *operands, [(False, True), (True, False)], (other_send,)
+    )
     other = quarter(other_keep, flip(other_send, 0))
-    own_keep = gradient(*operands, True, True, (own_send, other[1]))
+    (own_keep,) = gradient(*operands, [(True, True)], (own_send, other[1]))
     own = quarter(own_keep, flip(own_send, 0))
     other_gots, own_gots = trade(other[1:]), trade(own[1:])
     near_send, far_send = settle(full, other[0], other_gots, jnp.bfloat16)

time: 41.1 us -> 40.6 us (0.988)
  Pallas kernels: 17.4 us -> 16.9 us
    pallas_call x9 -> x8, Pallas kernels: 7.21 us -> 6.71 us  [the longest x5 4.3 us: project(): pl.pallas_call(functools.partial(project_kernel, flipped, low, min(width...]
  transfers between devices with their start and end apart: 17 -> 17, of which waited for: 4 -> 4; matrix products, arithmetic and copies ran while one was open for 0% -> 0% of each run, Pallas kernels for 34% -> 33%
where the time goes in v9:
time: 40.6 us; the launch traced here: 40.5 us
  starting transfers between devices  20.1 us (50%)
  Pallas kernels  16.9 us (42%)
  waiting for transfers between devices  2.66 us (7%)
  between operations  0.85 us (2%)
    ppermute x11, starting transfers between devices, flip(): lax.ppermute(value, 'dp', [(i, i ^ mask) for i in range(lax.axis_size('dp...  9.46 us
    pallas_call x1, Pallas kernels, stage(): pl.pallas_call(functools.partial(stage_kernel, parts), in_specs=[FAR] * 5...  4.98 us
    ppermute x2, starting transfers between devices, across(): return lax.ppermute(value, ('dp', 'tensor'), pairs)  4.46 us
    pallas_call x5, Pallas kernels, project(): pl.pallas_call(functools.partial(project_kernel, flipped, low, min(width...  4.3 us
    pallas_call x1, Pallas kernels, spread(): pl.pallas_call(functools.partial(spread_kernel, chunk), in_specs=[WHOLE]...  3.18 us
    ppermute x2, starting transfers between devices, two_panels(): lax.ppermute(w, 'tensor', SWAP)  3.11 us
    pallas_call x3, Pallas kernels, gradient(): pl.pallas_call(functools.partial(gradient_kernel, scale, places, jobs), i...  2.42 us
    ppermute x1, waiting for transfers between devices, two_panels(): parts_got = lax.ppermute(parts_send, 'tensor', SWAP)  2.28 us
  transfers between devices with their start and end apart: 17, of which 4 were waited for; matrix products, arithmetic and copies ran while one was open for 0% of the time, Pallas kernels for 33%

profile of v9, /device:TPU:0, one launch (start us, length us, event | category | flops | bytes accessed | tf_op | source)
XLA Modules:
  0.0 40.5 jit_solution(6562565306666573784)
XLA Ops:
  0.6 1.1 %pick.1 = (bf16[24,4096]{1,0:T(8,128)(2,1)S(1)}, bf16[24,2048]{1,0:T(8,128)(2,1)S(1)}, bf16[24,2048]{1,0:T(8,128)(2,1)S(1)}) custom-call(bf16[24,16384]{1,0:T(8,128)(2,1)} %refs_0_.1, bf16[24,16384]{1,0:T(8,128)(2,1)} %refs_2_.1), custom_call_target="tpu_custom_call" | custom-call | flops 1 | bytes 1 | tf_op jit(solution)/shard_map/pick/pallas_call | solution.py:412
  1.7 3.0 %collective-permute-start.1 = (bf16[24,4096]{1,0:T(8,128)(2,1)S(1)}, bf16[24,4096]{1,0:T(8,128)(2,1)S(1)}, u32[]{:S(2)}, u32[]{:S(2)}) collective-permute-start(bf16[24,4096]{1,0:T(8,128)(2,1)S(1)} %get-tuple-element.35.refs_4_), channel_id=1, source_target_pairs={{0,1},{1,0},{2,3},{3,2},{4,5},{5,4},{6,7},{7,6},{8,9},{9,8},{10,11... | collective-permute-start | bytes 589832 | tf_op jit(solution)/shard_map/ppermute | solution.py:452
  4.8 0.1 collective-permute-start
  4.8 0.8 %collective-permute-start.2 = (bf16[24,2048]{1,0:T(8,128)(2,1)S(1)}, bf16[24,2048]{1,0:T(8,128)(2,1)S(1)}, u32[]{:S(2)}, u32[]{:S(2)}) collective-permute-start(bf16[24,2048]{1,0:T(8,128)(2,1)S(1)} %get-tuple-element.37.refs_6_), channel_id=1, source_target_pairs={{0,3},{1,2},{2,1},{3,0},{4,7},{5,6},{6,5},{7,4},{8,11},{9,10},{10,... | collective-permute-start | bytes 294920 | tf_op jit(solution)/shard_map/ppermute | solution.py:147
  5.7 5.0 %stage.1 = (bf16[24,8192]{1,0:T(8,128)(2,1)S(1)}, bf16[384,8192]{1,0:T(8,128)(2,1)S(1)}, bf16[24,8192]{1,0:T(8,128)(2,1)S(1)}, bf16[384,8192]{1,0:T(8,128)(2,1)S(1)}, f32[8,128]{1,0:T(8,128)S(1)}) custom-call(s32[2]{0:T(128)} %rank.1, bf16[24,16384]{1,0:T(8,128)(2,1)} %refs_0_.1, bf16[384,8192]{1,0:T(8,128)(2,1)} %refs_1_.1, bf16[24,16384]{1,0:T(8,128)(2,1)} %refs_2_.1, ...), custom_call_target="tpu_custom_call" | custom-call | flops 1 | bytes 1 | tf_op jit(solution)/shard_map/stage/pallas_call | solution.py:130
  10.7 1.3 %collective-permute-start.4 = (bf16[24,4096]{1,0:T(8,128)(2,1)S(1)}, bf16[24,4096]{1,0:T(8,128)(2,1)S(1)}, u32[]{:S(2)}, u32[]{:S(2)}) collective-permute-start(bf16[24,4096]{1,0:T(8,128)(2,1)S(1)} %collective-permute-done.1.refs_1_), channel_id=1, source_target_pairs={{0,2},{2,0},{4,6},{6,4},{8,10},{10,8},{12,14},{14,12},{16,18},{18,... | collective-permute-start | bytes 589832 | tf_op jit(solution)/shard_map/ppermute | solution.py:93
  12.0 1.0 %project.5.refs_3_ = f32[64,384]{1,0:T(8,128)S(1)} custom-call(bf16[24,8192]{1,0:T(8,128)(2,1)S(1)} %get-tuple-element.40.refs_0_, bf16[24,4096]{1,0:T(8,128)(2,1)S(1)} %collective-permute-done.1.refs_1_, bf16[384,8192]{1,0:T(8,128)(2,1)S(1)} %get-tuple-element.42.refs_2_.refs_3_.refs_4_.refs_6_.cotangent), custom_call_target="tpu_custom_call" | custom-call | flops 1 | bytes 1 | tf_op jit(solution)/shard_map/project/pallas_call | solution.py:201
  13.0 0.6 %project.6.refs_3_ = f32[64,384]{1,0:T(8,128)S(1)} custom-call(bf16[24,8192]{1,0:T(8,128)(2,1)S(1)} %get-tuple-element.39.refs_0_.own, bf16[24,2048]{1,0:T(8,128)(2,1)S(1)} %collective-permute-done.refs_1_, bf16[384,8192]{1,0:T(8,128)(2,1)S(1)} %get-tuple-element.44.refs_2_.tokens, ...), custom_call_target="tpu_custom_call" | custom-call | flops 1 | bytes 1 | tf_op jit(solution)/shard_map/project/pallas_call | solution.py:201
  13.7 0.1 collective-permute-start.3
  13.8 0.6 %project.7.refs_4_.refs_3_ = f32[64,384]{1,0:T(8,128)S(1)} custom-call(bf16[24,8192]{1,0:T(8,128)(2,1)S(1)} %get-tuple-element.39.refs_0_.own, bf16[24,2048]{1,0:T(8,128)(2,1)S(1)} %collective-permute-done.2.refs_1_, bf16[384,8192]{1,0:T(8,128)(2,1)S(1)} %get-tuple-element.44.refs_2_.tokens, f32[64,384]{1,0:T(8,128)S(1)} %project.6.refs_3_, ...), custom_call_target="tpu_custom_call" | custom-call | flops 1 | bytes 1 | tf_op jit(solution)/shard_map/project/pallas_call | solution.py:201
  14.4 1.0 %project.8.refs_5_ = f32[64,384]{1,0:T(8,128)S(1)} custom-call(bf16[24,8192]{1,0:T(8,128)(2,1)S(1)} %get-tuple-element.40.refs_0_, bf16[24,4096]{1,0:T(8,128)(2,1)S(1)} %collective-permute-done.4.refs_1_, bf16[384,8192]{1,0:T(8,128)(2,1)S(1)} %get-tuple-element.42.refs_2_.refs_3_.refs_4_.refs_6_.cotangent, f32[64,384]{1,0:T(8,128)S(1)} %project.5.refs_3_, ...), custom_call_target="tpu_custom_call" | custom-call | flops 1 | bytes 1 | tf_op jit(solution)/shard_map/project/pallas_call | solution.py:201
  15.4 1.0 %project.9 = (f32[56,384]{1,0:T(8,128)S(1)}, bf16[56,384]{1,0:T(8,128)(2,1)S(1)}) custom-call(bf16[24,8192]{1,0:T(8,128)(2,1)S(1)} %get-tuple-element.39.refs_0_.own, bf16[24,4096]{1,0:T(8,128)(2,1)S(1)} %collective-permute-done.3.refs_1_.theirs, bf16[384,8192]{1,0:T(8,128)(2,1)S(1)} %get-tuple-element.44.refs_2_.tokens, ...), custom_call_target="tpu_custom_call" | custom-call | flops 1 | bytes 1 | tf_op jit(solution)/shard_map/project/pallas_call | solution.py:201
  16.5 1.8 %collective-permute-start.5 = (bf16[56,384]{1,0:T(8,128)(2,1)S(1)}, bf16[56,384]{1,0:T(8,128)(2,1)S(1)}, u32[]{:S(2)}, u32[]{:S(2)}) collective-permute-start(bf16[56,384]{1,0:T(8,128)(2,1)S(1)} %get-tuple-element.47), channel_id=1, source_target_pairs={{0,1},{1,0},{2,3},{3,2},{4,5},{5,4},{6,7},{7,6},{8,9},{9,8},{10,11... | collective-permute-start | bytes 129032 | tf_op jit(solution)/shard_map/ppermute | solution.py:472
  18.3 2.3 %collective-permute-done.5.got = bf16[56,384]{1,0:T(8,128)(2,1)S(1)} collective-permute-done((bf16[56,384]{1,0:T(8,128)(2,1)S(1)}, bf16[56,384]{1,0:T(8,128)(2,1)S(1)}, u32[]{:S(2)}, u32[]{:S(2)}) %collective-permute-start.5) | collective-permute-done | bytes 43040 | tf_op jit(solution)/shard_map/ppermute | solution.py:472
  20.6 0.6 %gradient.3.refs_0_ = bf16[4,56,512]{2,1,0:T(8,128)(2,1)S(1)} custom-call(f32[56,384]{1,0:T(8,128)S(1)} %get-tuple-element.46.parts, bf16[56,384]{1,0:T(8,128)(2,1)S(1)} %collective-permute-done.5.got, bf16[384,8192]{1,0:T(8,128)(2,1)S(1)} %get-tuple-element.44.refs_2_.tokens, bf16[384,8192]{1,0:T(8,128)(2,1)S(1)} %get-tuple-element.42.refs_2_.refs_3_.refs_4_.refs_6_.cotangent), custom_call_target="tpu_custom_call" | custom-call | flops 1 | bytes 1 | tf_op jit(solution)/shard_map/gradient/pallas_call | solution.py:264
  21.3 1.2 %gradient.4 = (f32[4,56,512]{2,1,0:T(8,128)S(1)}, bf16[4,56,512]{2,1,0:T(8,128)(2,1)S(1)}) custom-call(f32[56,384]{1,0:T(8,128)S(1)} %get-tuple-element.46.parts, bf16[56,384]{1,0:T(8,128)(2,1)S(1)} %collective-permute-done.5.got, bf16[384,8192]{1,0:T(8,128)(2,1)S(1)} %get-tuple-element.44.refs_2_.tokens, ...), custom_call_target="tpu_custom_call" | custom-call | flops 1 | bytes 1 | tf_op jit(solution)/shard_map/gradient/pallas_call | solution.py:264
  22.4 0.5 %collective-permute-start.7 = (bf16[4,56,512]{2,1,0:T(8,128)(2,1)S(1)}, bf16[4,56,512]{2,1,0:T(8,128)(2,1)S(1)}, u32[]{:S(2)}, u32[]{:S(2)}) collective-permute-start(bf16[4,56,512]{2,1,0:T(8,128)(2,1)S(1)} %get-tuple-element.48.refs_0_), channel_id=1, source_target_pairs={{0,2},{2,0},{4,6},{6,4},{8,10},{10,8},{12,14},{14,12},{16,18},{18,... | collective-permute-start | bytes 688136 | tf_op jit(solution)/shard_map/ppermute | solution.py:93
  23.0 2.8 %collective-permute-start.11 = (bf16[56,512]{1,0:T(8,128)(2,1)S(1)}, bf16[56,512]{1,0:T(8,128)(2,1)S(1)}, u32[]{:S(2)}, u32[]{:S(2)}) collective-permute-start(bf16[56,512]{1,0:T(8,128)(2,1)S(1)} %get-tuple-element.58), channel_id=1, source_target_pairs={{0,12},{2,14},{4,8},{6,10},{8,4},{10,6},{12,0},{14,2},{16,28},{18,... | collective-permute-start | bytes 172040 | tf_op jit(solution)/shard_map/ppermute | solution.py:93
  25.8 0.5 %collective-permute-start.13 = (bf16[56,512]{1,0:T(8,128)(2,1)S(1)}, bf16[56,512]{1,0:T(8,128)(2,1)S(1)}, u32[]{:S(2)}, u32[]{:S(2)}) collective-permute-start(bf16[56,512]{1,0:T(8,128)(2,1)S(1)} %get-tuple-element.59), channel_id=1, source_target_pairs={{0,8},{2,10},{4,12},{6,14},{8,0},{10,2},{12,4},{14,6},{16,24},{18,... | collective-permute-start | bytes 172040 | tf_op jit(solution)/shard_map/ppermute | solution.py:93
  26.3 0.3 collective-permute-start.12
  26.6 0.6 %gradient.5.keep = f32[4,56,512]{2,1,0:T(8,128)S(1)} custom-call(f32[56,384]{1,0:T(8,128)S(1)} %get-tuple-element.46.parts, bf16[56,384]{1,0:T(8,128)(2,1)S(1)} %collective-permute-done.5.got, bf16[384,8192]{1,0:T(8,128)(2,1)S(1)} %get-tuple-element.44.refs_2_.tokens, bf16[384,8192]{1,0:T(8,128)(2,1)S(1)} %get-tuple-element.42.refs_2_.refs_3_.refs_4_.refs_6_.cotangent, ...), custom_call_target="tpu_custom_call" | custom-call | flops 1 | bytes 1 | tf_op jit(solution)/shard_map/gradient/pallas_call | solution.py:264
  27.2 0.1 quarter.3
  27.3 2.8 %collective-permute-start.8 = (bf16[56,512]{1,0:T(8,128)(2,1)S(1)}, bf16[56,512]{1,0:T(8,128)(2,1)S(1)}, u32[]{:S(2)}, u32[]{:S(2)}) collective-permute-start(bf16[56,512]{1,0:T(8,128)(2,1)S(1)} %get-tuple-element.52), channel_id=1, source_target_pairs={{0,12},{2,14},{4,8},{6,10},{8,4},{10,6},{12,0},{14,2},{16,28},{18,... | collective-permute-start | bytes 172040 | tf_op jit(solution)/shard_map/ppermute | solution.py:93
  30.1 0.5 %collective-permute-start.9 = (bf16[56,512]{1,0:T(8,128)(2,1)S(1)}, bf16[56,512]{1,0:T(8,128)(2,1)S(1)}, u32[]{:S(2)}, u32[]{:S(2)}) collective-permute-start(bf16[56,512]{1,0:T(8,128)(2,1)S(1)} %get-tuple-element.53), channel_id=1, source_target_pairs={{0,4},{2,6},{4,0},{6,2},{8,12},{10,14},{12,8},{14,10},{16,20},{18,... | collective-permute-start | bytes 172040 | tf_op jit(solution)/shard_map/ppermute | solution.py:93
  30.6 0.2 collective-permute-start.10
  30.9 0.2 collective-permute-done.12.refs_1_
  31.1 3.6 %collective-permute-start.14 = (bf16[2,24,512]{2,1,0:T(8,128)(2,1)S(1)}, bf16[2,24,512]{2,1,0:T(8,128)(2,1)S(1)}, u32[]{:S(2)}, u32[]{:S(2)}) collective-permute-start(bf16[2,24,512]{2,1,0:T(8,128)(2,1)S(1)} %get-tuple-element.60), channel_id=1, source_target_pairs={{0,17},{1,16},{2,19},{3,18},{4,21},{5,20},{6,23},{7,22},{8,25},{9,... | collective-permute-start | bytes 147464 | tf_op jit(solution)/shard_map/ppermute | solution.py:147
  34.8 0.3 collective-permute-start.15
  35.1 0.1 collective-permute-done.10.refs_2_
  35.2 1.2 %collective-permute-start.16 = (bf16[2,24,512]{2,1,0:T(8,128)(2,1)S(1)}, bf16[2,24,512]{2,1,0:T(8,128)(2,1)S(1)}, u32[]{:S(2)}, u32[]{:S(2)}) collective-permute-start(bf16[2,24,512]{2,1,0:T(8,128)(2,1)S(1)} %get-tuple-element.55.after), channel_id=1, source_target_pairs={{0,1},{1,0},{2,3},{3,2},{4,5},{5,4},{6,7},{7,6},{8,9},{9,8},{10,11... | collective-permute-start | bytes 147464 | tf_op jit(solution)/shard_map/ppermute | solution.py:487
  36.5 3.2 %spread.1 = bf16[384,8192]{1,0:T(8,128)(2,1)} custom-call(f32[8,128]{1,0:T(8,128)S(1)} %get-tuple-element.38.refs_4_.full, f32[56,384]{1,0:T(8,128)S(1)} %get-tuple-element.46.parts, bf16[56,384]{1,0:T(8,128)(2,1)S(1)} %collective-permute-done.5.got, bf16[24,8192]{1,0:T(8,128)(2,1)S(1)} %get-tuple-element.39.refs_0_.own, ...), custom_call_target="tpu_custom_call" | custom-call | flops 10000000000 | bytes 100000000 | tf_op jit(solution)/shard_map/spread/pallas_call | solution.py:305
  39.8 0.7 %place.1 = (f32[24,2,1,512]{3,2,1,0:T(1,128)}, f32[24,2,1,512]{3,2,1,0:T(1,128)}) custom-call(f32[2,24,512]{2,1,0:T(8,128)S(1)} %gather.3.held, f32[2,24,512]{2,1,0:T(8,128)S(1)} %gather.2.far, bf16[2,24,512]{2,1,0:T(8,128)(2,1)S(1)} %collective-permute-done.16.got), custom_call_target="tpu_custom_call" | custom-call | flops 1 | bytes 1 | tf_op jit(solution)/shard_map/place/pallas_call | solution.py:378
  (22 shorter events, 0.4 us)
Async XLA Ops:
  1.7 8.9 %collective-permute-start.1 = (bf16[24,4096]{1,0:T(8,128)(2,1)S(1)}, bf16[24,4096]{1,0:T(8,128)(2,1)S(1)}, u32[]{:S(2)}, u32[]{:S(2)}) collective-permute-start(bf16[24,4096]{1,0:T(8,128)(2,1)S(1)} %get-tuple-element.35.refs_4_), channel_id=1, source_target_pairs={{0,1},{1,0},{2,3},{3,2},{4,5},{5,4},{6,7},{7,6},{8,9},{9,8},{10,11... | collective-permute-start | bytes 589832 | tf_op jit(solution)/shard_map/ppermute | solution.py:452
  4.8 8.2 %collective-permute-start = (bf16[24,2048]{1,0:T(8,128)(2,1)S(1)}, bf16[24,2048]{1,0:T(8,128)(2,1)S(1)}, u32[]{:S(2)}, u32[]{:S(2)}) collective-permute-start(bf16[24,2048]{1,0:T(8,128)(2,1)S(1)} %get-tuple-element.36.refs_5_), channel_id=1, source_target_pairs={{0,1},{1,0},{2,3},{3,2},{4,5},{5,4},{6,7},{7,6},{8,9},{9,8},{10,11... | collective-permute-start | bytes 294920 | tf_op jit(solution)/shard_map/ppermute | solution.py:452
  4.8 8.8 %collective-permute-start.2 = (bf16[24,2048]{1,0:T(8,128)(2,1)S(1)}, bf16[24,2048]{1,0:T(8,128)(2,1)S(1)}, u32[]{:S(2)}, u32[]{:S(2)}) collective-permute-start(bf16[24,2048]{1,0:T(8,128)(2,1)S(1)} %get-tuple-element.37.refs_6_), channel_id=1, source_target_pairs={{0,3},{1,2},{2,1},{3,0},{4,7},{5,6},{6,5},{7,4},{8,11},{9,10},{10,... | collective-permute-start | bytes 294920 | tf_op jit(solution)/shard_map/ppermute | solution.py:147
  10.7 3.7 %collective-permute-start.4 = (bf16[24,4096]{1,0:T(8,128)(2,1)S(1)}, bf16[24,4096]{1,0:T(8,128)(2,1)S(1)}, u32[]{:S(2)}, u32[]{:S(2)}) collective-permute-start(bf16[24,4096]{1,0:T(8,128)(2,1)S(1)} %collective-permute-done.1.refs_1_), channel_id=1, source_target_pairs={{0,2},{2,0},{4,6},{6,4},{8,10},{10,8},{12,14},{14,12},{16,18},{18,... | collective-permute-start | bytes 589832 | tf_op jit(solution)/shard_map/ppermute | solution.py:93
  13.7 1.8 %collective-permute-start.3 = (bf16[24,4096]{1,0:T(8,128)(2,1)S(1)}, bf16[24,4096]{1,0:T(8,128)(2,1)S(1)}, u32[]{:S(2)}, u32[]{:S(2)}) collective-permute-start(bf16[24,4096]{1,0:T(8,128)(2,1)S(1)} %constant_dynamic-update-slice_fusion.mine), channel_id=1, source_target_pairs={{0,2},{2,0},{4,6},{6,4},{8,10},{10,8},{12,14},{14,12},{16,18},{18,... | collective-permute-start | bytes 589832 | tf_op jit(solution)/shard_map/ppermute | solution.py:93
  16.5 4.1 %collective-permute-start.5 = (bf16[56,384]{1,0:T(8,128)(2,1)S(1)}, bf16[56,384]{1,0:T(8,128)(2,1)S(1)}, u32[]{:S(2)}, u32[]{:S(2)}) collective-permute-start(bf16[56,384]{1,0:T(8,128)(2,1)S(1)} %get-tuple-element.47), channel_id=1, source_target_pairs={{0,1},{1,0},{2,3},{3,2},{4,5},{5,4},{6,7},{7,6},{8,9},{9,8},{10,11... | collective-permute-start | bytes 129032 | tf_op jit(solution)/shard_map/ppermute | solution.py:472
  21.2 1.8 %collective-permute-start.6 = (bf16[4,56,512]{2,1,0:T(8,128)(2,1)S(1)}, bf16[4,56,512]{2,1,0:T(8,128)(2,1)S(1)}, u32[]{:S(2)}, u32[]{:S(2)}) collective-permute-start(bf16[4,56,512]{2,1,0:T(8,128)(2,1)S(1)} %gradient.3.refs_0_), channel_id=1, source_target_pairs={{0,2},{2,0},{4,6},{6,4},{8,10},{10,8},{12,14},{14,12},{16,18},{18,... | collective-permute-start | bytes 688136 | tf_op jit(solution)/shard_map/ppermute | solution.py:93
  22.4 4.8 %collective-permute-start.7 = (bf16[4,56,512]{2,1,0:T(8,128)(2,1)S(1)}, bf16[4,56,512]{2,1,0:T(8,128)(2,1)S(1)}, u32[]{:S(2)}, u32[]{:S(2)}) collective-permute-start(bf16[4,56,512]{2,1,0:T(8,128)(2,1)S(1)} %get-tuple-element.48.refs_0_), channel_id=1, source_target_pairs={{0,2},{2,0},{4,6},{6,4},{8,10},{10,8},{12,14},{14,12},{16,18},{18,... | collective-permute-start | bytes 688136 | tf_op jit(solution)/shard_map/ppermute | solution.py:93
  23.0 7.6 %collective-permute-start.11 = (bf16[56,512]{1,0:T(8,128)(2,1)S(1)}, bf16[56,512]{1,0:T(8,128)(2,1)S(1)}, u32[]{:S(2)}, u32[]{:S(2)}) collective-permute-start(bf16[56,512]{1,0:T(8,128)(2,1)S(1)} %get-tuple-element.58), channel_id=1, source_target_pairs={{0,12},{2,14},{4,8},{6,10},{8,4},{10,6},{12,0},{14,2},{16,28},{18,... | collective-permute-start | bytes 172040 | tf_op jit(solution)/shard_map/ppermute | solution.py:93
  25.8 5.0 %collective-permute-start.13 = (bf16[56,512]{1,0:T(8,128)(2,1)S(1)}, bf16[56,512]{1,0:T(8,128)(2,1)S(1)}, u32[]{:S(2)}, u32[]{:S(2)}) collective-permute-start(bf16[56,512]{1,0:T(8,128)(2,1)S(1)} %get-tuple-element.59), channel_id=1, source_target_pairs={{0,8},{2,10},{4,12},{6,14},{8,0},{10,2},{12,4},{14,6},{16,24},{18,... | collective-permute-start | bytes 172040 | tf_op jit(solution)/shard_map/ppermute | solution.py:93
  26.3 4.8 %collective-permute-start.12 = (bf16[56,512]{1,0:T(8,128)(2,1)S(1)}, bf16[56,512]{1,0:T(8,128)(2,1)S(1)}, u32[]{:S(2)}, u32[]{:S(2)}) collective-permute-start(bf16[56,512]{1,0:T(8,128)(2,1)S(1)} %get-tuple-element.50.refs_1_), channel_id=1, source_target_pairs={{0,4},{2,6},{4,0},{6,2},{8,12},{10,14},{12,8},{14,10},{16,20},{18,... | collective-permute-start | bytes 172040 | tf_op jit(solution)/shard_map/ppermute | solution.py:93
  27.3 7.8 %collective-permute-start.8 = (bf16[56,512]{1,0:T(8,128)(2,1)S(1)}, bf16[56,512]{1,0:T(8,128)(2,1)S(1)}, u32[]{:S(2)}, u32[]{:S(2)}) collective-permute-start(bf16[56,512]{1,0:T(8,128)(2,1)S(1)} %get-tuple-element.52), channel_id=1, source_target_pairs={{0,12},{2,14},{4,8},{6,10},{8,4},{10,6},{12,0},{14,2},{16,28},{18,... | collective-permute-start | bytes 172040 | tf_op jit(solution)/shard_map/ppermute | solution.py:93
  30.1 5.0 %collective-permute-start.9 = (bf16[56,512]{1,0:T(8,128)(2,1)S(1)}, bf16[56,512]{1,0:T(8,128)(2,1)S(1)}, u32[]{:S(2)}, u32[]{:S(2)}) collective-permute-start(bf16[56,512]{1,0:T(8,128)(2,1)S(1)} %get-tuple-element.53), channel_id=1, source_target_pairs={{0,4},{2,6},{4,0},{6,2},{8,12},{10,14},{12,8},{14,10},{16,20},{18,... | collective-permute-start | bytes 172040 | tf_op jit(solution)/shard_map/ppermute | solution.py:93
  30.6 4.5 %collective-permute-start.10 = (bf16[56,512]{1,0:T(8,128)(2,1)S(1)}, bf16[56,512]{1,0:T(8,128)(2,1)S(1)}, u32[]{:S(2)}, u32[]{:S(2)}) collective-permute-start(bf16[56,512]{1,0:T(8,128)(2,1)S(1)} %get-tuple-element.54), channel_id=1, source_target_pairs={{0,8},{2,10},{4,12},{6,14},{8,0},{10,2},{12,4},{14,6},{16,24},{18,... | collective-permute-start | bytes 172040 | tf_op jit(solution)/shard_map/ppermute | solution.py:93
  31.1 8.5 %collective-permute-start.14 = (bf16[2,24,512]{2,1,0:T(8,128)(2,1)S(1)}, bf16[2,24,512]{2,1,0:T(8,128)(2,1)S(1)}, u32[]{:S(2)}, u32[]{:S(2)}) collective-permute-start(bf16[2,24,512]{2,1,0:T(8,128)(2,1)S(1)} %get-tuple-element.60), channel_id=1, source_target_pairs={{0,17},{1,16},{2,19},{3,18},{4,21},{5,20},{6,23},{7,22},{8,25},{9,... | collective-permute-start | bytes 147464 | tf_op jit(solution)/shard_map/ppermute | solution.py:147
  34.8 5.0 %collective-permute-start.15 = (bf16[2,24,512]{2,1,0:T(8,128)(2,1)S(1)}, bf16[2,24,512]{2,1,0:T(8,128)(2,1)S(1)}, u32[]{:S(2)}, u32[]{:S(2)}) collective-permute-start(bf16[2,24,512]{2,1,0:T(8,128)(2,1)S(1)} %get-tuple-element.61), channel_id=1, source_target_pairs={{0,16},{2,18},{4,20},{6,22},{8,24},{10,26},{12,28},{14,30},{16,0},... | collective-permute-start | bytes 147464 | tf_op jit(solution)/shard_map/ppermute | solution.py:93
  35.2 4.5 %collective-permute-start.16 = (bf16[2,24,512]{2,1,0:T(8,128)(2,1)S(1)}, bf16[2,24,512]{2,1,0:T(8,128)(2,1)S(1)}, u32[]{:S(2)}, u32[]{:S(2)}) collective-permute-start(bf16[2,24,512]{2,1,0:T(8,128)(2,1)S(1)} %get-tuple-element.55.after), channel_id=1, source_target_pairs={{0,1},{1,0},{2,3},{3,2},{4,5},{5,4},{6,7},{7,6},{8,9},{9,8},{10,11... | collective-permute-start | bytes 147464 | tf_op jit(solution)/shard_map/ppermute | solution.py:487

commit v10 on v9

--- a/solution.py
+++ b/solution.py
@@ -156,13 +156,11 @@
     return jnp.concatenate([own, gap, piece, gap], axis=0)
 
 
-def project_kernel(flipped, low_column, chunk, given, *refs):
-    own, piece, acts = refs[:3]
-    others, out = refs[3 : 3 + given], refs[-1 if given < 3 else -2]
-    slots, width = piece.shape
+def add_up(total, own, piece, acts, flipped, low_column):
+    width = piece.shape[1]
+    chunk = min(width // 2, 512)
     core = lax.axis_index("dp") % 2
     start = (1 - core if flipped else core) * (own.shape[1] // 2) + low_column
-    total = others[0][...] if others else None
     turned = None
     for n, low in enumerate(range(0, width, chunk)):
         column = pl.ds(pl.multiple_of(start + low, chunk), chunk)
@@ -177,7 +175,34 @@
                 rows, acts[:, column], (((1,), (1,)), ((), ())), preferred_element_type=jnp.float32
             )
             total = part if total is None else total + part
-    total += turned.T
+    return total + turned.T
+
+
+def project_two_kernel(low, *refs):
+    first, second, (first_out, second_out) = refs[:4], refs[4:8], refs[-2:]
+    first_out[...] = add_up(first[3][...], *first[:3], False, low)
+    second_out[...] = add_up(second[3][...], *second[:3], True, 0)
+
+
+def project_two(first, low, second, held):
+    shape = pltpu.VMEM(first[3].shape, jnp.float32)
+    operands = (*first, *second, *held)
+    return pl.pallas_call(
+        functools.partial(project_two_kernel, low),
+        in_specs=[WHOLE] * len(operands),
+        out_specs=[WHOLE] * 2,
+        out_shape=[shape, shape],
+        compiler_params=PARAMS,
+        cost_estimate=SMALL,
+        name="project_two",
+    )(*map(near, operands))
+
+
+def project_kernel(flipped, low, given, *refs):
+    own, piece, acts = refs[:3]
+    others, out = refs[3 : 3 + given], refs[-1 if given < 3 else -2]
+    slots = piece.shape[0]
+    total = add_up(others[0][...] if others else None, own, piece, acts, flipped, low)
     if given < 3:
         out[...] = total
         return
@@ -193,13 +218,13 @@
 
 
 def project(own, piece, acts, flipped, others, held, low=0):
-    slots, width = piece.shape
+    slots = piece.shape[0]
     tokens = acts.shape[0]
     last = len(others) == 3
     shape = (2 * slots + (PAD if last else 2 * PAD), tokens)
     kinds = (jnp.float32, jnp.bfloat16) if last else (jnp.float32,)
     return pl.pallas_call(
-        functools.partial(project_kernel, flipped, low, min(width // 2, 512), len(others)),
+        functools.partial(project_kernel, flipped, low, len(others)),
         in_specs=[WHOLE] * (3 + len(others) + len(held)),
         out_specs=[WHOLE] * len(kinds),
         out_shape=[pltpu.VMEM(shape, kind) for kind in kinds],
@@ -462,10 +487,10 @@
     left_second = after_all(left_second, hidden)
     left_mine = jnp.concatenate([left_first, left_second], axis=1)
     left_theirs = flip(left_mine, 0)
-    (hidden,) = project(
-        left_own, left_second, tokens, False, (hidden,), (cotangent,), left_first.shape[1]
-    )
-    (back,) = project(right_own, right_theirs, cotangent, True, (back,), (hidden,))
+    hidden, back = project_two(
+        (left_own, left_second, tokens, hidden), left_first.shape[1],
+        (right_own, right_theirs, cotangent, back), (),
+    )
     parts, parts_send = project(
         left_own, left_theirs, tokens, True, (hidden, full, back), (cotangent,)
     )

time: 40.6 us -> 40.5 us (level)
    pallas_call x5 -> x4, Pallas kernels: 4.3 us -> 4.16 us  [the longest x3 2.66 us: project(): pl.pallas_call(functools.partial(project_kernel, flipped, low, len(others...]
where the time goes in v10:
time: 40.5 us; the launch traced here: 40.3 us
  starting transfers between devices  20.1 us (50%)
  Pallas kernels  16.8 us (41%)
  waiting for transfers between devices  2.66 us (7%)
  between operations  0.83 us (2%)
    ppermute x11, starting transfers between devices, flip(): lax.ppermute(value, 'dp', [(i, i ^ mask) for i in range(lax.axis_size('dp...  9.45 us
    pallas_call x1, Pallas kernels, stage(): pl.pallas_call(functools.partial(stage_kernel, parts), in_specs=[FAR] * 5...  4.98 us
    ppermute x2, starting transfers between devices, across(): return lax.ppermute(value, ('dp', 'tensor'), pairs)  4.47 us
    pallas_call x1, Pallas kernels, spread(): pl.pallas_call(functools.partial(spread_kernel, chunk), in_specs=[WHOLE]...  3.18 us
    ppermute x2, starting transfers between devices, two_panels(): lax.ppermute(w, 'tensor', SWAP)  3.11 us
    pallas_call x3, Pallas kernels, project(): pl.pallas_call(functools.partial(project_kernel, flipped, low, len(others...  2.66 us
    pallas_call x3, Pallas kernels, gradient(): pl.pallas_call(functools.partial(gradient_kernel, scale, places, jobs), i...  2.41 us
    ppermute x1, waiting for transfers between devices, two_panels(): parts_got = lax.ppermute(parts_send, 'tensor', SWAP)  2.28 us
  transfers between devices with their start and end apart: 17, of which 4 were waited for; matrix products, arithmetic and copies ran while one was open for 0% of the time, Pallas kernels for 33%

profile of v10, /device:TPU:0, one launch (start us, length us, event | category | flops | bytes accessed | tf_op | source)
XLA Modules:
  0.0 40.3 jit_solution(4802327212217752722)
XLA Ops:
  0.6 1.1 %pick.1 = (bf16[24,4096]{1,0:T(8,128)(2,1)S(1)}, bf16[24,2048]{1,0:T(8,128)(2,1)S(1)}, bf16[24,2048]{1,0:T(8,128)(2,1)S(1)}) custom-call(bf16[24,16384]{1,0:T(8,128)(2,1)} %refs_0_.1, bf16[24,16384]{1,0:T(8,128)(2,1)} %refs_2_.1), custom_call_target="tpu_custom_call" | custom-call | flops 1 | bytes 1 | tf_op jit(solution)/shard_map/pick/pallas_call | solution.py:437
  1.7 3.0 %collective-permute-start.1 = (bf16[24,4096]{1,0:T(8,128)(2,1)S(1)}, bf16[24,4096]{1,0:T(8,128)(2,1)S(1)}, u32[]{:S(2)}, u32[]{:S(2)}) collective-permute-start(bf16[24,4096]{1,0:T(8,128)(2,1)S(1)} %get-tuple-element.37.refs_4_), channel_id=1, source_target_pairs={{0,1},{1,0},{2,3},{3,2},{4,5},{5,4},{6,7},{7,6},{8,9},{9,8},{10,11... | collective-permute-start | bytes 589832 | tf_op jit(solution)/shard_map/ppermute | solution.py:477
  4.8 0.1 collective-permute-start
  4.8 0.8 %collective-permute-start.2 = (bf16[24,2048]{1,0:T(8,128)(2,1)S(1)}, bf16[24,2048]{1,0:T(8,128)(2,1)S(1)}, u32[]{:S(2)}, u32[]{:S(2)}) collective-permute-start(bf16[24,2048]{1,0:T(8,128)(2,1)S(1)} %get-tuple-element.39.refs_6_), channel_id=1, source_target_pairs={{0,3},{1,2},{2,1},{3,0},{4,7},{5,6},{6,5},{7,4},{8,11},{9,10},{10,... | collective-permute-start | bytes 294920 | tf_op jit(solution)/shard_map/ppermute | solution.py:147
  5.7 5.0 %stage.1 = (bf16[24,8192]{1,0:T(8,128)(2,1)S(1)}, bf16[384,8192]{1,0:T(8,128)(2,1)S(1)}, bf16[24,8192]{1,0:T(8,128)(2,1)S(1)}, bf16[384,8192]{1,0:T(8,128)(2,1)S(1)}, f32[8,128]{1,0:T(8,128)S(1)}) custom-call(s32[2]{0:T(128)} %rank.1, bf16[24,16384]{1,0:T(8,128)(2,1)} %refs_0_.1, bf16[384,8192]{1,0:T(8,128)(2,1)} %refs_1_.1, bf16[24,16384]{1,0:T(8,128)(2,1)} %refs_2_.1, ...), custom_call_target="tpu_custom_call" | custom-call | flops 1 | bytes 1 | tf_op jit(solution)/shard_map/stage/pallas_call | solution.py:130
  10.7 1.3 %collective-permute-start.4 = (bf16[24,4096]{1,0:T(8,128)(2,1)S(1)}, bf16[24,4096]{1,0:T(8,128)(2,1)S(1)}, u32[]{:S(2)}, u32[]{:S(2)}) collective-permute-start(bf16[24,4096]{1,0:T(8,128)(2,1)S(1)} %collective-permute-done.1.refs_1_), channel_id=1, source_target_pairs={{0,2},{2,0},{4,6},{6,4},{8,10},{10,8},{12,14},{14,12},{16,18},{18,... | collective-permute-start | bytes 589832 | tf_op jit(solution)/shard_map/ppermute | solution.py:93
  12.0 1.0 %project.3.refs_7_ = f32[64,384]{1,0:T(8,128)S(1)} custom-call(bf16[24,8192]{1,0:T(8,128)(2,1)S(1)} %get-tuple-element.42.refs_0_.refs_4_, bf16[24,4096]{1,0:T(8,128)(2,1)S(1)} %collective-permute-done.1.refs_1_, bf16[384,8192]{1,0:T(8,128)(2,1)S(1)} %get-tuple-element.44.refs_2_.refs_3_.refs_6_.cotangent), custom_call_target="tpu_custom_call" | custom-call | flops 1 | bytes 1 | tf_op jit(solution)/shard_map/project/pallas_call | solution.py:226
  13.0 0.6 %project.4.refs_3_ = f32[64,384]{1,0:T(8,128)S(1)} custom-call(bf16[24,8192]{1,0:T(8,128)(2,1)S(1)} %get-tuple-element.41.refs_0_.own, bf16[24,2048]{1,0:T(8,128)(2,1)S(1)} %collective-permute-done.refs_1_, bf16[384,8192]{1,0:T(8,128)(2,1)S(1)} %get-tuple-element.46.refs_2_.tokens, bf16[384,8192]{1,0:T(8,128)(2,1)S(1)} %get-tuple-element.44.refs_2_.refs_3_.refs_6_.cotangent), custom_call_target="tpu_custom_call" | custom-call | flops 1 | bytes 1 | tf_op jit(solution)/shard_map/project/pallas_call | solution.py:226
  13.7 0.1 collective-permute-start.3
  13.8 1.5 %project_two.1 = (f32[64,384]{1,0:T(8,128)S(1)}, f32[64,384]{1,0:T(8,128)S(1)}) custom-call(bf16[24,8192]{1,0:T(8,128)(2,1)S(1)} %get-tuple-element.41.refs_0_.own, bf16[24,2048]{1,0:T(8,128)(2,1)S(1)} %collective-permute-done.2.refs_1_, bf16[384,8192]{1,0:T(8,128)(2,1)S(1)} %get-tuple-element.46.refs_2_.tokens, f32[64,384]{1,0:T(8,128)S(1)} %project.4.refs_3_, ...), custom_call_target="tpu_custom_call" | custom-call | flops 1 | bytes 1 | tf_op jit(solution)/shard_map/project_two/pallas_call | solution.py:190
  15.3 1.0 %project.5 = (f32[56,384]{1,0:T(8,128)S(1)}, bf16[56,384]{1,0:T(8,128)(2,1)S(1)}) custom-call(bf16[24,8192]{1,0:T(8,128)(2,1)S(1)} %get-tuple-element.41.refs_0_.own, bf16[24,4096]{1,0:T(8,128)(2,1)S(1)} %collective-permute-done.3.refs_1_.theirs, bf16[384,8192]{1,0:T(8,128)(2,1)S(1)} %get-tuple-element.46.refs_2_.tokens, ...), custom_call_target="tpu_custom_call" | custom-call | flops 1 | bytes 1 | tf_op jit(solution)/shard_map/project/pallas_call | solution.py:226
  16.3 1.8 %collective-permute-start.5 = (bf16[56,384]{1,0:T(8,128)(2,1)S(1)}, bf16[56,384]{1,0:T(8,128)(2,1)S(1)}, u32[]{:S(2)}, u32[]{:S(2)}) collective-permute-start(bf16[56,384]{1,0:T(8,128)(2,1)S(1)} %get-tuple-element.51), channel_id=1, source_target_pairs={{0,1},{1,0},{2,3},{3,2},{4,5},{5,4},{6,7},{7,6},{8,9},{9,8},{10,11... | collective-permute-start | bytes 129032 | tf_op jit(solution)/shard_map/ppermute | solution.py:497
  18.1 2.3 %collective-permute-done.5.got = bf16[56,384]{1,0:T(8,128)(2,1)S(1)} collective-permute-done((bf16[56,384]{1,0:T(8,128)(2,1)S(1)}, bf16[56,384]{1,0:T(8,128)(2,1)S(1)}, u32[]{:S(2)}, u32[]{:S(2)}) %collective-permute-start.5) | collective-permute-done | bytes 43040 | tf_op jit(solution)/shard_map/ppermute | solution.py:497
  20.4 0.6 %gradient.3.refs_0_ = bf16[4,56,512]{2,1,0:T(8,128)(2,1)S(1)} custom-call(f32[56,384]{1,0:T(8,128)S(1)} %get-tuple-element.50.parts, bf16[56,384]{1,0:T(8,128)(2,1)S(1)} %collective-permute-done.5.got, bf16[384,8192]{1,0:T(8,128)(2,1)S(1)} %get-tuple-element.46.refs_2_.tokens, bf16[384,8192]{1,0:T(8,128)(2,1)S(1)} %get-tuple-element.44.refs_2_.refs_3_.refs_6_.cotangent), custom_call_target="tpu_custom_call" | custom-call | flops 1 | bytes 1 | tf_op jit(solution)/shard_map/gradient/pallas_call | solution.py:289
  21.0 0.1 collective-permute-start.6
  21.1 1.2 %gradient.4 = (f32[4,56,512]{2,1,0:T(8,128)S(1)}, bf16[4,56,512]{2,1,0:T(8,128)(2,1)S(1)}) custom-call(f32[56,384]{1,0:T(8,128)S(1)} %get-tuple-element.50.parts, bf16[56,384]{1,0:T(8,128)(2,1)S(1)} %collective-permute-done.5.got, bf16[384,8192]{1,0:T(8,128)(2,1)S(1)} %get-tuple-element.46.refs_2_.tokens, ...), custom_call_target="tpu_custom_call" | custom-call | flops 1 | bytes 1 | tf_op jit(solution)/shard_map/gradient/pallas_call | solution.py:289
  22.3 0.5 %collective-permute-start.7 = (bf16[4,56,512]{2,1,0:T(8,128)(2,1)S(1)}, bf16[4,56,512]{2,1,0:T(8,128)(2,1)S(1)}, u32[]{:S(2)}, u32[]{:S(2)}) collective-permute-start(bf16[4,56,512]{2,1,0:T(8,128)(2,1)S(1)} %get-tuple-element.52.refs_0_), channel_id=1, source_target_pairs={{0,2},{2,0},{4,6},{6,4},{8,10},{10,8},{12,14},{14,12},{16,18},{18,... | collective-permute-start | bytes 688136 | tf_op jit(solution)/shard_map/ppermute | solution.py:93
  22.9 2.8 %collective-permute-start.11 = (bf16[56,512]{1,0:T(8,128)(2,1)S(1)}, bf16[56,512]{1,0:T(8,128)(2,1)S(1)}, u32[]{:S(2)}, u32[]{:S(2)}) collective-permute-start(bf16[56,512]{1,0:T(8,128)(2,1)S(1)} %get-tuple-element.62), channel_id=1, source_target_pairs={{0,12},{2,14},{4,8},{6,10},{8,4},{10,6},{12,0},{14,2},{16,28},{18,... | collective-permute-start | bytes 172040 | tf_op jit(solution)/shard_map/ppermute | solution.py:93
  25.7 0.5 %collective-permute-start.13 = (bf16[56,512]{1,0:T(8,128)(2,1)S(1)}, bf16[56,512]{1,0:T(8,128)(2,1)S(1)}, u32[]{:S(2)}, u32[]{:S(2)}) collective-permute-start(bf16[56,512]{1,0:T(8,128)(2,1)S(1)} %get-tuple-element.63), channel_id=1, source_target_pairs={{0,8},{2,10},{4,12},{6,14},{8,0},{10,2},{12,4},{14,6},{16,24},{18,... | collective-permute-start | bytes 172040 | tf_op jit(solution)/shard_map/ppermute | solution.py:93
  26.1 0.3 collective-permute-start.12
  26.4 0.6 %gradient.5.keep = f32[4,56,512]{2,1,0:T(8,128)S(1)} custom-call(f32[56,384]{1,0:T(8,128)S(1)} %get-tuple-element.50.parts, bf16[56,384]{1,0:T(8,128)(2,1)S(1)} %collective-permute-done.5.got, bf16[384,8192]{1,0:T(8,128)(2,1)S(1)} %get-tuple-element.46.refs_2_.tokens, bf16[384,8192]{1,0:T(8,128)(2,1)S(1)} %get-tuple-element.44.refs_2_.refs_3_.refs_6_.cotangent, ...), custom_call_target="tpu_custom_call" | custom-call | flops 1 | bytes 1 | tf_op jit(solution)/shard_map/gradient/pallas_call | solution.py:289
  27.1 0.1 quarter.3
  27.2 2.8 %collective-permute-start.8 = (bf16[56,512]{1,0:T(8,128)(2,1)S(1)}, bf16[56,512]{1,0:T(8,128)(2,1)S(1)}, u32[]{:S(2)}, u32[]{:S(2)}) collective-permute-start(bf16[56,512]{1,0:T(8,128)(2,1)S(1)} %get-tuple-element.56), channel_id=1, source_target_pairs={{0,12},{2,14},{4,8},{6,10},{8,4},{10,6},{12,0},{14,2},{16,28},{18,... | collective-permute-start | bytes 172040 | tf_op jit(solution)/shard_map/ppermute | solution.py:93
  29.9 0.5 %collective-permute-start.9 = (bf16[56,512]{1,0:T(8,128)(2,1)S(1)}, bf16[56,512]{1,0:T(8,128)(2,1)S(1)}, u32[]{:S(2)}, u32[]{:S(2)}) collective-permute-start(bf16[56,512]{1,0:T(8,128)(2,1)S(1)} %get-tuple-element.57), channel_id=1, source_target_pairs={{0,4},{2,6},{4,0},{6,2},{8,12},{10,14},{12,8},{14,10},{16,20},{18,... | collective-permute-start | bytes 172040 | tf_op jit(solution)/shard_map/ppermute | solution.py:93
  30.5 0.2 collective-permute-start.10
  30.7 0.2 collective-permute-done.12.refs_1_
  31.0 3.6 %collective-permute-start.14 = (bf16[2,24,512]{2,1,0:T(8,128)(2,1)S(1)}, bf16[2,24,512]{2,1,0:T(8,128)(2,1)S(1)}, u32[]{:S(2)}, u32[]{:S(2)}) collective-permute-start(bf16[2,24,512]{2,1,0:T(8,128)(2,1)S(1)} %get-tuple-element.64), channel_id=1, source_target_pairs={{0,17},{1,16},{2,19},{3,18},{4,21},{5,20},{6,23},{7,22},{8,25},{9,... | collective-permute-start | bytes 147464 | tf_op jit(solution)/shard_map/ppermute | solution.py:147
  34.6 0.3 collective-permute-start.15
  35.1 1.2 %collective-permute-start.16 = (bf16[2,24,512]{2,1,0:T(8,128)(2,1)S(1)}, bf16[2,24,512]{2,1,0:T(8,128)(2,1)S(1)}, u32[]{:S(2)}, u32[]{:S(2)}) collective-permute-start(bf16[2,24,512]{2,1,0:T(8,128)(2,1)S(1)} %get-tuple-element.59.after), channel_id=1, source_target_pairs={{0,1},{1,0},{2,3},{3,2},{4,5},{5,4},{6,7},{7,6},{8,9},{9,8},{10,11... | collective-permute-start | bytes 147464 | tf_op jit(solution)/shard_map/ppermute | solution.py:512
  36.3 3.2 %spread.1 = bf16[384,8192]{1,0:T(8,128)(2,1)} custom-call(f32[8,128]{1,0:T(8,128)S(1)} %get-tuple-element.40.refs_4_.full, f32[56,384]{1,0:T(8,128)S(1)} %get-tuple-element.50.parts, bf16[56,384]{1,0:T(8,128)(2,1)S(1)} %collective-permute-done.5.got, bf16[24,8192]{1,0:T(8,128)(2,1)S(1)} %get-tuple-element.41.refs_0_.own, ...), custom_call_target="tpu_custom_call" | custom-call | flops 10000000000 | bytes 100000000 | tf_op jit(solution)/shard_map/spread/pallas_call | solution.py:330
  39.5 0.1 collective-permute-done.15.refs_1_
  39.6 0.7 %place.1 = (f32[24,2,1,512]{3,2,1,0:T(1,128)}, f32[24,2,1,512]{3,2,1,0:T(1,128)}) custom-call(f32[2,24,512]{2,1,0:T(8,128)S(1)} %gather.3.held, f32[2,24,512]{2,1,0:T(8,128)S(1)} %gather.2.far, bf16[2,24,512]{2,1,0:T(8,128)(2,1)S(1)} %collective-permute-done.16.got), custom_call_target="tpu_custom_call" | custom-call | flops 1 | bytes 1 | tf_op jit(solution)/shard_map/place/pallas_call | solution.py:403
  (21 shorter events, 0.3 us)
Async XLA Ops:
  1.7 8.9 %collective-permute-start.1 = (bf16[24,4096]{1,0:T(8,128)(2,1)S(1)}, bf16[24,4096]{1,0:T(8,128)(2,1)S(1)}, u32[]{:S(2)}, u32[]{:S(2)}) collective-permute-start(bf16[24,4096]{1,0:T(8,128)(2,1)S(1)} %get-tuple-element.37.refs_4_), channel_id=1, source_target_pairs={{0,1},{1,0},{2,3},{3,2},{4,5},{5,4},{6,7},{7,6},{8,9},{9,8},{10,11... | collective-permute-start | bytes 589832 | tf_op jit(solution)/shard_map/ppermute | solution.py:477
  4.8 8.2 %collective-permute-start = (bf16[24,2048]{1,0:T(8,128)(2,1)S(1)}, bf16[24,2048]{1,0:T(8,128)(2,1)S(1)}, u32[]{:S(2)}, u32[]{:S(2)}) collective-permute-start(bf16[24,2048]{1,0:T(8,128)(2,1)S(1)} %get-tuple-element.38.refs_5_), channel_id=1, source_target_pairs={{0,1},{1,0},{2,3},{3,2},{4,5},{5,4},{6,7},{7,6},{8,9},{9,8},{10,11... | collective-permute-start | bytes 294920 | tf_op jit(solution)/shard_map/ppermute | solution.py:477
  4.8 8.8 %collective-permute-start.2 = (bf16[24,2048]{1,0:T(8,128)(2,1)S(1)}, bf16[24,2048]{1,0:T(8,128)(2,1)S(1)}, u32[]{:S(2)}, u32[]{:S(2)}) collective-permute-start(bf16[24,2048]{1,0:T(8,128)(2,1)S(1)} %get-tuple-element.39.refs_6_), channel_id=1, source_target_pairs={{0,3},{1,2},{2,1},{3,0},{4,7},{5,6},{6,5},{7,4},{8,11},{9,10},{10,... | collective-permute-start | bytes 294920 | tf_op jit(solution)/shard_map/ppermute | solution.py:147
  10.7 3.1 %collective-permute-start.4 = (bf16[24,4096]{1,0:T(8,128)(2,1)S(1)}, bf16[24,4096]{1,0:T(8,128)(2,1)S(1)}, u32[]{:S(2)}, u32[]{:S(2)}) collective-permute-start(bf16[24,4096]{1,0:T(8,128)(2,1)S(1)} %collective-permute-done.1.refs_1_), channel_id=1, source_target_pairs={{0,2},{2,0},{4,6},{6,4},{8,10},{10,8},{12,14},{14,12},{16,18},{18,... | collective-permute-start | bytes 589832 | tf_op jit(solution)/shard_map/ppermute | solution.py:93
  13.7 1.6 %collective-permute-start.3 = (bf16[24,4096]{1,0:T(8,128)(2,1)S(1)}, bf16[24,4096]{1,0:T(8,128)(2,1)S(1)}, u32[]{:S(2)}, u32[]{:S(2)}) collective-permute-start(bf16[24,4096]{1,0:T(8,128)(2,1)S(1)} %constant_dynamic-update-slice_fusion.mine), channel_id=1, source_target_pairs={{0,2},{2,0},{4,6},{6,4},{8,10},{10,8},{12,14},{14,12},{16,18},{18,... | collective-permute-start | bytes 589832 | tf_op jit(solution)/shard_map/ppermute | solution.py:93
  16.3 4.1 %collective-permute-start.5 = (bf16[56,384]{1,0:T(8,128)(2,1)S(1)}, bf16[56,384]{1,0:T(8,128)(2,1)S(1)}, u32[]{:S(2)}, u32[]{:S(2)}) collective-permute-start(bf16[56,384]{1,0:T(8,128)(2,1)S(1)} %get-tuple-element.51), channel_id=1, source_target_pairs={{0,1},{1,0},{2,3},{3,2},{4,5},{5,4},{6,7},{7,6},{8,9},{9,8},{10,11... | collective-permute-start | bytes 129032 | tf_op jit(solution)/shard_map/ppermute | solution.py:497
  21.0 1.8 %collective-permute-start.6 = (bf16[4,56,512]{2,1,0:T(8,128)(2,1)S(1)}, bf16[4,56,512]{2,1,0:T(8,128)(2,1)S(1)}, u32[]{:S(2)}, u32[]{:S(2)}) collective-permute-start(bf16[4,56,512]{2,1,0:T(8,128)(2,1)S(1)} %gradient.3.refs_0_), channel_id=1, source_target_pairs={{0,2},{2,0},{4,6},{6,4},{8,10},{10,8},{12,14},{14,12},{16,18},{18,... | collective-permute-start | bytes 688136 | tf_op jit(solution)/shard_map/ppermute | solution.py:93
  22.3 4.8 %collective-permute-start.7 = (bf16[4,56,512]{2,1,0:T(8,128)(2,1)S(1)}, bf16[4,56,512]{2,1,0:T(8,128)(2,1)S(1)}, u32[]{:S(2)}, u32[]{:S(2)}) collective-permute-start(bf16[4,56,512]{2,1,0:T(8,128)(2,1)S(1)} %get-tuple-element.52.refs_0_), channel_id=1, source_target_pairs={{0,2},{2,0},{4,6},{6,4},{8,10},{10,8},{12,14},{14,12},{16,18},{18,... | collective-permute-start | bytes 688136 | tf_op jit(solution)/shard_map/ppermute | solution.py:93
  22.9 7.6 %collective-permute-start.11 = (bf16[56,512]{1,0:T(8,128)(2,1)S(1)}, bf16[56,512]{1,0:T(8,128)(2,1)S(1)}, u32[]{:S(2)}, u32[]{:S(2)}) collective-permute-start(bf16[56,512]{1,0:T(8,128)(2,1)S(1)} %get-tuple-element.62), channel_id=1, source_target_pairs={{0,12},{2,14},{4,8},{6,10},{8,4},{10,6},{12,0},{14,2},{16,28},{18,... | collective-permute-start | bytes 172040 | tf_op jit(solution)/shard_map/ppermute | solution.py:93
  25.7 5.1 %collective-permute-start.13 = (bf16[56,512]{1,0:T(8,128)(2,1)S(1)}, bf16[56,512]{1,0:T(8,128)(2,1)S(1)}, u32[]{:S(2)}, u32[]{:S(2)}) collective-permute-start(bf16[56,512]{1,0:T(8,128)(2,1)S(1)} %get-tuple-element.63), channel_id=1, source_target_pairs={{0,8},{2,10},{4,12},{6,14},{8,0},{10,2},{12,4},{14,6},{16,24},{18,... | collective-permute-start | bytes 172040 | tf_op jit(solution)/shard_map/ppermute | solution.py:93
  26.1 4.8 %collective-permute-start.12 = (bf16[56,512]{1,0:T(8,128)(2,1)S(1)}, bf16[56,512]{1,0:T(8,128)(2,1)S(1)}, u32[]{:S(2)}, u32[]{:S(2)}) collective-permute-start(bf16[56,512]{1,0:T(8,128)(2,1)S(1)} %get-tuple-element.54.refs_1_), channel_id=1, source_target_pairs={{0,4},{2,6},{4,0},{6,2},{8,12},{10,14},{12,8},{14,10},{16,20},{18,... | collective-permute-start | bytes 172040 | tf_op jit(solution)/shard_map/ppermute | solution.py:93
  27.2 7.8 %collective-permute-start.8 = (bf16[56,512]{1,0:T(8,128)(2,1)S(1)}, bf16[56,512]{1,0:T(8,128)(2,1)S(1)}, u32[]{:S(2)}, u32[]{:S(2)}) collective-permute-start(bf16[56,512]{1,0:T(8,128)(2,1)S(1)} %get-tuple-element.56), channel_id=1, source_target_pairs={{0,12},{2,14},{4,8},{6,10},{8,4},{10,6},{12,0},{14,2},{16,28},{18,... | collective-permute-start | bytes 172040 | tf_op jit(solution)/shard_map/ppermute | solution.py:93
  29.9 5.0 %collective-permute-start.9 = (bf16[56,512]{1,0:T(8,128)(2,1)S(1)}, bf16[56,512]{1,0:T(8,128)(2,1)S(1)}, u32[]{:S(2)}, u32[]{:S(2)}) collective-permute-start(bf16[56,512]{1,0:T(8,128)(2,1)S(1)} %get-tuple-element.57), channel_id=1, source_target_pairs={{0,4},{2,6},{4,0},{6,2},{8,12},{10,14},{12,8},{14,10},{16,20},{18,... | collective-permute-start | bytes 172040 | tf_op jit(solution)/shard_map/ppermute | solution.py:93
  30.5 4.5 %collective-permute-start.10 = (bf16[56,512]{1,0:T(8,128)(2,1)S(1)}, bf16[56,512]{1,0:T(8,128)(2,1)S(1)}, u32[]{:S(2)}, u32[]{:S(2)}) collective-permute-start(bf16[56,512]{1,0:T(8,128)(2,1)S(1)} %get-tuple-element.58), channel_id=1, source_target_pairs={{0,8},{2,10},{4,12},{6,14},{8,0},{10,2},{12,4},{14,6},{16,24},{18,... | collective-permute-start | bytes 172040 | tf_op jit(solution)/shard_map/ppermute | solution.py:93
  31.0 8.5 %collective-permute-start.14 = (bf16[2,24,512]{2,1,0:T(8,128)(2,1)S(1)}, bf16[2,24,512]{2,1,0:T(8,128)(2,1)S(1)}, u32[]{:S(2)}, u32[]{:S(2)}) collective-permute-start(bf16[2,24,512]{2,1,0:T(8,128)(2,1)S(1)} %get-tuple-element.64), channel_id=1, source_target_pairs={{0,17},{1,16},{2,19},{3,18},{4,21},{5,20},{6,23},{7,22},{8,25},{9,... | collective-permute-start | bytes 147464 | tf_op jit(solution)/shard_map/ppermute | solution.py:147
  34.6 5.0 %collective-permute-start.15 = (bf16[2,24,512]{2,1,0:T(8,128)(2,1)S(1)}, bf16[2,24,512]{2,1,0:T(8,128)(2,1)S(1)}, u32[]{:S(2)}, u32[]{:S(2)}) collective-permute-start(bf16[2,24,512]{2,1,0:T(8,128)(2,1)S(1)} %get-tuple-element.65), channel_id=1, source_target_pairs={{0,16},{2,18},{4,20},{6,22},{8,24},{10,26},{12,28},{14,30},{16,0},... | collective-permute-start | bytes 147464 | tf_op jit(solution)/shard_map/ppermute | solution.py:93
  35.1 4.5 %collective-permute-start.16 = (bf16[2,24,512]{2,1,0:T(8,128)(2,1)S(1)}, bf16[2,24,512]{2,1,0:T(8,128)(2,1)S(1)}, u32[]{:S(2)}, u32[]{:S(2)}) collective-permute-start(bf16[2,24,512]{2,1,0:T(8,128)(2,1)S(1)} %get-tuple-element.59.after), channel_id=1, source_target_pairs={{0,1},{1,0},{2,3},{3,2},{4,5},{5,4},{6,7},{7,6},{8,9},{9,8},{10,11... | collective-permute-start | bytes 147464 | tf_op jit(solution)/shard_map/ppermute | solution.py:512

commit v11 on v10

--- a/solution.py
+++ b/solution.py
@@ -158,7 +158,7 @@
 
 def add_up(total, own, piece, acts, flipped, low_column):
     width = piece.shape[1]
-    chunk = min(width // 2, 512)
+    chunk = min(width // 2, 256)
     core = lax.axis_index("dp") % 2
     start = (1 - core if flipped else core) * (own.shape[1] // 2) + low_column
     turned = None
@@ -466,6 +466,26 @@
     )(near(keep), near(got))
 
 
+def last_kernel(scale, places, parts, parts_got, tokens, cotangent, got, after, *refs):
+    outs, keep = refs[:-1], refs[-1]
+    gradient_kernel(scale, places, [(True, True)], parts, parts_got, tokens, cotangent, keep)
+    quarter_kernel(keep, got, *outs)
+
+
+def last_quarter(parts, parts_got, tokens, cotangent, scale, got, after):
+    shape = (4, parts.shape[0], tokens.shape[1] // lax.axis_size("dp"))
+    return pl.pallas_call(
+        functools.partial(last_kernel, scale, (0, 2, 1, 3)),
+        in_specs=[WHOLE] * 6,
+        out_specs=[WHOLE] * 4,
+        out_shape=[pltpu.VMEM(shape[1:], kind) for kind in [jnp.float32] + [jnp.bfloat16] * 3],
+        scratch_shapes=[pltpu.VMEM(shape, jnp.float32)],
+        compiler_params=PARAMS,
+        cost_estimate=SMALL,
+        name="last_quarter",
+    )(*map(near, (parts, parts_got, tokens, cotangent, got, after)))
+
+
 def trade(sends):
     return [flip(sends[2], 1, 2), flip(sends[0], 1), flip(sends[1], 2)]
 
@@ -502,8 +522,7 @@
         *operands, [(False, True), (True, False)], (other_send,)
     )
     other = quarter(other_keep, flip(other_send, 0))
-    (own_keep,) = gradient(*operands, [(True, True)], (own_send, other[1]))
-    own = quarter(own_keep, flip(own_send, 0))
+    own = last_quarter(*operands, flip(own_send, 0), other[1])
     other_gots, own_gots = trade(other[1:]), trade(own[1:])
     near_send, far_send = settle(full, other[0], other_gots, jnp.bfloat16)
     far_got = across(far_send, 17)

time: 40.5 us -> 40.4 us (level)
    pallas_call x0 -> x1, Pallas kernels: none -> 0.67 us  [last_quarter(): pl.pallas_call(functools.partial(last_kernel, scale, (0, 2, 1, 3)), in_sp...]
    pallas_call x3 -> x2, Pallas kernels: 2.41 us -> 1.79 us  [gradient(): pl.pallas_call(functools.partial(gradient_kernel, scale, places, jobs), i...]
where the time goes in v11:
time: 40.4 us; the launch traced here: 40.2 us
  starting transfers between devices  20.1 us (50%)
  Pallas kernels  16.6 us (41%)
  waiting for transfers between devices  2.71 us (7%)
  between operations  0.82 us (2%)
    ppermute x11, starting transfers between devices, flip(): lax.ppermute(value, 'dp', [(i, i ^ mask) for i in range(lax.axis_size('dp...  9.49 us
    pallas_call x1, Pallas kernels, stage(): pl.pallas_call(functools.partial(stage_kernel, parts), in_specs=[FAR] * 5...  4.98 us
    ppermute x2, starting transfers between devices, across(): return lax.ppermute(value, ('dp', 'tensor'), pairs)  4.44 us
    pallas_call x1, Pallas kernels, spread(): pl.pallas_call(functools.partial(spread_kernel, chunk), in_specs=[WHOLE]...  3.18 us
    ppermute x2, starting transfers between devices, two_panels(): lax.ppermute(w, 'tensor', SWAP)  3.11 us
    pallas_call x3, Pallas kernels, project(): pl.pallas_call(functools.partial(project_kernel, flipped, low, len(others...  2.64 us
    ppermute x1, waiting for transfers between devices, two_panels(): parts_got = lax.ppermute(parts_send, 'tensor', SWAP)  2.28 us
    ppermute x1, starting transfers between devices, two_panels(): parts_got = lax.ppermute(parts_send, 'tensor', SWAP)  1.81 us
  transfers between devices with their start and end apart: 17, of which 4 were waited for; matrix products, arithmetic and copies ran while one was open for 0% of the time, Pallas kernels for 33%

profile of v11, /device:TPU:0, one launch (start us, length us, event | category | flops | bytes accessed | tf_op | source)
XLA Modules:
  0.0 40.2 jit_solution(3573698332736392941)
XLA Ops:
  0.6 1.1 %pick.1 = (bf16[24,4096]{1,0:T(8,128)(2,1)S(1)}, bf16[24,2048]{1,0:T(8,128)(2,1)S(1)}, bf16[24,2048]{1,0:T(8,128)(2,1)S(1)}) custom-call(bf16[24,16384]{1,0:T(8,128)(2,1)} %refs_0_.1, bf16[24,16384]{1,0:T(8,128)(2,1)} %refs_2_.1), custom_call_target="tpu_custom_call" | custom-call | flops 1 | bytes 1 | tf_op jit(solution)/shard_map/pick/pallas_call | solution.py:437
  1.7 3.0 %collective-permute-start.1 = (bf16[24,4096]{1,0:T(8,128)(2,1)S(1)}, bf16[24,4096]{1,0:T(8,128)(2,1)S(1)}, u32[]{:S(2)}, u32[]{:S(2)}) collective-permute-start(bf16[24,4096]{1,0:T(8,128)(2,1)S(1)} %get-tuple-element.37.refs_4_), channel_id=1, source_target_pairs={{0,1},{1,0},{2,3},{3,2},{4,5},{5,4},{6,7},{7,6},{8,9},{9,8},{10,11... | collective-permute-start | bytes 589832 | tf_op jit(solution)/shard_map/ppermute | solution.py:497
  4.8 0.1 collective-permute-start
  4.8 0.8 %collective-permute-start.2 = (bf16[24,2048]{1,0:T(8,128)(2,1)S(1)}, bf16[24,2048]{1,0:T(8,128)(2,1)S(1)}, u32[]{:S(2)}, u32[]{:S(2)}) collective-permute-start(bf16[24,2048]{1,0:T(8,128)(2,1)S(1)} %get-tuple-element.39.refs_6_), channel_id=1, source_target_pairs={{0,3},{1,2},{2,1},{3,0},{4,7},{5,6},{6,5},{7,4},{8,11},{9,10},{10,... | collective-permute-start | bytes 294920 | tf_op jit(solution)/shard_map/ppermute | solution.py:147
  5.7 5.0 %stage.1 = (bf16[24,8192]{1,0:T(8,128)(2,1)S(1)}, bf16[384,8192]{1,0:T(8,128)(2,1)S(1)}, bf16[24,8192]{1,0:T(8,128)(2,1)S(1)}, bf16[384,8192]{1,0:T(8,128)(2,1)S(1)}, f32[8,128]{1,0:T(8,128)S(1)}) custom-call(s32[2]{0:T(128)} %rank.1, bf16[24,16384]{1,0:T(8,128)(2,1)} %refs_0_.1, bf16[384,8192]{1,0:T(8,128)(2,1)} %refs_1_.1, bf16[24,16384]{1,0:T(8,128)(2,1)} %refs_2_.1, ...), custom_call_target="tpu_custom_call" | custom-call | flops 1 | bytes 1 | tf_op jit(solution)/shard_map/stage/pallas_call | solution.py:130
  10.7 1.3 %collective-permute-start.4 = (bf16[24,4096]{1,0:T(8,128)(2,1)S(1)}, bf16[24,4096]{1,0:T(8,128)(2,1)S(1)}, u32[]{:S(2)}, u32[]{:S(2)}) collective-permute-start(bf16[24,4096]{1,0:T(8,128)(2,1)S(1)} %collective-permute-done.1.refs_1_), channel_id=1, source_target_pairs={{0,2},{2,0},{4,6},{6,4},{8,10},{10,8},{12,14},{14,12},{16,18},{18,... | collective-permute-start | bytes 589832 | tf_op jit(solution)/shard_map/ppermute | solution.py:93
  12.0 1.0 %project.3.refs_7_ = f32[64,384]{1,0:T(8,128)S(1)} custom-call(bf16[24,8192]{1,0:T(8,128)(2,1)S(1)} %get-tuple-element.42.refs_0_.refs_4_, bf16[24,4096]{1,0:T(8,128)(2,1)S(1)} %collective-permute-done.1.refs_1_, bf16[384,8192]{1,0:T(8,128)(2,1)S(1)} %get-tuple-element.44.refs_2_.refs_3_.refs_6_.cotangent), custom_call_target="tpu_custom_call" | custom-call | flops 1 | bytes 1 | tf_op jit(solution)/shard_map/project/pallas_call | solution.py:226
  13.0 0.6 %project.4.refs_3_ = f32[64,384]{1,0:T(8,128)S(1)} custom-call(bf16[24,8192]{1,0:T(8,128)(2,1)S(1)} %get-tuple-element.41.refs_0_.own, bf16[24,2048]{1,0:T(8,128)(2,1)S(1)} %collective-permute-done.refs_1_, bf16[384,8192]{1,0:T(8,128)(2,1)S(1)} %get-tuple-element.46.refs_2_.tokens, bf16[384,8192]{1,0:T(8,128)(2,1)S(1)} %get-tuple-element.44.refs_2_.refs_3_.refs_6_.cotangent), custom_call_target="tpu_custom_call" | custom-call | flops 1 | bytes 1 | tf_op jit(solution)/shard_map/project/pallas_call | solution.py:226
  13.6 0.1 collective-permute-start.3
  13.8 1.4 %project_two.1 = (f32[64,384]{1,0:T(8,128)S(1)}, f32[64,384]{1,0:T(8,128)S(1)}) custom-call(bf16[24,8192]{1,0:T(8,128)(2,1)S(1)} %get-tuple-element.41.refs_0_.own, bf16[24,2048]{1,0:T(8,128)(2,1)S(1)} %collective-permute-done.2.refs_1_, bf16[384,8192]{1,0:T(8,128)(2,1)S(1)} %get-tuple-element.46.refs_2_.tokens, f32[64,384]{1,0:T(8,128)S(1)} %project.4.refs_3_, ...), custom_call_target="tpu_custom_call" | custom-call | flops 1 | bytes 1 | tf_op jit(solution)/shard_map/project_two/pallas_call | solution.py:190
  15.2 1.0 %project.5 = (f32[56,384]{1,0:T(8,128)S(1)}, bf16[56,384]{1,0:T(8,128)(2,1)S(1)}) custom-call(bf16[24,8192]{1,0:T(8,128)(2,1)S(1)} %get-tuple-element.41.refs_0_.own, bf16[24,4096]{1,0:T(8,128)(2,1)S(1)} %collective-permute-done.3.refs_1_.theirs, bf16[384,8192]{1,0:T(8,128)(2,1)S(1)} %get-tuple-element.46.refs_2_.tokens, ...), custom_call_target="tpu_custom_call" | custom-call | flops 1 | bytes 1 | tf_op jit(solution)/shard_map/project/pallas_call | solution.py:226
  16.2 1.8 %collective-permute-start.5 = (bf16[56,384]{1,0:T(8,128)(2,1)S(1)}, bf16[56,384]{1,0:T(8,128)(2,1)S(1)}, u32[]{:S(2)}, u32[]{:S(2)}) collective-permute-start(bf16[56,384]{1,0:T(8,128)(2,1)S(1)} %get-tuple-element.51), channel_id=1, source_target_pairs={{0,1},{1,0},{2,3},{3,2},{4,5},{5,4},{6,7},{7,6},{8,9},{9,8},{10,11... | collective-permute-start | bytes 129032 | tf_op jit(solution)/shard_map/ppermute | solution.py:517
  18.0 2.3 %collective-permute-done.5.got.parts_got = bf16[56,384]{1,0:T(8,128)(2,1)S(1)} collective-permute-done((bf16[56,384]{1,0:T(8,128)(2,1)S(1)}, bf16[56,384]{1,0:T(8,128)(2,1)S(1)}, u32[]{:S(2)}, u32[]{:S(2)}) %collective-permute-start.5) | collective-permute-done | bytes 43040 | tf_op jit(solution)/shard_map/ppermute | solution.py:517
  20.3 0.6 %gradient.2.refs_0_ = bf16[4,56,512]{2,1,0:T(8,128)(2,1)S(1)} custom-call(f32[56,384]{1,0:T(8,128)S(1)} %get-tuple-element.50.parts, bf16[56,384]{1,0:T(8,128)(2,1)S(1)} %collective-permute-done.5.got.parts_got, bf16[384,8192]{1,0:T(8,128)(2,1)S(1)} %get-tuple-element.46.refs_2_.tokens, bf16[384,8192]{1,0:T(8,128)(2,1)S(1)} %get-tuple-element.44.refs_2_.refs_3_.refs_6_.cotangent), custom_call_target="tpu_custom_call" | custom-call | flops 1 | bytes 1 | tf_op jit(solution)/shard_map/gradient/pallas_call | solution.py:289
  20.9 0.1 collective-permute-start.7
  21.0 1.2 %gradient.3 = (f32[4,56,512]{2,1,0:T(8,128)S(1)}, bf16[4,56,512]{2,1,0:T(8,128)(2,1)S(1)}) custom-call(f32[56,384]{1,0:T(8,128)S(1)} %get-tuple-element.50.parts, bf16[56,384]{1,0:T(8,128)(2,1)S(1)} %collective-permute-done.5.got.parts_got, bf16[384,8192]{1,0:T(8,128)(2,1)S(1)} %get-tuple-element.46.refs_2_.tokens, ...), custom_call_target="tpu_custom_call" | custom-call | flops 1 | bytes 1 | tf_op jit(solution)/shard_map/gradient/pallas_call | solution.py:289
  22.2 0.5 %collective-permute-start.6 = (bf16[4,56,512]{2,1,0:T(8,128)(2,1)S(1)}, bf16[4,56,512]{2,1,0:T(8,128)(2,1)S(1)}, u32[]{:S(2)}, u32[]{:S(2)}) collective-permute-start(bf16[4,56,512]{2,1,0:T(8,128)(2,1)S(1)} %get-tuple-element.52), channel_id=1, source_target_pairs={{0,2},{2,0},{4,6},{6,4},{8,10},{10,8},{12,14},{14,12},{16,18},{18,... | collective-permute-start | bytes 688136 | tf_op jit(solution)/shard_map/ppermute | solution.py:93
  22.8 2.8 %collective-permute-start.11 = (bf16[56,512]{1,0:T(8,128)(2,1)S(1)}, bf16[56,512]{1,0:T(8,128)(2,1)S(1)}, u32[]{:S(2)}, u32[]{:S(2)}) collective-permute-start(bf16[56,512]{1,0:T(8,128)(2,1)S(1)} %get-tuple-element.62), channel_id=1, source_target_pairs={{0,12},{2,14},{4,8},{6,10},{8,4},{10,6},{12,0},{14,2},{16,28},{18,... | collective-permute-start | bytes 172040 | tf_op jit(solution)/shard_map/ppermute | solution.py:93
  25.6 0.5 %collective-permute-start.13 = (bf16[56,512]{1,0:T(8,128)(2,1)S(1)}, bf16[56,512]{1,0:T(8,128)(2,1)S(1)}, u32[]{:S(2)}, u32[]{:S(2)}) collective-permute-start(bf16[56,512]{1,0:T(8,128)(2,1)S(1)} %get-tuple-element.63), channel_id=1, source_target_pairs={{0,8},{2,10},{4,12},{6,14},{8,0},{10,2},{12,4},{14,6},{16,24},{18,... | collective-permute-start | bytes 172040 | tf_op jit(solution)/shard_map/ppermute | solution.py:93
  26.0 0.3 collective-permute-start.12
  26.4 0.7 %last_quarter.1 = (f32[56,512]{1,0:T(8,128)S(1)}, bf16[56,512]{1,0:T(8,128)(2,1)S(1)}, bf16[56,512]{1,0:T(8,128)(2,1)S(1)}, bf16[56,512]{1,0:T(8,128)(2,1)S(1)}) custom-call(f32[56,384]{1,0:T(8,128)S(1)} %get-tuple-element.50.parts, bf16[56,384]{1,0:T(8,128)(2,1)S(1)} %collective-permute-done.5.got.parts_got, ...), custom_call_target="tpu_custom_call" | custom-call | flops 1 | bytes 1 | tf_op jit(solution)/shard_map/last_quarter/pallas_call | solution.py:477
  27.0 2.8 %collective-permute-start.8 = (bf16[56,512]{1,0:T(8,128)(2,1)S(1)}, bf16[56,512]{1,0:T(8,128)(2,1)S(1)}, u32[]{:S(2)}, u32[]{:S(2)}) collective-permute-start(bf16[56,512]{1,0:T(8,128)(2,1)S(1)} %get-tuple-element.56), channel_id=1, source_target_pairs={{0,12},{2,14},{4,8},{6,10},{8,4},{10,6},{12,0},{14,2},{16,28},{18,... | collective-permute-start | bytes 172040 | tf_op jit(solution)/shard_map/ppermute | solution.py:93
  29.8 0.5 %collective-permute-start.9 = (bf16[56,512]{1,0:T(8,128)(2,1)S(1)}, bf16[56,512]{1,0:T(8,128)(2,1)S(1)}, u32[]{:S(2)}, u32[]{:S(2)}) collective-permute-start(bf16[56,512]{1,0:T(8,128)(2,1)S(1)} %get-tuple-element.57), channel_id=1, source_target_pairs={{0,4},{2,6},{4,0},{6,2},{8,12},{10,14},{12,8},{14,10},{16,20},{18,... | collective-permute-start | bytes 172040 | tf_op jit(solution)/shard_map/ppermute | solution.py:93
  30.4 0.2 collective-permute-start.10
  30.6 0.2 collective-permute-done.12.refs_1_
  30.9 3.6 %collective-permute-start.14 = (bf16[2,24,512]{2,1,0:T(8,128)(2,1)S(1)}, bf16[2,24,512]{2,1,0:T(8,128)(2,1)S(1)}, u32[]{:S(2)}, u32[]{:S(2)}) collective-permute-start(bf16[2,24,512]{2,1,0:T(8,128)(2,1)S(1)} %get-tuple-element.64), channel_id=1, source_target_pairs={{0,17},{1,16},{2,19},{3,18},{4,21},{5,20},{6,23},{7,22},{8,25},{9,... | collective-permute-start | bytes 147464 | tf_op jit(solution)/shard_map/ppermute | solution.py:147
  34.5 0.3 collective-permute-start.15
  34.8 0.1 collective-permute-done.10.refs_2_
  35.0 1.2 %collective-permute-start.16 = (bf16[2,24,512]{2,1,0:T(8,128)(2,1)S(1)}, bf16[2,24,512]{2,1,0:T(8,128)(2,1)S(1)}, u32[]{:S(2)}, u32[]{:S(2)}) collective-permute-start(bf16[2,24,512]{2,1,0:T(8,128)(2,1)S(1)} %get-tuple-element.59.after), channel_id=1, source_target_pairs={{0,1},{1,0},{2,3},{3,2},{4,5},{5,4},{6,7},{7,6},{8,9},{9,8},{10,11... | collective-permute-start | bytes 147464 | tf_op jit(solution)/shard_map/ppermute | solution.py:531
  36.2 3.2 %spread.1 = bf16[384,8192]{1,0:T(8,128)(2,1)} custom-call(f32[8,128]{1,0:T(8,128)S(1)} %get-tuple-element.40.refs_4_.full, f32[56,384]{1,0:T(8,128)S(1)} %get-tuple-element.50.parts, bf16[56,384]{1,0:T(8,128)(2,1)S(1)} %collective-permute-done.5.got.parts_got, bf16[24,8192]{1,0:T(8,128)(2,1)S(1)} %get-tuple-element.41.refs_0_.own, ...), custom_call_target="tpu_custom_call" | custom-call | flops 10000000000 | bytes 100000000 | tf_op jit(solution)/shard_map/spread/pallas_call | solution.py:330
  39.4 0.1 collective-permute-done.15.refs_1_
  39.5 0.7 %place.1 = (f32[24,2,1,512]{3,2,1,0:T(1,128)}, f32[24,2,1,512]{3,2,1,0:T(1,128)}) custom-call(f32[2,24,512]{2,1,0:T(8,128)S(1)} %gather.3.held, f32[2,24,512]{2,1,0:T(8,128)S(1)} %gather.2.far, bf16[2,24,512]{2,1,0:T(8,128)(2,1)S(1)} %collective-permute-done.16.got), custom_call_target="tpu_custom_call" | custom-call | flops 1 | bytes 1 | tf_op jit(solution)/shard_map/place/pallas_call | solution.py:403
  (20 shorter events, 0.2 us)
Async XLA Ops:
  1.7 8.9 %collective-permute-start.1 = (bf16[24,4096]{1,0:T(8,128)(2,1)S(1)}, bf16[24,4096]{1,0:T(8,128)(2,1)S(1)}, u32[]{:S(2)}, u32[]{:S(2)}) collective-permute-start(bf16[24,4096]{1,0:T(8,128)(2,1)S(1)} %get-tuple-element.37.refs_4_), channel_id=1, source_target_pairs={{0,1},{1,0},{2,3},{3,2},{4,5},{5,4},{6,7},{7,6},{8,9},{9,8},{10,11... | collective-permute-start | bytes 589832 | tf_op jit(solution)/shard_map/ppermute | solution.py:497
  4.8 8.2 %collective-permute-start = (bf16[24,2048]{1,0:T(8,128)(2,1)S(1)}, bf16[24,2048]{1,0:T(8,128)(2,1)S(1)}, u32[]{:S(2)}, u32[]{:S(2)}) collective-permute-start(bf16[24,2048]{1,0:T(8,128)(2,1)S(1)} %get-tuple-element.38.refs_5_), channel_id=1, source_target_pairs={{0,1},{1,0},{2,3},{3,2},{4,5},{5,4},{6,7},{7,6},{8,9},{9,8},{10,11... | collective-permute-start | bytes 294920 | tf_op jit(solution)/shard_map/ppermute | solution.py:497
  4.8 8.8 %collective-permute-start.2 = (bf16[24,2048]{1,0:T(8,128)(2,1)S(1)}, bf16[24,2048]{1,0:T(8,128)(2,1)S(1)}, u32[]{:S(2)}, u32[]{:S(2)}) collective-permute-start(bf16[24,2048]{1,0:T(8,128)(2,1)S(1)} %get-tuple-element.39.refs_6_), channel_id=1, source_target_pairs={{0,3},{1,2},{2,1},{3,0},{4,7},{5,6},{6,5},{7,4},{8,11},{9,10},{10,... | collective-permute-start | bytes 294920 | tf_op jit(solution)/shard_map/ppermute | solution.py:147
  10.7 3.1 %collective-permute-start.4 = (bf16[24,4096]{1,0:T(8,128)(2,1)S(1)}, bf16[24,4096]{1,0:T(8,128)(2,1)S(1)}, u32[]{:S(2)}, u32[]{:S(2)}) collective-permute-start(bf16[24,4096]{1,0:T(8,128)(2,1)S(1)} %collective-permute-done.1.refs_1_), channel_id=1, source_target_pairs={{0,2},{2,0},{4,6},{6,4},{8,10},{10,8},{12,14},{14,12},{16,18},{18,... | collective-permute-start | bytes 589832 | tf_op jit(solution)/shard_map/ppermute | solution.py:93
  13.6 1.6 %collective-permute-start.3 = (bf16[24,4096]{1,0:T(8,128)(2,1)S(1)}, bf16[24,4096]{1,0:T(8,128)(2,1)S(1)}, u32[]{:S(2)}, u32[]{:S(2)}) collective-permute-start(bf16[24,4096]{1,0:T(8,128)(2,1)S(1)} %constant_dynamic-update-slice_fusion.mine), channel_id=1, source_target_pairs={{0,2},{2,0},{4,6},{6,4},{8,10},{10,8},{12,14},{14,12},{16,18},{18,... | collective-permute-start | bytes 589832 | tf_op jit(solution)/shard_map/ppermute | solution.py:93
  16.2 4.1 %collective-permute-start.5 = (bf16[56,384]{1,0:T(8,128)(2,1)S(1)}, bf16[56,384]{1,0:T(8,128)(2,1)S(1)}, u32[]{:S(2)}, u32[]{:S(2)}) collective-permute-start(bf16[56,384]{1,0:T(8,128)(2,1)S(1)} %get-tuple-element.51), channel_id=1, source_target_pairs={{0,1},{1,0},{2,3},{3,2},{4,5},{5,4},{6,7},{7,6},{8,9},{9,8},{10,11... | collective-permute-start | bytes 129032 | tf_op jit(solution)/shard_map/ppermute | solution.py:517
  20.9 1.8 %collective-permute-start.7 = (bf16[4,56,512]{2,1,0:T(8,128)(2,1)S(1)}, bf16[4,56,512]{2,1,0:T(8,128)(2,1)S(1)}, u32[]{:S(2)}, u32[]{:S(2)}) collective-permute-start(bf16[4,56,512]{2,1,0:T(8,128)(2,1)S(1)} %gradient.2.refs_0_), channel_id=1, source_target_pairs={{0,2},{2,0},{4,6},{6,4},{8,10},{10,8},{12,14},{14,12},{16,18},{18,... | collective-permute-start | bytes 688136 | tf_op jit(solution)/shard_map/ppermute | solution.py:93
  22.2 4.2 %collective-permute-start.6 = (bf16[4,56,512]{2,1,0:T(8,128)(2,1)S(1)}, bf16[4,56,512]{2,1,0:T(8,128)(2,1)S(1)}, u32[]{:S(2)}, u32[]{:S(2)}) collective-permute-start(bf16[4,56,512]{2,1,0:T(8,128)(2,1)S(1)} %get-tuple-element.52), channel_id=1, source_target_pairs={{0,2},{2,0},{4,6},{6,4},{8,10},{10,8},{12,14},{14,12},{16,18},{18,... | collective-permute-start | bytes 688136 | tf_op jit(solution)/shard_map/ppermute | solution.py:93
  22.8 7.6 %collective-permute-start.11 = (bf16[56,512]{1,0:T(8,128)(2,1)S(1)}, bf16[56,512]{1,0:T(8,128)(2,1)S(1)}, u32[]{:S(2)}, u32[]{:S(2)}) collective-permute-start(bf16[56,512]{1,0:T(8,128)(2,1)S(1)} %get-tuple-element.62), channel_id=1, source_target_pairs={{0,12},{2,14},{4,8},{6,10},{8,4},{10,6},{12,0},{14,2},{16,28},{18,... | collective-permute-start | bytes 172040 | tf_op jit(solution)/shard_map/ppermute | solution.py:93
  25.6 5.0 %collective-permute-start.13 = (bf16[56,512]{1,0:T(8,128)(2,1)S(1)}, bf16[56,512]{1,0:T(8,128)(2,1)S(1)}, u32[]{:S(2)}, u32[]{:S(2)}) collective-permute-start(bf16[56,512]{1,0:T(8,128)(2,1)S(1)} %get-tuple-element.63), channel_id=1, source_target_pairs={{0,8},{2,10},{4,12},{6,14},{8,0},{10,2},{12,4},{14,6},{16,24},{18,... | collective-permute-start | bytes 172040 | tf_op jit(solution)/shard_map/ppermute | solution.py:93
  26.0 4.8 %collective-permute-start.12 = (bf16[56,512]{1,0:T(8,128)(2,1)S(1)}, bf16[56,512]{1,0:T(8,128)(2,1)S(1)}, u32[]{:S(2)}, u32[]{:S(2)}) collective-permute-start(bf16[56,512]{1,0:T(8,128)(2,1)S(1)} %get-tuple-element.54.after), channel_id=1, source_target_pairs={{0,4},{2,6},{4,0},{6,2},{8,12},{10,14},{12,8},{14,10},{16,20},{18,... | collective-permute-start | bytes 172040 | tf_op jit(solution)/shard_map/ppermute | solution.py:93
  27.0 7.8 %collective-permute-start.8 = (bf16[56,512]{1,0:T(8,128)(2,1)S(1)}, bf16[56,512]{1,0:T(8,128)(2,1)S(1)}, u32[]{:S(2)}, u32[]{:S(2)}) collective-permute-start(bf16[56,512]{1,0:T(8,128)(2,1)S(1)} %get-tuple-element.56), channel_id=1, source_target_pairs={{0,12},{2,14},{4,8},{6,10},{8,4},{10,6},{12,0},{14,2},{16,28},{18,... | collective-permute-start | bytes 172040 | tf_op jit(solution)/shard_map/ppermute | solution.py:93
  29.8 5.0 %collective-permute-start.9 = (bf16[56,512]{1,0:T(8,128)(2,1)S(1)}, bf16[56,512]{1,0:T(8,128)(2,1)S(1)}, u32[]{:S(2)}, u32[]{:S(2)}) collective-permute-start(bf16[56,512]{1,0:T(8,128)(2,1)S(1)} %get-tuple-element.57), channel_id=1, source_target_pairs={{0,4},{2,6},{4,0},{6,2},{8,12},{10,14},{12,8},{14,10},{16,20},{18,... | collective-permute-start | bytes 172040 | tf_op jit(solution)/shard_map/ppermute | solution.py:93
  30.4 4.5 %collective-permute-start.10 = (bf16[56,512]{1,0:T(8,128)(2,1)S(1)}, bf16[56,512]{1,0:T(8,128)(2,1)S(1)}, u32[]{:S(2)}, u32[]{:S(2)}) collective-permute-start(bf16[56,512]{1,0:T(8,128)(2,1)S(1)} %get-tuple-element.58), channel_id=1, source_target_pairs={{0,8},{2,10},{4,12},{6,14},{8,0},{10,2},{12,4},{14,6},{16,24},{18,... | collective-permute-start | bytes 172040 | tf_op jit(solution)/shard_map/ppermute | solution.py:93
  30.9 8.5 %collective-permute-start.14 = (bf16[2,24,512]{2,1,0:T(8,128)(2,1)S(1)}, bf16[2,24,512]{2,1,0:T(8,128)(2,1)S(1)}, u32[]{:S(2)}, u32[]{:S(2)}) collective-permute-start(bf16[2,24,512]{2,1,0:T(8,128)(2,1)S(1)} %get-tuple-element.64), channel_id=1, source_target_pairs={{0,17},{1,16},{2,19},{3,18},{4,21},{5,20},{6,23},{7,22},{8,25},{9,... | collective-permute-start | bytes 147464 | tf_op jit(solution)/shard_map/ppermute | solution.py:147
  34.5 5.0 %collective-permute-start.15 = (bf16[2,24,512]{2,1,0:T(8,128)(2,1)S(1)}, bf16[2,24,512]{2,1,0:T(8,128)(2,1)S(1)}, u32[]{:S(2)}, u32[]{:S(2)}) collective-permute-start(bf16[2,24,512]{2,1,0:T(8,128)(2,1)S(1)} %get-tuple-element.65), channel_id=1, source_target_pairs={{0,16},{2,18},{4,20},{6,22},{8,24},{10,26},{12,28},{14,30},{16,0},... | collective-permute-start | bytes 147464 | tf_op jit(solution)/shard_map/ppermute | solution.py:93
  35.0 4.5 %collective-permute-start.16 = (bf16[2,24,512]{2,1,0:T(8,128)(2,1)S(1)}, bf16[2,24,512]{2,1,0:T(8,128)(2,1)S(1)}, u32[]{:S(2)}, u32[]{:S(2)}) collective-permute-start(bf16[2,24,512]{2,1,0:T(8,128)(2,1)S(1)} %get-tuple-element.59.after), channel_id=1, source_target_pairs={{0,1},{1,0},{2,3},{3,2},{4,5},{5,4},{6,7},{7,6},{8,9},{9,8},{10,11... | collective-permute-start | bytes 147464 | tf_op jit(solution)/shard_map/ppermute | solution.py:531

commit v12 on v11

--- a/solution.py
+++ b/solution.py
@@ -126,7 +126,7 @@
 def stage(rank, right, cotangent, left, tokens, after):
     acts = pltpu.VMEM(tokens.shape, tokens.dtype)
     own = pltpu.VMEM((left.shape[0], tokens.shape[1]), left.dtype)
-    parts = 8 if tokens.shape[0] % 128 == 0 else 1
+    parts = 4 if tokens.shape[0] % 64 == 0 else 1
     return pl.pallas_call(
         functools.partial(stage_kernel, parts),
         in_specs=[FAR] * 5 + [WHOLE] * len(after),
@@ -503,7 +503,7 @@
     right_theirs = flip(right_mine, 0)
     (back,) = project(right_own, right_mine, cotangent, False, (), ())
     left_first = after_all(left_first, back)
-    (hidden,) = project(left_own, left_first, tokens, False, (), (cotangent,))
+    (hidden,) = project(left_own, left_first, tokens, False, (), ())
     left_second = after_all(left_second, hidden)
     left_mine = jnp.concatenate([left_first, left_second], axis=1)
     left_theirs = flip(left_mine, 0)
@@ -512,7 +512,7 @@
         (right_own, right_theirs, cotangent, back), (),
     )
     parts, parts_send = project(
-        left_own, left_theirs, tokens, True, (hidden, full, back), (cotangent,)
+        left_own, left_theirs, tokens, True, (hidden, full, back), ()
     )
     parts_got = lax.ppermute(parts_send, "tensor", SWAP)
 

time: 40.4 us -> 40.4 us (level)
  no operation moved by 1% of the time
where the time goes in v12:
time: 40.4 us; the launch traced here: 40.2 us
  starting transfers between devices  20.1 us (50%)
  Pallas kernels  16.6 us (41%)
  waiting for transfers between devices  2.71 us (7%)
  between operations  0.82 us (2%)
    ppermute x11, starting transfers between devices, flip(): lax.ppermute(value, 'dp', [(i, i ^ mask) for i in range(lax.axis_size('dp...  9.5 us
    pallas_call x1, Pallas kernels, stage(): pl.pallas_call(functools.partial(stage_kernel, parts), in_specs=[FAR] * 5...  4.96 us
    ppermute x2, starting transfers between devices, across(): return lax.ppermute(value, ('dp', 'tensor'), pairs)  4.44 us
    pallas_call x1, Pallas kernels, spread(): pl.pallas_call(functools.partial(spread_kernel, chunk), in_specs=[WHOLE]...  3.18 us
    ppermute x2, starting transfers between devices, two_panels(): lax.ppermute(w, 'tensor', SWAP)  3.11 us
    pallas_call x3, Pallas kernels, project(): pl.pallas_call(functools.partial(project_kernel, flipped, low, len(others...  2.64 us
    ppermute x1, waiting for transfers between devices, two_panels(): parts_got = lax.ppermute(parts_send, 'tensor', SWAP)  2.28 us
    ppermute x1, starting transfers between devices, two_panels(): parts_got = lax.ppermute(parts_send, 'tensor', SWAP)  1.81 us
  transfers between devices with their start and end apart: 17, of which 4 were waited for; matrix products, arithmetic and copies ran while one was open for 0% of the time, Pallas kernels for 33%

profile of v12, /device:TPU:0, one launch (start us, length us, event | category | flops | bytes accessed | tf_op | source)
XLA Modules:
  0.0 40.2 jit_solution(10846459553419645154)
XLA Ops:
  0.6 1.1 %pick.1 = (bf16[24,4096]{1,0:T(8,128)(2,1)S(1)}, bf16[24,2048]{1,0:T(8,128)(2,1)S(1)}, bf16[24,2048]{1,0:T(8,128)(2,1)S(1)}) custom-call(bf16[24,16384]{1,0:T(8,128)(2,1)} %refs_0_.1, bf16[24,16384]{1,0:T(8,128)(2,1)} %refs_2_.1), custom_call_target="tpu_custom_call" | custom-call | flops 1 | bytes 1 | tf_op jit(solution)/shard_map/pick/pallas_call | solution.py:437
  1.7 3.0 %collective-permute-start.1 = (bf16[24,4096]{1,0:T(8,128)(2,1)S(1)}, bf16[24,4096]{1,0:T(8,128)(2,1)S(1)}, u32[]{:S(2)}, u32[]{:S(2)}) collective-permute-start(bf16[24,4096]{1,0:T(8,128)(2,1)S(1)} %get-tuple-element.37.refs_4_), channel_id=1, source_target_pairs={{0,1},{1,0},{2,3},{3,2},{4,5},{5,4},{6,7},{7,6},{8,9},{9,8},{10,11... | collective-permute-start | bytes 589832 | tf_op jit(solution)/shard_map/ppermute | solution.py:497
  4.8 0.1 collective-permute-start
  4.8 0.8 %collective-permute-start.2 = (bf16[24,2048]{1,0:T(8,128)(2,1)S(1)}, bf16[24,2048]{1,0:T(8,128)(2,1)S(1)}, u32[]{:S(2)}, u32[]{:S(2)}) collective-permute-start(bf16[24,2048]{1,0:T(8,128)(2,1)S(1)} %get-tuple-element.39.refs_6_), channel_id=1, source_target_pairs={{0,3},{1,2},{2,1},{3,0},{4,7},{5,6},{6,5},{7,4},{8,11},{9,10},{10,... | collective-permute-start | bytes 294920 | tf_op jit(solution)/shard_map/ppermute | solution.py:147
  5.7 5.0 %stage.1 = (bf16[24,8192]{1,0:T(8,128)(2,1)S(1)}, bf16[384,8192]{1,0:T(8,128)(2,1)S(1)}, bf16[24,8192]{1,0:T(8,128)(2,1)S(1)}, bf16[384,8192]{1,0:T(8,128)(2,1)S(1)}, f32[8,128]{1,0:T(8,128)S(1)}) custom-call(s32[2]{0:T(128)} %rank.1, bf16[24,16384]{1,0:T(8,128)(2,1)} %refs_0_.1, bf16[384,8192]{1,0:T(8,128)(2,1)} %refs_1_.1, bf16[24,16384]{1,0:T(8,128)(2,1)} %refs_2_.1, ...), custom_call_target="tpu_custom_call" | custom-call | flops 1 | bytes 1 | tf_op jit(solution)/shard_map/stage/pallas_call | solution.py:130
  10.6 1.3 %collective-permute-start.4 = (bf16[24,4096]{1,0:T(8,128)(2,1)S(1)}, bf16[24,4096]{1,0:T(8,128)(2,1)S(1)}, u32[]{:S(2)}, u32[]{:S(2)}) collective-permute-start(bf16[24,4096]{1,0:T(8,128)(2,1)S(1)} %collective-permute-done.1.refs_1_), channel_id=1, source_target_pairs={{0,2},{2,0},{4,6},{6,4},{8,10},{10,8},{12,14},{14,12},{16,18},{18,... | collective-permute-start | bytes 589832 | tf_op jit(solution)/shard_map/ppermute | solution.py:93
  11.9 1.0 %project.3.refs_7_ = f32[64,384]{1,0:T(8,128)S(1)} custom-call(bf16[24,8192]{1,0:T(8,128)(2,1)S(1)} %get-tuple-element.42.refs_0_.refs_4_, bf16[24,4096]{1,0:T(8,128)(2,1)S(1)} %collective-permute-done.1.refs_1_, bf16[384,8192]{1,0:T(8,128)(2,1)S(1)} %get-tuple-element.44.refs_2_.refs_6_.cotangent), custom_call_target="tpu_custom_call" | custom-call | flops 1 | bytes 1 | tf_op jit(solution)/shard_map/project/pallas_call | solution.py:226
  13.0 0.6 %project.4.refs_3_ = f32[64,384]{1,0:T(8,128)S(1)} custom-call(bf16[24,8192]{1,0:T(8,128)(2,1)S(1)} %get-tuple-element.41.refs_0_.own, bf16[24,2048]{1,0:T(8,128)(2,1)S(1)} %collective-permute-done.refs_1_, bf16[384,8192]{1,0:T(8,128)(2,1)S(1)} %get-tuple-element.46.refs_2_.tokens), custom_call_target="tpu_custom_call" | custom-call | flops 1 | bytes 1 | tf_op jit(solution)/shard_map/project/pallas_call | solution.py:226
  13.6 0.2 collective-permute-start.3
  13.8 1.4 %project_two.1 = (f32[64,384]{1,0:T(8,128)S(1)}, f32[64,384]{1,0:T(8,128)S(1)}) custom-call(bf16[24,8192]{1,0:T(8,128)(2,1)S(1)} %get-tuple-element.41.refs_0_.own, bf16[24,2048]{1,0:T(8,128)(2,1)S(1)} %collective-permute-done.2.refs_1_, bf16[384,8192]{1,0:T(8,128)(2,1)S(1)} %get-tuple-element.46.refs_2_.tokens, f32[64,384]{1,0:T(8,128)S(1)} %project.4.refs_3_, ...), custom_call_target="tpu_custom_call" | custom-call | flops 1 | bytes 1 | tf_op jit(solution)/shard_map/project_two/pallas_call | solution.py:190
  15.2 1.0 %project.5 = (f32[56,384]{1,0:T(8,128)S(1)}, bf16[56,384]{1,0:T(8,128)(2,1)S(1)}) custom-call(bf16[24,8192]{1,0:T(8,128)(2,1)S(1)} %get-tuple-element.41.refs_0_.own, bf16[24,4096]{1,0:T(8,128)(2,1)S(1)} %collective-permute-done.3.refs_1_.theirs, bf16[384,8192]{1,0:T(8,128)(2,1)S(1)} %get-tuple-element.46.refs_2_.tokens, ...), custom_call_target="tpu_custom_call" | custom-call | flops 1 | bytes 1 | tf_op jit(solution)/shard_map/project/pallas_call | solution.py:226
  16.2 1.8 %collective-permute-start.5 = (bf16[56,384]{1,0:T(8,128)(2,1)S(1)}, bf16[56,384]{1,0:T(8,128)(2,1)S(1)}, u32[]{:S(2)}, u32[]{:S(2)}) collective-permute-start(bf16[56,384]{1,0:T(8,128)(2,1)S(1)} %get-tuple-element.51), channel_id=1, source_target_pairs={{0,1},{1,0},{2,3},{3,2},{4,5},{5,4},{6,7},{7,6},{8,9},{9,8},{10,11... | collective-permute-start | bytes 129032 | tf_op jit(solution)/shard_map/ppermute | solution.py:517
  18.0 2.3 %collective-permute-done.5.got.parts_got = bf16[56,384]{1,0:T(8,128)(2,1)S(1)} collective-permute-done((bf16[56,384]{1,0:T(8,128)(2,1)S(1)}, bf16[56,384]{1,0:T(8,128)(2,1)S(1)}, u32[]{:S(2)}, u32[]{:S(2)}) %collective-permute-start.5) | collective-permute-done | bytes 43040 | tf_op jit(solution)/shard_map/ppermute | solution.py:517
  20.3 0.6 %gradient.2.refs_0_ = bf16[4,56,512]{2,1,0:T(8,128)(2,1)S(1)} custom-call(f32[56,384]{1,0:T(8,128)S(1)} %get-tuple-element.50.parts, bf16[56,384]{1,0:T(8,128)(2,1)S(1)} %collective-permute-done.5.got.parts_got, bf16[384,8192]{1,0:T(8,128)(2,1)S(1)} %get-tuple-element.46.refs_2_.tokens, bf16[384,8192]{1,0:T(8,128)(2,1)S(1)} %get-tuple-element.44.refs_2_.refs_6_.cotangent), custom_call_target="tpu_custom_call" | custom-call | flops 1 | bytes 1 | tf_op jit(solution)/shard_map/gradient/pallas_call | solution.py:289
  21.0 0.1 collective-permute-start.7
  21.0 1.2 %gradient.3 = (f32[4,56,512]{2,1,0:T(8,128)S(1)}, bf16[4,56,512]{2,1,0:T(8,128)(2,1)S(1)}) custom-call(f32[56,384]{1,0:T(8,128)S(1)} %get-tuple-element.50.parts, bf16[56,384]{1,0:T(8,128)(2,1)S(1)} %collective-permute-done.5.got.parts_got, bf16[384,8192]{1,0:T(8,128)(2,1)S(1)} %get-tuple-element.46.refs_2_.tokens, ...), custom_call_target="tpu_custom_call" | custom-call | flops 1 | bytes 1 | tf_op jit(solution)/shard_map/gradient/pallas_call | solution.py:289
  22.2 0.5 %collective-permute-start.6 = (bf16[4,56,512]{2,1,0:T(8,128)(2,1)S(1)}, bf16[4,56,512]{2,1,0:T(8,128)(2,1)S(1)}, u32[]{:S(2)}, u32[]{:S(2)}) collective-permute-start(bf16[4,56,512]{2,1,0:T(8,128)(2,1)S(1)} %get-tuple-element.52), channel_id=1, source_target_pairs={{0,2},{2,0},{4,6},{6,4},{8,10},{10,8},{12,14},{14,12},{16,18},{18,... | collective-permute-start | bytes 688136 | tf_op jit(solution)/shard_map/ppermute | solution.py:93
  22.8 2.8 %collective-permute-start.11 = (bf16[56,512]{1,0:T(8,128)(2,1)S(1)}, bf16[56,512]{1,0:T(8,128)(2,1)S(1)}, u32[]{:S(2)}, u32[]{:S(2)}) collective-permute-start(bf16[56,512]{1,0:T(8,128)(2,1)S(1)} %get-tuple-element.62), channel_id=1, source_target_pairs={{0,12},{2,14},{4,8},{6,10},{8,4},{10,6},{12,0},{14,2},{16,28},{18,... | collective-permute-start | bytes 172040 | tf_op jit(solution)/shard_map/ppermute | solution.py:93
  25.6 0.5 %collective-permute-start.13 = (bf16[56,512]{1,0:T(8,128)(2,1)S(1)}, bf16[56,512]{1,0:T(8,128)(2,1)S(1)}, u32[]{:S(2)}, u32[]{:S(2)}) collective-permute-start(bf16[56,512]{1,0:T(8,128)(2,1)S(1)} %get-tuple-element.63), channel_id=1, source_target_pairs={{0,8},{2,10},{4,12},{6,14},{8,0},{10,2},{12,4},{14,6},{16,24},{18,... | collective-permute-start | bytes 172040 | tf_op jit(solution)/shard_map/ppermute | solution.py:93
  26.0 0.3 collective-permute-start.12
  26.4 0.7 %last_quarter.1 = (f32[56,512]{1,0:T(8,128)S(1)}, bf16[56,512]{1,0:T(8,128)(2,1)S(1)}, bf16[56,512]{1,0:T(8,128)(2,1)S(1)}, bf16[56,512]{1,0:T(8,128)(2,1)S(1)}) custom-call(f32[56,384]{1,0:T(8,128)S(1)} %get-tuple-element.50.parts, bf16[56,384]{1,0:T(8,128)(2,1)S(1)} %collective-permute-done.5.got.parts_got, ...), custom_call_target="tpu_custom_call" | custom-call | flops 1 | bytes 1 | tf_op jit(solution)/shard_map/last_quarter/pallas_call | solution.py:477
  27.0 2.8 %collective-permute-start.8 = (bf16[56,512]{1,0:T(8,128)(2,1)S(1)}, bf16[56,512]{1,0:T(8,128)(2,1)S(1)}, u32[]{:S(2)}, u32[]{:S(2)}) collective-permute-start(bf16[56,512]{1,0:T(8,128)(2,1)S(1)} %get-tuple-element.56), channel_id=1, source_target_pairs={{0,12},{2,14},{4,8},{6,10},{8,4},{10,6},{12,0},{14,2},{16,28},{18,... | collective-permute-start | bytes 172040 | tf_op jit(solution)/shard_map/ppermute | solution.py:93
  29.8 0.5 %collective-permute-start.9 = (bf16[56,512]{1,0:T(8,128)(2,1)S(1)}, bf16[56,512]{1,0:T(8,128)(2,1)S(1)}, u32[]{:S(2)}, u32[]{:S(2)}) collective-permute-start(bf16[56,512]{1,0:T(8,128)(2,1)S(1)} %get-tuple-element.57), channel_id=1, source_target_pairs={{0,4},{2,6},{4,0},{6,2},{8,12},{10,14},{12,8},{14,10},{16,20},{18,... | collective-permute-start | bytes 172040 | tf_op jit(solution)/shard_map/ppermute | solution.py:93
  30.4 0.2 collective-permute-start.10
  30.6 0.2 collective-permute-done.12.refs_1_
  30.9 3.6 %collective-permute-start.14 = (bf16[2,24,512]{2,1,0:T(8,128)(2,1)S(1)}, bf16[2,24,512]{2,1,0:T(8,128)(2,1)S(1)}, u32[]{:S(2)}, u32[]{:S(2)}) collective-permute-start(bf16[2,24,512]{2,1,0:T(8,128)(2,1)S(1)} %get-tuple-element.64), channel_id=1, source_target_pairs={{0,17},{1,16},{2,19},{3,18},{4,21},{5,20},{6,23},{7,22},{8,25},{9,... | collective-permute-start | bytes 147464 | tf_op jit(solution)/shard_map/ppermute | solution.py:147
  34.5 0.3 collective-permute-start.15
  34.9 0.1 collective-permute-done.10.refs_2_
  35.0 1.2 %collective-permute-start.16 = (bf16[2,24,512]{2,1,0:T(8,128)(2,1)S(1)}, bf16[2,24,512]{2,1,0:T(8,128)(2,1)S(1)}, u32[]{:S(2)}, u32[]{:S(2)}) collective-permute-start(bf16[2,24,512]{2,1,0:T(8,128)(2,1)S(1)} %get-tuple-element.59.after), channel_id=1, source_target_pairs={{0,1},{1,0},{2,3},{3,2},{4,5},{5,4},{6,7},{7,6},{8,9},{9,8},{10,11... | collective-permute-start | bytes 147464 | tf_op jit(solution)/shard_map/ppermute | solution.py:531
  36.2 3.2 %spread.1 = bf16[384,8192]{1,0:T(8,128)(2,1)} custom-call(f32[8,128]{1,0:T(8,128)S(1)} %get-tuple-element.40.refs_4_.full, f32[56,384]{1,0:T(8,128)S(1)} %get-tuple-element.50.parts, bf16[56,384]{1,0:T(8,128)(2,1)S(1)} %collective-permute-done.5.got.parts_got, bf16[24,8192]{1,0:T(8,128)(2,1)S(1)} %get-tuple-element.41.refs_0_.own, ...), custom_call_target="tpu_custom_call" | custom-call | flops 10000000000 | bytes 100000000 | tf_op jit(solution)/shard_map/spread/pallas_call | solution.py:330
  39.4 0.1 collective-permute-done.15.refs_1_
  39.5 0.7 %place.1 = (f32[24,2,1,512]{3,2,1,0:T(1,128)}, f32[24,2,1,512]{3,2,1,0:T(1,128)}) custom-call(f32[2,24,512]{2,1,0:T(8,128)S(1)} %gather.3.held, f32[2,24,512]{2,1,0:T(8,128)S(1)} %gather.2.far, bf16[2,24,512]{2,1,0:T(8,128)(2,1)S(1)} %collective-permute-done.16.got), custom_call_target="tpu_custom_call" | custom-call | flops 1 | bytes 1 | tf_op jit(solution)/shard_map/place/pallas_call | solution.py:403
  (20 shorter events, 0.2 us)
Async XLA Ops:
  1.7 8.9 %collective-permute-start.1 = (bf16[24,4096]{1,0:T(8,128)(2,1)S(1)}, bf16[24,4096]{1,0:T(8,128)(2,1)S(1)}, u32[]{:S(2)}, u32[]{:S(2)}) collective-permute-start(bf16[24,4096]{1,0:T(8,128)(2,1)S(1)} %get-tuple-element.37.refs_4_), channel_id=1, source_target_pairs={{0,1},{1,0},{2,3},{3,2},{4,5},{5,4},{6,7},{7,6},{8,9},{9,8},{10,11... | collective-permute-start | bytes 589832 | tf_op jit(solution)/shard_map/ppermute | solution.py:497
  4.8 8.2 %collective-permute-start = (bf16[24,2048]{1,0:T(8,128)(2,1)S(1)}, bf16[24,2048]{1,0:T(8,128)(2,1)S(1)}, u32[]{:S(2)}, u32[]{:S(2)}) collective-permute-start(bf16[24,2048]{1,0:T(8,128)(2,1)S(1)} %get-tuple-element.38.refs_5_), channel_id=1, source_target_pairs={{0,1},{1,0},{2,3},{3,2},{4,5},{5,4},{6,7},{7,6},{8,9},{9,8},{10,11... | collective-permute-start | bytes 294920 | tf_op jit(solution)/shard_map/ppermute | solution.py:497
  4.8 8.8 %collective-permute-start.2 = (bf16[24,2048]{1,0:T(8,128)(2,1)S(1)}, bf16[24,2048]{1,0:T(8,128)(2,1)S(1)}, u32[]{:S(2)}, u32[]{:S(2)}) collective-permute-start(bf16[24,2048]{1,0:T(8,128)(2,1)S(1)} %get-tuple-element.39.refs_6_), channel_id=1, source_target_pairs={{0,3},{1,2},{2,1},{3,0},{4,7},{5,6},{6,5},{7,4},{8,11},{9,10},{10,... | collective-permute-start | bytes 294920 | tf_op jit(solution)/shard_map/ppermute | solution.py:147
  10.6 3.1 %collective-permute-start.4 = (bf16[24,4096]{1,0:T(8,128)(2,1)S(1)}, bf16[24,4096]{1,0:T(8,128)(2,1)S(1)}, u32[]{:S(2)}, u32[]{:S(2)}) collective-permute-start(bf16[24,4096]{1,0:T(8,128)(2,1)S(1)} %collective-permute-done.1.refs_1_), channel_id=1, source_target_pairs={{0,2},{2,0},{4,6},{6,4},{8,10},{10,8},{12,14},{14,12},{16,18},{18,... | collective-permute-start | bytes 589832 | tf_op jit(solution)/shard_map/ppermute | solution.py:93
  13.6 1.6 %collective-permute-start.3 = (bf16[24,4096]{1,0:T(8,128)(2,1)S(1)}, bf16[24,4096]{1,0:T(8,128)(2,1)S(1)}, u32[]{:S(2)}, u32[]{:S(2)}) collective-permute-start(bf16[24,4096]{1,0:T(8,128)(2,1)S(1)} %constant_dynamic-update-slice_fusion.mine), channel_id=1, source_target_pairs={{0,2},{2,0},{4,6},{6,4},{8,10},{10,8},{12,14},{14,12},{16,18},{18,... | collective-permute-start | bytes 589832 | tf_op jit(solution)/shard_map/ppermute | solution.py:93
  16.2 4.1 %collective-permute-start.5 = (bf16[56,384]{1,0:T(8,128)(2,1)S(1)}, bf16[56,384]{1,0:T(8,128)(2,1)S(1)}, u32[]{:S(2)}, u32[]{:S(2)}) collective-permute-start(bf16[56,384]{1,0:T(8,128)(2,1)S(1)} %get-tuple-element.51), channel_id=1, source_target_pairs={{0,1},{1,0},{2,3},{3,2},{4,5},{5,4},{6,7},{7,6},{8,9},{9,8},{10,11... | collective-permute-start | bytes 129032 | tf_op jit(solution)/shard_map/ppermute | solution.py:517
  21.0 1.8 %collective-permute-start.7 = (bf16[4,56,512]{2,1,0:T(8,128)(2,1)S(1)}, bf16[4,56,512]{2,1,0:T(8,128)(2,1)S(1)}, u32[]{:S(2)}, u32[]{:S(2)}) collective-permute-start(bf16[4,56,512]{2,1,0:T(8,128)(2,1)S(1)} %gradient.2.refs_0_), channel_id=1, source_target_pairs={{0,2},{2,0},{4,6},{6,4},{8,10},{10,8},{12,14},{14,12},{16,18},{18,... | collective-permute-start | bytes 688136 | tf_op jit(solution)/shard_map/ppermute | solution.py:93
  22.2 4.2 %collective-permute-start.6 = (bf16[4,56,512]{2,1,0:T(8,128)(2,1)S(1)}, bf16[4,56,512]{2,1,0:T(8,128)(2,1)S(1)}, u32[]{:S(2)}, u32[]{:S(2)}) collective-permute-start(bf16[4,56,512]{2,1,0:T(8,128)(2,1)S(1)} %get-tuple-element.52), channel_id=1, source_target_pairs={{0,2},{2,0},{4,6},{6,4},{8,10},{10,8},{12,14},{14,12},{16,18},{18,... | collective-permute-start | bytes 688136 | tf_op jit(solution)/shard_map/ppermute | solution.py:93
  22.8 7.6 %collective-permute-start.11 = (bf16[56,512]{1,0:T(8,128)(2,1)S(1)}, bf16[56,512]{1,0:T(8,128)(2,1)S(1)}, u32[]{:S(2)}, u32[]{:S(2)}) collective-permute-start(bf16[56,512]{1,0:T(8,128)(2,1)S(1)} %get-tuple-element.62), channel_id=1, source_target_pairs={{0,12},{2,14},{4,8},{6,10},{8,4},{10,6},{12,0},{14,2},{16,28},{18,... | collective-permute-start | bytes 172040 | tf_op jit(solution)/shard_map/ppermute | solution.py:93
  25.6 5.0 %collective-permute-start.13 = (bf16[56,512]{1,0:T(8,128)(2,1)S(1)}, bf16[56,512]{1,0:T(8,128)(2,1)S(1)}, u32[]{:S(2)}, u32[]{:S(2)}) collective-permute-start(bf16[56,512]{1,0:T(8,128)(2,1)S(1)} %get-tuple-element.63), channel_id=1, source_target_pairs={{0,8},{2,10},{4,12},{6,14},{8,0},{10,2},{12,4},{14,6},{16,24},{18,... | collective-permute-start | bytes 172040 | tf_op jit(solution)/shard_map/ppermute | solution.py:93
  26.0 4.8 %collective-permute-start.12 = (bf16[56,512]{1,0:T(8,128)(2,1)S(1)}, bf16[56,512]{1,0:T(8,128)(2,1)S(1)}, u32[]{:S(2)}, u32[]{:S(2)}) collective-permute-start(bf16[56,512]{1,0:T(8,128)(2,1)S(1)} %get-tuple-element.54.after), channel_id=1, source_target_pairs={{0,4},{2,6},{4,0},{6,2},{8,12},{10,14},{12,8},{14,10},{16,20},{18,... | collective-permute-start | bytes 172040 | tf_op jit(solution)/shard_map/ppermute | solution.py:93
  27.0 7.8 %collective-permute-start.8 = (bf16[56,512]{1,0:T(8,128)(2,1)S(1)}, bf16[56,512]{1,0:T(8,128)(2,1)S(1)}, u32[]{:S(2)}, u32[]{:S(2)}) collective-permute-start(bf16[56,512]{1,0:T(8,128)(2,1)S(1)} %get-tuple-element.56), channel_id=1, source_target_pairs={{0,12},{2,14},{4,8},{6,10},{8,4},{10,6},{12,0},{14,2},{16,28},{18,... | collective-permute-start | bytes 172040 | tf_op jit(solution)/shard_map/ppermute | solution.py:93
  29.8 5.0 %collective-permute-start.9 = (bf16[56,512]{1,0:T(8,128)(2,1)S(1)}, bf16[56,512]{1,0:T(8,128)(2,1)S(1)}, u32[]{:S(2)}, u32[]{:S(2)}) collective-permute-start(bf16[56,512]{1,0:T(8,128)(2,1)S(1)} %get-tuple-element.57), channel_id=1, source_target_pairs={{0,4},{2,6},{4,0},{6,2},{8,12},{10,14},{12,8},{14,10},{16,20},{18,... | collective-permute-start | bytes 172040 | tf_op jit(solution)/shard_map/ppermute | solution.py:93
  30.4 4.5 %collective-permute-start.10 = (bf16[56,512]{1,0:T(8,128)(2,1)S(1)}, bf16[56,512]{1,0:T(8,128)(2,1)S(1)}, u32[]{:S(2)}, u32[]{:S(2)}) collective-permute-start(bf16[56,512]{1,0:T(8,128)(2,1)S(1)} %get-tuple-element.58), channel_id=1, source_target_pairs={{0,8},{2,10},{4,12},{6,14},{8,0},{10,2},{12,4},{14,6},{16,24},{18,... | collective-permute-start | bytes 172040 | tf_op jit(solution)/shard_map/ppermute | solution.py:93
  30.9 8.5 %collective-permute-start.14 = (bf16[2,24,512]{2,1,0:T(8,128)(2,1)S(1)}, bf16[2,24,512]{2,1,0:T(8,128)(2,1)S(1)}, u32[]{:S(2)}, u32[]{:S(2)}) collective-permute-start(bf16[2,24,512]{2,1,0:T(8,128)(2,1)S(1)} %get-tuple-element.64), channel_id=1, source_target_pairs={{0,17},{1,16},{2,19},{3,18},{4,21},{5,20},{6,23},{7,22},{8,25},{9,... | collective-permute-start | bytes 147464 | tf_op jit(solution)/shard_map/ppermute | solution.py:147
  34.5 5.0 %collective-permute-start.15 = (bf16[2,24,512]{2,1,0:T(8,128)(2,1)S(1)}, bf16[2,24,512]{2,1,0:T(8,128)(2,1)S(1)}, u32[]{:S(2)}, u32[]{:S(2)}) collective-permute-start(bf16[2,24,512]{2,1,0:T(8,128)(2,1)S(1)} %get-tuple-element.65), channel_id=1, source_target_pairs={{0,16},{2,18},{4,20},{6,22},{8,24},{10,26},{12,28},{14,30},{16,0},... | collective-permute-start | bytes 147464 | tf_op jit(solution)/shard_map/ppermute | solution.py:93
  35.0 4.5 %collective-permute-start.16 = (bf16[2,24,512]{2,1,0:T(8,128)(2,1)S(1)}, bf16[2,24,512]{2,1,0:T(8,128)(2,1)S(1)}, u32[]{:S(2)}, u32[]{:S(2)}) collective-permute-start(bf16[2,24,512]{2,1,0:T(8,128)(2,1)S(1)} %get-tuple-element.59.after), channel_id=1, source_target_pairs={{0,1},{1,0},{2,3},{3,2},{4,5},{5,4},{6,7},{7,6},{8,9},{9,8},{10,11... | collective-permute-start | bytes 147464 | tf_op jit(solution)/shard_map/ppermute | solution.py:531
